TPU v7x, 32 devices: a whole 2x2x4 slice. The times are simulated.
32 devices in a mesh: dp: 2 (over x), ctx: 4 (over z), wa: 4 (over y, core).
Axes of the slice: x: 2, y: 2, z: 4, core: 2. Of those that a mesh axis runs over, the one named last changes fastest.
Arguments:
- tokens: bfloat16 [2, 2048, 2048], P('dp', ('ctx', 'wa')), may hold values from -6 to 6
- doc_starts: int32 [2, 8], P('dp'), may hold values from 0 to 2047, as said below
- out_grad: bfloat16 [2, 2048, 2048], P('dp', ('ctx', 'wa')), may hold values from -6 to 6
- attn_gain: bfloat16 [2048], P(('ctx', 'wa')), may hold values from 0.25 to 1.75
- w_query: bfloat16 [2048, 2048], P(('ctx', 'wa')), may hold values from -0.125 to 0.125
- w_key: bfloat16 [2048, 512], P(('ctx', 'wa')), may hold values from -0.125 to 0.125
- w_value: bfloat16 [2048, 512], P(('ctx', 'wa')), may hold values from -0.125 to 0.125
- q_gain: bfloat16 [64], P(('ctx', 'wa')), may hold values from 0.25 to 1.75
- k_gain: bfloat16 [64], P(('ctx', 'wa')), may hold values from 0.25 to 1.75
- w_out: bfloat16 [2048, 2048], P(('ctx', 'wa')), may hold values from -0.75 to 0.75
- ffn_gain: bfloat16 [2048], P(('ctx', 'wa')), may hold values from 0.25 to 1.75
- w_gate: bfloat16 [2048, 8192], P(('ctx', 'wa')), may hold values from -0.125 to 0.125
- w_up: bfloat16 [2048, 8192], P(('ctx', 'wa')), may hold values from -0.125 to 0.125
- w_down: bfloat16 [8192, 2048], P(('ctx', 'wa')), may hold values from -0.0625 to 0.0625
Outputs:
- layer_out: bfloat16 [2, 2048, 2048], P('dp', ('ctx', 'wa'))
- input_grad: bfloat16 [2, 2048, 2048], P('dp', ('ctx', 'wa'))
- attn_gain_grad: float32 [2048], P(('ctx', 'wa'))
- w_query_grad: float32 [2048, 2048], P(('ctx', 'wa'))
- w_key_grad: float32 [2048, 512], P(('ctx', 'wa'))
- w_value_grad: float32 [2048, 512], P(('ctx', 'wa'))
- q_gain_grad: float32 [64], P(('ctx', 'wa'))
- k_gain_grad: float32 [64], P(('ctx', 'wa'))
- w_out_grad: float32 [2048, 2048], P(('ctx', 'wa'))
- ffn_gain_grad: float32 [2048], P(('ctx', 'wa'))
- w_gate_grad: float32 [2048, 8192], P(('ctx', 'wa'))
- w_up_grad: float32 [2048, 8192], P(('ctx', 'wa'))
- w_down_grad: float32 [8192, 2048], P(('ctx', 'wa'))
Inputs may be any that keep to these rules, and one draw needn't show every extreme that they name: `doc_starts`: for each stream the 8 document starts rise strictly from 0; every document has at most 1024 tokens and one document of each stream has exactly 1024.
All inputs are finite; a program needn't handle non-finite values.
Results may differ from a plain program's by a relative error of at most 0.019.
Values may be sent and summed in bfloat16 or wider, within the bound.
A program may use at most 576 MiB of HBM per device.

v0:
```python
from functools import partial

import jax
import jax.numpy as jnp
from jax import lax
from jax.sharding import PartitionSpec as P

H = 32
KV = 8
HD = 64
FF = 8192


EPS = 1e-05
THETA = 1000000.0


def stored_positions(index, tok_rows, n_ctx, n_wa):
    device = index // tok_rows
    local = index % tok_rows
    half_rows = tok_rows // 2
    ctx_part = device // n_wa
    wa_part = device % n_wa
    span_idx = jnp.where(local < half_rows, ctx_part, 2 * n_ctx - 1 - ctx_part)
    return span_idx * (half_rows * n_wa) + wa_part * half_rows + local % half_rows


def segments(position, starts):
    return jnp.sum((starts[None, :] <= position[:, None]).astype(jnp.int32), axis=1) - 1


def rms_norm(values, gain):
    return values * lax.rsqrt(jnp.mean(values * values, axis=-1, keepdims=True) + EPS) * gain


def rotate(values, position):
    half_dim = HD // 2
    frequency = THETA ** (-2.0 * jnp.arange(half_dim, dtype=jnp.float32) / HD)
    angles = position.astype(jnp.float32)[:, None] * frequency[None, :]
    cosine = jnp.cos(angles)[:, None, :]
    sine_part = jnp.sin(angles)[:, None, :]
    first_half = values[..., :half_dim]
    second_half = values[..., half_dim:]
    return jnp.concatenate(
        [
            first_half * cosine - second_half * sine_part,
            second_half * cosine + first_half * sine_part,
        ],
        axis=-1,
    )


def prepare(query_raw, key_raw, query_gain, key_gain, position):
    return (
        rotate(rms_norm(query_raw, query_gain), position),
        rotate(rms_norm(key_raw, key_gain), position),
    )


def per_device(
    tokens,
    doc_starts,
    out_grad,
    attn_gain,
    w_query,
    w_key,
    w_value,
    q_gain,
    k_gain,
    w_out,
    ffn_gain,
    w_gate,
    w_up,
    w_down,
):
    n_ctx = lax.axis_size("ctx")
    n_wa = lax.axis_size("wa")
    tok_rows = tokens.shape[1]
    stream_len = tok_rows * n_ctx * n_wa
    key_width = min(1024, stream_len)
    key_blocks = stream_len // key_width
    groups = H // KV
    scale = HD ** (-0.5)
    first_row = (lax.axis_index("ctx") * n_wa + lax.axis_index("wa")) * tok_rows
    own_pos = stored_positions(
        first_row + jnp.arange(tok_rows, dtype=jnp.int32), tok_rows, n_ctx, n_wa
    )
    starts = doc_starts[0]
    own_seg = segments(own_pos, starts)
    key_pos = stored_positions(jnp.arange(stream_len, dtype=jnp.int32), tok_rows, n_ctx, n_wa)
    key_seg = segments(key_pos, starts)
    residual = tokens[0].astype(jnp.float32)
    attn_set = (
        lax.all_gather(attn_gain, ("ctx", "wa"), axis=0, tiled=True),
        lax.all_gather(w_query, ("ctx", "wa"), axis=0, tiled=True),
        lax.all_gather(w_key, ("ctx", "wa"), axis=0, tiled=True),
        lax.all_gather(w_value, ("ctx", "wa"), axis=0, tiled=True),
        lax.all_gather(q_gain, ("ctx", "wa"), axis=0, tiled=True),
        lax.all_gather(k_gain, ("ctx", "wa"), axis=0, tiled=True),
        lax.all_gather(w_out, ("ctx", "wa"), axis=0, tiled=True),
    )
    g_attn, wq_full, wk_full, wv_full, gq_full, gk_full, wo_full = attn_set
    attn_gain32 = g_attn.astype(jnp.float32)
    qgain32 = gq_full.astype(jnp.float32)
    kgain32 = gk_full.astype(jnp.float32)
    normed_one = rms_norm(residual, attn_gain32).astype(jnp.bfloat16)
    query_raw = jnp.dot(normed_one, wq_full, preferred_element_type=jnp.float32).reshape(
        tok_rows, H, HD
    )
    key_raw = jnp.dot(normed_one, wk_full, preferred_element_type=jnp.float32).reshape(
        tok_rows, KV, HD
    )
    value_b = jnp.dot(normed_one, wv_full, preferred_element_type=jnp.float32).astype(jnp.bfloat16)
    query_rot, key_rot = prepare(query_raw, key_raw, qgain32, kgain32, own_pos)
    query_b = query_rot.astype(jnp.bfloat16).reshape(tok_rows, KV, groups, HD)
    key_b = key_rot.astype(jnp.bfloat16).reshape(tok_rows, KV * HD)
    all_keys, all_values = (
        lax.all_gather(key_b, ("ctx", "wa"), axis=0, tiled=True),
        lax.all_gather(value_b, ("ctx", "wa"), axis=0, tiled=True),
    )

    def key_block(keys_in, values_in, block_idx):
        begin = block_idx * key_width
        key_part = lax.dynamic_slice_in_dim(keys_in, begin, key_width, 0).reshape(key_width, KV, HD)
        value_part = lax.dynamic_slice_in_dim(values_in, begin, key_width, 0).reshape(
            key_width, KV, HD
        )
        pos_part = lax.dynamic_slice_in_dim(key_pos, begin, key_width, 0)
        seg_part = lax.dynamic_slice_in_dim(key_seg, begin, key_width, 0)
        scores = (
            jnp.einsum("rkgd,tkd->kgrt", query_b, key_part, preferred_element_type=jnp.float32)
            * scale
        )
        allowed = (
            (seg_part[None, :] == own_seg[:, None]) & (pos_part[None, :] <= own_pos[:, None])
        )[None, None]
        return (scores, allowed, key_part, value_part)

    def stat_step(block_idx, carry):
        row_max, row_total = carry
        scores, allowed, key_part, value_part = key_block(all_keys, all_values, block_idx)
        masked = jnp.where(allowed, scores, -1e30)
        new_max = jnp.maximum(row_max, jnp.max(masked, axis=-1))
        fresh = jnp.sum(jnp.where(allowed, jnp.exp(masked - new_max[..., None]), 0.0), axis=-1)
        return (new_max, row_total * jnp.exp(row_max - new_max) + fresh)

    stat_init = (
        jnp.full((KV, groups, tok_rows), -1e30, jnp.float32),
        jnp.zeros((KV, groups, tok_rows), jnp.float32),
    )
    row_max, row_total = lax.fori_loop(0, key_blocks, stat_step, stat_init)

    def out_step(block_idx, summed):
        scores, allowed, key_part, value_part = key_block(all_keys, all_values, block_idx)
        probability = (
            jnp.where(allowed, jnp.exp(scores - row_max[..., None]), 0.0) / row_total[..., None]
        )
        return summed + jnp.einsum(
            "kgrt,tkd->rkgd",
            probability.astype(jnp.bfloat16),
            value_part,
            preferred_element_type=jnp.float32,
        )

    attended = lax.fori_loop(
        0, key_blocks, out_step, jnp.zeros((tok_rows, KV, groups, HD), jnp.float32)
    )
    attended_b = attended.reshape(tok_rows, H * HD).astype(jnp.bfloat16)
    middle = residual + jnp.dot(attended_b, wo_full, preferred_element_type=jnp.float32)
    ffn_set = (
        lax.all_gather(ffn_gain, ("ctx", "wa"), axis=0, tiled=True),
        lax.all_gather(w_gate, ("ctx", "wa"), axis=0, tiled=True),
        lax.all_gather(w_up, ("ctx", "wa"), axis=0, tiled=True),
        lax.all_gather(w_down, ("ctx", "wa"), axis=0, tiled=True),
    )
    g_ffn, wg_full, wu_full, wd_full = ffn_set
    ffn_gain32 = g_ffn.astype(jnp.float32)
    normed_two = rms_norm(middle, ffn_gain32).astype(jnp.bfloat16)
    gate_act = jnp.dot(normed_two, wg_full, preferred_element_type=jnp.float32)
    up_act = jnp.dot(normed_two, wu_full, preferred_element_type=jnp.float32)
    sigmoid_gate = jax.nn.sigmoid(gate_act)
    silu_gate = gate_act * sigmoid_gate
    hidden = (silu_gate * up_act).astype(jnp.bfloat16)
    layer_out = (middle + jnp.dot(hidden, wd_full, preferred_element_type=jnp.float32)).astype(
        jnp.bfloat16
    )
    g_ffn, wg_full, wu_full, wd_full = (
        lax.all_gather(ffn_gain, ("ctx", "wa"), axis=0, tiled=True),
        lax.all_gather(w_gate, ("ctx", "wa"), axis=0, tiled=True),
        lax.all_gather(w_up, ("ctx", "wa"), axis=0, tiled=True),
        lax.all_gather(w_down, ("ctx", "wa"), axis=0, tiled=True),
    )
    d_out = out_grad[0].astype(jnp.float32)
    d_out_b = d_out.astype(jnp.bfloat16)
    d_hidden = jnp.einsum("rd,fd->rf", d_out_b, wd_full, preferred_element_type=jnp.float32)
    d_gate = (d_hidden * up_act * (sigmoid_gate * (1.0 + gate_act * (1.0 - sigmoid_gate)))).astype(
        jnp.bfloat16
    )
    d_up = (d_hidden * silu_gate).astype(jnp.bfloat16)
    d_normed_two = jnp.einsum(
        "rf,df->rd", d_gate, wg_full, preferred_element_type=jnp.float32
    ) + jnp.einsum("rf,df->rd", d_up, wu_full, preferred_element_type=jnp.float32)
    norm_out, norm_back = jax.vjp(rms_norm, middle, ffn_gain32)
    d_middle_part, d_ffn_gain = norm_back(d_normed_two)
    d_middle = d_out + d_middle_part
    gate_up = jnp.concatenate([d_gate, d_up], axis=1)
    part_rows = normed_two
    in_grad = lax.psum_scatter(
        jnp.einsum("rc,rf->cf", part_rows, gate_up, preferred_element_type=jnp.float32),
        ("ctx", "wa"),
        scatter_dimension=0,
        tiled=True,
    )
    part_rows = hidden
    down_grad = lax.psum_scatter(
        jnp.einsum("rc,rd->cd", part_rows, d_out_b, preferred_element_type=jnp.float32),
        ("ctx", "wa"),
        scatter_dimension=0,
        tiled=True,
    )
    g_attn, wq_full, wk_full, wv_full, gq_full, gk_full, wo_full = (
        lax.all_gather(attn_gain, ("ctx", "wa"), axis=0, tiled=True),
        lax.all_gather(w_query, ("ctx", "wa"), axis=0, tiled=True),
        lax.all_gather(w_key, ("ctx", "wa"), axis=0, tiled=True),
        lax.all_gather(w_value, ("ctx", "wa"), axis=0, tiled=True),
        lax.all_gather(q_gain, ("ctx", "wa"), axis=0, tiled=True),
        lax.all_gather(k_gain, ("ctx", "wa"), axis=0, tiled=True),
        lax.all_gather(w_out, ("ctx", "wa"), axis=0, tiled=True),
    )
    d_branch = d_middle.astype(jnp.bfloat16)
    wo_grad = jnp.einsum("re,rd->ed", attended_b, d_branch, preferred_element_type=jnp.float32)
    d_attended = jnp.einsum(
        "rd,ed->re", d_branch, wo_full, preferred_element_type=jnp.float32
    ).astype(jnp.bfloat16)
    d_att4 = d_attended.reshape(tok_rows, KV, groups, HD)
    delta = jnp.einsum("rkgd,rkgd->kgr", d_att4.astype(jnp.float32), attended)

    def back_step(d_query, block_idx):
        scores, allowed, key_part, value_part = key_block(all_keys, all_values, block_idx)
        probability = (
            jnp.where(allowed, jnp.exp(scores - row_max[..., None]), 0.0) / row_total[..., None]
        )
        d_prob = jnp.einsum(
            "rkgd,tkd->kgrt", d_att4, value_part, preferred_element_type=jnp.float32
        )
        d_scores = (probability * (d_prob - delta[..., None])).astype(jnp.bfloat16)
        d_query = (
            d_query
            + jnp.einsum("kgrt,tkd->rkgd", d_scores, key_part, preferred_element_type=jnp.float32)
            * scale
        )
        d_key_part = (
            jnp.einsum("kgrt,rkgd->tkd", d_scores, query_b, preferred_element_type=jnp.float32)
            * scale
        )
        d_value_part = jnp.einsum(
            "kgrt,rkgd->tkd",
            probability.astype(jnp.bfloat16),
            d_att4,
            preferred_element_type=jnp.float32,
        )
        return (
            d_query,
            (d_key_part.reshape(key_width, KV * HD), d_value_part.reshape(key_width, KV * HD)),
        )

    d_query, (d_keys, d_values) = lax.scan(
        back_step, jnp.zeros((tok_rows, KV, groups, HD), jnp.float32), jnp.arange(key_blocks)
    )
    d_key_own, d_value_own = (
        lax.psum_scatter(
            d_keys.reshape(stream_len, KV * HD), ("ctx", "wa"), scatter_dimension=0, tiled=True
        ),
        lax.psum_scatter(
            d_values.reshape(stream_len, KV * HD), ("ctx", "wa"), scatter_dimension=0, tiled=True
        ),
    )
    prep_out, prep_back = jax.vjp(
        partial(prepare, position=own_pos), query_raw, key_raw, qgain32, kgain32
    )
    d_query_raw, d_key_raw, d_qgain, d_kgain = prep_back(
        (d_query.reshape(tok_rows, H, HD), d_key_own.reshape(tok_rows, KV, HD))
    )
    dq_b = d_query_raw.reshape(tok_rows, H * HD).astype(jnp.bfloat16)
    dk_b = d_key_raw.reshape(tok_rows, KV * HD).astype(jnp.bfloat16)
    dv_b = d_value_own.astype(jnp.bfloat16)
    d_normed_one = (
        jnp.einsum("re,de->rd", dq_b, wq_full, preferred_element_type=jnp.float32)
        + jnp.einsum("re,de->rd", dk_b, wk_full, preferred_element_type=jnp.float32)
        + jnp.einsum("re,de->rd", dv_b, wv_full, preferred_element_type=jnp.float32)
    )
    first_out, first_back = jax.vjp(rms_norm, residual, attn_gain32)
    d_res_part, d_attn_gain = first_back(d_normed_one)
    input_grad = (d_middle + d_res_part).astype(jnp.bfloat16)
    wq_grad = jnp.einsum("rc,re->ce", normed_one, dq_b, preferred_element_type=jnp.float32)
    wk_grad = jnp.einsum("rc,re->ce", normed_one, dk_b, preferred_element_type=jnp.float32)
    wv_grad = jnp.einsum("rc,re->ce", normed_one, dv_b, preferred_element_type=jnp.float32)
    attn_terms = (d_attn_gain, wq_grad, wk_grad, wv_grad, d_qgain, d_kgain, d_ffn_gain, wo_grad)
    attn_shards = (
        lax.psum_scatter(attn_terms[0], ("ctx", "wa"), scatter_dimension=0, tiled=True),
        lax.psum_scatter(attn_terms[1], ("ctx", "wa"), scatter_dimension=0, tiled=True),
        lax.psum_scatter(attn_terms[2], ("ctx", "wa"), scatter_dimension=0, tiled=True),
        lax.psum_scatter(attn_terms[3], ("ctx", "wa"), scatter_dimension=0, tiled=True),
        lax.psum_scatter(attn_terms[4], ("ctx", "wa"), scatter_dimension=0, tiled=True),
        lax.psum_scatter(attn_terms[5], ("ctx", "wa"), scatter_dimension=0, tiled=True),
        lax.psum_scatter(attn_terms[6], ("ctx", "wa"), scatter_dimension=0, tiled=True),
        lax.psum_scatter(attn_terms[7], ("ctx", "wa"), scatter_dimension=0, tiled=True),
    )
    wo_shard = attn_shards[7]
    summed = (
        lax.psum(attn_shards[0].astype(jnp.bfloat16), "dp").astype(jnp.float32),
        lax.psum(attn_shards[1].astype(jnp.bfloat16), "dp").astype(jnp.float32),
        lax.psum(attn_shards[2].astype(jnp.bfloat16), "dp").astype(jnp.float32),
        lax.psum(attn_shards[3].astype(jnp.bfloat16), "dp").astype(jnp.float32),
        lax.psum(attn_shards[4].astype(jnp.bfloat16), "dp").astype(jnp.float32),
        lax.psum(attn_shards[5].astype(jnp.bfloat16), "dp").astype(jnp.float32),
        lax.psum(wo_shard.astype(jnp.bfloat16), "dp").astype(jnp.float32),
        lax.psum(attn_shards[6].astype(jnp.bfloat16), "dp").astype(jnp.float32),
        lax.psum(in_grad[:, :FF].astype(jnp.bfloat16), "dp").astype(jnp.float32),
        lax.psum(in_grad[:, FF:].astype(jnp.bfloat16), "dp").astype(jnp.float32),
        lax.psum(down_grad.astype(jnp.bfloat16), "dp").astype(jnp.float32),
    )
    return (layer_out[None], input_grad[None]) + tuple(summed)


def solution(mesh):
    placed = (
        P("dp", ("ctx", "wa"), None),
        P("dp", None),
        P("dp", ("ctx", "wa"), None),
        P(("ctx", "wa")),
        P(("ctx", "wa"), None),
        P(("ctx", "wa"), None),
        P(("ctx", "wa"), None),
        P(("ctx", "wa")),
        P(("ctx", "wa")),
        P(("ctx", "wa"), None),
        P(("ctx", "wa")),
        P(("ctx", "wa"), None),
        P(("ctx", "wa"), None),
        P(("ctx", "wa"), None),
    )
    return jax.shard_map(
        per_device,
        mesh=mesh,
        in_specs=placed,
        out_specs=(
            P("dp", ("ctx", "wa"), None),
            P("dp", ("ctx", "wa"), None),
            P(("ctx", "wa")),
            P(("ctx", "wa"), None),
            P(("ctx", "wa"), None),
            P(("ctx", "wa"), None),
            P(("ctx", "wa")),
            P(("ctx", "wa")),
            P(("ctx", "wa"), None),
            P(("ctx", "wa")),
            P(("ctx", "wa"), None),
            P(("ctx", "wa"), None),
            P(("ctx", "wa"), None),
        ),
        check_vma=False,
    )
```

profile of v0, /device:TPU:0, one launch (start us, length us, event | category | flops | bytes accessed | tf_op | source)
XLA Modules:
  0.0 3768.8 jit_solution(4658109753739868440)
XLA Ops:
  8.8 23.3 all-gather
  33.3 21.0 all-gather.12.cloned.1.call-done
  59.7 31.8 all-reduce.11
  91.7 5.0 all-gather.16.cloned.1.call-done
  104.9 19.4 all-gather.1
  125.1 14.6 all-gather.14.cloned.1.call-done
  139.7 4.0 copy.67
  143.7 71.8 %all-gather.20.cloned.1.call-done = bf16[2048,2048]{1,0:T(8,128)(2,1)} async-done(((bf16[128,2048]{1,0:T(8,128)(2,1)}), bf16[2048,2048]{1,0:T(8,128)(2,1)}) %all-gather.20.cloned.1.call-update) | async-done | bytes 8388624 | tf_op jit(solution)/shard_map/all_gather | solution.py:95
  215.4 12.3 copy.66
  227.8 5.9 multiply_reduce_fusion.5
  234.9 22.6 all-gather.18.cloned.1.call-done
  257.5 34.4 while.45
  259.2 7.5 fusion.196
  266.7 8.1 select_reduce_fusion.2
  276.6 7.3 fusion.196
  283.9 8.0 select_reduce_fusion.2
  291.9 20.9 while.46
  292.0 3.1 constant_dynamic-slice_fusion.10
  295.5 6.9 fusion.202
  305.5 7.2 fusion.202
  314.2 19.2 all-gather.22.cloned.1.call-done
  333.4 4.8 multiply_reduce_fusion.4
  338.3 163.0 %all-gather.24.cloned.1.call-done = bf16[2048,8192]{1,0:T(8,128)(2,1)} async-done(((bf16[128,8192]{1,0:T(8,128)(2,1)}), bf16[2048,8192]{1,0:T(8,128)(2,1)}) %all-gather.24.cloned.1.call-update) | async-done | bytes 33554448 | tf_op jit(solution)/shard_map/all_gather | solution.py:172
  501.3 18.4 fusion.120
  519.8 151.2 %all-gather.26.cloned.1.call-done = bf16[2048,8192]{1,0:T(8,128)(2,1)} async-done(((bf16[128,8192]{1,0:T(8,128)(2,1)}), bf16[2048,8192]{1,0:T(8,128)(2,1)}) %all-gather.26.cloned.1.call-update) | async-done | bytes 33554448 | tf_op jit(solution)/shard_map/all_gather | solution.py:173
  671.0 18.5 fusion.121
  689.5 151.2 %all-gather.28.cloned.1.call-done = bf16[8192,2048]{1,0:T(8,128)(2,1)} async-done(((bf16[512,2048]{1,0:T(8,128)(2,1)}), bf16[8192,2048]{1,0:T(8,128)(2,1)}) %all-gather.28.cloned.1.call-update) | async-done | bytes 33554448 | tf_op jit(solution)/shard_map/all_gather | solution.py:174
  840.7 21.2 multiply_convert_fusion
  861.9 17.4 fusion.122
  879.3 18.0 multiply_reduce_fusion
  899.9 6.4 convolution_convert_fusion
  908.5 105.8 %while.47 = (s32[]{:T(128)}, f32[128,8,4,64]{0,3,2,1:T(8,128)}, f32[2,1024,512]{2,1,0:T(8,128)}, f32[2,1024,512]{2,1,0:T(8,128)}, s32[2]{0:T(128)S(1)}, /*index=...) while((s32[]{:T(128)}, f32[128,8,4,64]{0,3,2,1:T(8,128)}, ...), condition=%wide.region_14.15_spmd.clone, body=%wide.region_13.14_spmd.clone.sunk | while | flops 2719620096 | bytes 116729656 | solution.py:267
  911.6 8.2 fusion.214
  921.1 9.7 fusion.215
  930.7 5.9 fusion.216
  936.7 8.4 fusion.217
  946.9 7.3 bitcast_multiply_fusion.2
  954.3 3.1 copy.116
  957.3 4.0 constant_dynamic-update-slice_fusion.3
  964.3 8.2 fusion.214
  973.8 9.7 fusion.215
  983.5 6.1 fusion.216
  989.6 8.4 fusion.217
  999.9 7.3 bitcast_multiply_fusion.2
  1010.3 4.0 constant_dynamic-update-slice_fusion.3
  1015.2 72.2 %reduce-scatter.9.cloned.1.call-done = f32[128,512]{1,0:T(8,128)} async-done(((f32[2048,512]{1,0:T(8,128)}), f32[128,512]{1,0:T(8,128)}) %reduce-scatter.9.cloned.1.call-update) | async-done | bytes 262160 | tf_op jit(solution)/shard_map/reduce_scatter | solution.py:271
  1092.2 70.8 %reduce-scatter.11.cloned.1.call-done = f32[128,512]{1,0:T(8,128)} async-done(((f32[2048,512]{1,0:T(8,128)}), f32[128,512]{1,0:T(8,128)}) %reduce-scatter.11.cloned.1.call-update) | async-done | bytes 262160 | tf_op jit(solution)/shard_map/reduce_scatter | solution.py:274
  1163.0 3.8 fusion.79
  1169.4 8.9 fusion.73
  1179.7 8.5 fusion.76
  1189.9 23.9 fusion.63
  1214.9 48.2 %fusion.38 = f32[2048,16384]{1,0:T(8,128)} fusion(bf16[128,2048]{1,0:T(8,128)(2,1)S(1)} %copy-done.16, bf16[128,8192]{1,0:T(8,128)(2,1)} %get-tuple-element.779, bf16[128,8192]{1,0:T(8,128)(2,1)} %get-tuple-element.780), kind=kOutput, calls=%fused_computation.99 | convolution fusion | flops 8598323200 | bytes 138936320 | tf_op jit(solution)/shard_map/rc,rf->cf/dot_general | solution.py:209
  1265.0 50.5 %reduce-scatter.17.cloned.1.call-done = f32[128,512]{1,0:T(8,128)} async-done(((f32[2048,512]{1,0:T(8,128)}), f32[128,512]{1,0:T(8,128)}) %reduce-scatter.17.cloned.1.call-update) | async-done | bytes 262160 | tf_op jit(solution)/shard_map/reduce_scatter | solution.py:303
  1317.1 180.0 %reduce-scatter.13.cloned.1.call-done = f32[128,2048]{1,0:T(8,128)} async-done(((f32[2048,2048]{1,0:T(8,128)}), f32[128,2048]{1,0:T(8,128)}) %reduce-scatter.13.cloned.1.call-update) | async-done | bytes 1048592 | tf_op jit(solution)/shard_map/reduce_scatter | solution.py:301
  1499.2 179.4 %reduce-scatter.19.cloned.1.call-done = f32[128,2048]{1,0:T(8,128)} async-done(((f32[2048,2048]{1,0:T(8,128)}), f32[128,2048]{1,0:T(8,128)}) %reduce-scatter.19.cloned.1.call-update) | async-done | bytes 1048592 | tf_op jit(solution)/shard_map/reduce_scatter | solution.py:307
  1680.7 638.0 %reduce-scatter.23.cloned.1.call-done = f32[512,2048]{1,0:T(8,128)} async-done(((f32[8192,2048]{1,0:T(8,128)}), f32[512,2048]{1,0:T(8,128)}) %reduce-scatter.23.cloned.1.call-update) | async-done | bytes 4194320 | tf_op jit(solution)/shard_map/reduce_scatter | solution.py:215
  2318.7 3.8 convert_element_type.237
  2322.5 1234.9 %reduce-scatter.21.cloned.1.call-done = f32[128,16384]{1,0:T(8,128)} async-done(((f32[2048,16384]{1,0:T(8,128)}), f32[128,16384]{1,0:T(8,128)}) %reduce-scatter.21.cloned.1.call-update) | async-done | bytes 8388624 | tf_op jit(solution)/shard_map/reduce_scatter | solution.py:208
  3557.4 3.9 convert.23
  3564.9 6.6 fusion.123
  3571.5 14.0 fusion.44
  3588.3 59.5 %all-reduce.10 = (bf16[2048]{0:T(1024)(128)(2,1)S(1)}, bf16[64]{0:T(256)(128)(2,1)S(1)}, bf16[64]{0:T(256)(128)(2,1)S(1)}, bf16[2048]{0:T(1024)(128)(2,1)S(1)}) all-reduce(f32[2048]{0:T(1024)S(1)} %get-tuple-element.680, f32[64]{0:T(128)S(1)} %copy-done.58, ...), channel_id=4, replica_groups=mesh['dp'=2,'ctx'=4,'wa'=4] {'ctx','wa'}, use_global_device_ids=true, to_apply=%region_21.22.clone | all-reduce | flops 4224 | bytes 25344
  3648.2 4.9 all-reduce.12
  3656.3 90.1 %all-reduce.16.cloned.1.call-done = (bf16[128,2048]{1,0:T(8,128)(2,1)}, bf16[128,512]{1,0:T(8,128)(2,1)}, bf16[128,512]{1,0:T(8,128)(2,1)}, bf16[128,2048]{1,0:T...) async-done(((bf16[128,2048]{1,0:T(8,128)(2,1)}, bf16[128,512]{1,0:T(8,128)(2,1)}, bf16[128,512]{1,0:T(8,128)(2,1)}, ...) | async-done | bytes 7602192 | tf_op jit(solution)/shard_map/psum | solution.py:312
  (289 shorter events, 88.2 us)
Async XLA Ops:
  7.2 50.7 %copy-start.56 = (u32[32]{0:T(128)S(1)}, u32[32]{0:T(128)}, u32[]{:S(2)}) copy-start(u32[32]{0:T(128)} %constant.294) | copy-start | bytes 388
  7.2 52.0 %copy-start.63 = (bf16[4]{0:T(256)(128)(2,1)S(1)}, bf16[4]{0:T(256)(128)(2,1)}, u32[]{:S(2)}) copy-start(bf16[4]{0:T(256)(128)(2,1)} %param.28) | copy-start | bytes 28
  7.2 52.2 %copy-start.64 = (bf16[4]{0:T(256)(128)(2,1)S(1)}, bf16[4]{0:T(256)(128)(2,1)}, u32[]{:S(2)}) copy-start(bf16[4]{0:T(256)(128)(2,1)} %param.27) | copy-start | bytes 28
  7.2 47.1 %all-gather.12.cloned.1.call-start = ((), (), s32[]{:S(2)}) async-start(), calls=%async_computation.8 | async-start | bytes 2228224 | tf_op jit(solution)/shard_map/all_gather | solution.py:97
  7.9 88.7 %all-gather.16.cloned.1.call-start = ((), (), s32[]{:S(2)}) async-start(), calls=%async_computation.10 | async-start | bytes 2228224 | tf_op jit(solution)/shard_map/all_gather | solution.py:96
  8.7 90.9 %copy-start.2 = (bf16[1,128,2048]{2,1,0:T(8,128)(2,1)S(1)}, bf16[1,128,2048]{2,1,0:T(8,128)(2,1)}, u32[]{:S(2)}) copy-start(bf16[1,128,2048]{2,1,0:T(8,128)(2,1)} %param.20) | copy-start | bytes 1572868
  8.7 131.0 %all-gather.14.cloned.1.call-start = ((), (), s32[]{:S(2)}) async-start(), calls=%async_computation.9 | async-start | bytes 2228224 | tf_op jit(solution)/shard_map/all_gather | solution.py:119
  32.1 195.7 %copy-start.32 = (f32[16,1,128]{2,1,0:T(1,128)}, f32[16,1,128]{2,1,0:T(1,128)S(1)}, u32[]{:S(2)}) copy-start(f32[16,1,128]{2,1,0:T(1,128)S(1)} %convert_element_type.240) | copy-start | bytes 24580
  33.3 58.2 %copy-start.59 = (f32[128]{0:T(128)}, f32[128]{0:T(128)S(1)}, u32[]{:S(2)}) copy-start(f32[128]{0:T(128)S(1)} %fusion.53) | copy-start | bytes 1540
  33.3 194.5 %copy-start.47 = (f32[128]{0:T(128)}, f32[128]{0:T(128)S(1)}, u32[]{:S(2)}) copy-start(f32[128]{0:T(128)S(1)} %fusion.110) | copy-start | bytes 1540
  57.3 158.2 %all-gather.20.cloned.1.call-start = ((), (), s32[]{:S(2)}) async-start(), calls=%async_computation.12 | async-start | bytes 8912896 | tf_op jit(solution)/shard_map/all_gather | solution.py:95
  57.9 199.6 %all-gather.18.cloned.1.call-start = ((), (), s32[]{:S(2)}) async-start(), calls=%async_computation.11 | async-start | bytes 2228224 | tf_op jit(solution)/shard_map/all_gather | solution.py:118
  91.5 10.5 copy-start.52
  91.7 143.0 %copy-start.35 = (f32[128,32]{0,1:T(8,128)}, f32[128,32]{0,1:T(8,128)S(1)}, u32[]{:S(2)}) copy-start(f32[128,32]{0,1:T(8,128)S(1)} %get-tuple-element.792) | copy-start | bytes 49156
  91.7 143.0 %copy-start.37 = (f32[128,32]{0,1:T(8,128)}, f32[128,32]{0,1:T(8,128)S(1)}, u32[]{:S(2)}) copy-start(f32[128,32]{0,1:T(8,128)S(1)} %get-tuple-element.793) | copy-start | bytes 49156
  100.4 4.4 copy-start.50
  100.4 4.5 copy-start.61
  100.4 24.5 copy-start.62
  101.9 231.4 %all-gather.22.cloned.1.call-start = ((), (), s32[]{:S(2)}) async-start(), calls=%async_computation.13 | async-start | bytes 8912896 | tf_op jit(solution)/shard_map/all_gather | solution.py:100
  102.5 398.8 %all-gather.24.cloned.1.call-start = ((), (), s32[]{:S(2)}) async-start(), calls=%async_computation.14 | async-start | bytes 35651584 | tf_op jit(solution)/shard_map/all_gather | solution.py:172
  103.3 567.7 %all-gather.26.cloned.1.call-start = ((), (), s32[]{:S(2)}) async-start(), calls=%async_computation.15 | async-start | bytes 35651584 | tf_op jit(solution)/shard_map/all_gather | solution.py:173
  104.0 736.7 %all-gather.28.cloned.1.call-start = ((), (), s32[]{:S(2)}) async-start(), calls=%async_computation.16 | async-start | bytes 35651584 | tf_op jit(solution)/shard_map/all_gather | solution.py:174
  104.7 982.6 %reduce-scatter.9.cloned.1.call-start = ((), (), s32[]{:S(2)}) async-start(), calls=%async_computation.17 | async-start | bytes 4456448 | tf_op jit(solution)/shard_map/reduce_scatter | solution.py:271
  104.9 128.8 %copy-start.54 = (f32[64]{0:T(128)}, f32[64]{0:T(128)S(1)}, u32[]{:S(2)}) copy-start(f32[64]{0:T(128)S(1)} %convert_element_type.201) | copy-start | bytes 772
  233.7 23.8 copy-start.41
  291.9 41.4 %copy-start.3 = (bf16[1,128,2048]{2,1,0:T(8,128)(2,1)S(1)}, bf16[1,128,2048]{2,1,0:T(8,128)(2,1)}, u32[]{:S(2)}) copy-start(bf16[1,128,2048]{2,1,0:T(8,128)(2,1)} %param.20) | copy-start | bytes 1572868
  314.2 24.0 copy-start.18
  333.4 4.8 copy-start.43
  338.1 559.2 %copy-start.6 = (f32[128,2048]{1,0:T(8,128)}, f32[128,2048]{1,0:T(8,128)S(1)}, u32[]{:S(2)}) copy-start(f32[128,2048]{1,0:T(8,128)S(1)} %get-tuple-element.801) | copy-start | bytes 3145732
  338.3 332.7 %copy-start.15 = (bf16[128,2048]{1,0:T(8,128)(2,1)}, bf16[128,2048]{1,0:T(8,128)(2,1)S(1)}, u32[]{:S(2)}) copy-start(bf16[128,2048]{1,0:T(8,128)(2,1)S(1)} %multiply_convert_fusion.3) | copy-start | bytes 1572868
  519.8 321.0 %copy-start.23 = (bf16[1,128,2048]{2,1,0:T(8,128)(2,1)S(1)}, bf16[1,128,2048]{2,1,0:T(8,128)(2,1)}, u32[]{:S(2)}) copy-start(bf16[1,128,2048]{2,1,0:T(8,128)(2,1)} %param.22) | copy-start | bytes 1572868
  861.9 17.4 copy-start.14
  899.9 7.4 copy-start.20
  954.2 3.1 copy-start
  1007.2 3.1 copy-start
  1014.3 74.1 %copy-start.36 = (f32[128,32]{0,1:T(8,128)S(1)}, f32[128,32]{0,1:T(8,128)}, u32[]{:S(2)}) copy-start(f32[128,32]{0,1:T(8,128)} %copy-done.35) | copy-start | bytes 49156
  1014.3 74.1 %copy-start.38 = (f32[128,32]{0,1:T(8,128)S(1)}, f32[128,32]{0,1:T(8,128)}, u32[]{:S(2)}) copy-start(f32[128,32]{0,1:T(8,128)} %copy-done.37) | copy-start | bytes 49156
  1014.3 74.2 %copy-start.22 = (f32[128,8,64]{0,2,1:T(8,128)S(1)}, f32[128,8,64]{0,2,1:T(8,128)}, u32[]{:S(2)}) copy-start(f32[128,8,64]{0,2,1:T(8,128)} %copy-done.21) | copy-start | bytes 786436
  1014.3 74.2 %copy-start.45 = (f32[128,8]{0,1:T(8,128)S(1)}, f32[128,8]{0,1:T(8,128)}, u32[]{:S(2)}) copy-start(f32[128,8]{0,1:T(8,128)} %copy-done.44) | copy-start | bytes 12292
  1014.3 74.2 %copy-start.53 = (f32[64]{0:T(128)S(1)}, f32[64]{0:T(128)}, u32[]{:S(2)}) copy-start(f32[64]{0:T(128)} %copy-done.52) | copy-start | bytes 772
  1014.3 74.8 %copy-start.51 = (f32[128,8]{0,1:T(8,128)S(1)}, f32[128,8]{0,1:T(8,128)}, u32[]{:S(2)}) copy-start(f32[128,8]{0,1:T(8,128)} %copy-done.50) | copy-start | bytes 12292
  1014.4 74.9 %copy-start.4 = (bf16[1,128,2048]{2,1,0:T(8,128)(2,1)S(1)}, bf16[1,128,2048]{2,1,0:T(8,128)(2,1)}, u32[]{:S(2)}) copy-start(bf16[1,128,2048]{2,1,0:T(8,128)(2,1)} %param.20) | copy-start | bytes 1572868
  1014.4 74.9 %copy-start.33 = (f32[16,1,128]{2,1,0:T(1,128)S(1)}, f32[16,1,128]{2,1,0:T(1,128)}, u32[]{:S(2)}) copy-start(f32[16,1,128]{2,1,0:T(1,128)} %copy-done.32) | copy-start | bytes 24580
  1014.4 74.9 %copy-start.48 = (f32[128]{0:T(128)S(1)}, f32[128]{0:T(128)}, u32[]{:S(2)}) copy-start(f32[128]{0:T(128)} %copy-done.47) | copy-start | bytes 1540
  1014.4 148.7 %reduce-scatter.11.cloned.1.call-start = ((), (), s32[]{:S(2)}) async-start(), calls=%async_computation.18 | async-start | bytes 4456448 | tf_op jit(solution)/shard_map/reduce_scatter | solution.py:274
  1015.1 248.3 %reduce-scatter.15.cloned.1.call-start = ((), (), s32[]{:S(2)}) async-start(), calls=%async_computation.20 | async-start | bytes 4456448 | tf_op jit(solution)/shard_map/reduce_scatter | solution.py:302
  1089.3 2.9 copy-start.29
  1092.2 74.9 %copy-start.1 = (f32[128,8,4,64]{0,3,2,1:T(8,128)S(1)}, f32[128,8,4,64]{0,3,2,1:T(8,128)}, u32[]{:S(2)}) copy-start(f32[128,8,4,64]{0,3,2,1:T(8,128)} %get-tuple-element.439) | copy-start | bytes 3145732
  1092.2 223.3 %reduce-scatter.17.cloned.1.call-start = ((), (), s32[]{:S(2)}) async-start(), calls=%async_computation.21 | async-start | bytes 4456448 | tf_op jit(solution)/shard_map/reduce_scatter | solution.py:303
  1166.8 330.3 %reduce-scatter.13.cloned.1.call-start = ((), (), s32[]{:S(2)}) async-start(), calls=%async_computation.19 | async-start | bytes 17825792 | tf_op jit(solution)/shard_map/reduce_scatter | solution.py:301
  1178.3 500.3 %reduce-scatter.19.cloned.1.call-start = ((), (), s32[]{:S(2)}) async-start(), calls=%async_computation.22 | async-start | bytes 17825792 | tf_op jit(solution)/shard_map/reduce_scatter | solution.py:307
  1188.3 1130.4 %reduce-scatter.23.cloned.1.call-start = ((), (), s32[]{:S(2)}) async-start(), calls=%async_computation.24 | async-start | bytes 71303168 | tf_op jit(solution)/shard_map/reduce_scatter | solution.py:215
  1213.9 2343.6 %reduce-scatter.21.cloned.1.call-start = ((), (), s32[]{:S(2)}) async-start(), calls=%async_computation.23 | async-start | bytes 142606336 | tf_op jit(solution)/shard_map/reduce_scatter | solution.py:208
  1263.1 2483.4 %all-reduce.16.cloned.1.call-start = ((), (), s32[]{:S(2)}) async-start(), calls=%async_computation.25 | async-start | bytes 15204352 | tf_op jit(solution)/shard_map/psum | solution.py:312
  3564.9 6.6 copy-start.7
  3571.5 14.0 copy-start.17
  3571.5 14.0 copy-start.30
  3585.6 2.7 copy-start.46
  3585.6 2.7 copy-start.57
  3585.6 2.7 copy-start.58
  3585.6 69.6 %copy-start.60 = (f32[128]{0:T(128)S(1)}, f32[128]{0:T(128)}, u32[]{:S(2)}) copy-start(f32[128]{0:T(128)} %copy-done.59) | copy-start | bytes 1540
  3585.6 69.6 %copy-start.10 = (f32[128,2048]{1,0:T(8,128)S(1)}, f32[128,2048]{1,0:T(8,128)}, u32[]{:S(2)}) copy-start(f32[128,2048]{1,0:T(8,128)} %copy-done.8) | copy-start | bytes 3145732
  3746.4 7.8 copy-start.27
  3750.3 6.3 copy-start.26
  (20 other events, 27.7 us)
Sparse Core Ops, SparseCore 0:
  10.2 44.0 all-gather.11
  56.5 40.0 all-gather.15
  99.4 40.3 all-gather.13
  141.7 73.6 all-gather.19
  218.0 39.4 all-gather.17
  259.5 73.8 all-gather.21
  335.0 166.2 all-gather.23
  502.9 168.0 all-gather.25
  672.6 168.0 all-gather.27
  1014.5 72.7 reduce-scatter.8
  1091.7 71.3 reduce-scatter.10
  1167.3 71.8 reduce-scatter.14
  1244.2 71.3 reduce-scatter.16
  1319.5 177.5 reduce-scatter.12
  1501.1 177.4 reduce-scatter.18
  1682.7 635.9 reduce-scatter.22
  2322.8 1234.6 reduce-scatter.20
  3563.7 182.6 all-reduce.15
where the time goes:
time: 3770 us
  waiting for transfers between devices  3140 us (83%)
  matrix products  341 us (9%)
  blocking collectives  139 us (4%)
  local copies, waits for them, and re-layouts  65.8 us (2%)
  other arithmetic  61.9 us (2%)
    reduce_scatter x1, waiting for transfers between devices, per_device(): lax.psum_scatter(jnp.einsum('rc,rf->cf', part_rows, gate_up, preferred_el...  1230 us
    reduce_scatter x1, waiting for transfers between devices, per_device(): lax.psum_scatter(jnp.einsum('rc,rd->cd', part_rows, d_out_b, preferred_el...  638 us
    reduce_scatter x1, waiting for transfers between devices, per_device(): lax.psum_scatter(attn_terms[1], ('ctx', 'wa'), scatter_dimension=0, tiled...  180 us
    reduce_scatter x1, waiting for transfers between devices, per_device(): lax.psum_scatter(attn_terms[7], ('ctx', 'wa'), scatter_dimension=0, tiled...  179 us
    all_gather x1, waiting for transfers between devices, per_device(): lax.all_gather(w_gate, ('ctx', 'wa'), axis=0, tiled=True)  163 us
    all_gather x1, waiting for transfers between devices, per_device(): lax.all_gather(w_down, ('ctx', 'wa'), axis=0, tiled=True)  151 us
    all_gather x1, waiting for transfers between devices, per_device(): lax.all_gather(w_up, ('ctx', 'wa'), axis=0, tiled=True)  151 us
    unnamed x2, blocking collectives  91.3 us
  transfers between devices with their start and end apart: 18, of which 17 were waited for; matrix products, arithmetic and copies ran while one was open for 7% of the time, Pallas kernels for 0%

commit v1 on v0

--- a/solution.py
+++ b/solution.py
@@ -3,6 +3,8 @@
 import jax
 import jax.numpy as jnp
 from jax import lax
+from jax.experimental import pallas as pl
+from jax.experimental.pallas import tpu as pltpu
 from jax.sharding import PartitionSpec as P
 
 H = 32
@@ -323,7 +325,342 @@
     return (layer_out[None], input_grad[None]) + tuple(summed)
 
 
+AXES = ("ctx", "wa")
+LANES = 2 * HD
+ROWS_BLOCK = 256
+LOG2E = 1.4426950408889634
+F32 = jnp.float32
+BF16 = jnp.bfloat16
+
+
+def to_position(rows, n_ctx, n_wa):
+    half = rows.shape[0] // (2 * n_ctx * n_wa)
+    parts = rows.reshape(n_ctx, n_wa, 2, half, -1)
+    ordered = jnp.concatenate([parts[:, :, 0], jnp.flip(parts[:, :, 1], axis=0)], axis=0)
+    return ordered.reshape(rows.shape)
+
+
+def to_stored(rows, n_ctx, n_wa):
+    half = rows.shape[0] // (2 * n_ctx * n_wa)
+    parts = rows.reshape(2 * n_ctx, n_wa, half, -1)
+    paired = jnp.stack([parts[:n_ctx], jnp.flip(parts[n_ctx:], axis=0)], axis=2)
+    return paired.reshape(rows.shape)
+
+
+def low_key(starts, row):
+    first = jnp.int32(0)
+    for doc in range(starts.shape[1]):
+        begin = starts[0, doc]
+        first = jnp.where(begin <= row, begin, first)
+    return first
+
+
+def block_mask(starts, q_begin, k_begin, bq, bk):
+    row = q_begin + lax.broadcasted_iota(jnp.int32, (bq, 1), 0)
+    first = low_key(starts, row)
+    col = k_begin + lax.broadcasted_iota(jnp.int32, (1, bk), 1)
+    return (col >= first) & (col <= row)
+
+
+def attend_kernel(starts, q_ref, kv_ref, ov_ref, att_ref, inv_ref):
+    block = pl.program_id(0)
+    bq = q_ref.shape[0]
+    q_begin = block * bq
+    q = q_ref[...]
+    zero = jnp.zeros((bq, HD), BF16)
+    q2 = jnp.concatenate(
+        [
+            jnp.concatenate([q[:, :HD], zero], axis=1),
+            jnp.concatenate([q[:, HD:], zero], axis=1),
+        ],
+        axis=0,
+    )
+
+    def step(j, acc):
+        k_begin = pl.multiple_of(j * bq, bq)
+        keys = kv_ref[pl.ds(k_begin, bq), :]
+        s = lax.dot_general(q2, keys, (((1,), (1,)), ((), ())), preferred_element_type=F32)
+        mask = block_mask(starts, q_begin, k_begin, bq, bq)
+        p = jnp.exp2(s * (LOG2E * HD**-0.5))
+        p = jnp.where(jnp.concatenate([mask, mask], axis=0), p, 0.0).astype(BF16)
+        return acc + jnp.dot(p, ov_ref[pl.ds(k_begin, bq), :], preferred_element_type=F32)
+
+    low = low_key(starts, q_begin) // bq
+    acc = lax.fori_loop(low, block + 1, step, jnp.zeros((2 * bq, LANES), F32))
+    inv = 1.0 / acc[:, :1]
+    out = acc[:, HD:] * inv
+    att_ref[...] = jnp.concatenate([out[:bq], out[bq:]], axis=1).astype(BF16)
+    inv_ref[...] = jnp.concatenate(
+        [jnp.broadcast_to(inv[:bq], (bq, HD)), jnp.broadcast_to(inv[bq:], (bq, HD))], axis=1
+    )
+
+
+def attend_back_kernel(starts, q_ref, kv_ref, att_ref, inv_ref, da_ref, dq_ref, dkv_ref):
+    block = pl.program_id(0)
+    bq = q_ref.shape[0]
+    q_begin = block * bq
+
+    @pl.when(block == 0)
+    def _():
+        dkv_ref[...] = jnp.zeros_like(dkv_ref)
+
+    q = q_ref[...]
+    da = da_ref[...]
+    zero = jnp.zeros((bq, HD), BF16)
+    q2 = jnp.concatenate(
+        [
+            jnp.concatenate([q[:, :HD], zero], axis=1),
+            jnp.concatenate([q[:, HD:], zero], axis=1),
+        ],
+        axis=0,
+    )
+    da2 = jnp.concatenate(
+        [
+            jnp.concatenate([zero, da[:, :HD]], axis=1),
+            jnp.concatenate([zero, da[:, HD:]], axis=1),
+        ],
+        axis=0,
+    )
+    prod = da.astype(F32) * att_ref[...].astype(F32)
+    delta = jnp.concatenate(
+        [
+            jnp.sum(prod[:, :HD], axis=1, keepdims=True),
+            jnp.sum(prod[:, HD:], axis=1, keepdims=True),
+        ],
+        axis=0,
+    )
+    inv_all = inv_ref[...]
+    inv = jnp.concatenate([inv_all[:, :1], inv_all[:, HD : HD + 1]], axis=0)
+
+    def step(j, dq):
+        k_begin = pl.multiple_of(j * bq, bq)
+        keys = kv_ref[pl.ds(k_begin, bq), :]
+        s = lax.dot_general(q2, keys, (((1,), (1,)), ((), ())), preferred_element_type=F32)
+        mask = block_mask(starts, q_begin, k_begin, bq, bq)
+        p = jnp.exp2(s * (LOG2E * HD**-0.5)) * inv
+        p = jnp.where(jnp.concatenate([mask, mask], axis=0), p, 0.0)
+        dp = lax.dot_general(da2, keys, (((1,), (1,)), ((), ())), preferred_element_type=F32)
+        ds = (p * (dp - delta)).astype(BF16)
+        back = (((0,), (0,)), ((), ()))
+        dkv_ref[pl.ds(k_begin, bq), :] += lax.dot_general(
+            ds, q2, back, preferred_element_type=F32
+        ) + lax.dot_general(p.astype(BF16), da2, back, preferred_element_type=F32)
+        return dq + jnp.dot(ds, keys, preferred_element_type=F32)
+
+    low = low_key(starts, q_begin) // bq
+    dq = lax.fori_loop(low, block + 1, step, jnp.zeros((2 * bq, LANES), F32))
+    dq_ref[...] = jnp.concatenate([dq[:bq, :HD], dq[bq:, :HD]], axis=1)
+
+
+def attend(starts, q, kv, ov):
+    stream = q.shape[0]
+    bq = ROWS_BLOCK
+    rows = pl.BlockSpec((bq, LANES), lambda i: (i, 0))
+    whole = pl.BlockSpec((stream, LANES), lambda i: (0, 0))
+    return pl.pallas_call(
+        attend_kernel,
+        grid=(stream // bq,),
+        in_specs=[pl.BlockSpec(memory_space=pltpu.SMEM), rows, whole, whole],
+        out_specs=[rows, rows],
+        out_shape=[
+            jax.ShapeDtypeStruct((stream, LANES), BF16),
+            jax.ShapeDtypeStruct((stream, LANES), F32),
+        ],
+        compiler_params=pltpu.CompilerParams(vmem_limit_bytes=32 * 2**20),
+        cost_estimate=pl.CostEstimate(
+            flops=4 * stream * 1024 * LANES, bytes_accessed=6 * stream * LANES * 2, transcendentals=0
+        ),
+    )(starts, q, kv, ov)
+
+
+def attend_back(starts, q, kv, att, inv, da):
+    stream = q.shape[0]
+    bq = ROWS_BLOCK
+    rows = pl.BlockSpec((bq, LANES), lambda i: (i, 0))
+    whole = pl.BlockSpec((stream, LANES), lambda i: (0, 0))
+    return pl.pallas_call(
+        attend_back_kernel,
+        grid=(stream // bq,),
+        in_specs=[pl.BlockSpec(memory_space=pltpu.SMEM), rows, whole, rows, rows, rows],
+        out_specs=[rows, whole],
+        out_shape=[
+            jax.ShapeDtypeStruct((stream, LANES), F32),
+            jax.ShapeDtypeStruct((stream, LANES), F32),
+        ],
+        compiler_params=pltpu.CompilerParams(vmem_limit_bytes=32 * 2**20),
+        cost_estimate=pl.CostEstimate(
+            flops=10 * stream * 1024 * LANES, bytes_accessed=8 * stream * LANES * 2, transcendentals=0
+        ),
+    )(starts, q, kv, att, inv, da)
+
+
+def head_prepare(q_raw, k_raw, q_gain, k_gain, position):
+    stream = q_raw.shape[0]
+    q, k = prepare(
+        q_raw.reshape(stream, 2, HD), k_raw.reshape(stream, 1, HD), q_gain, k_gain, position
+    )
+    return q.reshape(stream, LANES), k.reshape(stream, HD)
+
+
+def per_device_heads(
+    tokens,
+    doc_starts,
+    out_grad,
+    attn_gain,
+    w_query,
+    w_key,
+    w_value,
+    q_gain,
+    k_gain,
+    w_out,
+    ffn_gain,
+    w_gate,
+    w_up,
+    w_down,
+):
+    n_ctx = lax.axis_size("ctx")
+    n_wa = lax.axis_size("wa")
+    n = n_ctx * n_wa
+    me = lax.axis_index("ctx") * n_wa + lax.axis_index("wa")
+    even = lax.axis_index("wa") % 2 == 0
+    tok_rows, width = tokens.shape[1:]
+    d_rows = w_query.shape[0]
+    stream = tok_rows * n
+    ff_cols = FF // n
+    position = jnp.arange(stream, dtype=jnp.int32)
+
+    def gather_rows(own):
+        return to_position(lax.all_gather(own, AXES, axis=0, tiled=True), n_ctx, n_wa)
+
+    def scatter_rows(part):
+        return lax.psum_scatter(
+            to_stored(part, n_ctx, n_wa), AXES, scatter_dimension=0, tiled=True
+        ).astype(F32)
+
+    def mm(a, b):
+        return jnp.dot(a, b, preferred_element_type=F32)
+
+    def mm_t(a, b):
+        return lax.dot_general(a, b, (((1,), (1,)), ((), ())), preferred_element_type=F32)
+
+    def t_mm(a, b):
+        return lax.dot_general(a, b, (((0,), (0,)), ((), ())), preferred_element_type=F32)
+
+    gains = lax.all_gather(
+        jnp.concatenate([attn_gain, ffn_gain, q_gain, k_gain]), AXES, axis=0
+    ).astype(F32)
+    attn_gain32 = gains[:, :d_rows].reshape(-1)
+    ffn_gain32 = gains[:, d_rows : 2 * d_rows].reshape(-1)
+    per = HD // n
+    qgain32 = gains[:, 2 * d_rows : 2 * d_rows + per].reshape(-1)
+    kgain32 = gains[:, 2 * d_rows + per :].reshape(-1)
+
+    def pair(w):
+        return jnp.repeat(w.reshape(d_rows, KV, 1, HD), n // KV, axis=2).reshape(d_rows, n, HD)
+
+    columns = jnp.concatenate(
+        [
+            w_query.reshape(d_rows, n, LANES),
+            pair(w_key),
+            pair(w_value),
+            w_gate.reshape(d_rows, n, ff_cols),
+            w_up.reshape(d_rows, n, ff_cols),
+        ],
+        axis=2,
+    ).transpose(1, 0, 2)
+    columns = lax.all_to_all(columns, AXES, 0, 0, tiled=True).reshape(width, -1)
+    w_qkv = columns[:, : 2 * LANES]
+    w_gu = columns[:, 2 * LANES :]
+
+    x_all = gather_rows(tokens[0])
+    dy_all = gather_rows(out_grad[0])
+    x_own = tokens[0].astype(F32)
+    n1_all = rms_norm(x_all.astype(F32), attn_gain32).astype(BF16)
+    qkv = mm(n1_all, w_qkv)
+    q_raw, k_raw, v_raw = qkv[:, :LANES], qkv[:, LANES : LANES + HD], qkv[:, LANES + HD :]
+    v_b = v_raw.astype(BF16)
+    (q_rot, k_rot), prep_back = jax.vjp(
+        partial(head_prepare, position=position), q_raw, k_raw, qgain32, kgain32
+    )
+    q_b = q_rot.astype(BF16)
+    kv_b = jnp.concatenate([k_rot.astype(BF16), v_b], axis=1)
+    ov_b = jnp.concatenate([jnp.ones_like(v_b), v_b], axis=1)
+    att, inv = attend(doc_starts, q_b, kv_b, ov_b)
+    middle = x_own + scatter_rows(mm(att, w_out).astype(BF16))
+    n2_own, n2_back = jax.vjp(rms_norm, middle, ffn_gain32)
+    n2_all = gather_rows(n2_own.astype(BF16))
+    gate_up = mm(n2_all, w_gu)
+    gate, up = gate_up[:, :ff_cols], gate_up[:, ff_cols:]
+    sig = jax.nn.sigmoid(gate)
+    silu = gate * sig
+    hidden = (silu * up).astype(BF16)
+    layer_out = middle + scatter_rows(mm(hidden, w_down).astype(BF16))
+
+    d_hidden = mm_t(dy_all, w_down)
+    d_gu = jnp.concatenate(
+        [d_hidden * up * (sig * (1.0 + gate * (1.0 - sig))), d_hidden * silu], axis=1
+    ).astype(BF16)
+    d_n2 = scatter_rows(mm_t(d_gu, w_gu).astype(BF16))
+    down_grad = t_mm(hidden, dy_all)
+    gu_grad = t_mm(n2_all, d_gu)
+    d_mid_part, d_ffn_gain = n2_back(d_n2)
+    d_middle = out_grad[0].astype(F32) + d_mid_part
+    db_all = gather_rows(d_middle.astype(BF16))
+    out_w_grad = t_mm(att, db_all)
+    d_att = mm_t(db_all, w_out).astype(BF16)
+    dq, dkv = attend_back(doc_starts, q_b, kv_b, att, inv, d_att)
+    swap = [(i, i ^ 1) for i in range(n_wa)]
+    dkv = dkv + lax.ppermute(dkv, "wa", swap)
+    dq_raw, dk_raw, d_qgain, d_kgain = prep_back((dq * HD**-0.5, dkv[:, :HD] * HD**-0.5))
+    d_kgain = jnp.where(even, d_kgain, 0.0)
+    d_kv_own = jnp.where(even, dk_raw, dkv[:, HD:])
+    w_kv_own = jnp.where(even, w_qkv[:, LANES : LANES + HD], w_qkv[:, LANES + HD :])
+    d_qkv = jnp.concatenate([dq_raw, d_kv_own], axis=1).astype(BF16)
+    d_n1 = scatter_rows(mm_t(d_qkv, jnp.concatenate([w_qkv[:, :LANES], w_kv_own], axis=1)).astype(BF16))
+    qkv_grad = t_mm(n1_all, d_qkv)
+    _, n1_back = jax.vjp(rms_norm, x_own, attn_gain32)
+    d_x_part, d_attn_gain = n1_back(d_n1)
+    input_grad = d_middle + d_x_part
+
+    col_grads = jnp.concatenate([gu_grad, qkv_grad], axis=1).astype(BF16)
+    row_grads = lax.all_to_all(col_grads, AXES, 0, 0, tiled=True).reshape(n, d_rows, -1)
+    swap_dp = [(0, 1), (1, 0)]
+    row_other = lax.ppermute(row_grads, "dp", swap_dp)
+    row_grads = (row_grads.astype(F32) + row_other.astype(F32)).transpose(1, 0, 2)
+
+    def both(part):
+        return part + lax.ppermute(part.astype(BF16), "dp", swap_dp).astype(F32)
+
+    def flat(part):
+        return part.reshape(d_rows, -1)
+
+    kv_grads = row_grads[:, :, 2 * ff_cols + LANES :].reshape(d_rows, KV, 2, HD)
+    small = jnp.concatenate([d_attn_gain, d_ffn_gain, d_qgain, d_kgain])
+    small = lax.psum(small, ("dp",) + AXES)
+
+    def mine(total, begin, size):
+        return lax.dynamic_slice_in_dim(total, begin + me * size, size)
+
+    return (
+        layer_out.astype(BF16)[None],
+        input_grad.astype(BF16)[None],
+        mine(small, 0, d_rows),
+        flat(row_grads[:, :, 2 * ff_cols : 2 * ff_cols + LANES]),
+        flat(kv_grads[:, :, 0]),
+        flat(kv_grads[:, :, 1]),
+        mine(small, 2 * width, per),
+        mine(small, 2 * width + HD, per),
+        both(out_w_grad),
+        mine(small, width, d_rows),
+        flat(row_grads[:, :, :ff_cols]),
+        flat(row_grads[:, :, ff_cols : 2 * ff_cols]),
+        both(down_grad),
+    )
+
+
 def solution(mesh):
+    split = mesh.shape["ctx"] * mesh.shape["wa"]
+    by_heads = 2 * split == H
     placed = (
         P("dp", ("ctx", "wa"), None),
         P("dp", None),
@@ -341,7 +678,7 @@
         P(("ctx", "wa"), None),
     )
     return jax.shard_map(
-        per_device,
+        per_device_heads if by_heads else per_device,
         mesh=mesh,
         in_specs=placed,
         out_specs=(

time: 3770 us -> 1400 us (0.37)
  waiting for transfers between devices: 3140 us -> 636 us
  matrix products: 341 us -> 99 us
  local copies, waits for them, and re-layouts: 65.8 us -> 196 us
  blocking collectives: 139 us -> 248 us
  other arithmetic: 61.9 us -> 137 us
    reduce_scatter x8 -> x4, waiting for transfers between devices: 2430 us -> 206 us  [scatter_rows(): lax.psum_scatter(to_stored(part, n_ctx, n_wa), AXES, scatter_dimension=0,...]
    all_gather x9 -> x4, waiting for transfers between devices: 620 us -> 199 us  [gather_rows(): lax.all_gather(own, AXES, axis=0, tiled=True)]
    dot_general x34 -> x12, matrix products: 341 us -> 99 us  [the longest x4 38.3 us: t_mm(): lax.dot_general(a, b, (((0,), (0,)), ((), ())), preferred_element_type=F32)]
    ppermute x0 -> x4, waiting for transfers between devices: none -> 141 us  [the longest x2 141 us: both(): return part + lax.ppermute(part.astype(BF16), 'dp', swap_dp).astype(F32)]
    unnamed x2 -> x1, blocking collectives: 91.3 us -> 190 us
    psum x1 -> x0, waiting for transfers between devices: 90.1 us -> none  [per_device(): lax.psum(attn_shards[1].astype(jnp.bfloat16), 'dp').astype(jnp.float32)]
    all_to_all x0 -> x2, waiting for transfers between devices: none -> 89.4 us  [the longest x1 89.4 us: per_device_heads(): lax.all_to_all(col_grads, AXES, 0, 0, tiled=True).reshape(n, d_rows, -1)]
    psum x1, blocking collectives: 4.92 us -> 58.7 us  [per_device_heads(): small = lax.psum(small, ('dp',) + AXES)]
  transfers between devices with their start and end apart: 18 -> 14, of which waited for: 17 -> 8; matrix products, arithmetic and copies ran while one was open for 7% -> 15% of each run, Pallas kernels for 0% -> 0%
where the time goes in v1:
time: 1400 us; the launch traced here: 1380 us
  waiting for transfers between devices  636 us (45%)
  blocking collectives  248 us (18%)
  local copies, waits for them, and re-layouts  196 us (14%)
  other arithmetic  137 us (10%)
  matrix products  99 us (7%)
  Pallas kernels  30.9 us (2%)
  starting transfers between devices  16.3 us (1%)
  between operations  15.8 us (1%)
    reduce_scatter x4, waiting for transfers between devices, scatter_rows(): lax.psum_scatter(to_stored(part, n_ctx, n_wa), AXES, scatter_dimension=0,...  206 us
    all_gather x4, waiting for transfers between devices, gather_rows(): lax.all_gather(own, AXES, axis=0, tiled=True)  199 us
    unnamed x1, blocking collectives  190 us
    ppermute x2, waiting for transfers between devices, both(): return part + lax.ppermute(part.astype(BF16), 'dp', swap_dp).astype(F32)  141 us
    all_to_all x1, waiting for transfers between devices, per_device_heads(): lax.all_to_all(col_grads, AXES, 0, 0, tiled=True).reshape(n, d_rows, -1)  89.4 us
    psum x1, blocking collectives, per_device_heads(): small = lax.psum(small, ('dp',) + AXES)  58.7 us
    another operation x8, local copies, waits for them, and re-layouts, to_stored(): paired = jnp.stack([parts[:n_ctx], jnp.flip(parts[n_ctx:], axis=0)], axis=2)  42.7 us
    dot_general x4, matrix products, t_mm(): lax.dot_general(a, b, (((0,), (0,)), ((), ())), preferred_element_type=F32)  38.3 us
  transfers between devices with their start and end apart: 14, of which 8 were waited for; matrix products, arithmetic and copies ran while one was open for 15% of the time, Pallas kernels for 0%

profile of v1, /device:TPU:0, one launch (start us, length us, event | category | flops | bytes accessed | tf_op | source)
XLA Modules:
  0.0 1378.6 jit_solution(13825305491230629778)
XLA Ops:
  12.2 4.8 copy_bitcast_fusion
  18.1 9.0 concatenate.53
  27.1 7.6 all-to-all-start
  36.3 189.6 %all-reduce.5 = bf16[4224]{0:T(1024)(128)(2,1)S(1)} all-reduce(bf16[4224]{0:T(1024)(128)(2,1)S(1)} %dynamic-update-slice), channel_id=3, replica_groups=mesh['dp'=2,'ctx'=4,'wa'=4] {'ctx','wa'}, use_global_device_ids=true, to_apply=%add.5 | all-reduce | flops 4224 | bytes 16896
  227.3 6.2 slice_bitcast_fusion.7
  233.5 4.8 rev.25
  238.3 10.3 maximum_convert_fusion
  248.6 17.6 %copy.156 = f32[2048,2048]{0,1:T(8,128)} copy(f32[2048,2048]{1,0:T(8,128)} %bitcast.175) | data formatting | bytes 33554432 | tf_op jit(solution)/shard_map/convert_element_type | solution.py:578
  266.3 4.8 multiply_reduce_fusion
  271.2 9.5 multiply_convert_fusion
  280.7 6.0 fusion.39
  293.3 5.6 fusion.24
  305.0 12.2 shard_map.237
  321.4 2.6 fusion.62
  326.5 7.5 pad_maximum_fusion
  334.0 8.3 copy.168
  343.1 102.7 %reduce-scatter.5.cloned.1.call-done = bf16[128,2048]{1,0:T(8,128)(2,1)} async-done(((bf16[2048,2048]{1,0:T(8,128)(2,1)}), bf16[128,2048]{1,0:T(8,128)(2,1)}) %reduce-scatter.5.cloned.1.call-update) | async-done | bytes 524304 | tf_op jit(solution)/shard_map/reduce_scatter | solution.py:536
  449.5 73.1 %all-gather.14.cloned.1.call-done = bf16[1,2048,2048]{2,1,0:T(8,128)(2,1)} async-done(((bf16[1,128,2048]{2,1,0:T(8,128)(2,1)}), bf16[1,2048,2048]{2,1,0:T(8,128)(2,1)}) %all-gather.14.cloned.1.call-update) | async-done | bytes 8388624 | tf_op jit(solution)/shard_map/all_gather | solution.py:533
  522.6 6.1 slice_bitcast_fusion.3
  528.8 4.9 rev.29
  533.7 7.5 pad_maximum_fusion.3
  541.2 57.2 %all-gather.8.cloned.1.call-done = bf16[2048,2048]{1,0:T(8,128)(2,1)} async-done(((bf16[128,2048]{1,0:T(8,128)(2,1)}), bf16[2048,2048]{1,0:T(8,128)(2,1)}) %all-gather.8.cloned.1.call-update) | async-done | bytes 8388624 | tf_op jit(solution)/shard_map/all_gather | solution.py:533
  598.4 6.1 slice_bitcast_fusion.5
  604.6 4.8 rev.27
  609.3 7.4 pad_maximum_fusion.1
  616.8 13.1 fusion.4
  629.9 10.6 multiply_convert_fusion.2
  640.6 12.5 convolution_convert_fusion.1
  657.8 7.5 pad_maximum_fusion.4
  665.2 8.3 copy.172
  673.6 102.9 %reduce-scatter.9.cloned.1.call-done = bf16[128,2048]{1,0:T(8,128)(2,1)} async-done(((bf16[2048,2048]{1,0:T(8,128)(2,1)}), bf16[128,2048]{1,0:T(8,128)(2,1)}) %reduce-scatter.9.cloned.1.call-update) | async-done | bytes 524304 | tf_op jit(solution)/shard_map/reduce_scatter | solution.py:536
  778.6 2.8 fusion.57
  788.0 68.2 %all-gather.10.cloned.1.call-done = bf16[2048,2048]{1,0:T(8,128)(2,1)} async-done(((bf16[128,2048]{1,0:T(8,128)(2,1)}), bf16[2048,2048]{1,0:T(8,128)(2,1)}) %all-gather.10.cloned.1.call-update) | async-done | bytes 8388624 | tf_op jit(solution)/shard_map/all_gather | solution.py:533
  856.1 6.3 slice_bitcast_fusion.1
  862.5 4.8 rev.31
  867.3 7.4 pad_maximum_fusion.5
  874.7 5.9 convolution_convert_fusion.4.da_ref
  880.6 18.6 %shard_map.238 = (f32[2048,128]{1,0:T(8,128)S(1)}, f32[2048,128]{1,0:T(8,128)S(1)}) custom-call(s32[1,8]{1,0:T(1,128)S(1)} %copy-done.5, bf16[2048,128]{1,0:T(8,128)(2,1)S(1)} %copy.167.q_ref, bf16[2048,128]{1,0:T(8,128)(2,1)S(1)} %copy-done.4, bf16[2048,128]{1,0:T(8,128)(2,1)S(1)} %get-tuple-element.17.att_ref, f32[2048,128]{1,0:T(8,128)S(1)} %copy-done.7, ...), custom_call_target="tpu_custom_call" | custom-call | flops 2684354560 | bytes 4194304 | tf_op jit(solution)/shard_map/pallas_call | solution.py:481
  909.0 4.4 fusion.27
  917.4 3.6 convolution_convert_fusion
  921.0 2.7 fusion.59
  926.1 7.5 pad_maximum_fusion.6
  933.6 8.3 copy.177
  941.9 12.4 copy.178
  954.3 14.7 %fusion.6 = bf16[16,128,1024]{2,1,0:T(8,128)(2,1)} fusion(bf16[16,128,2048]{2,1,0:T(8,128)(2,1)} %bitcast.200, bf16[2048,512]{0,1:T(8,128)(2,1)} %copy-done.39, bf16[2048,512]{0,1:T(8,128)(2,1)} %copy-done.38), kind=kOutput, calls=%fused_computation.40 | convolution fusion | flops 8600420352 | bytes 16777216 | tf_op jit(solution)/shard_map/dot_general | solution.py:547
  969.0 6.7 convolution_convert_fusion.5
  978.0 5.6 pad_maximum_fusion.7
  983.5 7.8 copy.181
  991.3 4.6 all-to-all-start.1
  995.9 6.6 convolution_convert_fusion.2
  1007.2 7.6 pad_maximum_fusion.2
  1014.8 8.3 copy.170
  1023.1 89.4 %all-to-all-done.1 = bf16[16,128,1216]{1,2,0:T(8,128)(2,1)} async-done(((bf16[16,128,1216]{1,2,0:T(8,128)(2,1)}), bf16[16,128,1216]{1,2,0:T(8,128)(2,1)}, u32[]{:S(2)}, u32[]{:S(2)}) %all-to-all-start.1) | async-done | bytes 4980768 | tf_op jit(solution)/shard_map/all_to_all | solution.py:626
  1113.9 11.2 fusion.69
  1125.7 5.6 fusion.68
  1132.8 135.2 %collective-permute-done.3 = bf16[512,2048]{1,0:T(8,128)(2,1)} collective-permute-done((bf16[512,2048]{1,0:T(8,128)(2,1)}, bf16[512,2048]{1,0:T(8,128)(2,1)}, u32[]{:S(2)}, u32[]{:S(2)}) %collective-permute-start.3) | collective-permute-done | bytes 2097184 | tf_op jit(solution)/shard_map/ppermute | solution.py:632
  1268.0 4.4 convert_add_fusion
  1272.4 5.9 collective-permute-done.2
  1281.1 58.7 %psum.7 = f32[4224]{0:T(1024)S(1)} all-reduce(f32[4224]{0:T(1024)S(1)} %concatenate.64), channel_id=1, replica_groups=mesh['dp'=2,'ctx'=4,'wa'=4] {'dp','ctx','wa'}, use_global_device_ids=true, to_apply=%region_17.18 | all-reduce | flops 4224 | bytes 33792 | tf_op jit(solution)/shard_map/psum | solution.py:639
  1341.0 3.3 fusion.48
  1344.4 5.1 add_bitcast_fusion
  1349.5 4.6 fusion.58
  1356.1 5.6 copy.187
  1361.7 5.7 copy.188
  (185 shorter events, 82.0 us)
Async XLA Ops:
  7.2 622.7 %copy-start = (bf16[512,2048]{1,0:T(8,128)(2,1)S(1)}, bf16[512,2048]{1,0:T(8,128)(2,1)}, u32[]{:S(2)}) copy-start(bf16[512,2048]{1,0:T(8,128)(2,1)} %param.27) | copy-start | bytes 6291460
  7.2 220.1 %all-gather.12.cloned.1.call-start = ((), (), s32[]{:S(2)}) async-start(), calls=%async_computation.12 | async-start | bytes 8912896 | tf_op jit(solution)/shard_map/all_gather | solution.py:533
  12.2 5.0 copy-start.19
  27.0 7.7 copy-start.37
  27.0 8.9 copy-start.33
  27.0 8.9 copy-start.34
  27.0 8.9 copy-start.35
  27.0 8.9 copy-start.36
  27.1 253.7 %all-to-all-start = ((bf16[16,128,1280]{2,1,0:T(8,128)(2,1)}), bf16[16,128,1280]{2,1,0:T(8,128)(2,1)}, u32[]{:S(2)}, u32[]{:S(2)}) async-start(bf16[16,128,1280]{2,1,0:T(8,128)(2,1)} %bitcast.183), calls=%async_computation | async-start | bytes 10485760 | tf_op jit(solution)/shard_map/all_to_all | solution.py:571
  34.6 411.1 %reduce-scatter.5.cloned.1.call-start = ((), (), s32[]{:S(2)}) async-start(), calls=%async_computation.6 | async-start | bytes 8912896 | tf_op jit(solution)/shard_map/reduce_scatter | solution.py:536
  226.1 65.6 %copy-start.29 = (f32[64]{0:T(128)}, f32[64]{0:T(128)S(1)}, u32[]{:S(2)}) copy-start(f32[64]{0:T(128)S(1)} %mul.538) | copy-start | bytes 772
  226.2 67.0 %copy-start.31 = (f32[32]{0:T(128)}, f32[32]{0:T(128)S(1)}, u32[]{:S(2)}) copy-start(f32[32]{0:T(128)S(1)} %multiply_power_fusion) | copy-start | bytes 388
  226.2 67.0 %copy-start.23 = (f32[2048]{0:T(1024)}, f32[2048]{0:T(1024)S(1)}, u32[]{:S(2)}) copy-start(f32[2048]{0:T(1024)S(1)} %iota_convert_fusion) | copy-start | bytes 24580
  226.3 44.9 %copy-start.21 = (f32[2048]{0:T(1024)}, f32[2048]{0:T(1024)S(1)}, u32[]{:S(2)}) copy-start(f32[2048]{0:T(1024)S(1)} %get-tuple-element.118) | copy-start | bytes 24580
  227.3 74.0 %copy-start.15 = (f32[2048,32]{0,1:T(8,128)}, f32[2048,32]{0,1:T(8,128)S(1)}, u32[]{:S(2)}) copy-start(f32[2048,32]{0,1:T(8,128)S(1)} %get-tuple-element.126) | copy-start | bytes 786436
  286.7 1.3 copy-start.11
  291.0 0.6 copy-start.27
  291.7 7.2 copy-start.25
  301.3 3.7 copy-start.5
  301.8 17.3 %copy-start.20 = (bf16[128,2048]{1,0:T(8,128)(2,1)S(1)}, bf16[128,2048]{1,0:T(8,128)(2,1)}, u32[]{:S(2)}) copy-start(bf16[128,2048]{1,0:T(8,128)(2,1)} %param.23) | copy-start | bytes 1572868
  317.2 0.8 copy-start.3
  318.1 1.0 copy-start.6
  342.3 180.3 %all-gather.14.cloned.1.call-start = ((), (), s32[]{:S(2)}) async-start(), calls=%async_computation.13 | async-start | bytes 8912896 | tf_op jit(solution)/shard_map/all_gather | solution.py:533
  343.1 255.3 %all-gather.8.cloned.1.call-start = ((), (), s32[]{:S(2)}) async-start(), calls=%async_computation.7 | async-start | bytes 8912896 | tf_op jit(solution)/shard_map/all_gather | solution.py:533
  449.5 327.1 %reduce-scatter.9.cloned.1.call-start = ((), (), s32[]{:S(2)}) async-start(), calls=%async_computation.9 | async-start | bytes 8912896 | tf_op jit(solution)/shard_map/reduce_scatter | solution.py:536
  640.6 12.5 copy-start.38
  640.6 12.5 copy-start.39
  673.6 182.6 %all-gather.10.cloned.1.call-start = ((), (), s32[]{:S(2)}) async-start(), calls=%async_computation.10 | async-start | bytes 8912896 | tf_op jit(solution)/shard_map/all_gather | solution.py:533
  781.3 498.1 %reduce-scatter.11.cloned.1.call-start = ((), (), s32[]{:S(2)}) async-start(), calls=%async_computation.11 | async-start | bytes 8912896 | tf_op jit(solution)/shard_map/reduce_scatter | solution.py:536
  874.7 5.9 copy-start.4
  874.7 5.9 copy-start.7
  899.3 1.0 copy-start.1
  900.2 3.6 copy-start.16
  903.8 3.8 copy-start.12
  903.8 4.9 copy-start.2
  905.3 3.4 collective-permute-start
  907.6 1.4 copy-start.24
  907.6 1.4 copy-start.32
  908.7 4.6 copy-start.9
  908.7 4.6 copy-start.26
  908.7 4.6 copy-start.30
  908.9 5.3 copy-start.28
  913.3 4.0 copy-start.17
  954.3 14.7 %copy-start.18 = (bf16[2048,2,64]{0,2,1:T(8,128)(2,1)S(1)}, bf16[2048,2,64]{0,2,1:T(8,128)(2,1)}, u32[]{:S(2)}) copy-start(bf16[2048,2,64]{0,2,1:T(8,128)(2,1)} %fusion.30) | copy-start | bytes 1572868
  991.3 121.2 %all-to-all-start.1 = ((bf16[16,128,1216]{1,2,0:T(8,128)(2,1)}), bf16[16,128,1216]{1,2,0:T(8,128)(2,1)}, u32[]{:S(2)}, u32[]{:S(2)}) async-start(bf16[16,128,1216]{1,2,0:T(8,128)(2,1)} %copy.181), calls=%async_computation.5 | async-start | bytes 9961472 | tf_op jit(solution)/shard_map/all_to_all | solution.py:626
  995.9 345.1 %reduce-scatter.7.cloned.1.call-start = ((), (), s32[]{:S(2)}) async-start(), calls=%async_computation.8 | async-start | bytes 8912896 | tf_op jit(solution)/shard_map/reduce_scatter | solution.py:536
  1112.5 231.9 %collective-permute-start.1 = (bf16[16,128,1216]{1,2,0:T(8,128)(2,1)}, bf16[16,128,1216]{1,2,0:T(8,128)(2,1)}, u32[]{:S(2)}, u32[]{:S(2)}) collective-permute-start(bf16[16,128,1216]{1,2,0:T(8,128)(2,1)} %all-to-all-done.1), channel_id=1, source_target_pairs={{0,16},{16,0},{1,17},{17,1},{2,18},{18,2},{3,19},{19,3},{4,20},{20... | collective-permute-start | bytes 14942216 | tf_op jit(solution)/shard_map/ppermute | solution.py:628
  1125.1 142.9 %collective-permute-start.3 = (bf16[512,2048]{1,0:T(8,128)(2,1)}, bf16[512,2048]{1,0:T(8,128)(2,1)}, u32[]{:S(2)}, u32[]{:S(2)}) collective-permute-start(bf16[512,2048]{1,0:T(8,128)(2,1)} %get-tuple-element.129), channel_id=1, source_target_pairs={{0,16},{16,0},{1,17},{17,1},{2,18},{18,2},{3,19},{19,3},{4,20},{20... | collective-permute-start | bytes 6291464 | tf_op jit(solution)/shard_map/ppermute | solution.py:632
  1125.7 142.3 %copy-start.14 = (f32[512,2048]{1,0:T(8,128)S(1)}, f32[512,2048]{1,0:T(8,128)}, u32[]{:S(2)}) copy-start(f32[512,2048]{1,0:T(8,128)} %get-tuple-element.130) | copy-start | bytes 12582916
  1131.4 147.0 %collective-permute-start.2 = (bf16[128,2048]{1,0:T(8,128)(2,1)S(1)}, bf16[128,2048]{1,0:T(8,128)(2,1)S(1)}, u32[]{:S(2)}, u32[]{:S(2)}) collective-permute-start(bf16[128,2048]{1,0:T(8,128)(2,1)S(1)} %get-tuple-element.127), channel_id=1, source_target_pairs={{0,16},{16,0},{1,17},{17,1},{2,18},{18,2},{3,19},{19,3},{4,20},{20... | collective-permute-start | bytes 1572872 | tf_op jit(solution)/shard_map/ppermute | solution.py:632
  1268.0 11.4 copy-start.10
  1268.0 11.4 copy-start.22
  1268.0 73.0 %copy-start.13 = (bf16[128,2048]{1,0:T(8,128)(2,1)S(1)}, bf16[128,2048]{1,0:T(8,128)(2,1)}, u32[]{:S(2)}) copy-start(bf16[128,2048]{1,0:T(8,128)(2,1)} %reduce-scatter.5.cloned.1.call-done) | copy-start | bytes 1572868
  1349.5 6.6 copy-start.8
  1361.7 8.2 slice-start
Sparse Core Ops, SparseCore 0:
  10.2 148.1 all-gather.11
  342.4 103.2 reduce-scatter.4
  447.9 74.6 all-gather.13
  525.2 73.1 all-gather.7
  673.7 102.8 reduce-scatter.8
  781.5 74.6 all-gather.9
  942.0 169.7 reduce-scatter.10
  1115.9 105.1 reduce-scatter.6

commit v2 on v1

--- a/solution.py
+++ b/solution.py
@@ -333,20 +333,6 @@
 BF16 = jnp.bfloat16
 
 
-def to_position(rows, n_ctx, n_wa):
-    half = rows.shape[0] // (2 * n_ctx * n_wa)
-    parts = rows.reshape(n_ctx, n_wa, 2, half, -1)
-    ordered = jnp.concatenate([parts[:, :, 0], jnp.flip(parts[:, :, 1], axis=0)], axis=0)
-    return ordered.reshape(rows.shape)
-
-
-def to_stored(rows, n_ctx, n_wa):
-    half = rows.shape[0] // (2 * n_ctx * n_wa)
-    parts = rows.reshape(2 * n_ctx, n_wa, half, -1)
-    paired = jnp.stack([parts[:n_ctx], jnp.flip(parts[n_ctx:], axis=0)], axis=2)
-    return paired.reshape(rows.shape)
-
-
 def low_key(starts, row):
     first = jnp.int32(0)
     for doc in range(starts.shape[1]):
@@ -502,6 +488,273 @@
     return q.reshape(stream, LANES), k.reshape(stream, HD)
 
 
+MESH_ID = pl.DeviceIdType.MESH
+
+
+def meet_neighbours(ctx, wa, n_ctx):
+    barrier = pltpu.get_barrier_semaphore()
+
+    def greet(where):
+        pl.semaphore_signal(barrier, inc=1, device_id=where, device_id_type=MESH_ID)
+
+    greet({"wa": wa ^ 1})
+    greet({"wa": wa ^ 2})
+    pl.when(ctx > 0)(lambda: greet({"ctx": ctx - 1}))
+    pl.when(ctx < n_ctx - 1)(lambda: greet({"ctx": ctx + 1}))
+    ends = (ctx == 0).astype(jnp.int32) + (ctx == n_ctx - 1).astype(jnp.int32)
+    pl.semaphore_wait(barrier, 4 - ends)
+
+
+def piece_row(zc, wac, h, half, n_ctx, n_wa, by_position):
+    if by_position:
+        span = zc if h == 0 else 2 * n_ctx - 1 - zc
+        return pl.multiple_of((span * n_wa + wac) * half, half)
+    return pl.multiple_of(((zc * n_wa + wac) * 2 + h) * half, half)
+
+
+def gather_kernel(n_ctx, n_wa, by_position, own_ref, out_ref, own_sem, send_sem, recv_sem):
+    ctx = lax.axis_index("ctx")
+    wa = lax.axis_index("wa")
+    half = own_ref.shape[0] // 2
+    meet_neighbours(ctx, wa, n_ctx)
+    sends = []
+
+    def place(zc, wac, h):
+        return out_ref.at[pl.ds(piece_row(zc, wac, h, half, n_ctx, n_wa, by_position), half)]
+
+    def copy(src, zc, wac, h, where):
+        return pltpu.make_async_remote_copy(
+            src_ref=src,
+            dst_ref=place(zc, wac, h),
+            send_sem=send_sem.at[len(sends)],
+            recv_sem=recv_sem.at[(zc * n_wa + wac) * 2 + h],
+            device_id=where,
+            device_id_type=MESH_ID,
+        )
+
+    def send(cond, src, zc, wac, h, where):
+        made = copy(src, zc, wac, h, where)
+        if cond is None:
+            made.start()
+        else:
+            pl.when(cond)(made.start)
+        sends.append((cond, made))
+
+    def arrived(cond, zc, wac, h):
+        made = pltpu.make_async_remote_copy(
+            src_ref=place(zc, wac, h),
+            dst_ref=place(zc, wac, h),
+            send_sem=send_sem.at[0],
+            recv_sem=recv_sem.at[(zc * n_wa + wac) * 2 + h],
+            device_id={"wa": wa ^ 1},
+            device_id_type=MESH_ID,
+        )
+        if cond is None:
+            made.wait_recv()
+        else:
+            pl.when(cond)(made.wait_recv)
+
+    def inside(zc):
+        return (zc >= 0) & (zc < n_ctx)
+
+    own_copies = []
+    for h in range(2):
+        own = own_ref.at[pl.ds(h * half, half)]
+        for way in (-1, 1):
+            send(inside(ctx + way), own, ctx, wa, h, {"ctx": ctx + way})
+        send(None, own, ctx, wa, h, {"wa": wa ^ 2})
+        send(None, own, ctx, wa, h, {"wa": wa ^ 1})
+        made = pltpu.make_async_copy(own, place(ctx, wa, h), own_sem.at[h])
+        made.start()
+        own_copies.append(made)
+
+    def across(k, h):
+        for way in (-1, 1) if k else (1,):
+            zc = ctx + way * k
+            cond = inside(zc) if k else None
+            arrived(cond, zc, wa ^ 2, h)
+            send(cond, place(zc, wa ^ 2, h), zc, wa ^ 2, h, {"wa": wa ^ 1})
+
+    for k in range(1, n_ctx):
+        for h in range(2):
+            for way in (-1, 1):
+                zc = ctx + way * k
+                cond = inside(zc)
+                arrived(cond, zc, wa, h)
+                piece = place(zc, wa, h)
+                send(cond & inside(ctx - way), piece, zc, wa, h, {"ctx": ctx - way})
+                send(cond, piece, zc, wa, h, {"wa": wa ^ 2})
+                send(cond, piece, zc, wa, h, {"wa": wa ^ 1})
+            across(k - 1, h)
+    for h in range(2):
+        across(n_ctx - 1, h)
+    for zc in range(n_ctx):
+        for far in (0, 2):
+            for h in range(2):
+                arrived(None, zc, wa ^ 1 ^ far, h)
+    for cond, made in sends:
+        if cond is None:
+            made.wait_send()
+        else:
+            pl.when(cond)(made.wait_send)
+    for made in own_copies:
+        made.wait()
+
+
+def gather_tokens(own, n_ctx, n_wa, by_position, call_id):
+    rows, width = own.shape
+    n = n_ctx * n_wa
+    return pl.pallas_call(
+        partial(gather_kernel, n_ctx, n_wa, by_position),
+        in_specs=[pl.BlockSpec(memory_space=pl.ANY)],
+        out_specs=pl.BlockSpec(memory_space=pl.ANY),
+        out_shape=jax.ShapeDtypeStruct((rows * n, width), own.dtype),
+        scratch_shapes=[
+            pltpu.SemaphoreType.DMA((2,)),
+            pltpu.SemaphoreType.DMA((8 + 12 * (n_ctx - 1) + 2 * (2 * n_ctx - 1),)),
+            pltpu.SemaphoreType.DMA((2 * n,)),
+        ],
+        compiler_params=pltpu.CompilerParams(collective_id=call_id, has_side_effects=True),
+    )(own)
+
+
+def scatter_kernel(
+    n_ctx, n_wa, by_position, part_ref, out_ref, s1, s2, s3, send_sem, recv1, recv2, recv3
+):
+    ctx = lax.axis_index("ctx")
+    wa = lax.axis_index("wa")
+    half = out_ref.shape[0] // 2
+    slab = 16
+    y = wa // 2
+    sibling, across = {"wa": wa ^ 1}, {"wa": wa ^ 2}
+    meet_neighbours(ctx, wa, n_ctx)
+    sends = []
+
+    def begin(cond, act):
+        if cond is None:
+            act()
+        else:
+            pl.when(cond)(act)
+
+    def mine(zc, wac, h):
+        return part_ref.at[pl.ds(piece_row(zc, wac, h, half, n_ctx, n_wa, by_position), half)]
+
+    def copy(src, dst, sem, where):
+        made = pltpu.make_async_remote_copy(
+            src_ref=src,
+            dst_ref=dst,
+            send_sem=send_sem.at[len(sends)],
+            recv_sem=sem,
+            device_id=where,
+            device_id_type=MESH_ID,
+        )
+        return made
+
+    def send(cond, src, dst, sem, where):
+        made = copy(src, dst, sem, where)
+        begin(cond, made.start)
+        sends.append((cond, made))
+
+    def arrived(cond, dst, sem):
+        made = pltpu.make_async_remote_copy(
+            src_ref=dst,
+            dst_ref=dst,
+            send_sem=send_sem.at[0],
+            recv_sem=sem,
+            device_id=sibling,
+            device_id_type=MESH_ID,
+        )
+        begin(cond, made.wait_recv)
+
+    def add_up(dst, dst_row, srcs):
+        def step(i, carry):
+            at = pl.multiple_of(i * slab, slab)
+            total = srcs[0][pl.ds(at, slab), :].astype(F32)
+            for src in srcs[1:]:
+                total = total + src[pl.ds(at, slab), :].astype(F32)
+            dst[pl.ds(pl.multiple_of(dst_row + at, slab), slab), :] = total.astype(dst.dtype)
+            return carry
+
+        lax.fori_loop(0, half // slab, step, 0)
+
+    def inside(zc):
+        return (zc >= 0) & (zc < n_ctx)
+
+    def index1(zc, yc, h):
+        return (zc * 2 + yc) * 2 + h
+
+    def steps():
+        for k in range(n_ctx - 1, -1, -1):
+            for way in (-1, 1) if k else (1,):
+                for h in range(2):
+                    zc = ctx + way * k
+                    yield k, way, h, zc, (inside(zc) if k else None)
+
+    for other in (1, 0):
+        yc = y ^ 1 if other else y
+        for k, way, h, zc, cond in steps():
+            at = index1(zc, yc, h)
+            send(cond, mine(zc, yc * 2 + ((wa & 1) ^ 1), h), s1.at[at], recv1.at[at], sibling)
+    for k, way, h, zc, cond in steps():
+        at = index1(zc, y ^ 1, h)
+        arrived(cond, s1.at[at], recv1.at[at])
+        begin(cond, lambda: add_up(s1.at[at], 0, [s1.at[at], mine(zc, wa ^ 2, h)]))
+        send(cond, s1.at[at], s2.at[zc * 2 + h], recv2.at[zc * 2 + h], across)
+    for k, way, h, zc, cond in steps():
+        at = index1(zc, y, h)
+        arrived(cond, s1.at[at], recv1.at[at])
+        arrived(cond, s2.at[zc * 2 + h], recv2.at[zc * 2 + h])
+        base = [mine(zc, wa, h), s1.at[at], s2.at[zc * 2 + h]]
+        here = zc * 2 + h
+        low, high = here, (n_ctx + zc) * 2 + h
+        if k:
+            behind = low if way > 0 else high
+            more = cond & inside(ctx - way)
+            arrived(more, s3.at[behind], recv3.at[behind])
+            begin(more, lambda: add_up(s2.at[here], 0, base + [s3.at[behind]]))
+            first = cond & jnp.logical_not(inside(ctx - way))
+            begin(first, lambda: add_up(s2.at[here], 0, base))
+            send(cond, s2.at[here], s3.at[behind], recv3.at[behind], {"ctx": ctx + way})
+        else:
+            under, over = ctx > 0, ctx < n_ctx - 1
+            arrived(under, s3.at[low], recv3.at[low])
+            arrived(over, s3.at[high], recv3.at[high])
+            ways = [
+                (under & over, [s3.at[low], s3.at[high]]),
+                (under & jnp.logical_not(over), [s3.at[low]]),
+                (over & jnp.logical_not(under), [s3.at[high]]),
+            ]
+            for take, extra in ways:
+                begin(take, lambda extra=extra: add_up(out_ref, h * half, base + extra))
+    for cond, made in sends:
+        begin(cond, made.wait_send)
+
+
+def scatter_tokens(part, n_ctx, n_wa, by_position, call_id):
+    n = n_ctx * n_wa
+    rows, width = part.shape[0] // n, part.shape[1]
+    half = rows // 2
+    pieces = 2 * (2 * n_ctx - 1)
+    return pl.pallas_call(
+        partial(scatter_kernel, n_ctx, n_wa, by_position),
+        in_specs=[pl.BlockSpec(memory_space=pltpu.VMEM)],
+        out_specs=pl.BlockSpec(memory_space=pltpu.VMEM),
+        out_shape=jax.ShapeDtypeStruct((rows, width), F32),
+        scratch_shapes=[
+            pltpu.VMEM((4 * n_ctx, half, width), BF16),
+            pltpu.VMEM((2 * n_ctx, half, width), BF16),
+            pltpu.VMEM((4 * n_ctx, half, width), BF16),
+            pltpu.SemaphoreType.DMA((4 * pieces,)),
+            pltpu.SemaphoreType.DMA((4 * n_ctx,)),
+            pltpu.SemaphoreType.DMA((2 * n_ctx,)),
+            pltpu.SemaphoreType.DMA((4 * n_ctx,)),
+        ],
+        compiler_params=pltpu.CompilerParams(
+            collective_id=call_id, has_side_effects=True, vmem_limit_bytes=48 * 2**20
+        ),
+    )(part)
+
+
 def per_device_heads(
     tokens,
     doc_starts,
@@ -521,21 +774,15 @@
     n_ctx = lax.axis_size("ctx")
     n_wa = lax.axis_size("wa")
     n = n_ctx * n_wa
-    me = lax.axis_index("ctx") * n_wa + lax.axis_index("wa")
     even = lax.axis_index("wa") % 2 == 0
     tok_rows, width = tokens.shape[1:]
     d_rows = w_query.shape[0]
     stream = tok_rows * n
     ff_cols = FF // n
+    per = HD // n
+    extra = 16
     position = jnp.arange(stream, dtype=jnp.int32)
-
-    def gather_rows(own):
-        return to_position(lax.all_gather(own, AXES, axis=0, tiled=True), n_ctx, n_wa)
-
-    def scatter_rows(part):
-        return lax.psum_scatter(
-            to_stored(part, n_ctx, n_wa), AXES, scatter_dimension=0, tiled=True
-        ).astype(F32)
+    swap_dp = [(0, 1), (1, 0)]
 
     def mm(a, b):
         return jnp.dot(a, b, preferred_element_type=F32)
@@ -546,34 +793,41 @@
     def t_mm(a, b):
         return lax.dot_general(a, b, (((0,), (0,)), ((), ())), preferred_element_type=F32)
 
-    gains = lax.all_gather(
-        jnp.concatenate([attn_gain, ffn_gain, q_gain, k_gain]), AXES, axis=0
-    ).astype(F32)
+    def pair(w):
+        return jnp.repeat(w.reshape(d_rows, KV, 1, HD), n // KV, axis=2).reshape(d_rows, n, HD)
+
+    def swap(blocks):
+        return lax.all_to_all(blocks, AXES, 0, 0, tiled=True)
+
+    gains_own = jnp.concatenate([attn_gain, ffn_gain, q_gain, k_gain])
+    gains_row = jnp.pad(gains_own, (0, extra * 2 * LANES - gains_own.shape[0]))
+    attn_cols = jnp.concatenate(
+        [w_query.reshape(d_rows, n, LANES), pair(w_key), pair(w_value)], axis=2
+    ).transpose(1, 0, 2)
+    attn_cols = swap(
+        jnp.concatenate(
+            [
+                attn_cols,
+                jnp.broadcast_to(gains_row.reshape(1, extra, 2 * LANES), (n, extra, 2 * LANES)),
+            ],
+            axis=1,
+        )
+    )
+    x_all = gather_tokens(tokens[0], n_ctx, n_wa, True, 1)
+    w_qkv = attn_cols[:, :d_rows].reshape(width, 2 * LANES)
+    gains = attn_cols[:, d_rows:].reshape(n, -1).astype(F32)
     attn_gain32 = gains[:, :d_rows].reshape(-1)
     ffn_gain32 = gains[:, d_rows : 2 * d_rows].reshape(-1)
-    per = HD // n
     qgain32 = gains[:, 2 * d_rows : 2 * d_rows + per].reshape(-1)
-    kgain32 = gains[:, 2 * d_rows + per :].reshape(-1)
-
-    def pair(w):
-        return jnp.repeat(w.reshape(d_rows, KV, 1, HD), n // KV, axis=2).reshape(d_rows, n, HD)
-
-    columns = jnp.concatenate(
-        [
-            w_query.reshape(d_rows, n, LANES),
-            pair(w_key),
-            pair(w_value),
-            w_gate.reshape(d_rows, n, ff_cols),
-            w_up.reshape(d_rows, n, ff_cols),
-        ],
-        axis=2,
+    kgain32 = gains[:, 2 * d_rows + per : 2 * d_rows + 2 * per].reshape(-1)
+
+    w_gate_b, w_up_b, dy_b, _ = lax.optimization_barrier((w_gate, w_up, out_grad[0], x_all))
+    ff_blocks = jnp.concatenate(
+        [w_gate_b.reshape(d_rows, n, ff_cols), w_up_b.reshape(d_rows, n, ff_cols)], axis=2
     ).transpose(1, 0, 2)
-    columns = lax.all_to_all(columns, AXES, 0, 0, tiled=True).reshape(width, -1)
-    w_qkv = columns[:, : 2 * LANES]
-    w_gu = columns[:, 2 * LANES :]
-
-    x_all = gather_rows(tokens[0])
-    dy_all = gather_rows(out_grad[0])
+    w_gu = swap(ff_blocks).reshape(width, 2 * ff_cols)
+    dy_all = lax.all_gather(dy_b, AXES, axis=0, tiled=True)
+
     x_own = tokens[0].astype(F32)
     n1_all = rms_norm(x_all.astype(F32), attn_gain32).astype(BF16)
     qkv = mm(n1_all, w_qkv)
@@ -586,74 +840,93 @@
     kv_b = jnp.concatenate([k_rot.astype(BF16), v_b], axis=1)
     ov_b = jnp.concatenate([jnp.ones_like(v_b), v_b], axis=1)
     att, inv = attend(doc_starts, q_b, kv_b, ov_b)
-    middle = x_own + scatter_rows(mm(att, w_out).astype(BF16))
+    middle = x_own + scatter_tokens(mm(att, w_out).astype(BF16), n_ctx, n_wa, True, 3)
     n2_own, n2_back = jax.vjp(rms_norm, middle, ffn_gain32)
-    n2_all = gather_rows(n2_own.astype(BF16))
+    n2_all = gather_tokens(n2_own.astype(BF16), n_ctx, n_wa, False, 2)
     gate_up = mm(n2_all, w_gu)
     gate, up = gate_up[:, :ff_cols], gate_up[:, ff_cols:]
     sig = jax.nn.sigmoid(gate)
     silu = gate * sig
     hidden = (silu * up).astype(BF16)
-    layer_out = middle + scatter_rows(mm(hidden, w_down).astype(BF16))
+    down_part = mm(hidden, w_down).astype(BF16)
+    down = lax.psum_scatter(down_part, AXES, scatter_dimension=0, tiled=True).astype(F32)
+    layer_out = middle + down
 
     d_hidden = mm_t(dy_all, w_down)
     d_gu = jnp.concatenate(
         [d_hidden * up * (sig * (1.0 + gate * (1.0 - sig))), d_hidden * silu], axis=1
     ).astype(BF16)
-    d_n2 = scatter_rows(mm_t(d_gu, w_gu).astype(BF16))
+    gu_grad = t_mm(n2_all, d_gu).astype(BF16)
+    gu_rows = swap(gu_grad).reshape(n, d_rows, 2 * ff_cols)
     down_grad = t_mm(hidden, dy_all)
-    gu_grad = t_mm(n2_all, d_gu)
-    d_mid_part, d_ffn_gain = n2_back(d_n2)
+    d_n2 = scatter_tokens(mm_t(d_gu, w_gu).astype(BF16), n_ctx, n_wa, False, 4)
+    d_mid_part, _ = n2_back(d_n2)
     d_middle = out_grad[0].astype(F32) + d_mid_part
-    db_all = gather_rows(d_middle.astype(BF16))
+    db_all = gather_tokens(d_middle.astype(BF16), n_ctx, n_wa, True, 1)
     out_w_grad = t_mm(att, db_all)
     d_att = mm_t(db_all, w_out).astype(BF16)
     dq, dkv = attend_back(doc_starts, q_b, kv_b, att, inv, d_att)
-    swap = [(i, i ^ 1) for i in range(n_wa)]
-    dkv = dkv + lax.ppermute(dkv, "wa", swap)
+    dkv = dkv + lax.ppermute(dkv, "wa", [(i, i ^ 1) for i in range(n_wa)])
     dq_raw, dk_raw, d_qgain, d_kgain = prep_back((dq * HD**-0.5, dkv[:, :HD] * HD**-0.5))
     d_kgain = jnp.where(even, d_kgain, 0.0)
     d_kv_own = jnp.where(even, dk_raw, dkv[:, HD:])
     w_kv_own = jnp.where(even, w_qkv[:, LANES : LANES + HD], w_qkv[:, LANES + HD :])
     d_qkv = jnp.concatenate([dq_raw, d_kv_own], axis=1).astype(BF16)
-    d_n1 = scatter_rows(mm_t(d_qkv, jnp.concatenate([w_qkv[:, :LANES], w_kv_own], axis=1)).astype(BF16))
-    qkv_grad = t_mm(n1_all, d_qkv)
+    qkv_grad = t_mm(n1_all, d_qkv).astype(BF16)
+    head_gains = jnp.concatenate([d_qgain, d_kgain])
+    qkv_cols = LANES + HD
+    head_row = jnp.pad(head_gains.astype(BF16), (0, extra * qkv_cols - LANES))
+    qkv_rows = swap(
+        jnp.concatenate(
+            [
+                qkv_grad.reshape(n, d_rows, qkv_cols),
+                jnp.broadcast_to(head_row.reshape(1, extra, qkv_cols), (n, extra, qkv_cols)),
+            ],
+            axis=1,
+        )
+    )
+    d_n1_part = mm_t(d_qkv, jnp.concatenate([w_qkv[:, :LANES], w_kv_own], axis=1)).astype(BF16)
+    d_n1 = scatter_tokens(d_n1_part, n_ctx, n_wa, True, 3)
     _, n1_back = jax.vjp(rms_norm, x_own, attn_gain32)
-    d_x_part, d_attn_gain = n1_back(d_n1)
+    d_x_part, _ = n1_back(d_n1)
     input_grad = d_middle + d_x_part
 
-    col_grads = jnp.concatenate([gu_grad, qkv_grad], axis=1).astype(BF16)
-    row_grads = lax.all_to_all(col_grads, AXES, 0, 0, tiled=True).reshape(n, d_rows, -1)
-    swap_dp = [(0, 1), (1, 0)]
-    row_other = lax.ppermute(row_grads, "dp", swap_dp)
-    row_grads = (row_grads.astype(F32) + row_other.astype(F32)).transpose(1, 0, 2)
-
     def both(part):
-        return part + lax.ppermute(part.astype(BF16), "dp", swap_dp).astype(F32)
+        part = part.astype(BF16)
+        return part.astype(F32) + lax.ppermute(part, "dp", swap_dp).astype(F32)
 
     def flat(part):
-        return part.reshape(d_rows, -1)
-
-    kv_grads = row_grads[:, :, 2 * ff_cols + LANES :].reshape(d_rows, KV, 2, HD)
-    small = jnp.concatenate([d_attn_gain, d_ffn_gain, d_qgain, d_kgain])
-    small = lax.psum(small, ("dp",) + AXES)
-
-    def mine(total, begin, size):
-        return lax.dynamic_slice_in_dim(total, begin + me * size, size)
-
+        return part.transpose(1, 0, 2).reshape(d_rows, -1)
+
+    gu_rows = both(gu_rows)
+    gate_grad, up_grad = flat(gu_rows[:, :, :ff_cols]), flat(gu_rows[:, :, ff_cols:])
+    qkv_rows = both(qkv_rows)
+    q_grad = flat(qkv_rows[:, :d_rows, :LANES])
+    kv_grad = qkv_rows[:, :d_rows, LANES:].reshape(KV, 2, d_rows, HD)
+    k_grad, v_grad = flat(kv_grad[:, 0]), flat(kv_grad[:, 1])
+    head_sums = jnp.sum(qkv_rows[:, d_rows:].reshape(n, -1)[:, :LANES], axis=0)
+    me = lax.axis_index("ctx") * n_wa + lax.axis_index("wa")
+
+    def row_sum(weight, grad):
+        return jnp.sum(weight.astype(F32) * grad, axis=1)
+
+    attn_gain_grad = (
+        row_sum(w_query, q_grad) + row_sum(w_key, k_grad) + row_sum(w_value, v_grad)
+    ) / attn_gain.astype(F32)
+    ffn_gain_grad = (row_sum(w_gate, gate_grad) + row_sum(w_up, up_grad)) / ffn_gain.astype(F32)
     return (
         layer_out.astype(BF16)[None],
         input_grad.astype(BF16)[None],
-        mine(small, 0, d_rows),
-        flat(row_grads[:, :, 2 * ff_cols : 2 * ff_cols + LANES]),
-        flat(kv_grads[:, :, 0]),
-        flat(kv_grads[:, :, 1]),
-        mine(small, 2 * width, per),
-        mine(small, 2 * width + HD, per),
+        attn_gain_grad,
+        q_grad,
+        k_grad,
+        v_grad,
+        lax.dynamic_slice_in_dim(head_sums, me * per, per),
+        lax.dynamic_slice_in_dim(head_sums, HD + me * per, per),
         both(out_w_grad),
-        mine(small, width, d_rows),
-        flat(row_grads[:, :, :ff_cols]),
-        flat(row_grads[:, :, ff_cols : 2 * ff_cols]),
+        ffn_gain_grad,
+        gate_grad,
+        up_grad,
         both(down_grad),
     )
 

time: 1400 us -> 864 us (0.62); the launches traced: 1380 us -> 859 us
  waiting for transfers between devices: 636 us -> 142 us
  Pallas kernels: 30.9 us -> 439 us
  blocking collectives: 248 us -> 0 us
  local copies, waits for them, and re-layouts: 196 us -> 59.1 us
  other arithmetic: 137 us -> 71.1 us
    pallas_call x0 -> x6, Pallas kernels: none -> 412 us  [the longest x3 251 us: scatter_tokens(): pl.pallas_call(partial(scatter_kernel, n_ctx, n_wa, by_position), in_spec...]
    reduce_scatter x4 -> x1, waiting for transfers between devices: 206 us -> 0.01 us  [per_device_heads(): lax.psum_scatter(down_part, AXES, scatter_dimension=0, tiled=True)]
    all_gather x4 -> x1, waiting for transfers between devices: 199 us -> 0.01 us  [per_device_heads(): dy_all = lax.all_gather(dy_b, AXES, axis=0, tiled=True)]
    unnamed x1 -> x0, blocking collectives: 190 us -> none
    all_to_all x2 -> x4, waiting for transfers between devices: 89.4 us -> 28.8 us  [swap(): return lax.all_to_all(blocks, AXES, 0, 0, tiled=True)]
    psum x1 -> x0, blocking collectives: 58.7 us -> none  [per_device_heads(): small = lax.psum(small, ('dp',) + AXES)]
    another operation x10 -> x1, local copies, waits for them, and re-layouts: 46.2 us -> 1.24 us  [the longest x8 42.7 us: to_stored(): paired = jnp.stack([parts[:n_ctx], jnp.flip(parts[n_ctx:], axis=0)], axis=2)]
    another operation x8 -> x5, other arithmetic: 38.6 us -> 8.07 us  [the longest x4 30 us: to_stored(): paired = jnp.stack([parts[:n_ctx], jnp.flip(parts[n_ctx:], axis=0)], axis=2)]
  transfers between devices with their start and end apart: 14 -> 11, of which waited for: 8 -> 3; matrix products, arithmetic and copies ran while one was open for 15% -> 22% of each run, Pallas kernels for 0% -> 45%
where the time goes in v2:
time: 864 us; the launch traced here: 859 us
  Pallas kernels  439 us (51%)
  waiting for transfers between devices  142 us (16%)
  matrix products  104 us (12%)
  other arithmetic  71.1 us (8%)
  local copies, waits for them, and re-layouts  59.1 us (7%)
  starting transfers between devices  28.8 us (3%)
  between operations  15.6 us (2%)
    pallas_call x3, Pallas kernels, scatter_tokens(): pl.pallas_call(partial(scatter_kernel, n_ctx, n_wa, by_position), in_spec...  251 us
    pallas_call x3, Pallas kernels, gather_tokens(): pl.pallas_call(partial(gather_kernel, n_ctx, n_wa, by_position), in_specs...  161 us
    ppermute x4, waiting for transfers between devices, both(): return part.astype(F32) + lax.ppermute(part, 'dp', swap_dp).astype(F32)  113 us
    dot_general x4, matrix products, t_mm(): lax.dot_general(a, b, (((0,), (0,)), ((), ())), preferred_element_type=F32)  35.1 us
    dot_general x4, matrix products, mm_t(): lax.dot_general(a, b, (((1,), (1,)), ((), ())), preferred_element_type=F32)  35.1 us
    dot_general x4, matrix products, mm(): return jnp.dot(a, b, preferred_element_type=F32)  34.2 us
    all_to_all x4, waiting for transfers between devices, swap(): return lax.all_to_all(blocks, AXES, 0, 0, tiled=True)  28.8 us
    all_to_all x4, starting transfers between devices, swap(): return lax.all_to_all(blocks, AXES, 0, 0, tiled=True)  23.1 us
  transfers between devices with their start and end apart: 11, of which 3 were waited for; matrix products, arithmetic and copies ran while one was open for 22% of the time, Pallas kernels for 45%

profile of v2, /device:TPU:0, one launch (start us, length us, event | category | flops | bytes accessed | tf_op | source)
XLA Modules:
  0.0 859.3 jit_solution(12865859000997751688)
XLA Ops:
  7.3 52.6 %shard_map.237 = bf16[2048,2048]{1,0:T(8,128)(2,1)} custom-call(bf16[128,2048]{1,0:T(8,128)(2,1)} %bitcast.125), custom_call_target="tpu_custom_call" | custom-call | tf_op jit(solution)/shard_map/pallas_call | solution.py:607
  62.6 4.9 all-to-all-start
  67.5 4.2 copy.119
  71.7 4.1 copy.120
  75.8 4.6 maximum_bitcast_fusion
  80.4 28.8 %all-to-all-done = bf16[16,144,256]{2,1,0:T(8,128)(2,1)S(1)} async-done(((bf16[16,144,256]{2,1,0:T(8,128)(2,1)}), bf16[16,144,256]{2,1,0:T(8,128)(2,1)S(1)}, u32[]{:S(2)}, u32[]{:S(2)}) %all-to-all-start) | async-done | bytes 1179680 | tf_op jit(solution)/shard_map/all_to_all | solution.py:800
  109.2 8.0 all-to-all-start.1
  117.2 5.1 fusion
  122.3 1.8 multiply_cosine_fusion.1
  124.4 5.6 fusion.5
  135.8 1.3 multiply_reduce_fusion.8
  137.2 1.4 multiply_multiply_fusion
  139.1 1.8 multiply_reduce_fusion.7
  140.9 1.6 multiply_bitcast_fusion
  142.5 4.8 fusion.16
  148.1 10.6 %shard_map.238 = (bf16[2048,128]{1,0:T(8,128)(2,1)S(1)}, f32[2048,128]{1,0:T(8,128)S(1)}) custom-call(s32[1,8]{1,0:T(1,128)S(1)} %copy-done.11, bf16[2048,128]{1,0:T(8,128)(2,1)S(1)} %copy.118.q_ref, bf16[2048,128]{1,0:T(8,128)(2,1)S(1)} %get-tuple-element.103.kv_ref, bf16[2048,128]{1,0:T(8,128)(2,1)S(1)} %get-tuple-element.102.ov_ref), custom_call_target="tpu_custom_call" | custom-call | flops 1073741824 | bytes 3145728 | tf_op jit(solution)/shard_map/pallas_call | solution.py:446
  159.7 5.6 convolution_convert_fusion.3.part_ref
  166.1 95.2 %shard_map.239 = f32[128,2048]{1,0:T(8,128)S(1)} custom-call(bf16[2048,2048]{1,0:T(8,128)(2,1)} %convolution_convert_fusion.3.part_ref), custom_call_target="tpu_custom_call" | custom-call | tf_op jit(solution)/shard_map/pallas_call | solution.py:738
  262.5 54.3 %shard_map.240 = bf16[2048,2048]{1,0:T(8,128)(2,1)} custom-call(bf16[128,2048]{1,0:T(8,128)(2,1)} %multiply_convert_fusion.3.own_ref), custom_call_target="tpu_custom_call" | custom-call | tf_op jit(solution)/shard_map/pallas_call | solution.py:607
  316.8 6.4 copy.121
  323.2 14.6 %fusion.62 = f32[2048,1024]{0,1:T(8,128)} fusion(bf16[2048,2048]{1,0:T(8,128)(2,1)} %shard_map.240, bf16[2048,1024]{1,0:T(8,128)(2,1)} %bitcast.138), kind=kOutput, calls=%fused_computation.149 | convolution fusion | flops 8589934592 | bytes 20971520 | tf_op jit(solution)/shard_map/dot_general | solution.py:788
  337.8 11.9 %multiply_convert_fusion.1 = (bf16[2048,512]{0,1:T(8,128)(2,1)S(1)}, bf16[2048,512]{0,1:T(8,128)(2,1)S(1)}, bf16[2048,512]{0,1:T(8,128)(2,1)}) fusion(f32[2048,1024]{0,1:T(8,128)} %fusion.62, bf16[2048,2048]{1,0:T(8,128)(2,1)} %all-gather.2.cloned.1.call-done, bf16[512,2048]{1,0:T(8,128)(2,1)S(1)} %copy-done), kind=kOutput, calls=%fused_computation.18 | convolution fusion | flops 4310695936 | bytes 25165824 | tf_op jit(solution)/shard_map/dot_general | solution.py:791
  349.7 12.6 %convolution_convert_fusion.4 = bf16[2048,1024]{1,0:T(8,128)(2,1)} fusion(bf16[2048,2048]{1,0:T(8,128)(2,1)S(1)} %copy-done.24, bf16[2048,512]{0,1:T(8,128)(2,1)S(1)} %get-tuple-element.86, bf16[2048,512]{0,1:T(8,128)(2,1)S(1)} %get-tuple-element.85), kind=kOutput, calls=%fused_computation.22 | convolution fusion | flops 8600420352 | bytes 16777216 | tf_op jit(solution)/shard_map/dot_general | solution.py:794
  362.3 11.5 %convolution_convert_fusion.1.part_ref = bf16[2048,2048]{1,0:T(8,128)(2,1)} fusion(bf16[2048,1024]{1,0:T(8,128)(2,1)S(1)} %bitcast.139, bf16[2048,512]{0,1:T(8,128)(2,1)S(1)} %get-tuple-element.86, bf16[2048,512]{0,1:T(8,128)(2,1)S(1)} %get-tuple-element.85), kind=kOutput, calls=%fused_computation.7 | convolution fusion | flops 8602517504 | bytes 16777216 | tf_op jit(solution)/shard_map/dot_general | solution.py:791
  373.8 5.0 all-to-all-start.3
  379.0 9.9 %convolution_convert_fusion.5 = bf16[512,2048]{1,0:T(8,128)(2,1)} fusion(bf16[2048,512]{0,1:T(8,128)(2,1)} %get-tuple-element.89, bf16[2048,2048]{1,0:T(8,128)(2,1)} %all-gather.2.cloned.1.call-done), kind=kOutput, calls=%fused_computation.24 | convolution fusion | flops 4296015872 | bytes 12582912 | tf_op jit(solution)/shard_map/dot_general | solution.py:794
  388.9 1.5 collective-permute-start.4
  390.3 102.1 %shard_map.241 = f32[128,2048]{1,0:T(8,128)S(1)} custom-call(bf16[2048,2048]{1,0:T(8,128)(2,1)} %convolution_convert_fusion.1.part_ref), custom_call_target="tpu_custom_call" | custom-call | tf_op jit(solution)/shard_map/pallas_call | solution.py:738
  494.6 53.9 %shard_map.242 = bf16[2048,2048]{1,0:T(8,128)(2,1)} custom-call(bf16[128,2048]{1,0:T(8,128)(2,1)} %fusion.57.own_ref), custom_call_target="tpu_custom_call" | custom-call | tf_op jit(solution)/shard_map/pallas_call | solution.py:607
  548.6 8.4 convolution_convert_fusion.2
  557.0 5.9 convolution_convert_fusion.8.da_ref
  563.0 16.4 %shard_map.243 = (f32[2048,128]{1,0:T(8,128)S(1)}, f32[2048,128]{1,0:T(8,128)S(1)}) custom-call(s32[1,8]{1,0:T(1,128)S(1)} %copy-done.11, bf16[2048,128]{1,0:T(8,128)(2,1)S(1)} %copy-done.8, bf16[2048,128]{1,0:T(8,128)(2,1)S(1)} %copy-done.10, bf16[2048,128]{1,0:T(8,128)(2,1)S(1)} %copy-done.4, f32[2048,128]{1,0:T(8,128)S(1)} %copy-done.13, ...), custom_call_target="tpu_custom_call" | custom-call | flops 2684354560 | bytes 4194304 | tf_op jit(solution)/shard_map/pallas_call | solution.py:467
  581.5 2.5 copy.123
  584.5 1.6 multiply_add_fusion.1
  586.1 1.9 multiply_reduce_fusion.3
  589.3 4.4 fusion.19
  594.7 2.1 fusion.25
  598.0 7.0 convolution_convert_fusion.6
  604.9 2.2 copy.137
  607.4 2.5 pad_maximum_fusion.4
  609.8 5.2 all-to-all-start.2
  615.1 1.5 collective-permute-start.3
  616.6 5.7 convolution_convert_fusion.7
  624.0 1.4 slice_select_fusion
  625.4 94.1 %collective-permute-done.2 = bf16[128,2048]{1,0:T(8,128)(2,1)} collective-permute-done((bf16[128,2048]{1,0:T(8,128)(2,1)}, bf16[128,2048]{1,0:T(8,128)(2,1)}, u32[]{:S(2)}, u32[]{:S(2)}) %collective-permute-start.2) | collective-permute-done | bytes 524320 | tf_op jit(solution)/shard_map/ppermute | solution.py:896
  719.5 2.3 convert_add_fusion.4
  721.8 5.7 convolution_convert_fusion.part_ref
  727.5 53.5 %shard_map.244 = f32[128,2048]{1,0:T(8,128)S(1)} custom-call(bf16[2048,2048]{1,0:T(8,128)(2,1)} %convolution_convert_fusion.part_ref), custom_call_target="tpu_custom_call" | custom-call | tf_op jit(solution)/shard_map/pallas_call | solution.py:738
  782.2 1.5 collective-permute-start.1
  784.4 5.0 convert_add_fusion.1
  789.4 2.9 copy.126
  792.3 18.7 %collective-permute-done.1 = bf16[16,144,192]{2,1,0:T(8,128)(2,1)} collective-permute-done((bf16[16,144,192]{2,1,0:T(8,128)(2,1)}, bf16[16,144,192]{2,1,0:T(8,128)(2,1)}, u32[]{:S(2)}, u32[]{:S(2)}) %collective-permute-start.1) | collective-permute-done | bytes 884768 | tf_op jit(solution)/shard_map/ppermute | solution.py:896
  811.1 2.6 copy.127
  813.7 2.3 convert_add_fusion.2
  819.2 2.5 copy.128
  821.7 2.0 copy.131
  824.5 1.8 fusion.58
  827.1 1.8 copy.136
  831.3 1.5 multiply_reduce_fusion.2
  834.0 5.5 convert_add_fusion
  839.6 1.4 slice_bitcast_fusion
  842.0 1.6 copy-done.20
  844.7 2.0 copy-done.23
  848.1 3.8 fusion.37
  (194 shorter events, 36.7 us)
Async XLA Ops:
  7.2 330.6 %copy-start = (bf16[512,2048]{1,0:T(8,128)(2,1)S(1)}, bf16[512,2048]{1,0:T(8,128)(2,1)}, u32[]{:S(2)}) copy-start(bf16[512,2048]{1,0:T(8,128)(2,1)} %param.27) | copy-start | bytes 6291460
  7.2 330.6 %all-gather.2.cloned.1.call-start = ((), (), s32[]{:S(2)}) async-start(), calls=%async_computation.6 | async-start | bytes 8912896 | tf_op jit(solution)/shard_map/all_gather | solution.py:829
  7.2 52.7 %copy-start.37 = (bf16[128,512]{1,0:T(8,128)(2,1)S(1)}, bf16[128,512]{1,0:T(8,128)(2,1)}, u32[]{:S(2)}) copy-start(bf16[128,512]{1,0:T(8,128)(2,1)} %param.19) | copy-start | bytes 393220
  7.2 53.1 %copy-start.38 = (bf16[128,512]{1,0:T(8,128)(2,1)S(1)}, bf16[128,512]{1,0:T(8,128)(2,1)}, u32[]{:S(2)}) copy-start(bf16[128,512]{1,0:T(8,128)(2,1)} %param.20) | copy-start | bytes 393220
  7.3 53.4 %copy-start.48 = (bf16[128]{0:T(256)(128)(2,1)S(1)}, bf16[128]{0:T(256)(128)(2,1)}, u32[]{:S(2)}) copy-start(bf16[128]{0:T(256)(128)(2,1)} %param.17) | copy-start | bytes 772
  7.3 53.4 %copy-start.49 = (bf16[128]{0:T(256)(128)(2,1)S(1)}, bf16[128]{0:T(256)(128)(2,1)}, u32[]{:S(2)}) copy-start(bf16[128]{0:T(256)(128)(2,1)} %param.24) | copy-start | bytes 772
  7.3 53.4 %copy-start.55 = (bf16[4]{0:T(256)(128)(2,1)S(1)}, bf16[4]{0:T(256)(128)(2,1)}, u32[]{:S(2)}) copy-start(bf16[4]{0:T(256)(128)(2,1)} %param.22) | copy-start | bytes 28
  7.3 53.4 %copy-start.56 = (bf16[4]{0:T(256)(128)(2,1)S(1)}, bf16[4]{0:T(256)(128)(2,1)}, u32[]{:S(2)}) copy-start(bf16[4]{0:T(256)(128)(2,1)} %param.21) | copy-start | bytes 28
  7.3 53.5 %copy-start.29 = (bf16[128,2048]{1,0:T(8,128)(2,1)S(1)}, bf16[128,2048]{1,0:T(8,128)(2,1)}, u32[]{:S(2)}) copy-start(bf16[128,2048]{1,0:T(8,128)(2,1)} %param.18) | copy-start | bytes 1572868
  60.1 2.5 copy-start.32
  60.4 2.2 copy-start.34
  62.6 46.7 %all-to-all-start = ((bf16[16,144,256]{2,1,0:T(8,128)(2,1)}), bf16[16,144,256]{2,1,0:T(8,128)(2,1)S(1)}, u32[]{:S(2)}, u32[]{:S(2)}) async-start(bf16[16,144,256]{2,1,0:T(8,128)(2,1)} %pad_maximum_fusion.3), calls=%async_computation | async-start | bytes 2359296 | tf_op jit(solution)/shard_map/all_to_all | solution.py:800
  75.7 46.6 %copy-start.43 = (f32[32]{0:T(128)}, f32[32]{0:T(128)S(1)}, u32[]{:S(2)}) copy-start(f32[32]{0:T(128)S(1)} %multiply_power_fusion) | copy-start | bytes 388
  109.2 207.6 %all-to-all-start.1 = ((bf16[16,128,1024]{1,2,0:T(8,128)(2,1)}), bf16[16,128,1024]{1,2,0:T(8,128)(2,1)}, u32[]{:S(2)}, u32[]{:S(2)}) async-start(bf16[16,128,1024]{1,2,0:T(8,128)(2,1)} %maximum_bitcast_fusion), calls=%async_computation.1 | async-start | bytes 8388608 | tf_op jit(solution)/shard_map/all_to_all | solution.py:800
  122.3 7.7 copy-start.41
  124.3 5.8 copy-start.36
  124.4 5.7 copy-start.25
  124.4 5.6 copy-start.39
  130.1 1.3 copy-start.18
  130.1 8.5 copy-start.28
  138.6 3.9 copy-start.44
  139.1 9.0 %copy-start.7 = (bf16[2048,128]{1,0:T(8,128)(2,1)}, bf16[2048,128]{1,0:T(8,128)(2,1)S(1)}, u32[]{:S(2)}) copy-start(bf16[2048,128]{1,0:T(8,128)(2,1)S(1)} %copy.118.q_ref) | copy-start | bytes 1572868
  139.1 8.5 copy-start.31
  140.9 7.2 copy-start.11
  147.3 12.4 %copy-start.35 = (bf16[128,2048]{1,0:T(8,128)(2,1)S(1)}, bf16[128,2048]{1,0:T(8,128)(2,1)}, u32[]{:S(2)}) copy-start(bf16[128,2048]{1,0:T(8,128)(2,1)} %param.23) | copy-start | bytes 1572868
  148.1 10.6 %copy-start.9 = (bf16[2048,128]{1,0:T(8,128)(2,1)}, bf16[2048,128]{1,0:T(8,128)(2,1)S(1)}, u32[]{:S(2)}) copy-start(bf16[2048,128]{1,0:T(8,128)(2,1)S(1)} %get-tuple-element.103.kv_ref) | copy-start | bytes 1572868
  158.7 1.0 copy-start.12
  166.1 95.2 %copy-start.15 = (bf16[1,128,2048]{2,1,0:T(8,128)(2,1)S(1)}, bf16[1,128,2048]{2,1,0:T(8,128)(2,1)}, u32[]{:S(2)}) copy-start(bf16[1,128,2048]{2,1,0:T(8,128)(2,1)} %param.14) | copy-start | bytes 1572868
  261.6 231.8 %copy-start.45 = (f32[128]{0:T(128)}, f32[128]{0:T(128)S(1)}, u32[]{:S(2)}) copy-start(f32[128]{0:T(128)S(1)} %fusion.51) | copy-start | bytes 1540
  337.8 11.9 %copy-start.24 = (bf16[2048,2048]{1,0:T(8,128)(2,1)S(1)}, bf16[2048,2048]{1,0:T(8,128)(2,1)}, u32[]{:S(2)}) copy-start(bf16[2048,2048]{1,0:T(8,128)(2,1)} %shard_map.240) | copy-start | bytes 25165828
  349.7 12.6 %copy-start.27 = (bf16[16,128,1024]{2,1,0:T(8,128)(2,1)S(1)}, bf16[16,128,1024]{2,1,0:T(8,128)(2,1)}, u32[]{:S(2)}) copy-start(bf16[16,128,1024]{2,1,0:T(8,128)(2,1)} %copy.121) | copy-start | bytes 12582916
  373.8 236.1 %all-to-all-start.3 = ((bf16[16,128,1024]{2,1,0:T(8,128)(2,1)}), bf16[16,128,1024]{2,1,0:T(8,128)(2,1)}, u32[]{:S(2)}, u32[]{:S(2)}) async-start(bf16[16,128,1024]{2,1,0:T(8,128)(2,1)} %bitcast.137), calls=%async_computation.4 | async-start | bytes 8388608 | tf_op jit(solution)/shard_map/all_to_all | solution.py:800
  378.8 469.3 %reduce-scatter.2.cloned.1.call-start = ((), (), s32[]{:S(2)}) async-start(), calls=%async_computation.5 | async-start | bytes 8912896 | tf_op jit(solution)/shard_map/reduce_scatter | solution.py:852
  388.8 103.6 %copy-start.16 = (bf16[1,128,2048]{2,1,0:T(8,128)(2,1)S(1)}, bf16[1,128,2048]{2,1,0:T(8,128)(2,1)}, u32[]{:S(2)}) copy-start(bf16[1,128,2048]{2,1,0:T(8,128)(2,1)} %param.14) | copy-start | bytes 1572868
  388.9 104.6 %copy-start.26 = (bf16[1,128,2048]{2,1,0:T(8,128)(2,1)S(1)}, bf16[1,128,2048]{2,1,0:T(8,128)(2,1)}, u32[]{:S(2)}) copy-start(bf16[1,128,2048]{2,1,0:T(8,128)(2,1)} %param.16) | copy-start | bytes 1572868
  388.9 395.5 %collective-permute-start.4 = (bf16[512,2048]{1,0:T(8,128)(2,1)}, bf16[512,2048]{1,0:T(8,128)(2,1)}, u32[]{:S(2)}, u32[]{:S(2)}) collective-permute-start(bf16[512,2048]{1,0:T(8,128)(2,1)} %convolution_convert_fusion.5), channel_id=1, source_target_pairs={{0,16},{16,0},{1,17},{17,1},{2,18},{18,2},{3,19},{19,3},{4,20},{20... | collective-permute-start | bytes 6291464 | tf_op jit(solution)/shard_map/ppermute | solution.py:896
  493.5 55.1 %copy-start.51 = (f32[128]{0:T(128)}, f32[128]{0:T(128)S(1)}, u32[]{:S(2)}) copy-start(f32[128]{0:T(128)S(1)} %multiply_multiply_fusion.4) | copy-start | bytes 1540
  557.0 6.0 copy-start.4
  557.0 6.0 copy-start.8
  557.0 6.0 copy-start.10
  557.0 6.0 copy-start.13
  584.0 4.0 copy-start.19
  584.0 5.1 collective-permute-start
  584.5 4.7 copy-start.6
  589.1 4.6 copy-start.14
  593.7 4.3 copy-start.40
  593.7 4.3 copy-start.42
  609.8 172.4 %all-to-all-start.2 = ((bf16[16,144,192]{2,1,0:T(8,128)(2,1)}), bf16[16,144,192]{2,1,0:T(8,128)(2,1)}, u32[]{:S(2)}, u32[]{:S(2)}) async-start(bf16[16,144,192]{2,1,0:T(8,128)(2,1)} %pad_maximum_fusion.4), calls=%async_computation.3 | async-start | bytes 2359296 | tf_op jit(solution)/shard_map/all_to_all | solution.py:800
  615.1 218.9 %collective-permute-start.3 = (bf16[16,128,1024]{2,1,0:T(8,128)(2,1)}, bf16[16,128,1024]{2,1,0:T(8,128)(2,1)}, u32[]{:S(2)}, u32[]{:S(2)}) collective-permute-start(bf16[16,128,1024]{2,1,0:T(8,128)(2,1)} %all-to-all-done.3), channel_id=1, source_target_pairs={{0,16},{16,0},{1,17},{17,1},{2,18},{18,2},{3,19},{19,3},{4,20},{20... | collective-permute-start | bytes 12582920 | tf_op jit(solution)/shard_map/ppermute | solution.py:896
  622.3 97.1 %collective-permute-start.2 = (bf16[128,2048]{1,0:T(8,128)(2,1)}, bf16[128,2048]{1,0:T(8,128)(2,1)}, u32[]{:S(2)}, u32[]{:S(2)}) collective-permute-start(bf16[128,2048]{1,0:T(8,128)(2,1)} %convolution_convert_fusion.7), channel_id=1, source_target_pairs={{0,16},{16,0},{1,17},{17,1},{2,18},{18,2},{3,19},{19,3},{4,20},{20... | collective-permute-start | bytes 1572872 | tf_op jit(solution)/shard_map/ppermute | solution.py:896
  622.8 98.9 %copy-start.30 = (bf16[2048,2,64]{0,2,1:T(8,128)(2,1)S(1)}, bf16[2048,2,64]{0,2,1:T(8,128)(2,1)}, u32[]{:S(2)}) copy-start(bf16[2048,2,64]{0,2,1:T(8,128)(2,1)} %fusion.22) | copy-start | bytes 1572868
  727.5 54.5 %copy-start.17 = (bf16[1,128,2048]{2,1,0:T(8,128)(2,1)S(1)}, bf16[1,128,2048]{2,1,0:T(8,128)(2,1)}, u32[]{:S(2)}) copy-start(bf16[1,128,2048]{2,1,0:T(8,128)(2,1)} %param.14) | copy-start | bytes 1572868
  727.5 56.3 %copy-start.47 = (f32[128]{0:T(128)S(1)}, f32[128]{0:T(128)}, u32[]{:S(2)}) copy-start(f32[128]{0:T(128)} %get-tuple-element.83) | copy-start | bytes 1540
  781.0 1.0 copy-start.2
  782.2 28.8 %collective-permute-start.1 = (bf16[16,144,192]{2,1,0:T(8,128)(2,1)}, bf16[16,144,192]{2,1,0:T(8,128)(2,1)}, u32[]{:S(2)}, u32[]{:S(2)}) collective-permute-start(bf16[16,144,192]{2,1,0:T(8,128)(2,1)} %all-to-all-done.2), channel_id=1, source_target_pairs={{0,16},{16,0},{1,17},{17,1},{2,18},{18,2},{3,19},{19,3},{4,20},{20... | collective-permute-start | bytes 2654216 | tf_op jit(solution)/shard_map/ppermute | solution.py:896
  817.9 12.3 %copy-start.33 = (bf16[128,512]{0,1:T(8,128)(2,1)S(1)}, bf16[128,512]{0,1:T(8,128)(2,1)}, u32[]{:S(2)}) copy-start(bf16[128,512]{0,1:T(8,128)(2,1)} %copy-done.32) | copy-start | bytes 393220
  841.5 2.1 copy-start.20
  841.5 3.2 copy-start.22
  841.5 5.1 copy-start.23
  842.0 5.6 copy-start.21
  846.6 1.5 copy-start.46
  846.6 1.5 copy-start.52
  846.6 1.5 copy-start.53
  846.6 1.5 copy-start.54
  (4 other events, 3.7 us)
Sparse Core Ops, SparseCore 0:
  60.1 153.9 all-gather.1
  557.1 115.7 reduce-scatter.1

commit v3 on v2

--- a/solution.py
+++ b/solution.py
@@ -480,6 +480,82 @@
     )(starts, q, kv, att, inv, da)
 
 
+def pack_attn_kernel(query_ref, key_ref, value_ref, gains_ref, out_ref):
+    n, rows, _ = out_ref.shape
+    d_rows = query_ref.shape[0]
+    share = n // KV
+    for j in range(n):
+        head = j // share * HD
+        out_ref[j, :d_rows, :LANES] = query_ref[:, j * LANES : (j + 1) * LANES]
+        out_ref[j, :d_rows, LANES:] = jnp.concatenate(
+            [key_ref[:, head : head + HD], value_ref[:, head : head + HD]], axis=1
+        )
+        out_ref[j, d_rows:, :] = gains_ref[...]
+
+
+def pack_attn(w_query, w_key, w_value, gains, n):
+    d_rows = w_query.shape[0]
+    return pl.pallas_call(
+        pack_attn_kernel,
+        out_shape=jax.ShapeDtypeStruct((n, d_rows + gains.shape[0], 2 * LANES), BF16),
+    )(w_query, w_key, w_value, gains)
+
+
+def pack_pair_kernel(gate_ref, up_ref, out_ref):
+    cols = gate_ref.shape[1]
+    out_ref[0, :, :cols] = gate_ref[...]
+    out_ref[0, :, cols:] = up_ref[...]
+
+
+def pack_pair(w_gate, w_up, n):
+    d_rows, cols = w_gate.shape[0], w_gate.shape[1] // n
+    part = pl.BlockSpec((d_rows, cols), lambda j: (0, j))
+    return pl.pallas_call(
+        pack_pair_kernel,
+        grid=(n,),
+        in_specs=[part, part],
+        out_specs=pl.BlockSpec((1, d_rows, 2 * cols), lambda j: (j, 0, 0)),
+        out_shape=jax.ShapeDtypeStruct((n, d_rows, 2 * cols), BF16),
+    )(w_gate, w_up)
+
+
+def unpack_pair_kernel(own_ref, other_ref, gate_w, up_w, gate_ref, up_ref, sum_ref):
+    first = lax.axis_index("dp") == 0
+    own, other = own_ref[0].astype(F32), other_ref[0].astype(F32)
+    grads = jnp.concatenate(
+        [jnp.where(first, own, other), jnp.where(first, other, own)], axis=0
+    )
+    cols = gate_ref.shape[1]
+    gate, up = grads[:, :cols], grads[:, cols:]
+    gate_ref[...] = gate
+    up_ref[...] = up
+    total = gate * gate_w[...].astype(F32) + up * up_w[...].astype(F32)
+
+    @pl.when(pl.program_id(0) == 0)
+    def _():
+        sum_ref[...] = jnp.zeros_like(sum_ref)
+
+    sum_ref[...] += jnp.broadcast_to(jnp.sum(total, axis=1, keepdims=True), sum_ref.shape)
+
+
+def unpack_pair(own, other, w_gate, w_up):
+    n, half, both_cols = own.shape
+    cols = both_cols // 2
+    block = pl.BlockSpec((1, half, both_cols), lambda j: (j, 0, 0))
+    part = pl.BlockSpec((2 * half, cols), lambda j: (0, j))
+    return pl.pallas_call(
+        unpack_pair_kernel,
+        grid=(n,),
+        in_specs=[block, block, part, part],
+        out_specs=[part, part, pl.BlockSpec((2 * half, 128), lambda j: (0, 0))],
+        out_shape=[
+            jax.ShapeDtypeStruct(w_gate.shape, F32),
+            jax.ShapeDtypeStruct(w_up.shape, F32),
+            jax.ShapeDtypeStruct((2 * half, 128), F32),
+        ],
+    )(own, other, w_gate, w_up)
+
+
 def head_prepare(q_raw, k_raw, q_gain, k_gain, position):
     stream = q_raw.shape[0]
     q, k = prepare(
@@ -489,6 +565,7 @@
 
 
 MESH_ID = pl.DeviceIdType.MESH
+LINK_COST = pl.CostEstimate(flops=5 * 10**10, bytes_accessed=2**24, transcendentals=0)
 
 
 def meet_neighbours(ctx, wa, n_ctx):
@@ -497,12 +574,60 @@
     def greet(where):
         pl.semaphore_signal(barrier, inc=1, device_id=where, device_id_type=MESH_ID)
 
+    greet({"dp": lax.axis_index("dp") ^ 1})
     greet({"wa": wa ^ 1})
     greet({"wa": wa ^ 2})
     pl.when(ctx > 0)(lambda: greet({"ctx": ctx - 1}))
     pl.when(ctx < n_ctx - 1)(lambda: greet({"ctx": ctx + 1}))
     ends = (ctx == 0).astype(jnp.int32) + (ctx == n_ctx - 1).astype(jnp.int32)
-    pl.semaphore_wait(barrier, 4 - ends)
+    pl.semaphore_wait(barrier, 5 - ends)
+
+
+WHOLE, PLACE, PICK = 0, 1, 2
+
+
+def pair_shape(kind, src):
+    if kind == PLACE:
+        return (src.shape[0], 2) + src.shape[1:]
+    if kind == PICK:
+        return (src.shape[0],) + src.shape[2:]
+    return src.shape
+
+
+def start_pairs(kinds, srcs, dsts, sems):
+    dp = lax.axis_index("dp")
+    made = []
+    for at, (kind, src, dst) in enumerate(zip(kinds, srcs, dsts)):
+        if kind == PICK:
+            src = src.at[:, dp ^ 1]
+        if kind == PLACE:
+            dst = dst.at[:, dp]
+            keep = pltpu.make_async_copy(src, dst, sems.at[at, 2])
+            keep.start()
+            made.append((keep, keep.wait))
+        send = pltpu.make_async_remote_copy(
+            src_ref=src,
+            dst_ref=dst,
+            send_sem=sems.at[at, 0],
+            recv_sem=sems.at[at, 1],
+            device_id={"dp": dp ^ 1},
+            device_id_type=MESH_ID,
+        )
+        send.start()
+        if kind == PLACE:
+            got = pltpu.make_async_remote_copy(
+                src_ref=src,
+                dst_ref=dsts[at].at[:, dp ^ 1],
+                send_sem=sems.at[at, 0],
+                recv_sem=sems.at[at, 1],
+                device_id={"dp": dp ^ 1},
+                device_id_type=MESH_ID,
+            )
+            made.append((send, send.wait_send))
+            made.append((got, got.wait_recv))
+        else:
+            made.append((send, send.wait))
+    return made
 
 
 def piece_row(zc, wac, h, half, n_ctx, n_wa, by_position):
@@ -512,11 +637,15 @@
     return pl.multiple_of(((zc * n_wa + wac) * 2 + h) * half, half)
 
 
-def gather_kernel(n_ctx, n_wa, by_position, own_ref, out_ref, own_sem, send_sem, recv_sem):
+def gather_kernel(n_ctx, n_wa, by_position, kinds, own_ref, *refs):
+    pairs = len(kinds)
+    srcs, out_ref, dsts = refs[:pairs], refs[pairs], refs[pairs + 1 : 2 * pairs + 1]
+    own_sem, send_sem, recv_sem = refs[2 * pairs + 1 : 2 * pairs + 4]
     ctx = lax.axis_index("ctx")
     wa = lax.axis_index("wa")
     half = own_ref.shape[0] // 2
     meet_neighbours(ctx, wa, n_ctx)
+    pair_copies = start_pairs(kinds, srcs, dsts, refs[-1])
     sends = []
 
     def place(zc, wac, h):
@@ -599,28 +728,37 @@
             pl.when(cond)(made.wait_send)
     for made in own_copies:
         made.wait()
-
-
-def gather_tokens(own, n_ctx, n_wa, by_position, call_id):
+    for _, done in pair_copies:
+        done()
+
+
+def gather_tokens(own, pairs, n_ctx, n_wa, by_position, call_id):
     rows, width = own.shape
     n = n_ctx * n_wa
+    kinds = tuple(kind for kind, _ in pairs)
+    anywhere = pl.BlockSpec(memory_space=pl.ANY)
+    shapes = [jax.ShapeDtypeStruct((rows * n, width), own.dtype)]
+    shapes += [jax.ShapeDtypeStruct(pair_shape(*pair), BF16) for pair in pairs]
     return pl.pallas_call(
-        partial(gather_kernel, n_ctx, n_wa, by_position),
-        in_specs=[pl.BlockSpec(memory_space=pl.ANY)],
-        out_specs=pl.BlockSpec(memory_space=pl.ANY),
-        out_shape=jax.ShapeDtypeStruct((rows * n, width), own.dtype),
+        partial(gather_kernel, n_ctx, n_wa, by_position, kinds),
+        in_specs=[anywhere] * (1 + len(pairs)),
+        out_specs=[anywhere] * (1 + len(pairs)),
+        out_shape=shapes,
         scratch_shapes=[
             pltpu.SemaphoreType.DMA((2,)),
             pltpu.SemaphoreType.DMA((8 + 12 * (n_ctx - 1) + 2 * (2 * n_ctx - 1),)),
             pltpu.SemaphoreType.DMA((2 * n,)),
+            pltpu.SemaphoreType.DMA((max(1, len(pairs)), 3)),
         ],
         compiler_params=pltpu.CompilerParams(collective_id=call_id, has_side_effects=True),
-    )(own)
-
-
-def scatter_kernel(
-    n_ctx, n_wa, by_position, part_ref, out_ref, s1, s2, s3, send_sem, recv1, recv2, recv3
-):
+        cost_estimate=LINK_COST,
+    )(own, *[array for _, array in pairs])
+
+
+def scatter_kernel(n_ctx, n_wa, by_position, kinds, part_ref, *refs):
+    pairs = len(kinds)
+    srcs, out_ref, dsts = refs[:pairs], refs[pairs], refs[pairs + 1 : 2 * pairs + 1]
+    s1, s2, s3, send_sem, recv1, recv2, recv3, pair_sem = refs[2 * pairs + 1 :]
     ctx = lax.axis_index("ctx")
     wa = lax.axis_index("wa")
     half = out_ref.shape[0] // 2
@@ -628,6 +766,7 @@
     y = wa // 2
     sibling, across = {"wa": wa ^ 1}, {"wa": wa ^ 2}
     meet_neighbours(ctx, wa, n_ctx)
+    pair_copies = start_pairs(kinds, srcs, dsts, pair_sem)
     sends = []
 
     def begin(cond, act):
@@ -728,18 +867,24 @@
                 begin(take, lambda extra=extra: add_up(out_ref, h * half, base + extra))
     for cond, made in sends:
         begin(cond, made.wait_send)
-
-
-def scatter_tokens(part, n_ctx, n_wa, by_position, call_id):
+    for _, done in pair_copies:
+        done()
+
+
+def scatter_tokens(part, pairs, n_ctx, n_wa, by_position, call_id):
     n = n_ctx * n_wa
     rows, width = part.shape[0] // n, part.shape[1]
     half = rows // 2
     pieces = 2 * (2 * n_ctx - 1)
+    kinds = tuple(kind for kind, _ in pairs)
+    anywhere = pl.BlockSpec(memory_space=pl.ANY)
+    shapes = [jax.ShapeDtypeStruct((rows, width), F32)]
+    shapes += [jax.ShapeDtypeStruct(pair_shape(*pair), BF16) for pair in pairs]
     return pl.pallas_call(
-        partial(scatter_kernel, n_ctx, n_wa, by_position),
-        in_specs=[pl.BlockSpec(memory_space=pltpu.VMEM)],
-        out_specs=pl.BlockSpec(memory_space=pltpu.VMEM),
-        out_shape=jax.ShapeDtypeStruct((rows, width), F32),
+        partial(scatter_kernel, n_ctx, n_wa, by_position, kinds),
+        in_specs=[pl.BlockSpec(memory_space=pltpu.VMEM)] + [anywhere] * len(pairs),
+        out_specs=[pl.BlockSpec(memory_space=pltpu.VMEM)] + [anywhere] * len(pairs),
+        out_shape=shapes,
         scratch_shapes=[
             pltpu.VMEM((4 * n_ctx, half, width), BF16),
             pltpu.VMEM((2 * n_ctx, half, width), BF16),
@@ -748,11 +893,13 @@
             pltpu.SemaphoreType.DMA((4 * n_ctx,)),
             pltpu.SemaphoreType.DMA((2 * n_ctx,)),
             pltpu.SemaphoreType.DMA((4 * n_ctx,)),
+            pltpu.SemaphoreType.DMA((max(1, len(pairs)), 3)),
         ],
         compiler_params=pltpu.CompilerParams(
             collective_id=call_id, has_side_effects=True, vmem_limit_bytes=48 * 2**20
         ),
-    )(part)
+        cost_estimate=LINK_COST,
+    )(part, *[array for _, array in pairs])
 
 
 def per_device_heads(
@@ -793,27 +940,26 @@
     def t_mm(a, b):
         return lax.dot_general(a, b, (((0,), (0,)), ((), ())), preferred_element_type=F32)
 
-    def pair(w):
-        return jnp.repeat(w.reshape(d_rows, KV, 1, HD), n // KV, axis=2).reshape(d_rows, n, HD)
-
     def swap(blocks):
         return lax.all_to_all(blocks, AXES, 0, 0, tiled=True)
 
+    def both(part):
+        part = part.astype(BF16)
+        return part.astype(F32) + lax.ppermute(part, "dp", swap_dp).astype(F32)
+
     gains_own = jnp.concatenate([attn_gain, ffn_gain, q_gain, k_gain])
     gains_row = jnp.pad(gains_own, (0, extra * 2 * LANES - gains_own.shape[0]))
-    attn_cols = jnp.concatenate(
-        [w_query.reshape(d_rows, n, LANES), pair(w_key), pair(w_value)], axis=2
-    ).transpose(1, 0, 2)
-    attn_cols = swap(
-        jnp.concatenate(
-            [
-                attn_cols,
-                jnp.broadcast_to(gains_row.reshape(1, extra, 2 * LANES), (n, extra, 2 * LANES)),
-            ],
-            axis=1,
-        )
-    )
-    x_all = gather_tokens(tokens[0], n_ctx, n_wa, True, 1)
+    attn_cols = pack_attn(w_query, w_key, w_value, gains_row.reshape(extra, 2 * LANES), n)
+    half = d_rows // 2
+    dp = lax.axis_index("dp")
+    ff_blocks = pack_pair(
+        lax.dynamic_slice_in_dim(w_gate, dp * half, half),
+        lax.dynamic_slice_in_dim(w_up, dp * half, half),
+        n,
+    )
+    attn_cols, tokens_b, ff_blocks = lax.optimization_barrier((attn_cols, tokens[0], ff_blocks))
+    attn_cols = swap(attn_cols)
+    (x_all,) = gather_tokens(tokens_b, [], n_ctx, n_wa, True, 1)
     w_qkv = attn_cols[:, :d_rows].reshape(width, 2 * LANES)
     gains = attn_cols[:, d_rows:].reshape(n, -1).astype(F32)
     attn_gain32 = gains[:, :d_rows].reshape(-1)
@@ -821,11 +967,8 @@
     qgain32 = gains[:, 2 * d_rows : 2 * d_rows + per].reshape(-1)
     kgain32 = gains[:, 2 * d_rows + per : 2 * d_rows + 2 * per].reshape(-1)
 
-    w_gate_b, w_up_b, dy_b, _ = lax.optimization_barrier((w_gate, w_up, out_grad[0], x_all))
-    ff_blocks = jnp.concatenate(
-        [w_gate_b.reshape(d_rows, n, ff_cols), w_up_b.reshape(d_rows, n, ff_cols)], axis=2
-    ).transpose(1, 0, 2)
-    w_gu = swap(ff_blocks).reshape(width, 2 * ff_cols)
+    ff_blocks, dy_b, _ = lax.optimization_barrier((ff_blocks, out_grad[0], x_all))
+    ff_half = swap(ff_blocks)
     dy_all = lax.all_gather(dy_b, AXES, axis=0, tiled=True)
 
     x_own = tokens[0].astype(F32)
@@ -840,9 +983,13 @@
     kv_b = jnp.concatenate([k_rot.astype(BF16), v_b], axis=1)
     ov_b = jnp.concatenate([jnp.ones_like(v_b), v_b], axis=1)
     att, inv = attend(doc_starts, q_b, kv_b, ov_b)
-    middle = x_own + scatter_tokens(mm(att, w_out).astype(BF16), n_ctx, n_wa, True, 3)
+    branch, w_gu = scatter_tokens(
+        mm(att, w_out).astype(BF16), [(PLACE, ff_half)], n_ctx, n_wa, True, 3
+    )
+    w_gu = w_gu.reshape(width, 2 * ff_cols)
+    middle = x_own + branch
     n2_own, n2_back = jax.vjp(rms_norm, middle, ffn_gain32)
-    n2_all = gather_tokens(n2_own.astype(BF16), n_ctx, n_wa, False, 2)
+    (n2_all,) = gather_tokens(n2_own.astype(BF16), [], n_ctx, n_wa, False, 2)
     gate_up = mm(n2_all, w_gu)
     gate, up = gate_up[:, :ff_cols], gate_up[:, ff_cols:]
     sig = jax.nn.sigmoid(gate)
@@ -856,14 +1003,19 @@
     d_gu = jnp.concatenate(
         [d_hidden * up * (sig * (1.0 + gate * (1.0 - sig))), d_hidden * silu], axis=1
     ).astype(BF16)
-    gu_grad = t_mm(n2_all, d_gu).astype(BF16)
-    gu_rows = swap(gu_grad).reshape(n, d_rows, 2 * ff_cols)
-    down_grad = t_mm(hidden, dy_all)
-    d_n2 = scatter_tokens(mm_t(d_gu, w_gu).astype(BF16), n_ctx, n_wa, False, 4)
+    gu_grad = t_mm(n2_all, d_gu).astype(BF16).reshape(n, 2, half, 2 * ff_cols)
+    d_n2, gu_other = scatter_tokens(
+        mm_t(d_gu, w_gu).astype(BF16), [(PICK, gu_grad)], n_ctx, n_wa, False, 4
+    )
+    gu_mine = lax.dynamic_index_in_dim(gu_grad, dp, 1, keepdims=False)
+    gu_rows = swap((gu_mine.astype(F32) + gu_other.astype(F32)).astype(BF16))
+    down_grad = t_mm(hidden, dy_all).astype(BF16)
     d_mid_part, _ = n2_back(d_n2)
     d_middle = out_grad[0].astype(F32) + d_mid_part
-    db_all = gather_tokens(d_middle.astype(BF16), n_ctx, n_wa, True, 1)
-    out_w_grad = t_mm(att, db_all)
+    db_all, down_other = gather_tokens(
+        d_middle.astype(BF16), [(WHOLE, down_grad)], n_ctx, n_wa, True, 5
+    )
+    out_w_grad = t_mm(att, db_all).astype(BF16)
     d_att = mm_t(db_all, w_out).astype(BF16)
     dq, dkv = attend_back(doc_starts, q_b, kv_b, att, inv, d_att)
     dkv = dkv + lax.ppermute(dkv, "wa", [(i, i ^ 1) for i in range(n_wa)])
@@ -886,20 +1038,17 @@
         )
     )
     d_n1_part = mm_t(d_qkv, jnp.concatenate([w_qkv[:, :LANES], w_kv_own], axis=1)).astype(BF16)
-    d_n1 = scatter_tokens(d_n1_part, n_ctx, n_wa, True, 3)
+    d_n1, gu_others, out_w_other = scatter_tokens(
+        d_n1_part, [(WHOLE, gu_rows), (WHOLE, out_w_grad)], n_ctx, n_wa, True, 6
+    )
     _, n1_back = jax.vjp(rms_norm, x_own, attn_gain32)
     d_x_part, _ = n1_back(d_n1)
     input_grad = d_middle + d_x_part
 
-    def both(part):
-        part = part.astype(BF16)
-        return part.astype(F32) + lax.ppermute(part, "dp", swap_dp).astype(F32)
-
     def flat(part):
         return part.transpose(1, 0, 2).reshape(d_rows, -1)
 
-    gu_rows = both(gu_rows)
-    gate_grad, up_grad = flat(gu_rows[:, :, :ff_cols]), flat(gu_rows[:, :, ff_cols:])
+    gate_grad, up_grad, gu_sums = unpack_pair(gu_rows, gu_others, w_gate, w_up)
     qkv_rows = both(qkv_rows)
     q_grad = flat(qkv_rows[:, :d_rows, :LANES])
     kv_grad = qkv_rows[:, :d_rows, LANES:].reshape(KV, 2, d_rows, HD)
@@ -913,7 +1062,7 @@
     attn_gain_grad = (
         row_sum(w_query, q_grad) + row_sum(w_key, k_grad) + row_sum(w_value, v_grad)
     ) / attn_gain.astype(F32)
-    ffn_gain_grad = (row_sum(w_gate, gate_grad) + row_sum(w_up, up_grad)) / ffn_gain.astype(F32)
+    ffn_gain_grad = gu_sums[:, 0] / ffn_gain.astype(F32)
     return (
         layer_out.astype(BF16)[None],
         input_grad.astype(BF16)[None],
@@ -923,11 +1072,11 @@
         v_grad,
         lax.dynamic_slice_in_dim(head_sums, me * per, per),
         lax.dynamic_slice_in_dim(head_sums, HD + me * per, per),
-        both(out_w_grad),
+        out_w_grad.astype(F32) + out_w_other.astype(F32),
         ffn_gain_grad,
         gate_grad,
         up_grad,
-        both(down_grad),
+        down_grad.astype(F32) + down_other.astype(F32),
     )
 
 

time: 864 us -> 793 us (0.918)
  waiting for transfers between devices: 142 us -> 75.9 us
  local copies, waits for them, and re-layouts: 59.1 us -> 43 us
  starting transfers between devices: 28.8 us -> 38.1 us
    ppermute x4 -> x1, waiting for transfers between devices: 113 us -> 9.54 us  [both(): return part.astype(F32) + lax.ppermute(part, 'dp', swap_dp).astype(F32)]
    all_to_all x4, waiting for transfers between devices: 28.8 us -> 66.4 us  [swap(): return lax.all_to_all(blocks, AXES, 0, 0, tiled=True)]
    all_to_all x4, starting transfers between devices: 23.1 us -> 36.4 us  [swap(): return lax.all_to_all(blocks, AXES, 0, 0, tiled=True)]
    add x4 -> x1, other arithmetic: 15.2 us -> 2.29 us  [both(): return part.astype(F32) + lax.ppermute(part, 'dp', swap_dp).astype(F32)]
    pallas_call x6 -> x9, Pallas kernels: 412 us -> 415 us  [the longest x3 215 us: scatter_tokens(): pl.pallas_call(partial(scatter_kernel, n_ctx, n_wa, by_position, kinds),...]
  transfers between devices with their start and end apart: 11 -> 8, of which waited for: 3 -> 3; matrix products, arithmetic and copies ran while one was open for 22% -> 17% of each run, Pallas kernels for 45% -> 39%
where the time goes in v3:
time: 793 us; the launch traced here: 786 us
  Pallas kernels  442 us (56%)
  matrix products  103 us (13%)
  waiting for transfers between devices  75.9 us (10%)
  other arithmetic  68.1 us (9%)
  local copies, waits for them, and re-layouts  43 us (5%)
  starting transfers between devices  38.1 us (5%)
  between operations  15.5 us (2%)
    pallas_call x3, Pallas kernels, scatter_tokens(): pl.pallas_call(partial(scatter_kernel, n_ctx, n_wa, by_position, kinds),...  215 us
    pallas_call x3, Pallas kernels, gather_tokens(): pl.pallas_call(partial(gather_kernel, n_ctx, n_wa, by_position, kinds), i...  175 us
    all_to_all x4, waiting for transfers between devices, swap(): return lax.all_to_all(blocks, AXES, 0, 0, tiled=True)  66.4 us
    all_to_all x4, starting transfers between devices, swap(): return lax.all_to_all(blocks, AXES, 0, 0, tiled=True)  36.4 us
    dot_general x4, matrix products, t_mm(): lax.dot_general(a, b, (((0,), (0,)), ((), ())), preferred_element_type=F32)  35.9 us
    dot_general x4, matrix products, mm_t(): lax.dot_general(a, b, (((1,), (1,)), ((), ())), preferred_element_type=F32)  34 us
    dot_general x4, matrix products, mm(): return jnp.dot(a, b, preferred_element_type=F32)  33.1 us
    pallas_call x1, Pallas kernels, attend_back(): pl.pallas_call(attend_back_kernel, grid=(stream // bq,), in_specs=[pl.Blo...  16.6 us
  transfers between devices with their start and end apart: 8, of which 3 were waited for; matrix products, arithmetic and copies ran while one was open for 17% of the time, Pallas kernels for 39%

profile of v3, /device:TPU:0, one launch (start us, length us, event | category | flops | bytes accessed | tf_op | source)
XLA Modules:
  0.0 785.8 jit_solution(6213331589639100096)
XLA Ops:
  8.7 3.0 constant_dynamic-slice_fusion
  11.8 9.3 %shard_map.238 = bf16[16,64,1024]{2,1,0:T(8,128)(2,1)} custom-call(bf16[64,8192]{1,0:T(8,128)(2,1)} %get-tuple-element.141.gate_ref, bf16[64,8192]{1,0:T(8,128)(2,1)} %get-tuple-element.140.up_ref), custom_call_target="tpu_custom_call" | custom-call | tf_op jit(solution)/shard_map/pallas_call | solution.py:513
  21.1 2.4 shard_map.237
  23.4 7.4 all-to-all-start
  30.9 68.7 %shard_map.239 = bf16[2048,2048]{1,0:T(8,128)(2,1)} custom-call(bf16[128,2048]{1,0:T(8,128)(2,1)} %bitcast.107), custom_call_target="tpu_custom_call" | custom-call | flops 49999998976 | bytes 16777216 | tf_op jit(solution)/shard_map/pallas_call | solution.py:742
  99.6 5.1 fusion
  105.3 1.7 multiply_cosine_fusion.1
  107.1 6.9 all-to-all-start.1
  115.2 5.7 fusion.6
  121.0 1.3 copy-done.25
  122.6 2.5 multiply_multiply_fusion
  127.3 1.3 copy.102
  129.7 1.3 subtract_convert_fusion
  131.4 1.8 multiply_reduce_fusion.5
  133.2 1.6 multiply_bitcast_fusion
  134.8 4.8 fusion.17
  140.5 10.6 %shard_map.240 = (bf16[2048,128]{1,0:T(8,128)(2,1)S(1)}, f32[2048,128]{1,0:T(8,128)S(1)}) custom-call(s32[1,8]{1,0:T(1,128)S(1)} %copy-done.18, bf16[2048,128]{1,0:T(8,128)(2,1)S(1)} %copy.85.q_ref, bf16[2048,128]{1,0:T(8,128)(2,1)S(1)} %get-tuple-element.129.kv_ref, bf16[2048,128]{1,0:T(8,128)(2,1)S(1)} %get-tuple-element.128.ov_ref), custom_call_target="tpu_custom_call" | custom-call | flops 1073741824 | bytes 3145728 | tf_op jit(solution)/shard_map/pallas_call | solution.py:446
  152.0 5.6 convolution_convert_fusion.3.part_ref
  158.4 27.2 %all-to-all-done.1.refs_0_ = bf16[16,64,1024]{2,1,0:T(8,128)(2,1)} async-done(((bf16[16,64,1024]{2,1,0:T(8,128)(2,1)}), bf16[16,64,1024]{2,1,0:T(8,128)(2,1)}, u32[]{:S(2)}, u32[]{:S(2)}) %all-to-all-start.1) | async-done | bytes 2097184 | tf_op jit(solution)/shard_map/all_to_all | solution.py:944
  185.6 86.9 %shard_map.241 = (f32[128,2048]{1,0:T(8,128)S(1)}, bf16[16,2,64,1024]{3,2,1,0:T(8,128)(2,1)}) custom-call(bf16[2048,2048]{1,0:T(8,128)(2,1)} %convolution_convert_fusion.3.part_ref, bf16[16,64,1024]{2,1,0:T(8,128)(2,1)} %all-to-all-done.1.refs_0_), custom_call_target="tpu_custom_call" | custom-call | flops 49999998976 | bytes 16777216 | tf_op jit(solution)/shard_map/pallas_call | solution.py:883
  274.5 56.6 %shard_map.242 = bf16[2048,2048]{1,0:T(8,128)(2,1)} custom-call(bf16[128,2048]{1,0:T(8,128)(2,1)} %multiply_convert_fusion.3.own_ref), custom_call_target="tpu_custom_call" | custom-call | flops 49999998976 | bytes 16777216 | tf_op jit(solution)/shard_map/pallas_call | solution.py:742
  331.1 14.8 %fusion.63 = f32[2048,1024]{0,1:T(8,128)} fusion(bf16[2048,2048]{1,0:T(8,128)(2,1)} %shard_map.242, bf16[2048,1024]{1,0:T(8,128)(2,1)} %bitcast.127), kind=kOutput, calls=%fused_computation.145 | convolution fusion | flops 8589934592 | bytes 20971520 | tf_op jit(solution)/shard_map/dot_general | solution.py:935
  346.0 10.7 %multiply_convert_fusion.1 = (bf16[2048,512]{0,1:T(8,128)(2,1)S(1)}, bf16[2048,512]{0,1:T(8,128)(2,1)S(1)}, bf16[2048,512]{0,1:T(8,128)(2,1)S(1)}) fusion(f32[2048,1024]{0,1:T(8,128)} %fusion.63, bf16[2048,2048]{1,0:T(8,128)(2,1)} %all-gather.2.cloned.1.call-done, bf16[512,2048]{1,0:T(8,128)(2,1)S(1)} %copy-done), kind=kOutput, calls=%fused_computation.14 | convolution fusion | flops 4310695936 | bytes 25165824 | tf_op jit(solution)/shard_map/dot_general | solution.py:938
  356.7 13.5 %convolution_convert_fusion.4 = bf16[2048,1024]{1,0:T(8,128)(2,1)} fusion(bf16[2048,2048]{1,0:T(8,128)(2,1)} %shard_map.242, bf16[2048,512]{0,1:T(8,128)(2,1)S(1)} %get-tuple-element.114, bf16[2048,512]{0,1:T(8,128)(2,1)S(1)} %get-tuple-element.113), kind=kOutput, calls=%fused_computation.18 | convolution fusion | flops 8600420352 | bytes 16777216 | tf_op jit(solution)/shard_map/dot_general | solution.py:941
  370.2 11.7 %convolution_convert_fusion.1.part_ref = bf16[2048,2048]{1,0:T(8,128)(2,1)} fusion(bf16[2048,1024]{1,0:T(8,128)(2,1)S(1)} %bitcast.128, bf16[2048,512]{0,1:T(8,128)(2,1)S(1)} %get-tuple-element.114, bf16[2048,512]{0,1:T(8,128)(2,1)S(1)} %get-tuple-element.113), kind=kOutput, calls=%fused_computation.6 | convolution fusion | flops 8602517504 | bytes 16777216 | tf_op jit(solution)/shard_map/dot_general | solution.py:938
  381.9 54.1 %shard_map.243 = (f32[128,2048]{1,0:T(8,128)S(1)}, bf16[16,64,1024]{2,1,0:T(8,128)(2,1)S(1)}) custom-call(bf16[2048,2048]{1,0:T(8,128)(2,1)} %convolution_convert_fusion.1.part_ref, bf16[16,2,64,1024]{3,2,1,0:T(8,128)(2,1)} %bitcast.122), custom_call_target="tpu_custom_call" | custom-call | flops 49999998976 | bytes 16777216 | tf_op jit(solution)/shard_map/pallas_call | solution.py:883
  436.0 1.2 fusion.29
  437.3 1.2 fusion.58.own_ref
  438.5 7.0 convolution_convert_fusion.2
  445.4 9.9 %convolution_convert_fusion.5.refs_0_ = bf16[512,2048]{1,0:T(8,128)(2,1)} fusion(bf16[2048,512]{0,1:T(8,128)(2,1)} %copy-done.75, bf16[2048,2048]{1,0:T(8,128)(2,1)} %all-gather.2.cloned.1.call-done), kind=kOutput, calls=%fused_computation.20 | convolution fusion | flops 4296015872 | bytes 12582912 | tf_op jit(solution)/shard_map/dot_general | solution.py:941
  455.4 50.2 %shard_map.244 = (bf16[2048,2048]{1,0:T(8,128)(2,1)}, bf16[512,2048]{1,0:T(8,128)(2,1)}) custom-call(bf16[128,2048]{1,0:T(8,128)(2,1)} %fusion.58.own_ref, bf16[512,2048]{1,0:T(8,128)(2,1)} %convolution_convert_fusion.5.refs_0_), custom_call_target="tpu_custom_call" | custom-call | flops 49999998976 | bytes 16777216 | tf_op jit(solution)/shard_map/pallas_call | solution.py:742
  505.6 5.9 convolution_convert_fusion.8.da_ref
  511.5 16.6 %shard_map.245 = (f32[2048,128]{1,0:T(8,128)S(1)}, f32[2048,128]{1,0:T(8,128)S(1)}) custom-call(s32[1,8]{1,0:T(1,128)S(1)} %copy-done.19, bf16[2048,128]{1,0:T(8,128)(2,1)S(1)} %copy-done.14, bf16[2048,128]{1,0:T(8,128)(2,1)S(1)} %copy-done.16, bf16[2048,128]{1,0:T(8,128)(2,1)S(1)} %copy-done.6, f32[2048,128]{1,0:T(8,128)S(1)} %copy-done.21, ...), custom_call_target="tpu_custom_call" | custom-call | flops 2684354560 | bytes 4194304 | tf_op jit(solution)/shard_map/pallas_call | solution.py:467
  530.2 2.6 copy.87
  532.8 2.2 multiply_add_fusion.1
  535.7 2.2 multiply_reduce_fusion.1
  537.9 2.4 fusion.23
  540.4 1.6 add.158
  542.1 4.4 fusion.20
  548.8 7.7 convolution_convert_fusion.6
  556.6 2.2 copy.100
  559.0 2.4 pad_maximum_fusion.3
  561.4 4.4 all-to-all-start.3
  565.8 4.7 fusion.3
  570.5 39.2 %all-to-all-done.3 = bf16[16,144,192]{2,1,0:T(8,128)(2,1)} async-done(((bf16[16,144,192]{2,1,0:T(8,128)(2,1)}), bf16[16,144,192]{2,1,0:T(8,128)(2,1)}, u32[]{:S(2)}, u32[]{:S(2)}) %all-to-all-start.3) | async-done | bytes 884768 | tf_op jit(solution)/shard_map/all_to_all | solution.py:944
  609.7 17.7 %all-to-all-start.2 = ((bf16[16,64,1024]{2,1,0:T(8,128)(2,1)}), bf16[16,64,1024]{2,1,0:T(8,128)(2,1)}, u32[]{:S(2)}, u32[]{:S(2)}) async-start(bf16[16,64,1024]{2,1,0:T(8,128)(2,1)} %fusion.3), calls=%async_computation.3 | async-start | bytes 4194304 | tf_op jit(solution)/shard_map/all_to_all | solution.py:944
  629.4 1.5 slice_select_fusion
  632.0 5.0 convert_add_fusion.1
  637.0 4.7 convolution_convert_fusion.7.refs_1_
  641.8 5.8 convolution_convert_fusion.part_ref
  647.5 2.6 copy.91
  650.2 9.5 %collective-permute-done.1 = bf16[16,144,192]{2,1,0:T(8,128)(2,1)} collective-permute-done((bf16[16,144,192]{2,1,0:T(8,128)(2,1)}, bf16[16,144,192]{2,1,0:T(8,128)(2,1)}, u32[]{:S(2)}, u32[]{:S(2)}) %collective-permute-start.1) | collective-permute-done | bytes 884768 | tf_op jit(solution)/shard_map/ppermute | solution.py:948
  659.7 2.6 copy.92
  662.3 2.3 convert_add_fusion.2
  666.5 1.3 slice.133
  667.8 2.5 copy.93
  670.3 2.0 copy.96
  677.3 1.5 multiply_reduce_fusion
  679.4 74.5 %shard_map.246 = (f32[128,2048]{1,0:T(8,128)S(1)}, bf16[16,64,1024]{2,1,0:T(8,128)(2,1)S(1)}, bf16[128,2048]{1,0:T(8,128)(2,1)S(1)}) custom-call(bf16[2048,2048]{1,0:T(8,128)(2,1)} %convolution_convert_fusion.part_ref, bf16[16,64,1024]{2,1,0:T(8,128)(2,1)} %all-to-all-done.2.refs_0_.own_ref, bf16[128,2048]{1,0:T(8,128)(2,1)S(1)} %convolution_convert_fusion.7.refs_1_), custom_call_target="tpu_custom_call" | custom-call | flops 49999998976 | bytes 16777216 | tf_op jit(solution)/shard_map/pallas_call | solution.py:883
  754.9 1.3 copy-done.10
  757.0 12.5 %shard_map.247 = (f32[128,8192]{1,0:T(8,128)}, f32[128,8192]{1,0:T(8,128)}, f32[128,128]{1,0:T(8,128)}) custom-call(bf16[16,64,1024]{2,1,0:T(8,128)(2,1)} %all-to-all-done.2.refs_0_.own_ref, bf16[16,64,1024]{2,1,0:T(8,128)(2,1)} %copy-done.10, bf16[128,8192]{1,0:T(8,128)(2,1)} %gate_w.1, bf16[128,8192]{1,0:T(8,128)(2,1)} %up_w.1), custom_call_target="tpu_custom_call" | custom-call | tf_op jit(solution)/shard_map/pallas_call | solution.py:546
  770.5 1.6 fusion.30
  772.6 2.3 convert_add_fusion.4
  774.9 3.8 fusion.38
  (217 shorter events, 30.8 us)
Async XLA Ops:
  7.2 338.8 %copy-start = (bf16[512,2048]{1,0:T(8,128)(2,1)S(1)}, bf16[512,2048]{1,0:T(8,128)(2,1)}, u32[]{:S(2)}) copy-start(bf16[512,2048]{1,0:T(8,128)(2,1)} %param.27) | copy-start | bytes 6291460
  23.4 83.6 %all-to-all-start = ((bf16[16,144,256]{2,1,0:T(8,128)(2,1)}), bf16[16,144,256]{2,1,0:T(8,128)(2,1)S(1)}, u32[]{:S(2)}, u32[]{:S(2)}) async-start(bf16[16,144,256]{2,1,0:T(8,128)(2,1)} %shard_map.237), calls=%async_computation | async-start | bytes 2359296 | tf_op jit(solution)/shard_map/all_to_all | solution.py:944
  30.8 315.1 %all-gather.2.cloned.1.call-start = ((), (), s32[]{:S(2)}) async-start(), calls=%async_computation.6 | async-start | bytes 8912896 | tf_op jit(solution)/shard_map/all_gather | solution.py:972
  99.6 5.7 copy-start.61
  99.6 35.2 %copy-start.46 = (f32[2048]{0:T(1024)}, f32[2048]{0:T(1024)S(1)}, u32[]{:S(2)}) copy-start(f32[2048]{0:T(1024)S(1)} %iota_convert_fusion) | copy-start | bytes 24580
  107.1 22.6 %copy-start.29 = (f32[2048,32]{0,1:T(8,128)}, f32[2048,32]{0,1:T(8,128)S(1)}, u32[]{:S(2)}) copy-start(f32[2048,32]{0,1:T(8,128)S(1)} %get-tuple-element.134) | copy-start | bytes 786436
  107.1 78.6 %all-to-all-start.1 = ((bf16[16,64,1024]{2,1,0:T(8,128)(2,1)}), bf16[16,64,1024]{2,1,0:T(8,128)(2,1)}, u32[]{:S(2)}, u32[]{:S(2)}) async-start(bf16[16,64,1024]{2,1,0:T(8,128)(2,1)} %shard_map.238), calls=%async_computation.1 | async-start | bytes 4194304 | tf_op jit(solution)/shard_map/all_to_all | solution.py:944
  114.0 660.9 %reduce-scatter.2.cloned.1.call-start = ((), (), s32[]{:S(2)}) async-start(), calls=%async_computation.5 | async-start | bytes 8912896 | tf_op jit(solution)/shard_map/reduce_scatter | solution.py:999
  114.4 6.5 copy-start.50
  114.4 158.4 %copy-start.41 = (f32[2048]{0:T(1024)}, f32[2048]{0:T(1024)S(1)}, u32[]{:S(2)}) copy-start(f32[2048]{0:T(1024)S(1)} %get-tuple-element.133) | copy-start | bytes 24580
  115.2 5.7 copy-start.27
  115.2 7.2 copy-start.55
  122.3 6.3 copy-start.54
  122.4 4.9 slice-start
  122.4 7.3 copy-start.31
  122.5 6.1 copy-start.58
  128.6 6.2 copy-start.62
  128.7 10.9 %copy-start.56 = (f32[64]{0:T(128)}, f32[64]{0:T(128)S(1)}, u32[]{:S(2)}) copy-start(f32[64]{0:T(128)S(1)} %mul.535) | copy-start | bytes 772
  131.4 9.1 %copy-start.13 = (bf16[2048,128]{1,0:T(8,128)(2,1)}, bf16[2048,128]{1,0:T(8,128)(2,1)S(1)}, u32[]{:S(2)}) copy-start(bf16[2048,128]{1,0:T(8,128)(2,1)S(1)} %copy.85.q_ref) | copy-start | bytes 1572868
  131.4 8.6 %copy-start.33 = (bf16[2048,64]{1,0:T(8,128)(2,1)S(1)}, bf16[2048,64]{1,0:T(8,128)(2,1)}, u32[]{:S(2)}) copy-start(bf16[2048,64]{1,0:T(8,128)(2,1)} %copy.103) | copy-start | bytes 786436
  133.2 7.2 copy-start.52
  133.2 7.2 copy-start.48
  133.2 7.2 copy-start.18
  139.6 12.4 %copy-start.37 = (bf16[128,2048]{1,0:T(8,128)(2,1)S(1)}, bf16[128,2048]{1,0:T(8,128)(2,1)}, u32[]{:S(2)}) copy-start(bf16[128,2048]{1,0:T(8,128)(2,1)} %param.23) | copy-start | bytes 1572868
  140.4 10.6 %copy-start.15 = (bf16[2048,128]{1,0:T(8,128)(2,1)}, bf16[2048,128]{1,0:T(8,128)(2,1)S(1)}, u32[]{:S(2)}) copy-start(bf16[2048,128]{1,0:T(8,128)(2,1)S(1)} %get-tuple-element.129.kv_ref) | copy-start | bytes 1572868
  158.4 114.2 %copy-start.23 = (bf16[1,128,2048]{2,1,0:T(8,128)(2,1)S(1)}, bf16[1,128,2048]{2,1,0:T(8,128)(2,1)}, u32[]{:S(2)}) copy-start(bf16[1,128,2048]{2,1,0:T(8,128)(2,1)} %param.14) | copy-start | bytes 1572868
  272.8 58.3 %copy-start.71 = (f32[128]{0:T(128)}, f32[128]{0:T(128)S(1)}, u32[]{:S(2)}) copy-start(f32[128]{0:T(128)S(1)} %multiply_reduce_fusion.4) | copy-start | bytes 1540
  272.8 58.3 %copy-start.64 = (f32[128]{0:T(128)}, f32[128]{0:T(128)S(1)}, u32[]{:S(2)}) copy-start(f32[128]{0:T(128)S(1)} %fusion.52) | copy-start | bytes 1540
  356.7 81.8 %copy-start.75 = (bf16[2048,512]{0,1:T(8,128)(2,1)}, bf16[2048,512]{0,1:T(8,128)(2,1)S(1)}, u32[]{:S(2)}) copy-start(bf16[2048,512]{0,1:T(8,128)(2,1)S(1)} %get-tuple-element.115) | copy-start | bytes 6291460
  356.7 13.5 %copy-start.74 = (bf16[16,2,64,1024]{3,2,1,0:T(8,128)(2,1)S(1)}, bf16[16,2,64,1024]{3,2,1,0:T(8,128)(2,1)}, u32[]{:S(2)}) copy-start(bf16[16,2,64,1024]{3,2,1,0:T(8,128)(2,1)} %get-tuple-element.40) | copy-start | bytes 12582916
  381.9 54.1 %copy-start.2 = (f32[128,2048]{1,0:T(8,128)S(1)}, f32[128,2048]{1,0:T(8,128)}, u32[]{:S(2)}) copy-start(f32[128,2048]{1,0:T(8,128)} %copy-done.1) | copy-start | bytes 3145732
  381.9 54.2 %copy-start.24 = (bf16[1,128,2048]{2,1,0:T(8,128)(2,1)S(1)}, bf16[1,128,2048]{2,1,0:T(8,128)(2,1)}, u32[]{:S(2)}) copy-start(bf16[1,128,2048]{2,1,0:T(8,128)(2,1)} %param.14) | copy-start | bytes 1572868
  381.9 54.2 %copy-start.42 = (f32[2048]{0:T(1024)S(1)}, f32[2048]{0:T(1024)}, u32[]{:S(2)}) copy-start(f32[2048]{0:T(1024)} %copy-done.41) | copy-start | bytes 24580
  381.9 55.4 %copy-start.72 = (f32[128]{0:T(128)S(1)}, f32[128]{0:T(128)}, u32[]{:S(2)}) copy-start(f32[128]{0:T(128)} %copy-done.71) | copy-start | bytes 1540
  381.9 55.4 %copy-start.28 = (bf16[1,128,2048]{2,1,0:T(8,128)(2,1)S(1)}, bf16[1,128,2048]{2,1,0:T(8,128)(2,1)}, u32[]{:S(2)}) copy-start(bf16[1,128,2048]{2,1,0:T(8,128)(2,1)} %param.16) | copy-start | bytes 1572868
  381.9 55.4 %copy-start.65 = (f32[128]{0:T(128)S(1)}, f32[128]{0:T(128)}, u32[]{:S(2)}) copy-start(f32[128]{0:T(128)} %copy-done.64) | copy-start | bytes 1540
  455.4 50.2 %copy-start.38 = (bf16[128,2048]{1,0:T(8,128)(2,1)S(1)}, bf16[128,2048]{1,0:T(8,128)(2,1)}, u32[]{:S(2)}) copy-start(bf16[128,2048]{1,0:T(8,128)(2,1)} %param.23) | copy-start | bytes 1572868
  505.6 5.9 copy-start.6
  505.6 5.9 copy-start.14
  505.6 5.9 copy-start.16
  505.6 5.9 copy-start.19
  505.6 5.9 copy-start.21
  535.0 5.4 collective-permute-start
  535.4 5.0 copy-start.12
  537.9 4.2 copy-start.63
  540.4 6.1 copy-start.22
  540.4 6.1 copy-start.49
  540.4 6.1 copy-start.57
  542.1 5.3 copy-start.53
  561.4 48.3 %all-to-all-start.3 = ((bf16[16,144,192]{2,1,0:T(8,128)(2,1)}), bf16[16,144,192]{2,1,0:T(8,128)(2,1)}, u32[]{:S(2)}, u32[]{:S(2)}) async-start(bf16[16,144,192]{2,1,0:T(8,128)(2,1)} %pad_maximum_fusion.3), calls=%async_computation.4 | async-start | bytes 2359296 | tf_op jit(solution)/shard_map/all_to_all | solution.py:944
  565.8 61.6 %copy-start.35 = (bf16[128,512]{1,0:T(8,128)(2,1)S(1)}, bf16[128,512]{1,0:T(8,128)(2,1)}, u32[]{:S(2)}) copy-start(bf16[128,512]{1,0:T(8,128)(2,1)} %key_ref.1) | copy-start | bytes 393220
  565.8 62.3 %copy-start.36 = (bf16[128,512]{1,0:T(8,128)(2,1)S(1)}, bf16[128,512]{1,0:T(8,128)(2,1)}, u32[]{:S(2)}) copy-start(bf16[128,512]{1,0:T(8,128)(2,1)} %value_ref.1) | copy-start | bytes 393220
  609.7 69.7 %all-to-all-start.2 = ((bf16[16,64,1024]{2,1,0:T(8,128)(2,1)}), bf16[16,64,1024]{2,1,0:T(8,128)(2,1)}, u32[]{:S(2)}, u32[]{:S(2)}) async-start(bf16[16,64,1024]{2,1,0:T(8,128)(2,1)} %fusion.3), calls=%async_computation.3 | async-start | bytes 4194304 | tf_op jit(solution)/shard_map/all_to_all | solution.py:944
  630.9 28.8 %collective-permute-start.1 = (bf16[16,144,192]{2,1,0:T(8,128)(2,1)}, bf16[16,144,192]{2,1,0:T(8,128)(2,1)}, u32[]{:S(2)}, u32[]{:S(2)}) collective-permute-start(bf16[16,144,192]{2,1,0:T(8,128)(2,1)} %all-to-all-done.3), channel_id=1, source_target_pairs={{0,16},{16,0},{1,17},{17,1},{2,18},{18,2},{3,19},{19,3},{4,20},{20... | collective-permute-start | bytes 2654216 | tf_op jit(solution)/shard_map/ppermute | solution.py:948
  637.0 4.7 copy-start.32
  641.7 37.7 %copy-start.9 = (bf16[128,2048]{1,0:T(8,128)(2,1)}, bf16[128,2048]{1,0:T(8,128)(2,1)S(1)}, u32[]{:S(2)}) copy-start(bf16[128,2048]{1,0:T(8,128)(2,1)S(1)} %convolution_convert_fusion.7.refs_1_) | copy-start | bytes 1572868
  666.5 10.7 %copy-start.34 = (bf16[128,512]{0,1:T(8,128)(2,1)S(1)}, bf16[128,512]{0,1:T(8,128)(2,1)}, u32[]{:S(2)}) copy-start(bf16[128,512]{0,1:T(8,128)(2,1)} %copy.94) | copy-start | bytes 393220
  667.8 11.1 %copy-start.68 = (bf16[128]{0:T(256)(128)(2,1)S(1)}, bf16[128]{0:T(256)(128)(2,1)}, u32[]{:S(2)}) copy-start(bf16[128]{0:T(256)(128)(2,1)} %param.17) | copy-start | bytes 772
  757.0 15.1 %copy-start.73 = (bf16[128]{0:T(256)(128)(2,1)S(1)}, bf16[128]{0:T(256)(128)(2,1)}, u32[]{:S(2)}) copy-start(bf16[128]{0:T(256)(128)(2,1)} %param.24) | copy-start | bytes 772
  757.0 15.6 %copy-start.67 = (f32[128]{0:T(128)S(1)}, f32[128]{0:T(128)}, u32[]{:S(2)}) copy-start(f32[128]{0:T(128)} %get-tuple-element.111) | copy-start | bytes 1540
  757.0 17.9 %copy-start.3 = (f32[128,2048]{1,0:T(8,128)S(1)}, f32[128,2048]{1,0:T(8,128)}, u32[]{:S(2)}) copy-start(f32[128,2048]{1,0:T(8,128)} %copy-done.1) | copy-start | bytes 3145732
  757.0 17.9 %copy-start.43 = (f32[2048]{0:T(1024)S(1)}, f32[2048]{0:T(1024)}, u32[]{:S(2)}) copy-start(f32[2048]{0:T(1024)} %copy-done.41) | copy-start | bytes 24580
  757.0 17.9 %copy-start.66 = (f32[128]{0:T(128)S(1)}, f32[128]{0:T(128)}, u32[]{:S(2)}) copy-start(f32[128]{0:T(128)} %copy-done.64) | copy-start | bytes 1540
  757.0 17.9 %copy-start.70 = (f32[128]{0:T(128)S(1)}, f32[128]{0:T(128)}, u32[]{:S(2)}) copy-start(f32[128]{0:T(128)} %copy-done.69) | copy-start | bytes 1540
  (21 other events, 39.9 us)
Sparse Core Ops, SparseCore 0:
  99.7 112.5 all-gather.1
  535.6 154.8 reduce-scatter.1

commit v4 on v3

--- a/solution.py
+++ b/solution.py
@@ -2,6 +2,7 @@
 
 import jax
 import jax.numpy as jnp
+import numpy as np
 from jax import lax
 from jax.experimental import pallas as pl
 from jax.experimental.pallas import tpu as pltpu
@@ -328,6 +329,7 @@
 AXES = ("ctx", "wa")
 LANES = 2 * HD
 ROWS_BLOCK = 256
+FFN_BLOCK = 256
 LOG2E = 1.4426950408889634
 F32 = jnp.float32
 BF16 = jnp.bfloat16
@@ -348,66 +350,173 @@
     return (col >= first) & (col <= row)
 
 
-def attend_kernel(starts, q_ref, kv_ref, ov_ref, att_ref, inv_ref):
+def rope_tables(stream):
+    frequency = np.float32(THETA) ** (-2.0 * np.arange(HD // 2, dtype=np.float32) / np.float32(HD))
+    angles = np.arange(stream, dtype=np.float32)[:, None] * frequency.astype(np.float32)[None, :]
+    cosine = np.cos(angles.astype(np.float64)).astype(np.float32)
+    sine = np.sin(angles.astype(np.float64)).astype(np.float32)
+    return np.tile(cosine, (1, 4)), np.tile(np.concatenate([-sine, sine], axis=1), (1, 2))
+
+
+def lane_ids():
+    return lax.broadcasted_iota(jnp.int32, (1, LANES), 1)
+
+
+def head_mean(values):
+    low = jnp.sum(values[:, :HD], axis=1, keepdims=True)
+    high = jnp.sum(values[:, HD:], axis=1, keepdims=True)
+    return jnp.where(lane_ids() < HD, low, high) * (1.0 / HD)
+
+
+def swap_halves(values):
+    first = lane_ids() % HD < HD // 2
+    return jnp.where(
+        first, pltpu.roll(values, LANES - HD // 2, 1), pltpu.roll(values, HD // 2, 1)
+    )
+
+
+def norm_rope(raw, gain, cosine, sine):
+    scaled = raw * lax.rsqrt(head_mean(raw * raw) + EPS) * gain
+    return scaled * cosine + swap_halves(scaled) * sine
+
+
+def norm_rope_back(grad, raw, gain, cosine, sine):
+    inverse = lax.rsqrt(head_mean(raw * raw) + EPS)
+    unit = raw * inverse
+    d_scaled = grad * cosine + swap_halves(grad * sine)
+    d_unit = d_scaled * gain
+    return inverse * (d_unit - unit * head_mean(d_unit * unit)), d_scaled * unit
+
+
+def stack_heads(rows, at_low):
+    lanes = lane_ids()
+    zero = jnp.zeros_like(rows)
+    low, high = jnp.where(lanes < HD, rows, zero), jnp.where(lanes < HD, zero, rows)
+    turned = pltpu.roll(high if at_low else low, HD, 1)
+    return jnp.concatenate([low, turned] if at_low else [turned, high], axis=0)
+
+
+def dot(a, b):
+    return jnp.dot(a, b, preferred_element_type=F32)
+
+
+def dot_t(a, b):
+    return lax.dot_general(a, b, (((1,), (1,)), ((), ())), preferred_element_type=F32)
+
+
+def t_dot(a, b):
+    return lax.dot_general(a, b, (((0,), (0,)), ((), ())), preferred_element_type=F32)
+
+
+def attend_kernel(
+    starts, x_ref, gain_ref, w_ref, head_gain_ref, cos_ref, sin_ref, w_out_ref,
+    normed_ref, raw_ref, q_ref, kv_ref, att_ref, inv_ref, part_ref, ov_ref,
+):
     block = pl.program_id(0)
-    bq = q_ref.shape[0]
-    q_begin = block * bq
-    q = q_ref[...]
-    zero = jnp.zeros((bq, HD), BF16)
-    q2 = jnp.concatenate(
-        [
-            jnp.concatenate([q[:, :HD], zero], axis=1),
-            jnp.concatenate([q[:, HD:], zero], axis=1),
-        ],
-        axis=0,
-    )
+    bq = x_ref.shape[0]
+    q_begin = pl.multiple_of(block * bq, bq)
+    x = x_ref[...].astype(F32)
+    inverse = lax.rsqrt(jnp.mean(x * x, axis=1, keepdims=True) + EPS)
+    normed = (x * inverse * gain_ref[...]).astype(BF16)
+    normed_ref[...] = normed
+    raw = dot(normed, w_ref[...])
+    raw_ref[...] = raw
+    cosine, sine = cos_ref[...], sin_ref[...]
+    q = norm_rope(raw[:, :LANES], head_gain_ref[:, :LANES], cosine, sine)
+    q_ref[...] = q.astype(BF16)
+    kv_raw = raw[:, LANES:]
+    is_key = lane_ids() < HD
+    turned = norm_rope(kv_raw, head_gain_ref[:, LANES:], cosine, sine)
+    kv_ref[pl.ds(q_begin, bq), :] = jnp.where(is_key, turned, kv_raw).astype(BF16)
+    ov_ref[pl.ds(q_begin, bq), :] = jnp.where(is_key, 1.0, kv_raw).astype(BF16)
+    q2 = stack_heads(q, True).astype(BF16)
 
     def step(j, acc):
         k_begin = pl.multiple_of(j * bq, bq)
-        keys = kv_ref[pl.ds(k_begin, bq), :]
-        s = lax.dot_general(q2, keys, (((1,), (1,)), ((), ())), preferred_element_type=F32)
+        s = dot_t(q2, kv_ref[pl.ds(k_begin, bq), :])
         mask = block_mask(starts, q_begin, k_begin, bq, bq)
         p = jnp.exp2(s * (LOG2E * HD**-0.5))
         p = jnp.where(jnp.concatenate([mask, mask], axis=0), p, 0.0).astype(BF16)
-        return acc + jnp.dot(p, ov_ref[pl.ds(k_begin, bq), :], preferred_element_type=F32)
+        return acc + dot(p, ov_ref[pl.ds(k_begin, bq), :])
 
     low = low_key(starts, q_begin) // bq
     acc = lax.fori_loop(low, block + 1, step, jnp.zeros((2 * bq, LANES), F32))
     inv = 1.0 / acc[:, :1]
-    out = acc[:, HD:] * inv
-    att_ref[...] = jnp.concatenate([out[:bq], out[bq:]], axis=1).astype(BF16)
-    inv_ref[...] = jnp.concatenate(
-        [jnp.broadcast_to(inv[:bq], (bq, HD)), jnp.broadcast_to(inv[bq:], (bq, HD))], axis=1
-    )
-
-
-def attend_back_kernel(starts, q_ref, kv_ref, att_ref, inv_ref, da_ref, dq_ref, dkv_ref):
+    out = acc * inv
+    att = jnp.where(is_key, pltpu.roll(out[:bq], HD, 1), out[bq:]).astype(BF16)
+    att_ref[...] = att
+    inv_ref[...] = jnp.where(is_key, inv[:bq], inv[bq:])
+    part_ref[...] = dot(att, w_out_ref[...]).astype(BF16)
+
+
+def attend(starts, x_all, gain, w_qkv, head_gain, cosine, sine, w_out):
+    stream, width = x_all.shape
+    bq = ROWS_BLOCK
+
+    def rows(cols):
+        return pl.BlockSpec((bq, cols), lambda i: (i, 0))
+
+    def whole(shape):
+        return pl.BlockSpec(shape, lambda i: (0, 0), pipeline_mode=pl.Buffered(1))
+
+    return pl.pallas_call(
+        attend_kernel,
+        grid=(stream // bq,),
+        in_specs=[
+            pl.BlockSpec(memory_space=pltpu.SMEM),
+            rows(width),
+            whole((1, width)),
+            whole(w_qkv.shape),
+            whole((1, 2 * LANES)),
+            rows(LANES),
+            rows(LANES),
+            whole(w_out.shape),
+        ],
+        out_specs=[
+            rows(width),
+            rows(2 * LANES),
+            rows(LANES),
+            pl.BlockSpec((stream, LANES), lambda i: (0, 0)),
+            rows(LANES),
+            rows(LANES),
+            rows(width),
+        ],
+        out_shape=[
+            jax.ShapeDtypeStruct((stream, width), BF16),
+            jax.ShapeDtypeStruct((stream, 2 * LANES), F32),
+            jax.ShapeDtypeStruct((stream, LANES), BF16),
+            jax.ShapeDtypeStruct((stream, LANES), BF16),
+            jax.ShapeDtypeStruct((stream, LANES), BF16),
+            jax.ShapeDtypeStruct((stream, LANES), F32),
+            jax.ShapeDtypeStruct((stream, width), BF16),
+        ],
+        scratch_shapes=[pltpu.VMEM((stream, LANES), BF16)],
+        compiler_params=pltpu.CompilerParams(vmem_limit_bytes=48 * 2**20),
+        cost_estimate=pl.CostEstimate(flops=2 * 10**10, bytes_accessed=2**25, transcendentals=0),
+    )(starts, x_all, gain, w_qkv, head_gain, cosine, sine, w_out)
+
+
+def attend_back_kernel(
+    starts, db_ref, w_out_ref, q_ref, kv_ref, att_ref, inv_ref, raw_ref, head_gain_ref, cos_ref, sin_ref,
+    d_ref, w_grad_ref, gain_ref, dkv_ref, w_acc_ref,
+):
     block = pl.program_id(0)
-    bq = q_ref.shape[0]
-    q_begin = block * bq
+    bq = db_ref.shape[0]
+    q_begin = pl.multiple_of(block * bq, bq)
 
     @pl.when(block == 0)
     def _():
         dkv_ref[...] = jnp.zeros_like(dkv_ref)
-
-    q = q_ref[...]
-    da = da_ref[...]
-    zero = jnp.zeros((bq, HD), BF16)
-    q2 = jnp.concatenate(
-        [
-            jnp.concatenate([q[:, :HD], zero], axis=1),
-            jnp.concatenate([q[:, HD:], zero], axis=1),
-        ],
-        axis=0,
-    )
-    da2 = jnp.concatenate(
-        [
-            jnp.concatenate([zero, da[:, :HD]], axis=1),
-            jnp.concatenate([zero, da[:, HD:]], axis=1),
-        ],
-        axis=0,
-    )
-    prod = da.astype(F32) * att_ref[...].astype(F32)
+        w_acc_ref[...] = jnp.zeros_like(w_acc_ref)
+        gain_ref[...] = jnp.zeros_like(gain_ref)
+
+    db = db_ref[...]
+    att = att_ref[...]
+    da = dot_t(db, w_out_ref[...])
+    w_acc_ref[...] += t_dot(att, db)
+    q2 = stack_heads(q_ref[...].astype(F32), True).astype(BF16)
+    da2 = stack_heads(da, False).astype(BF16)
+    prod = da.astype(BF16).astype(F32) * att.astype(F32)
     delta = jnp.concatenate(
         [
             jnp.sum(prod[:, :HD], axis=1, keepdims=True),
@@ -421,63 +530,209 @@
     def step(j, dq):
         k_begin = pl.multiple_of(j * bq, bq)
         keys = kv_ref[pl.ds(k_begin, bq), :]
-        s = lax.dot_general(q2, keys, (((1,), (1,)), ((), ())), preferred_element_type=F32)
+        s = dot_t(q2, keys)
         mask = block_mask(starts, q_begin, k_begin, bq, bq)
         p = jnp.exp2(s * (LOG2E * HD**-0.5)) * inv
         p = jnp.where(jnp.concatenate([mask, mask], axis=0), p, 0.0)
-        dp = lax.dot_general(da2, keys, (((1,), (1,)), ((), ())), preferred_element_type=F32)
-        ds = (p * (dp - delta)).astype(BF16)
-        back = (((0,), (0,)), ((), ()))
-        dkv_ref[pl.ds(k_begin, bq), :] += lax.dot_general(
-            ds, q2, back, preferred_element_type=F32
-        ) + lax.dot_general(p.astype(BF16), da2, back, preferred_element_type=F32)
-        return dq + jnp.dot(ds, keys, preferred_element_type=F32)
+        ds = (p * (dot_t(da2, keys) - delta)).astype(BF16)
+        dkv_ref[pl.ds(k_begin, bq), :] += t_dot(ds, q2) * HD**-0.5 + t_dot(p.astype(BF16), da2)
+        return dq + dot(ds, keys)
 
     low = low_key(starts, q_begin) // bq
     dq = lax.fori_loop(low, block + 1, step, jnp.zeros((2 * bq, LANES), F32))
-    dq_ref[...] = jnp.concatenate([dq[:bq, :HD], dq[bq:, :HD]], axis=1)
-
-
-def attend(starts, q, kv, ov):
-    stream = q.shape[0]
+    is_key = lane_ids() < HD
+    dq = jnp.where(is_key, dq[:bq], pltpu.roll(dq[bq:], HD, 1)) * HD**-0.5
+    here = pl.ds(q_begin, bq)
+    d_raw, d_gain = norm_rope_back(
+        dq, raw_ref[here, :LANES], head_gain_ref[:, :LANES], cos_ref[here, :], sin_ref[here, :]
+    )
+    d_ref[here, :LANES] = d_raw.astype(BF16)
+    gain_ref[0:1, :] += jnp.sum(d_gain, axis=0, keepdims=True)
+
+    @pl.when(block == pl.num_programs(0) - 1)
+    def _():
+        def finish(j, carry):
+            rows = pl.ds(pl.multiple_of(j * bq, bq), bq)
+            dkv = dkv_ref[rows, :]
+            d_raw, d_gain = norm_rope_back(
+                dkv, raw_ref[rows, LANES:], head_gain_ref[:, LANES:], cos_ref[rows, :], sin_ref[rows, :]
+            )
+            d_ref[rows, LANES:] = jnp.where(is_key, d_raw, dkv).astype(BF16)
+            gain_ref[1:2, :] += jnp.sum(d_gain, axis=0, keepdims=True)
+            return carry
+
+        lax.fori_loop(0, pl.num_programs(0), finish, 0)
+        w_grad_ref[...] = w_acc_ref[...].astype(BF16)
+
+
+def attend_back(starts, db_all, w_out, q, kv, att, inv, raw, head_gain, cosine, sine):
+    stream, width = db_all.shape
     bq = ROWS_BLOCK
-    rows = pl.BlockSpec((bq, LANES), lambda i: (i, 0))
-    whole = pl.BlockSpec((stream, LANES), lambda i: (0, 0))
-    return pl.pallas_call(
-        attend_kernel,
-        grid=(stream // bq,),
-        in_specs=[pl.BlockSpec(memory_space=pltpu.SMEM), rows, whole, whole],
-        out_specs=[rows, rows],
-        out_shape=[
-            jax.ShapeDtypeStruct((stream, LANES), BF16),
-            jax.ShapeDtypeStruct((stream, LANES), F32),
-        ],
-        compiler_params=pltpu.CompilerParams(vmem_limit_bytes=32 * 2**20),
-        cost_estimate=pl.CostEstimate(
-            flops=4 * stream * 1024 * LANES, bytes_accessed=6 * stream * LANES * 2, transcendentals=0
-        ),
-    )(starts, q, kv, ov)
-
-
-def attend_back(starts, q, kv, att, inv, da):
-    stream = q.shape[0]
-    bq = ROWS_BLOCK
-    rows = pl.BlockSpec((bq, LANES), lambda i: (i, 0))
-    whole = pl.BlockSpec((stream, LANES), lambda i: (0, 0))
+
+    def rows(cols):
+        return pl.BlockSpec((bq, cols), lambda i: (i, 0))
+
+    def whole(shape):
+        return pl.BlockSpec(shape, lambda i: (0, 0), pipeline_mode=pl.Buffered(1))
+
+    def kept(shape):
+        return pl.BlockSpec(shape, lambda i: (0, 0))
+
     return pl.pallas_call(
         attend_back_kernel,
         grid=(stream // bq,),
-        in_specs=[pl.BlockSpec(memory_space=pltpu.SMEM), rows, whole, rows, rows, rows],
-        out_specs=[rows, whole],
+        in_specs=[
+            pl.BlockSpec(memory_space=pltpu.SMEM),
+            rows(width),
+            whole(w_out.shape),
+            rows(LANES),
+            whole((stream, LANES)),
+            rows(LANES),
+            rows(LANES),
+            whole((stream, 2 * LANES)),
+            whole((1, 2 * LANES)),
+            whole((stream, LANES)),
+            whole((stream, LANES)),
+        ],
+        out_specs=[kept((stream, 2 * LANES)), kept(w_out.shape), kept((8, LANES))],
         out_shape=[
-            jax.ShapeDtypeStruct((stream, LANES), F32),
-            jax.ShapeDtypeStruct((stream, LANES), F32),
+            jax.ShapeDtypeStruct((stream, 2 * LANES), BF16),
+            jax.ShapeDtypeStruct(w_out.shape, BF16),
+            jax.ShapeDtypeStruct((8, LANES), F32),
+        ],
+        scratch_shapes=[pltpu.VMEM((stream, LANES), F32), pltpu.VMEM(w_out.shape, F32)],
+        compiler_params=pltpu.CompilerParams(vmem_limit_bytes=48 * 2**20),
+        cost_estimate=pl.CostEstimate(flops=3 * 10**10, bytes_accessed=2**25, transcendentals=0),
+    )(starts, db_all, w_out, q, kv, att, inv, raw, head_gain, cosine, sine)
+
+
+def ffn_kernel(
+    n2_ref, dy_ref, own_ref, other_ref, w_down_ref,
+    down_ref, d_n2_ref, gu_grad_ref, down_grad_ref, gu_acc, down_acc, w_gu_ref,
+):
+    block = pl.program_id(0)
+    first = lax.axis_index("dp") == 0
+
+    @pl.when(block == 0)
+    def _():
+        half = own_ref.shape[1]
+        own_row = jnp.where(first, 0, half)
+
+        def put(j, carry):
+            for begin, ref in ((own_row, own_ref), (half - own_row, other_ref)):
+                at = pl.multiple_of(2 * half * j + begin, half)
+                w_gu_ref[pl.ds(at, half), :] = ref[j]
+            return carry
+
+        lax.fori_loop(0, own_ref.shape[0], put, 0)
+        gu_acc[...] = jnp.zeros_like(gu_acc)
+        down_acc[...] = jnp.zeros_like(down_acc)
+
+    cols = w_down_ref.shape[0]
+    n2, dy = n2_ref[...], dy_ref[...]
+    gate_up = dot(n2, w_gu_ref[...])
+    gate, up = gate_up[:, :cols], gate_up[:, cols:]
+    sig = jax.nn.sigmoid(gate)
+    silu = gate * sig
+    hidden = (silu * up).astype(BF16)
+    down_ref[...] = dot(hidden, w_down_ref[...]).astype(BF16)
+    d_hidden = dot_t(dy, w_down_ref[...])
+    d_gu = jnp.concatenate(
+        [
+            (d_hidden * up * (sig * (1.0 + gate * (1.0 - sig)))).astype(BF16),
+            (d_hidden * silu).astype(BF16),
+        ],
+        axis=1,
+    )
+    d_n2_ref[...] = dot_t(d_gu, w_gu_ref[...]).astype(BF16)
+    gu_acc[...] += t_dot(n2, d_gu)
+    down_acc[...] += t_dot(hidden, dy)
+
+    @pl.when(block == pl.num_programs(0) - 1)
+    def _():
+        gu_grad_ref[...] = gu_acc[...].astype(BF16)
+        down_grad_ref[...] = down_acc[...].astype(BF16)
+
+
+def ffn(n2_all, dy_all, own, other, w_down):
+    stream, width = n2_all.shape
+    gu_shape = (width, own.shape[2])
+    bt = FFN_BLOCK
+    rows = pl.BlockSpec((bt, width), lambda i: (i, 0))
+
+    def whole(shape):
+        return pl.BlockSpec(shape, lambda i: (0,) * len(shape), pipeline_mode=pl.Buffered(1))
+
+    return pl.pallas_call(
+        ffn_kernel,
+        grid=(stream // bt,),
+        in_specs=[rows, rows, whole(own.shape), whole(own.shape), whole(w_down.shape)],
+        out_specs=[rows, rows, whole(gu_shape), whole(w_down.shape)],
+        out_shape=[
+            jax.ShapeDtypeStruct((stream, width), BF16),
+            jax.ShapeDtypeStruct((stream, width), BF16),
+            jax.ShapeDtypeStruct(gu_shape, BF16),
+            jax.ShapeDtypeStruct(w_down.shape, BF16),
+        ],
+        scratch_shapes=[
+            pltpu.VMEM(gu_shape, F32),
+            pltpu.VMEM(w_down.shape, F32),
+            pltpu.VMEM(gu_shape, BF16),
+        ],
+        compiler_params=pltpu.CompilerParams(vmem_limit_bytes=58 * 2**20),
+        cost_estimate=pl.CostEstimate(
+            flops=18 * stream * width * w_down.shape[0], bytes_accessed=2**25, transcendentals=0
+        ),
+    )(n2_all, dy_all, own, other, w_down)
+
+
+def unpack_attn_kernel(
+    own_ref, other_ref, wq_ref, wk_ref, wv_ref, q_ref, k_ref, v_ref, sum_ref, gains_ref
+):
+    n, half = own_ref.shape[0], wq_ref.shape[0] // 2
+    first = lax.axis_index("dp") == 0
+    low = jnp.where(first, 0, half)
+    high = half - low
+    share = n // KV
+    gains_ref[...] = jnp.sum(own_ref[:, half : half + 8, :].astype(F32), axis=0)
+    for begin, ref in ((low, own_ref), (high, other_ref)):
+        rows = pl.ds(pl.multiple_of(begin, half), half)
+        total = jnp.zeros((half, 1), F32)
+        for j in range(n):
+            cols = slice(j * LANES, (j + 1) * LANES)
+            q = ref[j, :half, :LANES].astype(F32)
+            q_ref[rows, cols] = q
+            total += jnp.sum(q * wq_ref[rows, cols].astype(F32), axis=1, keepdims=True)
+        for pair in range(KV // 2):
+            cols = slice(pair * LANES, (pair + 1) * LANES)
+            heads = []
+            for head in (2 * pair, 2 * pair + 1):
+                kv = ref[head * share, :half, LANES:].astype(F32)
+                for more in range(1, share):
+                    kv = kv + ref[head * share + more, :half, LANES:].astype(F32)
+                heads.append(kv)
+            k = jnp.concatenate([heads[0][:, :HD], heads[1][:, :HD]], axis=1)
+            v = jnp.concatenate([heads[0][:, HD:], heads[1][:, HD:]], axis=1)
+            k_ref[rows, cols] = k
+            v_ref[rows, cols] = v
+            both = k * wk_ref[rows, cols].astype(F32) + v * wv_ref[rows, cols].astype(F32)
+            total += jnp.sum(both, axis=1, keepdims=True)
+        sum_ref[rows, :] = jnp.broadcast_to(total, (half, LANES))
+
+
+def unpack_attn(own, other, w_query, w_key, w_value):
+    d_rows = w_query.shape[0]
+    return pl.pallas_call(
+        unpack_attn_kernel,
+        out_shape=[
+            jax.ShapeDtypeStruct(w_query.shape, F32),
+            jax.ShapeDtypeStruct(w_key.shape, F32),
+            jax.ShapeDtypeStruct(w_value.shape, F32),
+            jax.ShapeDtypeStruct((d_rows, LANES), F32),
+            jax.ShapeDtypeStruct((8, 2 * LANES), F32),
         ],
         compiler_params=pltpu.CompilerParams(vmem_limit_bytes=32 * 2**20),
-        cost_estimate=pl.CostEstimate(
-            flops=10 * stream * 1024 * LANES, bytes_accessed=8 * stream * LANES * 2, transcendentals=0
-        ),
-    )(starts, q, kv, att, inv, da)
+    )(own, other, w_query, w_key, w_value)
 
 
 def pack_attn_kernel(query_ref, key_ref, value_ref, gains_ref, out_ref):
@@ -501,51 +756,63 @@
     )(w_query, w_key, w_value, gains)
 
 
-def pack_pair_kernel(gate_ref, up_ref, out_ref):
-    cols = gate_ref.shape[1]
-    out_ref[0, :, :cols] = gate_ref[...]
-    out_ref[0, :, cols:] = up_ref[...]
+def pack_pair_kernel(dp_ref, gate_ref, up_ref, out_ref):
+    count, _, both = out_ref.shape
+    cols = both // 2
+    for j in range(count):
+        out_ref[j, :, :cols] = gate_ref[:, j * cols : (j + 1) * cols]
+        out_ref[j, :, cols:] = up_ref[:, j * cols : (j + 1) * cols]
 
 
 def pack_pair(w_gate, w_up, n):
-    d_rows, cols = w_gate.shape[0], w_gate.shape[1] // n
-    part = pl.BlockSpec((d_rows, cols), lambda j: (0, j))
+    half, cols = w_gate.shape[0] // 2, w_gate.shape[1] // n
+    count = 4
+    part = pl.BlockSpec((half, count * cols), lambda j, dp: (dp[0], j))
     return pl.pallas_call(
         pack_pair_kernel,
-        grid=(n,),
-        in_specs=[part, part],
-        out_specs=pl.BlockSpec((1, d_rows, 2 * cols), lambda j: (j, 0, 0)),
-        out_shape=jax.ShapeDtypeStruct((n, d_rows, 2 * cols), BF16),
-    )(w_gate, w_up)
+        grid_spec=pltpu.PrefetchScalarGridSpec(
+            num_scalar_prefetch=1,
+            grid=(n // count,),
+            in_specs=[part, part],
+            out_specs=pl.BlockSpec((count, half, 2 * cols), lambda j, dp: (j, 0, 0)),
+        ),
+        out_shape=jax.ShapeDtypeStruct((n, half, 2 * cols), BF16),
+        compiler_params=pltpu.CompilerParams(vmem_limit_bytes=32 * 2**20),
+    )(lax.axis_index("dp").reshape(1), w_gate, w_up)
 
 
 def unpack_pair_kernel(own_ref, other_ref, gate_w, up_w, gate_ref, up_ref, sum_ref):
+    count, half, both = own_ref.shape
+    cols = both // 2
     first = lax.axis_index("dp") == 0
-    own, other = own_ref[0].astype(F32), other_ref[0].astype(F32)
-    grads = jnp.concatenate(
-        [jnp.where(first, own, other), jnp.where(first, other, own)], axis=0
-    )
-    cols = gate_ref.shape[1]
-    gate, up = grads[:, :cols], grads[:, cols:]
-    gate_ref[...] = gate
-    up_ref[...] = up
-    total = gate * gate_w[...].astype(F32) + up * up_w[...].astype(F32)
 
     @pl.when(pl.program_id(0) == 0)
     def _():
         sum_ref[...] = jnp.zeros_like(sum_ref)
 
-    sum_ref[...] += jnp.broadcast_to(jnp.sum(total, axis=1, keepdims=True), sum_ref.shape)
+    own_row = pl.multiple_of(jnp.where(first, 0, half), half)
+    for begin, ref in ((own_row, own_ref), (half - own_row, other_ref)):
+        rows = pl.ds(pl.multiple_of(begin, half), half)
+        total = jnp.zeros((half, 128), F32)
+        for j in range(count):
+            for at in range(0, cols, 128):
+                here = slice(j * cols + at, j * cols + at + 128)
+                gate = ref[j, :, at : at + 128].astype(F32)
+                up = ref[j, :, cols + at : cols + at + 128].astype(F32)
+                gate_ref[rows, here] = gate
+                up_ref[rows, here] = up
+                total += gate * gate_w[rows, here].astype(F32) + up * up_w[rows, here].astype(F32)
+        sum_ref[rows, :] += total
 
 
 def unpack_pair(own, other, w_gate, w_up):
-    n, half, both_cols = own.shape
-    cols = both_cols // 2
-    block = pl.BlockSpec((1, half, both_cols), lambda j: (j, 0, 0))
-    part = pl.BlockSpec((2 * half, cols), lambda j: (0, j))
+    n, half, both = own.shape
+    count = 4
+    block = pl.BlockSpec((count, half, both), lambda j: (j, 0, 0))
+    part = pl.BlockSpec((2 * half, count * both // 2), lambda j: (0, j))
     return pl.pallas_call(
         unpack_pair_kernel,
-        grid=(n,),
+        grid=(n // count,),
         in_specs=[block, block, part, part],
         out_specs=[part, part, pl.BlockSpec((2 * half, 128), lambda j: (0, 0))],
         out_shape=[
@@ -553,28 +820,32 @@
             jax.ShapeDtypeStruct(w_up.shape, F32),
             jax.ShapeDtypeStruct((2 * half, 128), F32),
         ],
+        compiler_params=pltpu.CompilerParams(vmem_limit_bytes=32 * 2**20),
     )(own, other, w_gate, w_up)
-
-
-def head_prepare(q_raw, k_raw, q_gain, k_gain, position):
-    stream = q_raw.shape[0]
-    q, k = prepare(
-        q_raw.reshape(stream, 2, HD), k_raw.reshape(stream, 1, HD), q_gain, k_gain, position
-    )
-    return q.reshape(stream, LANES), k.reshape(stream, HD)
 
 
 MESH_ID = pl.DeviceIdType.MESH
 LINK_COST = pl.CostEstimate(flops=5 * 10**10, bytes_accessed=2**24, transcendentals=0)
 
 
-def meet_neighbours(ctx, wa, n_ctx):
+def meet_neighbours(ctx, wa, n_ctx, n_wa, everyone):
     barrier = pltpu.get_barrier_semaphore()
 
     def greet(where):
         pl.semaphore_signal(barrier, inc=1, device_id=where, device_id_type=MESH_ID)
 
     greet({"dp": lax.axis_index("dp") ^ 1})
+    if everyone:
+        n = n_ctx * n_wa
+
+        def step(i, carry):
+            other = lax.rem(ctx * n_wa + wa + i, n)
+            greet({"ctx": other // n_wa, "wa": lax.rem(other, n_wa)})
+            return carry
+
+        lax.fori_loop(1, n, step, 0)
+        pl.semaphore_wait(barrier, n)
+        return
     greet({"wa": wa ^ 1})
     greet({"wa": wa ^ 2})
     pl.when(ctx > 0)(lambda: greet({"ctx": ctx - 1}))
@@ -583,28 +854,57 @@
     pl.semaphore_wait(barrier, 5 - ends)
 
 
-WHOLE, PLACE, PICK = 0, 1, 2
+WHOLE, PICK, SPREAD = 0, 1, 2
 
 
 def pair_shape(kind, src):
-    if kind == PLACE:
-        return (src.shape[0], 2) + src.shape[1:]
     if kind == PICK:
         return (src.shape[0],) + src.shape[2:]
     return src.shape
 
 
-def start_pairs(kinds, srcs, dsts, sems):
+def start_spread(src, dst, n_wa, sems):
+    n = src.shape[0]
+    me = lax.axis_index("ctx") * n_wa + lax.axis_index("wa")
+    keep = pltpu.make_async_copy(src.at[me], dst.at[me], sems.at[0, 0])
+    keep.start()
+
+    def made(step, arriving):
+        other = lax.rem(me + step, n)
+        return pltpu.make_async_remote_copy(
+            src_ref=src.at[other],
+            dst_ref=dst.at[other if arriving else me],
+            send_sem=sems.at[0, step],
+            recv_sem=sems.at[1, other if arriving else me],
+            device_id={"ctx": other // n_wa, "wa": lax.rem(other, n_wa)},
+            device_id_type=MESH_ID,
+        )
+
+    def loop(act):
+        def step(i, carry):
+            act(i)
+            return carry
+
+        lax.fori_loop(1, n, step, 0)
+
+    def finish():
+        keep.wait()
+        loop(lambda i: made(i, True).wait_recv())
+        loop(lambda i: made(i, False).wait_send())
+
+    loop(lambda i: made(i, False).start())
+    return finish
+
+
+def start_pairs(kinds, srcs, dsts, n_wa, sems, spread_sems):
     dp = lax.axis_index("dp")
-    made = []
+    waits = []
     for at, (kind, src, dst) in enumerate(zip(kinds, srcs, dsts)):
+        if kind == SPREAD:
+            waits.append(start_spread(src, dst, n_wa, spread_sems))
+            continue
         if kind == PICK:
             src = src.at[:, dp ^ 1]
-        if kind == PLACE:
-            dst = dst.at[:, dp]
-            keep = pltpu.make_async_copy(src, dst, sems.at[at, 2])
-            keep.start()
-            made.append((keep, keep.wait))
         send = pltpu.make_async_remote_copy(
             src_ref=src,
             dst_ref=dst,
@@ -614,20 +914,8 @@
             device_id_type=MESH_ID,
         )
         send.start()
-        if kind == PLACE:
-            got = pltpu.make_async_remote_copy(
-                src_ref=src,
-                dst_ref=dsts[at].at[:, dp ^ 1],
-                send_sem=sems.at[at, 0],
-                recv_sem=sems.at[at, 1],
-                device_id={"dp": dp ^ 1},
-                device_id_type=MESH_ID,
-            )
-            made.append((send, send.wait_send))
-            made.append((got, got.wait_recv))
-        else:
-            made.append((send, send.wait))
-    return made
+        waits.append(send.wait)
+    return waits
 
 
 def piece_row(zc, wac, h, half, n_ctx, n_wa, by_position):
@@ -640,12 +928,11 @@
 def gather_kernel(n_ctx, n_wa, by_position, kinds, own_ref, *refs):
     pairs = len(kinds)
     srcs, out_ref, dsts = refs[:pairs], refs[pairs], refs[pairs + 1 : 2 * pairs + 1]
-    own_sem, send_sem, recv_sem = refs[2 * pairs + 1 : 2 * pairs + 4]
+    own_sem, send_sem, recv_sem, pair_sem, spread_sem = refs[2 * pairs + 1 :]
     ctx = lax.axis_index("ctx")
     wa = lax.axis_index("wa")
     half = own_ref.shape[0] // 2
-    meet_neighbours(ctx, wa, n_ctx)
-    pair_copies = start_pairs(kinds, srcs, dsts, refs[-1])
+    meet_neighbours(ctx, wa, n_ctx, n_wa, SPREAD in kinds)
     sends = []
 
     def place(zc, wac, h):
@@ -696,6 +983,7 @@
         made = pltpu.make_async_copy(own, place(ctx, wa, h), own_sem.at[h])
         made.start()
         own_copies.append(made)
+    pair_waits = start_pairs(kinds, srcs, dsts, n_wa, pair_sem, spread_sem)
 
     def across(k, h):
         for way in (-1, 1) if k else (1,):
@@ -728,8 +1016,8 @@
             pl.when(cond)(made.wait_send)
     for made in own_copies:
         made.wait()
-    for _, done in pair_copies:
-        done()
+    for wait in pair_waits:
+        wait()
 
 
 def gather_tokens(own, pairs, n_ctx, n_wa, by_position, call_id):
@@ -748,7 +1036,8 @@
             pltpu.SemaphoreType.DMA((2,)),
             pltpu.SemaphoreType.DMA((8 + 12 * (n_ctx - 1) + 2 * (2 * n_ctx - 1),)),
             pltpu.SemaphoreType.DMA((2 * n,)),
-            pltpu.SemaphoreType.DMA((max(1, len(pairs)), 3)),
+            pltpu.SemaphoreType.DMA((max(1, len(pairs)), 2)),
+            pltpu.SemaphoreType.DMA((2, n)),
         ],
         compiler_params=pltpu.CompilerParams(collective_id=call_id, has_side_effects=True),
         cost_estimate=LINK_COST,
@@ -758,15 +1047,15 @@
 def scatter_kernel(n_ctx, n_wa, by_position, kinds, part_ref, *refs):
     pairs = len(kinds)
     srcs, out_ref, dsts = refs[:pairs], refs[pairs], refs[pairs + 1 : 2 * pairs + 1]
-    s1, s2, s3, send_sem, recv1, recv2, recv3, pair_sem = refs[2 * pairs + 1 :]
+    s1, s2, s3, send_sem, recv1, recv2, recv3, pair_sem, spread_sem = refs[2 * pairs + 1 :]
     ctx = lax.axis_index("ctx")
     wa = lax.axis_index("wa")
     half = out_ref.shape[0] // 2
     slab = 16
     y = wa // 2
     sibling, across = {"wa": wa ^ 1}, {"wa": wa ^ 2}
-    meet_neighbours(ctx, wa, n_ctx)
-    pair_copies = start_pairs(kinds, srcs, dsts, pair_sem)
+    meet_neighbours(ctx, wa, n_ctx, n_wa, SPREAD in kinds)
+    pair_waits = start_pairs(kinds, srcs, dsts, n_wa, pair_sem, spread_sem)
     sends = []
 
     def begin(cond, act):
@@ -867,8 +1156,8 @@
                 begin(take, lambda extra=extra: add_up(out_ref, h * half, base + extra))
     for cond, made in sends:
         begin(cond, made.wait_send)
-    for _, done in pair_copies:
-        done()
+    for wait in pair_waits:
+        wait()
 
 
 def scatter_tokens(part, pairs, n_ctx, n_wa, by_position, call_id):
@@ -893,7 +1182,8 @@
             pltpu.SemaphoreType.DMA((4 * n_ctx,)),
             pltpu.SemaphoreType.DMA((2 * n_ctx,)),
             pltpu.SemaphoreType.DMA((4 * n_ctx,)),
-            pltpu.SemaphoreType.DMA((max(1, len(pairs)), 3)),
+            pltpu.SemaphoreType.DMA((max(1, len(pairs)), 2)),
+            pltpu.SemaphoreType.DMA((2, n)),
         ],
         compiler_params=pltpu.CompilerParams(
             collective_id=call_id, has_side_effects=True, vmem_limit_bytes=48 * 2**20
@@ -921,18 +1211,13 @@
     n_ctx = lax.axis_size("ctx")
     n_wa = lax.axis_size("wa")
     n = n_ctx * n_wa
-    even = lax.axis_index("wa") % 2 == 0
     tok_rows, width = tokens.shape[1:]
     d_rows = w_query.shape[0]
     stream = tok_rows * n
     ff_cols = FF // n
     per = HD // n
     extra = 16
-    position = jnp.arange(stream, dtype=jnp.int32)
     swap_dp = [(0, 1), (1, 0)]
-
-    def mm(a, b):
-        return jnp.dot(a, b, preferred_element_type=F32)
 
     def mm_t(a, b):
         return lax.dot_general(a, b, (((1,), (1,)), ((), ())), preferred_element_type=F32)
@@ -943,23 +1228,12 @@
     def swap(blocks):
         return lax.all_to_all(blocks, AXES, 0, 0, tiled=True)
 
-    def both(part):
-        part = part.astype(BF16)
-        return part.astype(F32) + lax.ppermute(part, "dp", swap_dp).astype(F32)
-
+    half = d_rows // 2
+    dp = lax.axis_index("dp")
     gains_own = jnp.concatenate([attn_gain, ffn_gain, q_gain, k_gain])
     gains_row = jnp.pad(gains_own, (0, extra * 2 * LANES - gains_own.shape[0]))
     attn_cols = pack_attn(w_query, w_key, w_value, gains_row.reshape(extra, 2 * LANES), n)
-    half = d_rows // 2
-    dp = lax.axis_index("dp")
-    ff_blocks = pack_pair(
-        lax.dynamic_slice_in_dim(w_gate, dp * half, half),
-        lax.dynamic_slice_in_dim(w_up, dp * half, half),
-        n,
-    )
-    attn_cols, tokens_b, ff_blocks = lax.optimization_barrier((attn_cols, tokens[0], ff_blocks))
-    attn_cols = swap(attn_cols)
-    (x_all,) = gather_tokens(tokens_b, [], n_ctx, n_wa, True, 1)
+    x_all, attn_cols = gather_tokens(tokens[0], [(SPREAD, attn_cols)], n_ctx, n_wa, True, 1)
     w_qkv = attn_cols[:, :d_rows].reshape(width, 2 * LANES)
     gains = attn_cols[:, d_rows:].reshape(n, -1).astype(F32)
     attn_gain32 = gains[:, :d_rows].reshape(-1)
@@ -967,102 +1241,73 @@
     qgain32 = gains[:, 2 * d_rows : 2 * d_rows + per].reshape(-1)
     kgain32 = gains[:, 2 * d_rows + per : 2 * d_rows + 2 * per].reshape(-1)
 
-    ff_blocks, dy_b, _ = lax.optimization_barrier((ff_blocks, out_grad[0], x_all))
+    w_gate_b, dy_b, x_all = lax.optimization_barrier((w_gate, out_grad[0], x_all))
+    ff_blocks = pack_pair(w_gate_b, w_up, n)
     ff_half = swap(ff_blocks)
     dy_all = lax.all_gather(dy_b, AXES, axis=0, tiled=True)
 
     x_own = tokens[0].astype(F32)
-    n1_all = rms_norm(x_all.astype(F32), attn_gain32).astype(BF16)
-    qkv = mm(n1_all, w_qkv)
-    q_raw, k_raw, v_raw = qkv[:, :LANES], qkv[:, LANES : LANES + HD], qkv[:, LANES + HD :]
-    v_b = v_raw.astype(BF16)
-    (q_rot, k_rot), prep_back = jax.vjp(
-        partial(head_prepare, position=position), q_raw, k_raw, qgain32, kgain32
-    )
-    q_b = q_rot.astype(BF16)
-    kv_b = jnp.concatenate([k_rot.astype(BF16), v_b], axis=1)
-    ov_b = jnp.concatenate([jnp.ones_like(v_b), v_b], axis=1)
-    att, inv = attend(doc_starts, q_b, kv_b, ov_b)
-    branch, w_gu = scatter_tokens(
-        mm(att, w_out).astype(BF16), [(PLACE, ff_half)], n_ctx, n_wa, True, 3
-    )
-    w_gu = w_gu.reshape(width, 2 * ff_cols)
+    cosine, sine = rope_tables(stream)
+    head_gain = jnp.concatenate([qgain32, qgain32, kgain32, kgain32]).reshape(1, 2 * LANES)
+    n1_all, raw, q_b, kv_b, att, inv, branch_part = attend(
+        doc_starts, x_all, attn_gain32.reshape(1, width), w_qkv, head_gain, cosine, sine, w_out
+    )
+    (branch,) = scatter_tokens(branch_part, [], n_ctx, n_wa, True, 3)
     middle = x_own + branch
     n2_own, n2_back = jax.vjp(rms_norm, middle, ffn_gain32)
-    (n2_all,) = gather_tokens(n2_own.astype(BF16), [], n_ctx, n_wa, False, 2)
-    gate_up = mm(n2_all, w_gu)
-    gate, up = gate_up[:, :ff_cols], gate_up[:, ff_cols:]
-    sig = jax.nn.sigmoid(gate)
-    silu = gate * sig
-    hidden = (silu * up).astype(BF16)
-    down_part = mm(hidden, w_down).astype(BF16)
+    n2_all, ff_other = gather_tokens(
+        n2_own.astype(BF16), [(WHOLE, ff_half)], n_ctx, n_wa, False, 2
+    )
+    down_part, d_n2_part, gu_grad, down_grad = ffn(n2_all, dy_all, ff_half, ff_other, w_down)
     down = lax.psum_scatter(down_part, AXES, scatter_dimension=0, tiled=True).astype(F32)
     layer_out = middle + down
-
-    d_hidden = mm_t(dy_all, w_down)
-    d_gu = jnp.concatenate(
-        [d_hidden * up * (sig * (1.0 + gate * (1.0 - sig))), d_hidden * silu], axis=1
-    ).astype(BF16)
-    gu_grad = t_mm(n2_all, d_gu).astype(BF16).reshape(n, 2, half, 2 * ff_cols)
-    d_n2, gu_other = scatter_tokens(
-        mm_t(d_gu, w_gu).astype(BF16), [(PICK, gu_grad)], n_ctx, n_wa, False, 4
-    )
+    gu_grad = gu_grad.reshape(n, 2, half, 2 * ff_cols)
+    d_n2, gu_other = scatter_tokens(d_n2_part, [(PICK, gu_grad)], n_ctx, n_wa, False, 4)
     gu_mine = lax.dynamic_index_in_dim(gu_grad, dp, 1, keepdims=False)
-    gu_rows = swap((gu_mine.astype(F32) + gu_other.astype(F32)).astype(BF16))
-    down_grad = t_mm(hidden, dy_all).astype(BF16)
+    gu_sum = (gu_mine.astype(F32) + gu_other.astype(F32)).astype(BF16)
     d_mid_part, _ = n2_back(d_n2)
     d_middle = out_grad[0].astype(F32) + d_mid_part
     db_all, down_other = gather_tokens(
         d_middle.astype(BF16), [(WHOLE, down_grad)], n_ctx, n_wa, True, 5
     )
-    out_w_grad = t_mm(att, db_all).astype(BF16)
-    d_att = mm_t(db_all, w_out).astype(BF16)
-    dq, dkv = attend_back(doc_starts, q_b, kv_b, att, inv, d_att)
-    dkv = dkv + lax.ppermute(dkv, "wa", [(i, i ^ 1) for i in range(n_wa)])
-    dq_raw, dk_raw, d_qgain, d_kgain = prep_back((dq * HD**-0.5, dkv[:, :HD] * HD**-0.5))
-    d_kgain = jnp.where(even, d_kgain, 0.0)
-    d_kv_own = jnp.where(even, dk_raw, dkv[:, HD:])
-    w_kv_own = jnp.where(even, w_qkv[:, LANES : LANES + HD], w_qkv[:, LANES + HD :])
-    d_qkv = jnp.concatenate([dq_raw, d_kv_own], axis=1).astype(BF16)
-    qkv_grad = t_mm(n1_all, d_qkv).astype(BF16)
-    head_gains = jnp.concatenate([d_qgain, d_kgain])
-    qkv_cols = LANES + HD
-    head_row = jnp.pad(head_gains.astype(BF16), (0, extra * qkv_cols - LANES))
-    qkv_rows = swap(
-        jnp.concatenate(
-            [
-                qkv_grad.reshape(n, d_rows, qkv_cols),
-                jnp.broadcast_to(head_row.reshape(1, extra, qkv_cols), (n, extra, qkv_cols)),
-            ],
-            axis=1,
-        )
-    )
-    d_n1_part = mm_t(d_qkv, jnp.concatenate([w_qkv[:, :LANES], w_kv_own], axis=1)).astype(BF16)
-    d_n1, gu_others, out_w_other = scatter_tokens(
-        d_n1_part, [(WHOLE, gu_rows), (WHOLE, out_w_grad)], n_ctx, n_wa, True, 6
-    )
+    gu_sum, db_all = lax.optimization_barrier((gu_sum, db_all))
+    gu_rows = swap(gu_sum)
+    d_qkv, out_w_grad, head_grad = attend_back(
+        doc_starts, db_all, w_out, q_b, kv_b, att, inv, raw, head_gain, cosine, sine
+    )
+    out_w_other = lax.ppermute(out_w_grad, "dp", swap_dp)
+    qkv_grad = t_mm(n1_all, d_qkv).astype(BF16).reshape(n, 2, half, 2 * LANES)
+    head_grad = head_grad + lax.ppermute(head_grad, "dp", swap_dp)
+    head_row = jnp.concatenate([head_grad, jnp.zeros_like(head_grad)], axis=1).astype(BF16)
+    head_row = jnp.concatenate([head_row, jnp.zeros_like(head_row)], axis=0)
+    qkv_other = lax.ppermute(
+        lax.dynamic_index_in_dim(qkv_grad, 1 - dp, 1, keepdims=False), "dp", swap_dp
+    )
+    qkv_mine = lax.dynamic_index_in_dim(qkv_grad, dp, 1, keepdims=False)
+    qkv_sum = (qkv_mine.astype(F32) + qkv_other.astype(F32)).astype(BF16)
+    d_n1_part = mm_t(d_qkv, w_qkv).astype(BF16)
+    gu_rows, d_n1_part, qkv_sum = lax.optimization_barrier((gu_rows, d_n1_part, qkv_sum))
+    qkv_out = jnp.concatenate(
+        [qkv_sum, jnp.broadcast_to(head_row[None], (n,) + head_row.shape)], axis=1
+    )
+    d_n1, gu_others, qkv_rows = scatter_tokens(
+        d_n1_part, [(WHOLE, gu_rows), (SPREAD, qkv_out)], n_ctx, n_wa, True, 6
+    )
+    out_w_other, d_n1 = lax.optimization_barrier((out_w_other, d_n1))
     _, n1_back = jax.vjp(rms_norm, x_own, attn_gain32)
     d_x_part, _ = n1_back(d_n1)
     input_grad = d_middle + d_x_part
 
-    def flat(part):
-        return part.transpose(1, 0, 2).reshape(d_rows, -1)
-
     gate_grad, up_grad, gu_sums = unpack_pair(gu_rows, gu_others, w_gate, w_up)
-    qkv_rows = both(qkv_rows)
-    q_grad = flat(qkv_rows[:, :d_rows, :LANES])
-    kv_grad = qkv_rows[:, :d_rows, LANES:].reshape(KV, 2, d_rows, HD)
-    k_grad, v_grad = flat(kv_grad[:, 0]), flat(kv_grad[:, 1])
-    head_sums = jnp.sum(qkv_rows[:, d_rows:].reshape(n, -1)[:, :LANES], axis=0)
+    qkv_others = lax.ppermute(qkv_rows, "dp", swap_dp)
+    q_grad, k_grad, v_grad, attn_sums, head_sums = unpack_attn(
+        qkv_rows, qkv_others, w_query, w_key, w_value
+    )
     me = lax.axis_index("ctx") * n_wa + lax.axis_index("wa")
-
-    def row_sum(weight, grad):
-        return jnp.sum(weight.astype(F32) * grad, axis=1)
-
-    attn_gain_grad = (
-        row_sum(w_query, q_grad) + row_sum(w_key, k_grad) + row_sum(w_value, v_grad)
-    ) / attn_gain.astype(F32)
-    ffn_gain_grad = gu_sums[:, 0] / ffn_gain.astype(F32)
+    q_gain_grad = head_sums[0, :HD] + head_sums[0, HD:LANES]
+    k_gain_grad = head_sums[1, :HD]
+    attn_gain_grad = attn_sums[:, 0] / attn_gain.astype(F32)
+    ffn_gain_grad = jnp.sum(gu_sums, axis=1) / ffn_gain.astype(F32)
     return (
         layer_out.astype(BF16)[None],
         input_grad.astype(BF16)[None],
@@ -1070,8 +1315,8 @@
         q_grad,
         k_grad,
         v_grad,
-        lax.dynamic_slice_in_dim(head_sums, me * per, per),
-        lax.dynamic_slice_in_dim(head_sums, HD + me * per, per),
+        lax.dynamic_slice_in_dim(q_gain_grad, me * per, per),
+        lax.dynamic_slice_in_dim(k_gain_grad, me * per, per),
         out_w_grad.astype(F32) + out_w_other.astype(F32),
         ffn_gain_grad,
         gate_grad,

time: 793 us -> 619 us (0.78)
  matrix products: 103 us -> 11.8 us
  Pallas kernels: 442 us -> 530 us
  waiting for transfers between devices: 75.9 us -> 16.1 us
  other arithmetic: 68.1 us -> 20.1 us
  local copies, waits for them, and re-layouts: 43 us -> 14 us
  starting transfers between devices: 38.1 us -> 12.4 us
    all_to_all x4 -> x2, waiting for transfers between devices: 66.4 us -> 0.01 us  [swap(): return lax.all_to_all(blocks, AXES, 0, 0, tiled=True)]
    pallas_call x2 -> x4, Pallas kernels: 21.8 us -> 60.6 us  [the longest x1 51.3 us: ffn(): pl.pallas_call(ffn_kernel, grid=(stream // bt,), in_specs=[rows, rows, wh...]
    dot_general x4 -> x0, matrix products: 33.1 us -> none  [mm(): return jnp.dot(a, b, preferred_element_type=F32)]
    dot_general x4 -> x1, matrix products: 35.9 us -> 6.08 us  [t_mm(): lax.dot_general(a, b, (((0,), (0,)), ((), ())), preferred_element_type=F32)]
    dot_general x4 -> x1, matrix products: 34 us -> 5.67 us  [mm_t(): lax.dot_general(a, b, (((1,), (1,)), ((), ())), preferred_element_type=F32)]
    all_to_all x4 -> x2, starting transfers between devices: 36.4 us -> 9.18 us  [swap(): return lax.all_to_all(blocks, AXES, 0, 0, tiled=True)]
    pallas_call x1, Pallas kernels: 10.6 us -> 31.7 us  [attend(): pl.pallas_call(attend_kernel, grid=(stream // bq,), in_specs=[pl.BlockSpe...]
    pallas_call x1, Pallas kernels: 16.6 us -> 35.8 us  [attend_back(): pl.pallas_call(attend_back_kernel, grid=(stream // bq,), in_specs=[pl.Blo...]
  transfers between devices with their start and end apart: 8 -> 8, of which waited for: 3 -> 2; matrix products, arithmetic and copies ran while one was open for 17% -> 5% of each run, Pallas kernels for 39% -> 57%
where the time goes in v4:
time: 619 us; the launch traced here: 618 us
  Pallas kernels  530 us (86%)
  other arithmetic  20.1 us (3%)
  waiting for transfers between devices  16.1 us (3%)
  between operations  14.6 us (2%)
  local copies, waits for them, and re-layouts  14 us (2%)
  starting transfers between devices  12.4 us (2%)
  matrix products  11.8 us (2%)
    pallas_call x3, Pallas kernels, scatter_tokens(): pl.pallas_call(partial(scatter_kernel, n_ctx, n_wa, by_position, kinds),...  206 us
    pallas_call x3, Pallas kernels, gather_tokens(): pl.pallas_call(partial(gather_kernel, n_ctx, n_wa, by_position, kinds), i...  193 us
    pallas_call x1, Pallas kernels, ffn(): pl.pallas_call(ffn_kernel, grid=(stream // bt,), in_specs=[rows, rows, wh...  51.3 us
    pallas_call x1, Pallas kernels, attend_back(): pl.pallas_call(attend_back_kernel, grid=(stream // bq,), in_specs=[pl.Blo...  35.8 us
    pallas_call x1, Pallas kernels, attend(): pl.pallas_call(attend_kernel, grid=(stream // bq,), in_specs=[pl.BlockSpe...  31.7 us
  transfers between devices with their start and end apart: 8, of which 2 were waited for; matrix products, arithmetic and copies ran while one was open for 5% of the time, Pallas kernels for 57%

profile of v4, /device:TPU:0, one launch (start us, length us, event | category | flops | bytes accessed | tf_op | source)
XLA Modules:
  0.0 618.5 jit_solution(12359909119096165712)
XLA Ops:
  7.2 0.0 all-gather.2.cloned.1.call-start
  7.2 0.8 fusion.15
  8.0 0.6 reshape.95.gains_ref
  8.6 2.4 shard_map.255.refs_0_
  11.0 72.1 %shard_map.256 = (bf16[2048,2048]{1,0:T(8,128)(2,1)}, bf16[16,144,256]{2,1,0:T(8,128)(2,1)}) custom-call(bf16[128,2048]{1,0:T(8,128)(2,1)} %bitcast.66, bf16[16,144,256]{2,1,0:T(8,128)(2,1)} %shard_map.255.refs_0_), custom_call_target="tpu_custom_call" | custom-call | flops 49999998976 | bytes 16777216 | tf_op jit(solution)/shard_map/pallas_call | solution.py:1030
  83.1 0.0 all-gather.2.cloned.1.call-update
  83.1 0.0 copy-start.6
  83.2 1.6 copy-done.6
  84.7 2.0 shard_map.259
  86.7 5.0 all-to-all-start
  91.7 0.0 reduce-scatter.2.cloned.1.call-start
  91.7 1.4 slice.32
  93.2 1.1 slice_convert_fusion
  94.3 0.2 copy.34
  94.4 0.1 fusion.21
  94.5 0.1 reshape.97
  94.6 0.1 reshape.98
  94.7 0.1 pad_maximum_fusion.1
  94.8 0.6 slice_bitcast_fusion.1
  95.4 31.7 %shard_map.257 = (bf16[2048,2048]{1,0:T(8,128)(2,1)}, f32[2048,256]{1,0:T(8,128)}, bf16[2048,128]{1,0:T(8,128)(2,1)S(1)}, bf16[2048,128]{1,0:T(8,128)(2,1)S(1)},...) custom-call(s32[1,8]{1,0:T(1,128)S(1)} %copy-done.19, ...), custom_call_target="tpu_custom_call" | custom-call | flops 20000000000 | bytes 33554432 | tf_op jit(solution)/shard_map/pallas_call | solution.py:462
  127.1 86.1 %shard_map.258 = f32[128,2048]{1,0:T(8,128)S(1)} custom-call(bf16[2048,2048]{1,0:T(8,128)(2,1)} %get-tuple-element.59.part_ref), custom_call_target="tpu_custom_call" | custom-call | flops 49999998976 | bytes 16777216 | tf_op jit(solution)/shard_map/pallas_call | solution.py:1172
  213.3 0.2 multiply_reduce_fusion.1
  213.5 1.0 multiply_convert_fusion.own_ref
  214.5 57.9 %shard_map.260 = (bf16[2048,2048]{1,0:T(8,128)(2,1)}, bf16[16,64,1024]{2,1,0:T(8,128)(2,1)}) custom-call(bf16[128,2048]{1,0:T(8,128)(2,1)} %multiply_convert_fusion.own_ref, bf16[16,64,1024]{2,1,0:T(8,128)(2,1)} %all-to-all-done.refs_0_.own_ref), custom_call_target="tpu_custom_call" | custom-call | flops 49999998976 | bytes 16777216 | tf_op jit(solution)/shard_map/pallas_call | solution.py:1030
  272.4 0.0 all-gather.2.cloned.1.call-done.dy_ref
  272.5 51.3 %shard_map.261 = (bf16[2048,2048]{1,0:T(8,128)(2,1)}, bf16[2048,2048]{1,0:T(8,128)(2,1)}, bf16[2048,1024]{1,0:T(8,128)(2,1)}, bf16[512,2048]{1,0:T(8,128)(2,1)}) custom-call(bf16[2048,2048]{1,0:T(8,128)(2,1)} %get-tuple-element.61.n2_ref, bf16[2048,2048]{1,0:T(8,128)(2,1)} %all-gather.2.cloned.1.call-done.dy_ref, ...), custom_call_target="tpu_custom_call" | custom-call | flops 38654705664 | bytes 33554432 | tf_op jit(solution)/shard_map/pallas_call | solution.py:666
  323.8 54.3 %shard_map.262 = (f32[128,2048]{1,0:T(8,128)S(1)}, bf16[16,64,1024]{2,1,0:T(8,128)(2,1)S(1)}) custom-call(bf16[2048,2048]{1,0:T(8,128)(2,1)} %get-tuple-element.65.part_ref, bf16[16,2,64,1024]{3,2,1,0:T(8,128)(2,1)} %bitcast.68), custom_call_target="tpu_custom_call" | custom-call | flops 49999998976 | bytes 16777216 | tf_op jit(solution)/shard_map/pallas_call | solution.py:1172
  378.2 0.8 fusion.4
  379.0 1.2 fusion.20.own_ref
  380.2 0.0 reduce-scatter.2.cloned.1.call-update
  380.3 63.2 %shard_map.263 = (bf16[2048,2048]{1,0:T(8,128)(2,1)}, bf16[512,2048]{1,0:T(8,128)(2,1)}) custom-call(bf16[128,2048]{1,0:T(8,128)(2,1)} %fusion.20.own_ref, bf16[512,2048]{1,0:T(8,128)(2,1)} %get-tuple-element.69.refs_0_), custom_call_target="tpu_custom_call" | custom-call | flops 49999998976 | bytes 16777216 | tf_op jit(solution)/shard_map/pallas_call | solution.py:1030
  443.5 3.9 fusion
  447.4 4.2 all-to-all-start.1
  451.7 0.0 copy-start.22
  451.7 1.2 copy-done.22
  452.9 1.2 copy-done.24
  454.2 1.1 copy-done.28
  455.2 1.0 copy-done.30
  456.3 35.8 %shard_map.264 = (bf16[2048,256]{1,0:T(8,128)(2,1)S(1)}, bf16[128,2048]{1,0:T(8,128)(2,1)}, f32[8,128]{1,0:T(8,128)S(1)}) custom-call(s32[1,8]{1,0:T(1,128)S(1)} %copy-done.20, bf16[2048,2048]{1,0:T(8,128)(2,1)} %get-tuple-element.71.db_ref, bf16[128,2048]{1,0:T(8,128)(2,1)S(1)} %copy-done.18, bf16[2048,128]{1,0:T(8,128)(2,1)S(1)} %copy-done.26, ...), custom_call_target="tpu_custom_call" | custom-call | flops 30000001024 | bytes 33554432 | tf_op jit(solution)/shard_map/pallas_call | solution.py:581
  492.1 6.1 convolution_convert_fusion.1
  498.2 0.1 dynamic-slice_bitcast_fusion
  498.3 2.1 collective-permute-start.1
  500.4 2.8 convert_add_fusion.1
  503.2 5.7 convolution_convert_fusion.part_ref
  508.9 0.0 collective-permute-start
  508.9 4.2 collective-permute-done.1
  513.1 0.2 fusion.6
  513.3 1.2 copy-done.8
  514.6 65.4 %shard_map.265 = (f32[128,2048]{1,0:T(8,128)S(1)}, bf16[16,64,1024]{2,1,0:T(8,128)(2,1)S(1)}, bf16[16,80,256]{2,1,0:T(8,128)(2,1)}) custom-call(bf16[2048,2048]{1,0:T(8,128)(2,1)} %convolution_convert_fusion.part_ref, bf16[16,64,1024]{2,1,0:T(8,128)(2,1)} %copy-done.8, bf16[16,80,256]{2,1,0:T(8,128)(2,1)S(1)} %pad_maximum_fusion.refs_1_), custom_call_target="tpu_custom_call" | custom-call | flops 49999998976 | bytes 16777216 | tf_op jit(solution)/shard_map/pallas_call | solution.py:1172
  580.0 1.6 copy-done.9
  581.6 4.3 shard_map.267
  585.9 1.0 collective-permute-start.3
  586.9 0.1 reduce_sum.57
  587.1 1.3 fusion.5
  588.4 0.5 convert_divide_fusion
  588.9 2.3 convert_add_fusion.4
  591.2 11.8 %collective-permute-done.3.other_ref = bf16[16,80,256]{2,1,0:T(8,128)(2,1)} collective-permute-done((bf16[16,80,256]{2,1,0:T(8,128)(2,1)}, bf16[16,80,256]{2,1,0:T(8,128)(2,1)}, u32[]{:S(2)}, u32[]{:S(2)}) %collective-permute-start.3) | collective-permute-done | bytes 655392 | tf_op jit(solution)/shard_map/ppermute | solution.py:1302
  603.0 1.0 copy-done.12
  604.1 3.1 shard_map.266
  607.1 0.1 fusion.22
  607.2 0.6 fusion.16
  607.8 0.1 slice_reduce_fusion
  607.9 0.5 convert_divide_fusion.1
  608.5 3.2 fusion.8
  (95 shorter events, 0.3 us)
Async XLA Ops:
  7.2 265.3 %all-gather.2.cloned.1.call-start = ((), (), s32[]{:S(2)}) async-start(), calls=%async_computation.3 | async-start | bytes 8912896 | tf_op jit(solution)/shard_map/all_gather | solution.py:1247
  11.0 72.1 %copy-start.4 = (bf16[128,8192]{1,0:T(8,128)(2,1)S(1)}, bf16[128,8192]{1,0:T(8,128)(2,1)}, u32[]{:S(2)}) copy-start(bf16[128,8192]{1,0:T(8,128)(2,1)} %gate_w.1) | copy-start | bytes 6291460
  83.1 1.6 copy-start.6
  86.7 8.7 %copy-start.17 = (bf16[128,2048]{1,0:T(8,128)(2,1)S(1)}, bf16[128,2048]{1,0:T(8,128)(2,1)}, u32[]{:S(2)}) copy-start(bf16[128,2048]{1,0:T(8,128)(2,1)} %w_out_ref.3) | copy-start | bytes 1572868
  86.7 8.7 %copy-start.19 = (s32[1,8]{1,0:T(1,128)S(1)}, s32[1,8]{1,0:T(1,128)}, u32[]{:S(2)}) copy-start(s32[1,8]{1,0:T(1,128)} %starts.3) | copy-start | bytes 100
  86.7 8.7 %copy-start.21 = (f32[2048,128]{1,0:T(8,128)S(1)}, f32[2048,128]{1,0:T(8,128)}, u32[]{:S(2)}) copy-start(f32[2048,128]{1,0:T(8,128)} %constant.57.clone.cos_ref) | copy-start | bytes 3145732
  86.7 127.8 %all-to-all-start = ((bf16[16,64,1024]{2,1,0:T(8,128)(2,1)}), bf16[16,64,1024]{2,1,0:T(8,128)(2,1)}, u32[]{:S(2)}, u32[]{:S(2)}) async-start(bf16[16,64,1024]{2,1,0:T(8,128)(2,1)} %shard_map.259), calls=%async_computation | async-start | bytes 4194304 | tf_op jit(solution)/shard_map/all_to_all | solution.py:1229
  91.7 516.7 %reduce-scatter.2.cloned.1.call-start = ((), (), s32[]{:S(2)}) async-start(), calls=%async_computation.4 | async-start | bytes 8912896 | tf_op jit(solution)/shard_map/reduce_scatter | solution.py:1262
  93.2 33.9 %copy-start.10 = (bf16[16,128,256]{2,1,0:T(8,128)(2,1)}, bf16[16,128,256]{2,1,0:T(8,128)(2,1)S(1)}, u32[]{:S(2)}) copy-start(bf16[16,128,256]{2,1,0:T(8,128)(2,1)S(1)} %slice.32) | copy-start | bytes 3145732
  94.8 32.3 %copy-start.15 = (f32[256]{0:T(256)}, f32[256]{0:T(256)S(1)}, u32[]{:S(2)}) copy-start(f32[256]{0:T(256)S(1)} %pad_maximum_fusion.1) | copy-start | bytes 3076
  95.4 283.6 %copy-start.36 = (f32[2048]{0:T(1024)}, f32[2048]{0:T(1024)S(1)}, u32[]{:S(2)}) copy-start(f32[2048]{0:T(1024)S(1)} %get-tuple-element.104) | copy-start | bytes 24580
  127.1 86.2 %copy-start.23 = (f32[2048,128]{1,0:T(8,128)}, f32[2048,128]{1,0:T(8,128)S(1)}, u32[]{:S(2)}) copy-start(f32[2048,128]{1,0:T(8,128)S(1)} %get-tuple-element.75.inv_ref) | copy-start | bytes 3145732
  127.1 86.2 %copy-start.25 = (bf16[2048,128]{1,0:T(8,128)(2,1)}, bf16[2048,128]{1,0:T(8,128)(2,1)S(1)}, u32[]{:S(2)}) copy-start(bf16[2048,128]{1,0:T(8,128)(2,1)S(1)} %get-tuple-element.72.q_ref) | copy-start | bytes 1572868
  127.1 86.2 %copy-start.27 = (bf16[2048,128]{1,0:T(8,128)(2,1)}, bf16[2048,128]{1,0:T(8,128)(2,1)S(1)}, u32[]{:S(2)}) copy-start(bf16[2048,128]{1,0:T(8,128)(2,1)S(1)} %get-tuple-element.73.kv_ref) | copy-start | bytes 1572868
  127.1 86.2 %copy-start.29 = (bf16[2048,128]{1,0:T(8,128)(2,1)}, bf16[2048,128]{1,0:T(8,128)(2,1)S(1)}, u32[]{:S(2)}) copy-start(bf16[2048,128]{1,0:T(8,128)(2,1)S(1)} %get-tuple-element.74.att_ref) | copy-start | bytes 1572868
  127.1 86.2 %copy-start.31 = (bf16[1,128,2048]{2,1,0:T(8,128)(2,1)S(1)}, bf16[1,128,2048]{2,1,0:T(8,128)(2,1)}, u32[]{:S(2)}) copy-start(bf16[1,128,2048]{2,1,0:T(8,128)(2,1)} %param.16) | copy-start | bytes 1572868
  213.3 165.7 %copy-start = (f32[128,2048]{1,0:T(8,128)}, f32[128,2048]{1,0:T(8,128)S(1)}, u32[]{:S(2)}) copy-start(f32[128,2048]{1,0:T(8,128)S(1)} %shard_map.258) | copy-start | bytes 3145732
  213.5 165.5 %copy-start.39 = (f32[128]{0:T(128)}, f32[128]{0:T(128)S(1)}, u32[]{:S(2)}) copy-start(f32[128]{0:T(128)S(1)} %fusion.18) | copy-start | bytes 1540
  323.8 54.4 %copy-start.32 = (bf16[1,128,2048]{2,1,0:T(8,128)(2,1)S(1)}, bf16[1,128,2048]{2,1,0:T(8,128)(2,1)}, u32[]{:S(2)}) copy-start(bf16[1,128,2048]{2,1,0:T(8,128)(2,1)} %param.16) | copy-start | bytes 1572868
  323.8 55.2 %copy-start.33 = (bf16[1,128,2048]{2,1,0:T(8,128)(2,1)S(1)}, bf16[1,128,2048]{2,1,0:T(8,128)(2,1)}, u32[]{:S(2)}) copy-start(bf16[1,128,2048]{2,1,0:T(8,128)(2,1)} %param.18) | copy-start | bytes 1572868
  378.1 2.1 copy-start.2
  379.0 1.2 copy-start.42
  443.5 8.2 %copy-start.16 = (f32[256]{0:T(256)S(1)}, f32[256]{0:T(256)}, u32[]{:S(2)}) copy-start(f32[256]{0:T(256)} %copy-done.15) | copy-start | bytes 3076
  443.5 8.2 %copy-start.20 = (s32[1,8]{1,0:T(1,128)S(1)}, s32[1,8]{1,0:T(1,128)}, u32[]{:S(2)}) copy-start(s32[1,8]{1,0:T(1,128)} %starts.3) | copy-start | bytes 100
  447.4 4.3 copy-start.18
  447.4 4.3 copy-start.26
  447.4 65.8 %all-to-all-start.1 = ((bf16[16,64,1024]{2,1,0:T(8,128)(2,1)}), bf16[16,64,1024]{2,1,0:T(8,128)(2,1)S(1)}, u32[]{:S(2)}, u32[]{:S(2)}) async-start(bf16[16,64,1024]{2,1,0:T(8,128)(2,1)} %fusion), calls=%async_computation.2 | async-start | bytes 4194304 | tf_op jit(solution)/shard_map/all_to_all | solution.py:1229
  451.7 1.2 copy-start.22
  452.9 1.2 copy-start.24
  454.2 1.1 copy-start.28
  455.2 1.0 copy-start.30
  492.1 16.8 %collective-permute-start.2 = (f32[8,128]{1,0:T(8,128)S(1)}, f32[8,128]{1,0:T(8,128)S(1)}, u32[]{:S(2)}, u32[]{:S(2)}) collective-permute-start(f32[8,128]{1,0:T(8,128)S(1)} %get-tuple-element.84), channel_id=1, source_target_pairs={{0,16},{16,0},{1,17},{17,1},{2,18},{18,2},{3,19},{19,3},{4,20},{20... | collective-permute-start | bytes 12296 | tf_op jit(solution)/shard_map/ppermute | solution.py:1280
  492.1 8.2 %copy-start.34 = (bf16[512,2048]{1,0:T(8,128)(2,1)S(1)}, bf16[512,2048]{1,0:T(8,128)(2,1)}, u32[]{:S(2)}) copy-start(bf16[512,2048]{1,0:T(8,128)(2,1)} %get-tuple-element.69.refs_0_) | copy-start | bytes 6291460
  492.1 8.2 %copy-start.35 = (bf16[512,2048]{1,0:T(8,128)(2,1)S(1)}, bf16[512,2048]{1,0:T(8,128)(2,1)}, u32[]{:S(2)}) copy-start(bf16[512,2048]{1,0:T(8,128)(2,1)} %get-tuple-element.98) | copy-start | bytes 6291460
  498.3 14.8 %collective-permute-start.1 = (bf16[16,64,256]{2,1,0:T(8,128)(2,1)S(1)}, bf16[16,64,256]{2,1,0:T(8,128)(2,1)S(1)}, u32[]{:S(2)}, u32[]{:S(2)}) collective-permute-start(bf16[16,64,256]{2,1,0:T(8,128)(2,1)S(1)} %dynamic-slice_bitcast_fusion), channel_id=1, source_target_pairs={{0,16},{16,0},{1,17},{17,1},{2,18},{18,2},{3,19},{19,3},{4,20},{20... | collective-permute-start | bytes 1572872 | tf_op jit(solution)/shard_map/ppermute | solution.py:1283
  500.4 2.8 copy-start.11
  508.9 77.1 %collective-permute-start = (bf16[128,2048]{1,0:T(8,128)(2,1)}, bf16[128,2048]{1,0:T(8,128)(2,1)}, u32[]{:S(2)}, u32[]{:S(2)}) collective-permute-start(bf16[128,2048]{1,0:T(8,128)(2,1)} %get-tuple-element.77), channel_id=1, source_target_pairs={{0,16},{16,0},{1,17},{17,1},{2,18},{18,2},{3,19},{19,3},{4,20},{20... | collective-permute-start | bytes 1572872 | tf_op jit(solution)/shard_map/ppermute | solution.py:1278
  513.3 1.3 copy-start.8
  514.6 65.4 %copy-start.5 = (bf16[128,8192]{1,0:T(8,128)(2,1)S(1)}, bf16[128,8192]{1,0:T(8,128)(2,1)}, u32[]{:S(2)}) copy-start(bf16[128,8192]{1,0:T(8,128)(2,1)} %gate_w.1) | copy-start | bytes 6291460
  514.6 65.4 %copy-start.7 = (bf16[128,8192]{1,0:T(8,128)(2,1)S(1)}, bf16[128,8192]{1,0:T(8,128)(2,1)}, u32[]{:S(2)}) copy-start(bf16[128,8192]{1,0:T(8,128)(2,1)} %up_w.1) | copy-start | bytes 6291460
  580.0 1.6 copy-start.9
  581.6 5.5 copy-start.38
  581.6 6.8 %copy-start.41 = (f32[128]{0:T(128)S(1)}, f32[128]{0:T(128)}, u32[]{:S(2)}) copy-start(f32[128]{0:T(128)} %get-tuple-element.99) | copy-start | bytes 1540
  581.6 6.8 %copy-start.44 = (bf16[128]{0:T(256)(128)(2,1)S(1)}, bf16[128]{0:T(256)(128)(2,1)}, u32[]{:S(2)}) copy-start(bf16[128]{0:T(256)(128)(2,1)} %param.26) | copy-start | bytes 772
  581.6 21.4 %copy-start.13 = (bf16[128,512]{1,0:T(8,128)(2,1)S(1)}, bf16[128,512]{1,0:T(8,128)(2,1)}, u32[]{:S(2)}) copy-start(bf16[128,512]{1,0:T(8,128)(2,1)} %wk_ref.1) | copy-start | bytes 393220
  581.6 21.4 %copy-start.14 = (bf16[128,512]{1,0:T(8,128)(2,1)S(1)}, bf16[128,512]{1,0:T(8,128)(2,1)}, u32[]{:S(2)}) copy-start(bf16[128,512]{1,0:T(8,128)(2,1)} %wv_ref.1) | copy-start | bytes 393220
  585.9 22.0 %copy-start.45 = (bf16[128]{0:T(256)(128)(2,1)S(1)}, bf16[128]{0:T(256)(128)(2,1)}, u32[]{:S(2)}) copy-start(bf16[128]{0:T(256)(128)(2,1)} %param.19) | copy-start | bytes 772
  585.9 22.5 %copy-start.1 = (f32[128,2048]{1,0:T(8,128)S(1)}, f32[128,2048]{1,0:T(8,128)}, u32[]{:S(2)}) copy-start(f32[128,2048]{1,0:T(8,128)} %copy-done) | copy-start | bytes 3145732
  585.9 22.5 %copy-start.3 = (f32[128,2048]{1,0:T(8,128)S(1)}, f32[128,2048]{1,0:T(8,128)}, u32[]{:S(2)}) copy-start(f32[128,2048]{1,0:T(8,128)} %copy-done.2) | copy-start | bytes 3145732
  585.9 22.5 %copy-start.37 = (f32[2048]{0:T(1024)S(1)}, f32[2048]{0:T(1024)}, u32[]{:S(2)}) copy-start(f32[2048]{0:T(1024)} %copy-done.36) | copy-start | bytes 24580
  585.9 22.5 %copy-start.40 = (f32[128]{0:T(128)S(1)}, f32[128]{0:T(128)}, u32[]{:S(2)}) copy-start(f32[128]{0:T(128)} %copy-done.39) | copy-start | bytes 1540
  585.9 22.5 %copy-start.43 = (f32[128]{0:T(128)S(1)}, f32[128]{0:T(128)}, u32[]{:S(2)}) copy-start(f32[128]{0:T(128)} %copy-done.42) | copy-start | bytes 1540
  585.9 17.1 %collective-permute-start.3 = (bf16[16,80,256]{2,1,0:T(8,128)(2,1)}, bf16[16,80,256]{2,1,0:T(8,128)(2,1)}, u32[]{:S(2)}, u32[]{:S(2)}) collective-permute-start(bf16[16,80,256]{2,1,0:T(8,128)(2,1)} %get-tuple-element.87.own_ref), channel_id=1, source_target_pairs={{0,16},{16,0},{1,17},{17,1},{2,18},{18,2},{3,19},{19,3},{4,20},{20... | collective-permute-start | bytes 1966088 | tf_op jit(solution)/shard_map/ppermute | solution.py:1302
  603.0 1.0 copy-start.12
Sparse Core Ops, SparseCore 0:
  83.2 131.9 all-gather.1
  380.4 132.5 reduce-scatter.1

commit v5 on v4

--- a/solution.py
+++ b/solution.py
@@ -330,6 +330,7 @@
 LANES = 2 * HD
 ROWS_BLOCK = 256
 FFN_BLOCK = 256
+ROOM = 60 * 2**20
 LOG2E = 1.4426950408889634
 F32 = jnp.float32
 BF16 = jnp.bfloat16
@@ -408,11 +409,28 @@
     return lax.dot_general(a, b, (((0,), (0,)), ((), ())), preferred_element_type=F32)
 
 
+def join_halves(half, own_ref, other_ref, whole_ref):
+    own_row = jnp.where(lax.axis_index("dp") == 0, 0, half)
+
+    def put(j, carry):
+        for begin, ref in ((own_row, own_ref), (half - own_row, other_ref)):
+            at = pl.multiple_of(2 * half * j + begin, half)
+            whole_ref[pl.ds(at, half), :] = ref[j, :half, :]
+        return carry
+
+    lax.fori_loop(0, own_ref.shape[0], put, 0)
+
+
 def attend_kernel(
-    starts, x_ref, gain_ref, w_ref, head_gain_ref, cos_ref, sin_ref, w_out_ref,
-    normed_ref, raw_ref, q_ref, kv_ref, att_ref, inv_ref, part_ref, ov_ref,
+    starts, x_ref, gain_ref, own_ref, other_ref, head_gain_ref, cos_ref, sin_ref,
+    normed_ref, raw_ref, q_ref, kv_ref, att_ref, inv_ref, w_ref, ov_ref,
 ):
     block = pl.program_id(0)
+
+    @pl.when(block == 0)
+    def _():
+        join_halves(w_ref.shape[0] // own_ref.shape[0] // 2, own_ref, other_ref, w_ref)
+
     bq = x_ref.shape[0]
     q_begin = pl.multiple_of(block * bq, bq)
     x = x_ref[...].astype(F32)
@@ -446,10 +464,9 @@
     att = jnp.where(is_key, pltpu.roll(out[:bq], HD, 1), out[bq:]).astype(BF16)
     att_ref[...] = att
     inv_ref[...] = jnp.where(is_key, inv[:bq], inv[bq:])
-    part_ref[...] = dot(att, w_out_ref[...]).astype(BF16)
-
-
-def attend(starts, x_all, gain, w_qkv, head_gain, cosine, sine, w_out):
+
+
+def attend(starts, x_all, gain, own, other, head_gain, cosine, sine):
     stream, width = x_all.shape
     bq = ROWS_BLOCK
 
@@ -457,7 +474,7 @@
         return pl.BlockSpec((bq, cols), lambda i: (i, 0))
 
     def whole(shape):
-        return pl.BlockSpec(shape, lambda i: (0, 0), pipeline_mode=pl.Buffered(1))
+        return pl.BlockSpec(shape, lambda i: (0,) * len(shape), pipeline_mode=pl.Buffered(1))
 
     return pl.pallas_call(
         attend_kernel,
@@ -466,11 +483,11 @@
             pl.BlockSpec(memory_space=pltpu.SMEM),
             rows(width),
             whole((1, width)),
-            whole(w_qkv.shape),
+            whole(own.shape),
+            whole(own.shape),
             whole((1, 2 * LANES)),
             rows(LANES),
             rows(LANES),
-            whole(w_out.shape),
         ],
         out_specs=[
             rows(width),
@@ -479,7 +496,7 @@
             pl.BlockSpec((stream, LANES), lambda i: (0, 0)),
             rows(LANES),
             rows(LANES),
-            rows(width),
+            whole((width, 2 * LANES)),
         ],
         out_shape=[
             jax.ShapeDtypeStruct((stream, width), BF16),
@@ -488,12 +505,12 @@
             jax.ShapeDtypeStruct((stream, LANES), BF16),
             jax.ShapeDtypeStruct((stream, LANES), BF16),
             jax.ShapeDtypeStruct((stream, LANES), F32),
-            jax.ShapeDtypeStruct((stream, width), BF16),
+            jax.ShapeDtypeStruct((width, 2 * LANES), BF16),
         ],
         scratch_shapes=[pltpu.VMEM((stream, LANES), BF16)],
-        compiler_params=pltpu.CompilerParams(vmem_limit_bytes=48 * 2**20),
+        compiler_params=pltpu.CompilerParams(vmem_limit_bytes=ROOM),
         cost_estimate=pl.CostEstimate(flops=2 * 10**10, bytes_accessed=2**25, transcendentals=0),
-    )(starts, x_all, gain, w_qkv, head_gain, cosine, sine, w_out)
+    )(starts, x_all, gain, own, other, head_gain, cosine, sine)
 
 
 def attend_back_kernel(
@@ -601,7 +618,7 @@
             jax.ShapeDtypeStruct((8, LANES), F32),
         ],
         scratch_shapes=[pltpu.VMEM((stream, LANES), F32), pltpu.VMEM(w_out.shape, F32)],
-        compiler_params=pltpu.CompilerParams(vmem_limit_bytes=48 * 2**20),
+        compiler_params=pltpu.CompilerParams(vmem_limit_bytes=ROOM),
         cost_estimate=pl.CostEstimate(flops=3 * 10**10, bytes_accessed=2**25, transcendentals=0),
     )(starts, db_all, w_out, q, kv, att, inv, raw, head_gain, cosine, sine)
 
@@ -611,20 +628,10 @@
     down_ref, d_n2_ref, gu_grad_ref, down_grad_ref, gu_acc, down_acc, w_gu_ref,
 ):
     block = pl.program_id(0)
-    first = lax.axis_index("dp") == 0
 
     @pl.when(block == 0)
     def _():
-        half = own_ref.shape[1]
-        own_row = jnp.where(first, 0, half)
-
-        def put(j, carry):
-            for begin, ref in ((own_row, own_ref), (half - own_row, other_ref)):
-                at = pl.multiple_of(2 * half * j + begin, half)
-                w_gu_ref[pl.ds(at, half), :] = ref[j]
-            return carry
-
-        lax.fori_loop(0, own_ref.shape[0], put, 0)
+        join_halves(own_ref.shape[1], own_ref, other_ref, w_gu_ref)
         gu_acc[...] = jnp.zeros_like(gu_acc)
         down_acc[...] = jnp.zeros_like(down_acc)
 
@@ -679,7 +686,7 @@
             pltpu.VMEM(w_down.shape, F32),
             pltpu.VMEM(gu_shape, BF16),
         ],
-        compiler_params=pltpu.CompilerParams(vmem_limit_bytes=58 * 2**20),
+        compiler_params=pltpu.CompilerParams(vmem_limit_bytes=ROOM),
         cost_estimate=pl.CostEstimate(
             flops=18 * stream * width * w_down.shape[0], bytes_accessed=2**25, transcendentals=0
         ),
@@ -697,12 +704,12 @@
     gains_ref[...] = jnp.sum(own_ref[:, half : half + 8, :].astype(F32), axis=0)
     for begin, ref in ((low, own_ref), (high, other_ref)):
         rows = pl.ds(pl.multiple_of(begin, half), half)
-        total = jnp.zeros((half, 1), F32)
+        total = jnp.zeros((half, LANES), F32)
         for j in range(n):
             cols = slice(j * LANES, (j + 1) * LANES)
             q = ref[j, :half, :LANES].astype(F32)
             q_ref[rows, cols] = q
-            total += jnp.sum(q * wq_ref[rows, cols].astype(F32), axis=1, keepdims=True)
+            total += q * wq_ref[rows, cols].astype(F32)
         for pair in range(KV // 2):
             cols = slice(pair * LANES, (pair + 1) * LANES)
             heads = []
@@ -715,9 +722,8 @@
             v = jnp.concatenate([heads[0][:, HD:], heads[1][:, HD:]], axis=1)
             k_ref[rows, cols] = k
             v_ref[rows, cols] = v
-            both = k * wk_ref[rows, cols].astype(F32) + v * wv_ref[rows, cols].astype(F32)
-            total += jnp.sum(both, axis=1, keepdims=True)
-        sum_ref[rows, :] = jnp.broadcast_to(total, (half, LANES))
+            total += k * wk_ref[rows, cols].astype(F32) + v * wv_ref[rows, cols].astype(F32)
+        sum_ref[rows, :] = total
 
 
 def unpack_attn(own, other, w_query, w_key, w_value):
@@ -736,23 +742,25 @@
 
 
 def pack_attn_kernel(query_ref, key_ref, value_ref, gains_ref, out_ref):
-    n, rows, _ = out_ref.shape
-    d_rows = query_ref.shape[0]
+    n = out_ref.shape[0]
+    half = query_ref.shape[0] // 2
     share = n // KV
+    rows = pl.ds(pl.multiple_of(lax.axis_index("dp") * half, half), half)
+    keys, values = key_ref[rows, :], value_ref[rows, :]
     for j in range(n):
         head = j // share * HD
-        out_ref[j, :d_rows, :LANES] = query_ref[:, j * LANES : (j + 1) * LANES]
-        out_ref[j, :d_rows, LANES:] = jnp.concatenate(
-            [key_ref[:, head : head + HD], value_ref[:, head : head + HD]], axis=1
-        )
-        out_ref[j, d_rows:, :] = gains_ref[...]
+        out_ref[j, :half, :LANES] = query_ref[rows, j * LANES : (j + 1) * LANES]
+        out_ref[j, :half, LANES:] = jnp.concatenate(
+            [keys[:, head : head + HD], values[:, head : head + HD]], axis=1
+        )
+        out_ref[j, half:, :] = gains_ref[...]
 
 
 def pack_attn(w_query, w_key, w_value, gains, n):
-    d_rows = w_query.shape[0]
+    half = w_query.shape[0] // 2
     return pl.pallas_call(
         pack_attn_kernel,
-        out_shape=jax.ShapeDtypeStruct((n, d_rows + gains.shape[0], 2 * LANES), BF16),
+        out_shape=jax.ShapeDtypeStruct((n, half + gains.shape[0], 2 * LANES), BF16),
     )(w_query, w_key, w_value, gains)
 
 
@@ -777,7 +785,7 @@
             out_specs=pl.BlockSpec((count, half, 2 * cols), lambda j, dp: (j, 0, 0)),
         ),
         out_shape=jax.ShapeDtypeStruct((n, half, 2 * cols), BF16),
-        compiler_params=pltpu.CompilerParams(vmem_limit_bytes=32 * 2**20),
+        compiler_params=pltpu.CompilerParams(vmem_limit_bytes=ROOM),
     )(lax.axis_index("dp").reshape(1), w_gate, w_up)
 
 
@@ -857,6 +865,10 @@
 WHOLE, PICK, SPREAD = 0, 1, 2
 
 
+def pair_outs(kind):
+    return 2 if kind == SPREAD else 1
+
+
 def pair_shape(kind, src):
     if kind == PICK:
         return (src.shape[0],) + src.shape[2:]
@@ -898,13 +910,10 @@
 
 def start_pairs(kinds, srcs, dsts, n_wa, sems, spread_sems):
     dp = lax.axis_index("dp")
-    waits = []
-    for at, (kind, src, dst) in enumerate(zip(kinds, srcs, dsts)):
-        if kind == SPREAD:
-            waits.append(start_spread(src, dst, n_wa, spread_sems))
-            continue
-        if kind == PICK:
-            src = src.at[:, dp ^ 1]
+    dsts = list(dsts)
+    midway = []
+
+    def exchange(at, src, dst):
         send = pltpu.make_async_remote_copy(
             src_ref=src,
             dst_ref=dst,
@@ -914,8 +923,24 @@
             device_id_type=MESH_ID,
         )
         send.start()
-        waits.append(send.wait)
-    return waits
+        return send.wait
+
+    for at, (kind, src) in enumerate(zip(kinds, srcs)):
+        dst = dsts.pop(0)
+        if kind == SPREAD:
+            finish, other = start_spread(src, dst, n_wa, spread_sems), dsts.pop(0)
+
+            def pass_on(at=at, finish=finish, dst=dst, other=other):
+                finish()
+                return exchange(at, dst, other)
+
+            midway.append(pass_on)
+            continue
+        if kind == PICK:
+            src = src.at[:, dp ^ 1]
+        wait = exchange(at, src, dst)
+        midway.append(lambda wait=wait: wait)
+    return midway
 
 
 def piece_row(zc, wac, h, half, n_ctx, n_wa, by_position):
@@ -927,8 +952,9 @@
 
 def gather_kernel(n_ctx, n_wa, by_position, kinds, own_ref, *refs):
     pairs = len(kinds)
-    srcs, out_ref, dsts = refs[:pairs], refs[pairs], refs[pairs + 1 : 2 * pairs + 1]
-    own_sem, send_sem, recv_sem, pair_sem, spread_sem = refs[2 * pairs + 1 :]
+    outs = sum(pair_outs(kind) for kind in kinds)
+    srcs, out_ref, dsts = refs[:pairs], refs[pairs], refs[pairs + 1 : pairs + outs + 1]
+    own_sem, send_sem, recv_sem, pair_sem, spread_sem = refs[pairs + outs + 1 :]
     ctx = lax.axis_index("ctx")
     wa = lax.axis_index("wa")
     half = own_ref.shape[0] // 2
@@ -1003,6 +1029,8 @@
                 send(cond, piece, zc, wa, h, {"wa": wa ^ 2})
                 send(cond, piece, zc, wa, h, {"wa": wa ^ 1})
             across(k - 1, h)
+        if k == 1:
+            pair_waits = [wait() for wait in pair_waits]
     for h in range(2):
         across(n_ctx - 1, h)
     for zc in range(n_ctx):
@@ -1026,11 +1054,15 @@
     kinds = tuple(kind for kind, _ in pairs)
     anywhere = pl.BlockSpec(memory_space=pl.ANY)
     shapes = [jax.ShapeDtypeStruct((rows * n, width), own.dtype)]
-    shapes += [jax.ShapeDtypeStruct(pair_shape(*pair), BF16) for pair in pairs]
+    shapes += [
+        jax.ShapeDtypeStruct(pair_shape(*pair), BF16)
+        for pair in pairs
+        for _ in range(pair_outs(pair[0]))
+    ]
     return pl.pallas_call(
         partial(gather_kernel, n_ctx, n_wa, by_position, kinds),
         in_specs=[anywhere] * (1 + len(pairs)),
-        out_specs=[anywhere] * (1 + len(pairs)),
+        out_specs=[anywhere] * len(shapes),
         out_shape=shapes,
         scratch_shapes=[
             pltpu.SemaphoreType.DMA((2,)),
@@ -1044,10 +1076,15 @@
     )(own, *[array for _, array in pairs])
 
 
-def scatter_kernel(n_ctx, n_wa, by_position, kinds, part_ref, *refs):
+def scatter_kernel(n_ctx, n_wa, by_position, product, turned, kinds, *refs):
+    left_ref, right_ref = refs[0], refs[1]
+    refs = refs[2:] if product else refs[1:]
     pairs = len(kinds)
-    srcs, out_ref, dsts = refs[:pairs], refs[pairs], refs[pairs + 1 : 2 * pairs + 1]
-    s1, s2, s3, send_sem, recv1, recv2, recv3, pair_sem, spread_sem = refs[2 * pairs + 1 :]
+    outs = sum(pair_outs(kind) for kind in kinds)
+    srcs, out_ref, dsts = refs[:pairs], refs[pairs], refs[pairs + 1 : pairs + outs + 1]
+    refs = refs[pairs + outs + 1 :]
+    part_ref = refs[0] if product else left_ref
+    s1, s2, s3, send_sem, recv1, recv2, recv3, pair_sem, spread_sem = refs[1 if product else 0 :]
     ctx = lax.axis_index("ctx")
     wa = lax.axis_index("wa")
     half = out_ref.shape[0] // 2
@@ -1067,7 +1104,7 @@
     def mine(zc, wac, h):
         return part_ref.at[pl.ds(piece_row(zc, wac, h, half, n_ctx, n_wa, by_position), half)]
 
-    def copy(src, dst, sem, where):
+    def send(src, dst, sem, where):
         made = pltpu.make_async_remote_copy(
             src_ref=src,
             dst_ref=dst,
@@ -1076,12 +1113,8 @@
             device_id=where,
             device_id_type=MESH_ID,
         )
-        return made
-
-    def send(cond, src, dst, sem, where):
-        made = copy(src, dst, sem, where)
-        begin(cond, made.start)
-        sends.append((cond, made))
+        made.start()
+        sends.append(made)
 
     def arrived(cond, dst, sem):
         made = pltpu.make_async_remote_copy(
@@ -1111,74 +1144,109 @@
     def index1(zc, yc, h):
         return (zc * 2 + yc) * 2 + h
 
-    def steps():
-        for k in range(n_ctx - 1, -1, -1):
-            for way in (-1, 1) if k else (1,):
-                for h in range(2):
-                    zc = ctx + way * k
-                    yield k, way, h, zc, (inside(zc) if k else None)
-
-    for other in (1, 0):
-        yc = y ^ 1 if other else y
-        for k, way, h, zc, cond in steps():
-            at = index1(zc, yc, h)
-            send(cond, mine(zc, yc * 2 + ((wa & 1) ^ 1), h), s1.at[at], recv1.at[at], sibling)
-    for k, way, h, zc, cond in steps():
-        at = index1(zc, y ^ 1, h)
-        arrived(cond, s1.at[at], recv1.at[at])
-        begin(cond, lambda: add_up(s1.at[at], 0, [s1.at[at], mine(zc, wa ^ 2, h)]))
-        send(cond, s1.at[at], s2.at[zc * 2 + h], recv2.at[zc * 2 + h], across)
-    for k, way, h, zc, cond in steps():
-        at = index1(zc, y, h)
-        arrived(cond, s1.at[at], recv1.at[at])
-        arrived(cond, s2.at[zc * 2 + h], recv2.at[zc * 2 + h])
-        base = [mine(zc, wa, h), s1.at[at], s2.at[zc * 2 + h]]
-        here = zc * 2 + h
-        low, high = here, (n_ctx + zc) * 2 + h
-        if k:
-            behind = low if way > 0 else high
-            more = cond & inside(ctx - way)
-            arrived(more, s3.at[behind], recv3.at[behind])
-            begin(more, lambda: add_up(s2.at[here], 0, base + [s3.at[behind]]))
-            first = cond & jnp.logical_not(inside(ctx - way))
-            begin(first, lambda: add_up(s2.at[here], 0, base))
-            send(cond, s2.at[here], s3.at[behind], recv3.at[behind], {"ctx": ctx + way})
-        else:
-            under, over = ctx > 0, ctx < n_ctx - 1
-            arrived(under, s3.at[low], recv3.at[low])
-            arrived(over, s3.at[high], recv3.at[high])
-            ways = [
-                (under & over, [s3.at[low], s3.at[high]]),
-                (under & jnp.logical_not(over), [s3.at[low]]),
-                (over & jnp.logical_not(under), [s3.at[high]]),
-            ]
-            for take, extra in ways:
-                begin(take, lambda extra=extra: add_up(out_ref, h * half, base + extra))
-    for cond, made in sends:
-        begin(cond, made.wait_send)
+    def target(i):
+        mirrored = 2 * ctx >= n_ctx
+        near = jnp.where(mirrored, n_ctx - 1 - ctx, ctx)
+        later = i - (n_ctx - 1 - 2 * near)
+        step = jnp.maximum(later, 0) // 2
+        paired = jnp.where(lax.rem(jnp.maximum(later, 0), 2) == 0, 2 * near - step, step)
+        zc = jnp.where(later < 0, n_ctx - 1 - i, paired)
+        return jnp.where(mirrored, n_ctx - 1 - zc, zc)
+
+    def multiply(zc):
+        count = n_wa * half
+
+        def step(h, carry):
+            if by_position:
+                begin_row = jnp.where(h == 0, zc, 2 * n_ctx - 1 - zc) * count
+            else:
+                begin_row = (zc * 2 + h) * count
+            rows = pl.ds(pl.multiple_of(begin_row, count), count)
+            left = left_ref[rows, :]
+            product = dot_t(left, right_ref[...]) if turned else dot(left, right_ref[...])
+            part_ref[rows, :] = product.astype(BF16)
+            return carry
+
+        lax.fori_loop(0, 2, step, 0)
+
+    def cross(zc):
+        for h in range(2):
+            at = index1(zc, y ^ 1, h)
+            arrived(None, s1.at[at], recv1.at[at])
+            add_up(s1.at[at], 0, [s1.at[at], mine(zc, wa ^ 2, h)])
+            send(s1.at[at], s2.at[zc * 2 + h], recv2.at[zc * 2 + h], across)
+
+    targets = [target(i) for i in range(n_ctx)]
+    for i, zc in enumerate(targets):
+        if product:
+            multiply(zc)
+        for yc in (y ^ 1, y):
+            for h in range(2):
+                at = index1(zc, yc, h)
+                send(mine(zc, yc * 2 + ((wa & 1) ^ 1), h), s1.at[at], recv1.at[at], sibling)
+        if i:
+            cross(targets[i - 1])
+    cross(targets[-1])
+    pair_waits = [wait() for wait in pair_waits]
+    for i, zc in enumerate(targets):
+        for h in range(2):
+            at = index1(zc, y, h)
+            here = zc * 2 + h
+            arrived(None, s1.at[at], recv1.at[at])
+            arrived(None, s2.at[here], recv2.at[here])
+            base = [mine(zc, wa, h), s1.at[at], s2.at[here]]
+            low, high = here, (n_ctx + zc) * 2 + h
+            if i < n_ctx - 1:
+                way = jnp.where(zc > ctx, 1, -1)
+                behind = jnp.where(zc > ctx, low, high)
+                more = inside(ctx - way)
+                arrived(more, s3.at[behind], recv3.at[behind])
+                pl.when(more)(lambda: add_up(s2.at[here], 0, base + [s3.at[behind]]))
+                pl.when(jnp.logical_not(more))(lambda: add_up(s2.at[here], 0, base))
+                send(s2.at[here], s3.at[behind], recv3.at[behind], {"ctx": ctx + way})
+            else:
+                under, over = ctx > 0, ctx < n_ctx - 1
+                arrived(under, s3.at[low], recv3.at[low])
+                arrived(over, s3.at[high], recv3.at[high])
+                ways = [
+                    (under & over, [s3.at[low], s3.at[high]]),
+                    (under & jnp.logical_not(over), [s3.at[low]]),
+                    (over & jnp.logical_not(under), [s3.at[high]]),
+                ]
+                for take, extra in ways:
+                    begin(take, lambda extra=extra: add_up(out_ref, h * half, base + extra))
+    for made in sends:
+        made.wait_send()
     for wait in pair_waits:
         wait()
 
 
-def scatter_tokens(part, pairs, n_ctx, n_wa, by_position, call_id):
+def scatter_tokens(left, right, turned, pairs, n_ctx, n_wa, by_position, call_id):
     n = n_ctx * n_wa
-    rows, width = part.shape[0] // n, part.shape[1]
+    rows = left.shape[0] // n
+    product = right is not None
+    operands = [left, right] if product else [left]
+    width = (right.shape[0] if turned else right.shape[1]) if product else left.shape[1]
     half = rows // 2
-    pieces = 2 * (2 * n_ctx - 1)
     kinds = tuple(kind for kind, _ in pairs)
     anywhere = pl.BlockSpec(memory_space=pl.ANY)
-    shapes = [jax.ShapeDtypeStruct((rows, width), F32)]
-    shapes += [jax.ShapeDtypeStruct(pair_shape(*pair), BF16) for pair in pairs]
+    vmem = pl.BlockSpec(memory_space=pltpu.VMEM)
+    shapes = [
+        jax.ShapeDtypeStruct(pair_shape(*pair), BF16)
+        for pair in pairs
+        for _ in range(pair_outs(pair[0]))
+    ]
     return pl.pallas_call(
-        partial(scatter_kernel, n_ctx, n_wa, by_position, kinds),
-        in_specs=[pl.BlockSpec(memory_space=pltpu.VMEM)] + [anywhere] * len(pairs),
-        out_specs=[pl.BlockSpec(memory_space=pltpu.VMEM)] + [anywhere] * len(pairs),
-        out_shape=shapes,
-        scratch_shapes=[
+        partial(scatter_kernel, n_ctx, n_wa, by_position, product, turned, kinds),
+        in_specs=[vmem] * len(operands) + [anywhere] * len(pairs),
+        out_specs=[vmem] + [anywhere] * len(shapes),
+        out_shape=[jax.ShapeDtypeStruct((rows, width), F32)] + shapes,
+        scratch_shapes=[pltpu.VMEM((rows * n, width), BF16)] * product
+        + [
             pltpu.VMEM((4 * n_ctx, half, width), BF16),
             pltpu.VMEM((2 * n_ctx, half, width), BF16),
             pltpu.VMEM((4 * n_ctx, half, width), BF16),
-            pltpu.SemaphoreType.DMA((4 * pieces,)),
+            pltpu.SemaphoreType.DMA((8 * n_ctx,)),
             pltpu.SemaphoreType.DMA((4 * n_ctx,)),
             pltpu.SemaphoreType.DMA((2 * n_ctx,)),
             pltpu.SemaphoreType.DMA((4 * n_ctx,)),
@@ -1186,10 +1254,10 @@
             pltpu.SemaphoreType.DMA((2, n)),
         ],
         compiler_params=pltpu.CompilerParams(
-            collective_id=call_id, has_side_effects=True, vmem_limit_bytes=48 * 2**20
+            collective_id=call_id, has_side_effects=True, vmem_limit_bytes=ROOM
         ),
         cost_estimate=LINK_COST,
-    )(part, *[array for _, array in pairs])
+    )(*operands, *[array for _, array in pairs])
 
 
 def per_device_heads(
@@ -1219,9 +1287,6 @@
     extra = 16
     swap_dp = [(0, 1), (1, 0)]
 
-    def mm_t(a, b):
-        return lax.dot_general(a, b, (((1,), (1,)), ((), ())), preferred_element_type=F32)
-
     def t_mm(a, b):
         return lax.dot_general(a, b, (((0,), (0,)), ((), ())), preferred_element_type=F32)
 
@@ -1233,9 +1298,10 @@
     gains_own = jnp.concatenate([attn_gain, ffn_gain, q_gain, k_gain])
     gains_row = jnp.pad(gains_own, (0, extra * 2 * LANES - gains_own.shape[0]))
     attn_cols = pack_attn(w_query, w_key, w_value, gains_row.reshape(extra, 2 * LANES), n)
-    x_all, attn_cols = gather_tokens(tokens[0], [(SPREAD, attn_cols)], n_ctx, n_wa, True, 1)
-    w_qkv = attn_cols[:, :d_rows].reshape(width, 2 * LANES)
-    gains = attn_cols[:, d_rows:].reshape(n, -1).astype(F32)
+    x_all, attn_half, attn_other = gather_tokens(
+        tokens[0], [(SPREAD, attn_cols)], n_ctx, n_wa, True, 1
+    )
+    gains = attn_half[:, half:].reshape(n, -1).astype(F32)
     attn_gain32 = gains[:, :d_rows].reshape(-1)
     ffn_gain32 = gains[:, d_rows : 2 * d_rows].reshape(-1)
     qgain32 = gains[:, 2 * d_rows : 2 * d_rows + per].reshape(-1)
@@ -1249,22 +1315,23 @@
     x_own = tokens[0].astype(F32)
     cosine, sine = rope_tables(stream)
     head_gain = jnp.concatenate([qgain32, qgain32, kgain32, kgain32]).reshape(1, 2 * LANES)
-    n1_all, raw, q_b, kv_b, att, inv, branch_part = attend(
-        doc_starts, x_all, attn_gain32.reshape(1, width), w_qkv, head_gain, cosine, sine, w_out
-    )
-    (branch,) = scatter_tokens(branch_part, [], n_ctx, n_wa, True, 3)
+    n1_all, raw, q_b, kv_b, att, inv, w_qkv = attend(
+        doc_starts, x_all, attn_gain32.reshape(1, width), attn_half, attn_other, head_gain, cosine, sine
+    )
+    (branch,) = scatter_tokens(att, w_out, False, [], n_ctx, n_wa, True, 3)
     middle = x_own + branch
     n2_own, n2_back = jax.vjp(rms_norm, middle, ffn_gain32)
     n2_all, ff_other = gather_tokens(
         n2_own.astype(BF16), [(WHOLE, ff_half)], n_ctx, n_wa, False, 2
     )
     down_part, d_n2_part, gu_grad, down_grad = ffn(n2_all, dy_all, ff_half, ff_other, w_down)
+    gu_grad = gu_grad.reshape(n, 2, half, 2 * ff_cols)
+    d_n2, gu_other = scatter_tokens(d_n2_part, None, False, [(PICK, gu_grad)], n_ctx, n_wa, False, 4)
+    gu_mine = lax.dynamic_index_in_dim(gu_grad, dp, 1, keepdims=False)
+    gu_sum = (gu_mine.astype(F32) + gu_other.astype(F32)).astype(BF16)
+    down_part, d_n2 = lax.optimization_barrier((down_part, d_n2))
     down = lax.psum_scatter(down_part, AXES, scatter_dimension=0, tiled=True).astype(F32)
     layer_out = middle + down
-    gu_grad = gu_grad.reshape(n, 2, half, 2 * ff_cols)
-    d_n2, gu_other = scatter_tokens(d_n2_part, [(PICK, gu_grad)], n_ctx, n_wa, False, 4)
-    gu_mine = lax.dynamic_index_in_dim(gu_grad, dp, 1, keepdims=False)
-    gu_sum = (gu_mine.astype(F32) + gu_other.astype(F32)).astype(BF16)
     d_mid_part, _ = n2_back(d_n2)
     d_middle = out_grad[0].astype(F32) + d_mid_part
     db_all, down_other = gather_tokens(
@@ -1277,36 +1344,34 @@
     )
     out_w_other = lax.ppermute(out_w_grad, "dp", swap_dp)
     qkv_grad = t_mm(n1_all, d_qkv).astype(BF16).reshape(n, 2, half, 2 * LANES)
-    head_grad = head_grad + lax.ppermute(head_grad, "dp", swap_dp)
-    head_row = jnp.concatenate([head_grad, jnp.zeros_like(head_grad)], axis=1).astype(BF16)
-    head_row = jnp.concatenate([head_row, jnp.zeros_like(head_row)], axis=0)
     qkv_other = lax.ppermute(
         lax.dynamic_index_in_dim(qkv_grad, 1 - dp, 1, keepdims=False), "dp", swap_dp
     )
+    head_grad = head_grad + lax.ppermute(head_grad, "dp", swap_dp)
+    qkv_other, head_grad, gu_rows = lax.optimization_barrier((qkv_other, head_grad, gu_rows))
+    gu_others = lax.ppermute(gu_rows, "dp", swap_dp)
     qkv_mine = lax.dynamic_index_in_dim(qkv_grad, dp, 1, keepdims=False)
     qkv_sum = (qkv_mine.astype(F32) + qkv_other.astype(F32)).astype(BF16)
-    d_n1_part = mm_t(d_qkv, w_qkv).astype(BF16)
-    gu_rows, d_n1_part, qkv_sum = lax.optimization_barrier((gu_rows, d_n1_part, qkv_sum))
+    head_row = jnp.pad(head_grad.astype(BF16), ((0, 8), (0, LANES)))
     qkv_out = jnp.concatenate(
         [qkv_sum, jnp.broadcast_to(head_row[None], (n,) + head_row.shape)], axis=1
     )
-    d_n1, gu_others, qkv_rows = scatter_tokens(
-        d_n1_part, [(WHOLE, gu_rows), (SPREAD, qkv_out)], n_ctx, n_wa, True, 6
-    )
-    out_w_other, d_n1 = lax.optimization_barrier((out_w_other, d_n1))
+    d_n1, qkv_rows, qkv_others = scatter_tokens(
+        d_qkv, w_qkv, True, [(SPREAD, qkv_out)], n_ctx, n_wa, True, 6
+    )
+    out_w_other, gu_others, d_n1 = lax.optimization_barrier((out_w_other, gu_others, d_n1))
     _, n1_back = jax.vjp(rms_norm, x_own, attn_gain32)
     d_x_part, _ = n1_back(d_n1)
     input_grad = d_middle + d_x_part
 
     gate_grad, up_grad, gu_sums = unpack_pair(gu_rows, gu_others, w_gate, w_up)
-    qkv_others = lax.ppermute(qkv_rows, "dp", swap_dp)
     q_grad, k_grad, v_grad, attn_sums, head_sums = unpack_attn(
         qkv_rows, qkv_others, w_query, w_key, w_value
     )
     me = lax.axis_index("ctx") * n_wa + lax.axis_index("wa")
     q_gain_grad = head_sums[0, :HD] + head_sums[0, HD:LANES]
     k_gain_grad = head_sums[1, :HD]
-    attn_gain_grad = attn_sums[:, 0] / attn_gain.astype(F32)
+    attn_gain_grad = jnp.sum(attn_sums, axis=1) / attn_gain.astype(F32)
     ffn_gain_grad = jnp.sum(gu_sums, axis=1) / ffn_gain.astype(F32)
     return (
         layer_out.astype(BF16)[None],

time: 619 us -> 597 us (0.964)
  Pallas kernels: 530 us -> 521 us
  local copies, waits for them, and re-layouts: 14 us -> 7.57 us
    pallas_call x3, Pallas kernels: 193 us -> 175 us  [gather_tokens(): pl.pallas_call(partial(gather_kernel, n_ctx, n_wa, by_position, kinds), i...]
    ppermute x1, waiting for transfers between devices: 11.8 us -> 0.01 us  [per_device_heads(): gu_others = lax.ppermute(gu_rows, 'dp', swap_dp)]
    pallas_call x4, Pallas kernels: 208 us -> 219 us  [the longest x3 217 us: scatter_tokens(): pl.pallas_call(partial(scatter_kernel, n_ctx, n_wa, by_position, product,...]
  transfers between devices with their start and end apart: 8 -> 8, of which waited for: 2 -> 1; matrix products, arithmetic and copies ran while one was open for 5% -> 4% of each run, Pallas kernels for 57% -> 59%
where the time goes in v5:
time: 597 us
  Pallas kernels  521 us (87%)
  other arithmetic  23.8 us (4%)
  between operations  14.5 us (2%)
  starting transfers between devices  13.4 us (2%)
  waiting for transfers between devices  9.97 us (2%)
  local copies, waits for them, and re-layouts  7.57 us (1%)
  matrix products  6.27 us (1%)
    pallas_call x3, Pallas kernels, scatter_tokens(): pl.pallas_call(partial(scatter_kernel, n_ctx, n_wa, by_position, product,...  217 us
    pallas_call x3, Pallas kernels, gather_tokens(): pl.pallas_call(partial(gather_kernel, n_ctx, n_wa, by_position, kinds), i...  175 us
    pallas_call x1, Pallas kernels, ffn(): pl.pallas_call(ffn_kernel, grid=(stream // bt,), in_specs=[rows, rows, wh...  51.2 us
    pallas_call x1, Pallas kernels, attend_back(): pl.pallas_call(attend_back_kernel, grid=(stream // bq,), in_specs=[pl.Blo...  35.6 us
    pallas_call x1, Pallas kernels, attend(): pl.pallas_call(attend_kernel, grid=(stream // bq,), in_specs=[pl.BlockSpe...  28.4 us
  transfers between devices with their start and end apart: 8, of which 1 were waited for; matrix products, arithmetic and copies ran while one was open for 4% of the time, Pallas kernels for 59%

profile of v5, /device:TPU:0, one launch (start us, length us, event | category | flops | bytes accessed | tf_op | source)
XLA Modules:
  0.0 596.6 jit_solution(15123223555651997366)
XLA Ops:
  7.2 0.0 all-gather.2.cloned.1.call-start
  7.2 0.8 fusion.15
  8.0 0.6 reshape.92.gains_ref
  8.6 2.1 shard_map.255.refs_0_
  10.7 62.5 %shard_map.256 = (bf16[2048,2048]{1,0:T(8,128)(2,1)}, bf16[16,80,256]{2,1,0:T(8,128)(2,1)}, bf16[16,80,256]{2,1,0:T(8,128)(2,1)}) custom-call(bf16[128,2048]{1,0:T(8,128)(2,1)} %bitcast.58, bf16[16,80,256]{2,1,0:T(8,128)(2,1)} %shard_map.255.refs_0_), custom_call_target="tpu_custom_call" | custom-call | flops 49999998976 | bytes 16777216 | tf_op jit(solution)/shard_map/pallas_call | solution.py:1062
  73.2 0.0 all-gather.2.cloned.1.call-update
  73.3 3.8 shard_map.259
  77.0 4.5 all-to-all-start
  81.5 0.0 reduce-scatter.2.cloned.1.call-start
  81.5 0.9 slice_convert_fusion
  82.5 0.2 copy.34
  82.6 0.1 fusion.21
  82.7 0.1 reshape.93
  82.8 0.1 reshape.94
  82.9 0.6 pad_maximum_fusion.1
  83.5 0.6 slice_bitcast_fusion.1
  84.1 28.4 %shard_map.257 = (bf16[2048,2048]{1,0:T(8,128)(2,1)}, f32[2048,256]{1,0:T(8,128)}, bf16[2048,128]{1,0:T(8,128)(2,1)}, bf16[2048,128]{1,0:T(8,128)(2,1)}, bf16[20...) custom-call(s32[1,8]{1,0:T(1,128)} %starts.3, bf16[2048,2048]{1,0:T(8,128)(2,1)} %get-tuple-element.61.x_ref, ...), custom_call_target="tpu_custom_call" | custom-call | flops 20000000000 | bytes 33554432 | tf_op jit(solution)/shard_map/pallas_call | solution.py:479
  112.6 93.3 %shard_map.258 = f32[128,2048]{1,0:T(8,128)} custom-call(bf16[2048,128]{1,0:T(8,128)(2,1)} %get-tuple-element.64.refs_0_.att_ref, bf16[128,2048]{1,0:T(8,128)(2,1)} %w_out_ref.1), custom_call_target="tpu_custom_call" | custom-call | flops 49999998976 | bytes 16777216 | tf_op jit(solution)/shard_map/pallas_call | solution.py:1239
  205.9 1.5 multiply_reduce_fusion.1
  207.5 1.0 multiply_convert_fusion.own_ref
  208.4 0.0 all-to-all-done.refs_0_.own_ref
  208.4 50.5 %shard_map.260 = (bf16[2048,2048]{1,0:T(8,128)(2,1)}, bf16[16,64,1024]{2,1,0:T(8,128)(2,1)}) custom-call(bf16[128,2048]{1,0:T(8,128)(2,1)} %multiply_convert_fusion.own_ref, bf16[16,64,1024]{2,1,0:T(8,128)(2,1)} %all-to-all-done.refs_0_.own_ref), custom_call_target="tpu_custom_call" | custom-call | flops 49999998976 | bytes 16777216 | tf_op jit(solution)/shard_map/pallas_call | solution.py:1062
  258.9 0.0 all-gather.2.cloned.1.call-done.dy_ref
  258.9 51.2 %shard_map.261 = (bf16[2048,2048]{1,0:T(8,128)(2,1)}, bf16[2048,2048]{1,0:T(8,128)(2,1)}, bf16[2048,1024]{1,0:T(8,128)(2,1)}, bf16[512,2048]{1,0:T(8,128)(2,1)}) custom-call(bf16[2048,2048]{1,0:T(8,128)(2,1)} %get-tuple-element.66.n2_ref, bf16[2048,2048]{1,0:T(8,128)(2,1)} %all-gather.2.cloned.1.call-done.dy_ref, ...), custom_call_target="tpu_custom_call" | custom-call | flops 38654705664 | bytes 33554432 | tf_op jit(solution)/shard_map/pallas_call | solution.py:673
  310.2 55.2 %shard_map.262 = (f32[128,2048]{1,0:T(8,128)}, bf16[16,64,1024]{2,1,0:T(8,128)(2,1)}) custom-call(bf16[2048,2048]{1,0:T(8,128)(2,1)} %get-tuple-element.70.refs_0_, bf16[16,2,64,1024]{3,2,1,0:T(8,128)(2,1)} %bitcast.60), custom_call_target="tpu_custom_call" | custom-call | flops 49999998976 | bytes 16777216 | tf_op jit(solution)/shard_map/pallas_call | solution.py:1239
  365.4 0.0 copy-start.13
  365.4 2.2 fusion.4
  367.6 0.5 copy-done.29
  368.1 1.2 fusion.20.own_ref
  369.3 0.0 reduce-scatter.2.cloned.1.call-update
  369.3 61.8 %shard_map.263 = (bf16[2048,2048]{1,0:T(8,128)(2,1)}, bf16[512,2048]{1,0:T(8,128)(2,1)}) custom-call(bf16[128,2048]{1,0:T(8,128)(2,1)} %fusion.20.own_ref, bf16[512,2048]{1,0:T(8,128)(2,1)} %get-tuple-element.76.refs_0_), custom_call_target="tpu_custom_call" | custom-call | flops 49999998976 | bytes 16777216 | tf_op jit(solution)/shard_map/pallas_call | solution.py:1062
  431.1 3.9 fusion
  435.0 4.7 all-to-all-start.1
  439.7 35.6 %shard_map.264 = (bf16[2048,256]{1,0:T(8,128)(2,1)}, bf16[128,2048]{1,0:T(8,128)(2,1)}, f32[8,128]{1,0:T(8,128)}) custom-call(s32[1,8]{1,0:T(1,128)} %starts.3, bf16[2048,2048]{1,0:T(8,128)(2,1)} %get-tuple-element.78.db_ref, bf16[128,2048]{1,0:T(8,128)(2,1)} %w_out_ref.1, bf16[2048,128]{1,0:T(8,128)(2,1)} %get-tuple-element.79.q_ref, ...), custom_call_target="tpu_custom_call" | custom-call | flops 30000001024 | bytes 33554432 | tf_op jit(solution)/shard_map/pallas_call | solution.py:598
  475.3 0.7 collective-permute-start.2
  476.0 6.3 %convolution_convert_fusion = bf16[2048,256]{1,0:T(8,128)(2,1)S(1)} fusion(bf16[2048,2048]{1,0:T(8,128)(2,1)} %get-tuple-element.84, bf16[2048,256]{1,0:T(8,128)(2,1)} %get-tuple-element.85.refs_0_), kind=kOutput, calls=%fused_computation.3 | convolution fusion | flops 2148007936 | bytes 10485760 | tf_op jit(solution)/shard_map/dot_general | solution.py:1291
  482.2 0.1 dynamic-slice_bitcast_fusion
  482.3 1.5 collective-permute-start.1
  483.8 2.8 convert_add_fusion.1
  486.6 0.6 collective-permute-start
  487.2 0.0 collective-permute-done.2
  487.2 9.9 %collective-permute-done.1 = bf16[16,64,256]{2,1,0:T(8,128)(2,1)S(1)} collective-permute-done((bf16[16,64,256]{2,1,0:T(8,128)(2,1)S(1)}, bf16[16,64,256]{2,1,0:T(8,128)(2,1)S(1)}, u32[]{:S(2)}, u32[]{:S(2)}) %collective-permute-start.1) | collective-permute-done | bytes 524320 | tf_op jit(solution)/shard_map/ppermute | solution.py:1347
  497.1 0.0 all-to-all-done.1.own_ref
  497.1 1.4 collective-permute-start.3
  498.6 0.2 fusion.6
  498.8 0.9 pad_maximum_fusion.refs_2_
  499.6 68.9 %shard_map.265 = (f32[128,2048]{1,0:T(8,128)}, bf16[16,80,256]{2,1,0:T(8,128)(2,1)}, bf16[16,80,256]{2,1,0:T(8,128)(2,1)}) custom-call(bf16[2048,256]{1,0:T(8,128)(2,1)} %get-tuple-element.85.refs_0_, bf16[2048,256]{1,0:T(8,128)(2,1)} %get-tuple-element.89.refs_1_, bf16[16,80,256]{2,1,0:T(8,128)(2,1)} %pad_maximum_fusion.refs_2_), custom_call_target="tpu_custom_call" | custom-call | flops 49999998976 | bytes 16777216 | tf_op jit(solution)/shard_map/pallas_call | solution.py:1239
  568.5 0.0 copy-start
  568.6 1.2 copy-done.3
  569.8 1.1 copy-done.4
  570.9 1.4 shard_map.266
  572.2 0.1 reduce_sum.66
  572.3 0.1 fusion.22
  572.4 0.6 fusion.16
  573.0 0.0 collective-permute-done
  573.0 0.8 copy-done.19
  573.8 1.6 copy-done.1
  575.4 0.0 copy-start.28
  575.4 6.5 %shard_map.267 = (f32[128,8192]{1,0:T(8,128)}, f32[128,8192]{1,0:T(8,128)}, f32[128,128]{1,0:T(8,128)S(1)}) custom-call(bf16[16,64,1024]{2,1,0:T(8,128)(2,1)} %all-to-all-done.1.own_ref, bf16[16,64,1024]{2,1,0:T(8,128)(2,1)} %collective-permute-done.3.other_ref, bf16[128,8192]{1,0:T(8,128)(2,1)S(1)} %copy-done, bf16[128,8192]{1,0:T(8,128)(2,1)S(1)} %copy-done.1), custom_call_target="tpu_custom_call" | custom-call | tf_op jit(solution)/shard_map/pallas_call | solution.py:821
  581.9 0.1 reduce_sum.67
  582.1 1.6 fusion.5
  583.7 0.5 convert_divide_fusion
  584.2 2.3 convert_add_fusion.4
  586.6 3.2 fusion.8
  (62 shorter events, 0.2 us)
Async XLA Ops:
  7.2 251.8 %all-gather.2.cloned.1.call-start = ((), (), s32[]{:S(2)}) async-start(), calls=%async_computation.3 | async-start | bytes 8912896 | tf_op jit(solution)/shard_map/all_gather | solution.py:1313
  77.0 131.4 %all-to-all-start = ((bf16[16,64,1024]{2,1,0:T(8,128)(2,1)}), bf16[16,64,1024]{2,1,0:T(8,128)(2,1)}, u32[]{:S(2)}, u32[]{:S(2)}) async-start(bf16[16,64,1024]{2,1,0:T(8,128)(2,1)} %shard_map.259), calls=%async_computation | async-start | bytes 4194304 | tf_op jit(solution)/shard_map/all_to_all | solution.py:1294
  81.5 505.0 %reduce-scatter.2.cloned.1.call-start = ((), (), s32[]{:S(2)}) async-start(), calls=%async_computation.4 | async-start | bytes 8912896 | tf_op jit(solution)/shard_map/reduce_scatter | solution.py:1333
  84.1 283.4 %copy-start.20 = (f32[2048]{0:T(1024)}, f32[2048]{0:T(1024)S(1)}, u32[]{:S(2)}) copy-start(f32[2048]{0:T(1024)S(1)} %get-tuple-element.112) | copy-start | bytes 24580
  112.6 93.3 %copy-start.9 = (bf16[1,128,2048]{2,1,0:T(8,128)(2,1)S(1)}, bf16[1,128,2048]{2,1,0:T(8,128)(2,1)}, u32[]{:S(2)}) copy-start(bf16[1,128,2048]{2,1,0:T(8,128)(2,1)} %param.16) | copy-start | bytes 1572868
  205.9 1.6 copy-start.7
  207.5 160.1 %copy-start.23 = (f32[128]{0:T(128)}, f32[128]{0:T(128)S(1)}, u32[]{:S(2)}) copy-start(f32[128]{0:T(128)S(1)} %fusion.18) | copy-start | bytes 1540
  365.4 2.7 copy-start.11
  365.4 2.7 copy-start.13
  367.6 0.5 copy-start.29
  369.3 61.8 %copy-start.15 = (bf16[16,64,1024]{2,1,0:T(8,128)(2,1)S(1)}, bf16[16,64,1024]{2,1,0:T(8,128)(2,1)}, u32[]{:S(2)}) copy-start(bf16[16,64,1024]{2,1,0:T(8,128)(2,1)} %get-tuple-element.75) | copy-start | bytes 6291460
  435.0 62.2 %all-to-all-start.1 = ((bf16[16,64,1024]{2,1,0:T(8,128)(2,1)}), bf16[16,64,1024]{2,1,0:T(8,128)(2,1)}, u32[]{:S(2)}, u32[]{:S(2)}) async-start(bf16[16,64,1024]{2,1,0:T(8,128)(2,1)} %fusion), calls=%async_computation.2 | async-start | bytes 4194304 | tf_op jit(solution)/shard_map/all_to_all | solution.py:1294
  475.3 11.9 %collective-permute-start.2 = (f32[8,128]{1,0:T(8,128)}, f32[8,128]{1,0:T(8,128)S(1)}, u32[]{:S(2)}, u32[]{:S(2)}) collective-permute-start(f32[8,128]{1,0:T(8,128)} %get-tuple-element.86), channel_id=1, source_target_pairs={{0,16},{16,0},{1,17},{17,1},{2,18},{18,2},{3,19},{19,3},{4,20},{20... | collective-permute-start | bytes 12296 | tf_op jit(solution)/shard_map/ppermute | solution.py:1350
  476.0 7.8 %copy-start.16 = (bf16[512,2048]{1,0:T(8,128)(2,1)S(1)}, bf16[512,2048]{1,0:T(8,128)(2,1)}, u32[]{:S(2)}) copy-start(bf16[512,2048]{1,0:T(8,128)(2,1)} %get-tuple-element.76.refs_0_) | copy-start | bytes 6291460
  476.0 7.8 %copy-start.17 = (bf16[512,2048]{1,0:T(8,128)(2,1)S(1)}, bf16[512,2048]{1,0:T(8,128)(2,1)}, u32[]{:S(2)}) copy-start(bf16[512,2048]{1,0:T(8,128)(2,1)} %get-tuple-element.106) | copy-start | bytes 6291460
  482.3 14.8 %collective-permute-start.1 = (bf16[16,64,256]{2,1,0:T(8,128)(2,1)S(1)}, bf16[16,64,256]{2,1,0:T(8,128)(2,1)S(1)}, u32[]{:S(2)}, u32[]{:S(2)}) collective-permute-start(bf16[16,64,256]{2,1,0:T(8,128)(2,1)S(1)} %dynamic-slice_bitcast_fusion), channel_id=1, source_target_pairs={{0,16},{16,0},{1,17},{17,1},{2,18},{18,2},{3,19},{19,3},{4,20},{20... | collective-permute-start | bytes 1572872 | tf_op jit(solution)/shard_map/ppermute | solution.py:1347
  483.8 2.8 copy-start.18
  483.8 3.4 copy-start.25
  486.6 86.4 %collective-permute-start = (bf16[128,2048]{1,0:T(8,128)(2,1)S(1)}, bf16[128,2048]{1,0:T(8,128)(2,1)S(1)}, u32[]{:S(2)}, u32[]{:S(2)}) collective-permute-start(bf16[128,2048]{1,0:T(8,128)(2,1)S(1)} %copy-done.18), channel_id=1, source_target_pairs={{0,16},{16,0},{1,17},{17,1},{2,18},{18,2},{3,19},{19,3},{4,20},{20... | collective-permute-start | bytes 1572872 | tf_op jit(solution)/shard_map/ppermute | solution.py:1345
  497.1 75.9 %collective-permute-start.3 = (bf16[16,64,1024]{2,1,0:T(8,128)(2,1)}, bf16[16,64,1024]{2,1,0:T(8,128)(2,1)}, u32[]{:S(2)}, u32[]{:S(2)}) collective-permute-start(bf16[16,64,1024]{2,1,0:T(8,128)(2,1)} %all-to-all-done.1.own_ref), channel_id=1, source_target_pairs={{0,16},{16,0},{1,17},{17,1},{2,18},{18,2},{3,19},{19,3},{4,20},{20... | collective-permute-start | bytes 6291464 | tf_op jit(solution)/shard_map/ppermute | solution.py:1352
  499.6 68.9 %copy-start.2 = (bf16[128,2048]{1,0:T(8,128)(2,1)S(1)}, bf16[128,2048]{1,0:T(8,128)(2,1)}, u32[]{:S(2)}) copy-start(bf16[128,2048]{1,0:T(8,128)(2,1)} %wq_ref.1) | copy-start | bytes 1572868
  499.6 68.9 %copy-start.5 = (bf16[128,512]{1,0:T(8,128)(2,1)S(1)}, bf16[128,512]{1,0:T(8,128)(2,1)}, u32[]{:S(2)}) copy-start(bf16[128,512]{1,0:T(8,128)(2,1)} %wk_ref.1) | copy-start | bytes 393220
  499.6 68.9 %copy-start.6 = (bf16[128,512]{1,0:T(8,128)(2,1)S(1)}, bf16[128,512]{1,0:T(8,128)(2,1)}, u32[]{:S(2)}) copy-start(bf16[128,512]{1,0:T(8,128)(2,1)} %wv_ref.1) | copy-start | bytes 393220
  568.5 5.3 copy-start
  568.6 1.2 copy-start.3
  569.8 1.1 copy-start.4
  573.0 0.8 copy-start.19
  573.8 1.6 copy-start.1
  575.4 6.6 %copy-start.10 = (bf16[1,128,2048]{2,1,0:T(8,128)(2,1)S(1)}, bf16[1,128,2048]{2,1,0:T(8,128)(2,1)}, u32[]{:S(2)}) copy-start(bf16[1,128,2048]{2,1,0:T(8,128)(2,1)} %param.16) | copy-start | bytes 1572868
  575.4 6.7 %copy-start.22 = (f32[2048]{0:T(1024)S(1)}, f32[2048]{0:T(1024)}, u32[]{:S(2)}) copy-start(f32[2048]{0:T(1024)} %get-tuple-element.111) | copy-start | bytes 24580
  575.4 8.3 %copy-start.26 = (f32[128]{0:T(128)S(1)}, f32[128]{0:T(128)}, u32[]{:S(2)}) copy-start(f32[128]{0:T(128)} %get-tuple-element.107) | copy-start | bytes 1540
  575.4 8.3 %copy-start.27 = (bf16[128]{0:T(256)(128)(2,1)S(1)}, bf16[128]{0:T(256)(128)(2,1)}, u32[]{:S(2)}) copy-start(bf16[128]{0:T(256)(128)(2,1)} %param.26) | copy-start | bytes 772
  575.4 8.3 %copy-start.28 = (bf16[128]{0:T(256)(128)(2,1)S(1)}, bf16[128]{0:T(256)(128)(2,1)}, u32[]{:S(2)}) copy-start(bf16[128]{0:T(256)(128)(2,1)} %param.19) | copy-start | bytes 772
  581.9 4.6 copy-start.8
  581.9 4.6 copy-start.12
  581.9 4.6 copy-start.14
  581.9 4.6 copy-start.21
  581.9 4.6 copy-start.24
  581.9 4.6 copy-start.30
Sparse Core Ops, SparseCore 0:
  73.4 130.9 all-gather.1
  369.4 132.7 reduce-scatter.1

commit v6 on v5

--- a/solution.py
+++ b/solution.py
@@ -331,6 +331,7 @@
 ROWS_BLOCK = 256
 FFN_BLOCK = 256
 ROOM = 60 * 2**20
+SIDE_ROWS = 256
 LOG2E = 1.4426950408889634
 F32 = jnp.float32
 BF16 = jnp.bfloat16
@@ -624,8 +625,7 @@
 
 
 def ffn_kernel(
-    n2_ref, dy_ref, own_ref, other_ref, w_down_ref,
-    down_ref, d_n2_ref, gu_grad_ref, down_grad_ref, gu_acc, down_acc, w_gu_ref,
+    n2_ref, dy_ref, own_ref, other_ref, w_down_ref, hidden_ref, d_gu_ref, gu_grad_ref, w_gu_ref, gu_acc
 ):
     block = pl.program_id(0)
 
@@ -633,17 +633,15 @@
     def _():
         join_halves(own_ref.shape[1], own_ref, other_ref, w_gu_ref)
         gu_acc[...] = jnp.zeros_like(gu_acc)
-        down_acc[...] = jnp.zeros_like(down_acc)
-
-    cols = w_down_ref.shape[0]
-    n2, dy = n2_ref[...], dy_ref[...]
+
+    cols = hidden_ref.shape[1]
+    n2 = n2_ref[...]
     gate_up = dot(n2, w_gu_ref[...])
+    d_hidden = dot_t(dy_ref[...], w_down_ref[...])
     gate, up = gate_up[:, :cols], gate_up[:, cols:]
     sig = jax.nn.sigmoid(gate)
     silu = gate * sig
-    hidden = (silu * up).astype(BF16)
-    down_ref[...] = dot(hidden, w_down_ref[...]).astype(BF16)
-    d_hidden = dot_t(dy, w_down_ref[...])
+    hidden_ref[...] = (silu * up).astype(BF16)
     d_gu = jnp.concatenate(
         [
             (d_hidden * up * (sig * (1.0 + gate * (1.0 - sig)))).astype(BF16),
@@ -651,21 +649,21 @@
         ],
         axis=1,
     )
-    d_n2_ref[...] = dot_t(d_gu, w_gu_ref[...]).astype(BF16)
+    d_gu_ref[...] = d_gu
     gu_acc[...] += t_dot(n2, d_gu)
-    down_acc[...] += t_dot(hidden, dy)
 
     @pl.when(block == pl.num_programs(0) - 1)
     def _():
         gu_grad_ref[...] = gu_acc[...].astype(BF16)
-        down_grad_ref[...] = down_acc[...].astype(BF16)
 
 
 def ffn(n2_all, dy_all, own, other, w_down):
     stream, width = n2_all.shape
-    gu_shape = (width, own.shape[2])
+    both = own.shape[2]
     bt = FFN_BLOCK
-    rows = pl.BlockSpec((bt, width), lambda i: (i, 0))
+
+    def rows(cols):
+        return pl.BlockSpec((bt, cols), lambda i: (i, 0))
 
     def whole(shape):
         return pl.BlockSpec(shape, lambda i: (0,) * len(shape), pipeline_mode=pl.Buffered(1))
@@ -673,22 +671,18 @@
     return pl.pallas_call(
         ffn_kernel,
         grid=(stream // bt,),
-        in_specs=[rows, rows, whole(own.shape), whole(own.shape), whole(w_down.shape)],
-        out_specs=[rows, rows, whole(gu_shape), whole(w_down.shape)],
+        in_specs=[rows(width), rows(width), whole(own.shape), whole(own.shape), whole(w_down.shape)],
+        out_specs=[rows(both // 2), rows(both), whole((width, both)), whole((width, both))],
         out_shape=[
-            jax.ShapeDtypeStruct((stream, width), BF16),
-            jax.ShapeDtypeStruct((stream, width), BF16),
-            jax.ShapeDtypeStruct(gu_shape, BF16),
-            jax.ShapeDtypeStruct(w_down.shape, BF16),
+            jax.ShapeDtypeStruct((stream, both // 2), BF16),
+            jax.ShapeDtypeStruct((stream, both), BF16),
+            jax.ShapeDtypeStruct((width, both), BF16),
+            jax.ShapeDtypeStruct((width, both), BF16),
         ],
-        scratch_shapes=[
-            pltpu.VMEM(gu_shape, F32),
-            pltpu.VMEM(w_down.shape, F32),
-            pltpu.VMEM(gu_shape, BF16),
-        ],
+        scratch_shapes=[pltpu.VMEM((width, both), F32)],
         compiler_params=pltpu.CompilerParams(vmem_limit_bytes=ROOM),
         cost_estimate=pl.CostEstimate(
-            flops=18 * stream * width * w_down.shape[0], bytes_accessed=2**25, transcendentals=0
+            flops=5 * stream * width * both, bytes_accessed=2**25, transcendentals=0
         ),
     )(n2_all, dy_all, own, other, w_down)
 
@@ -764,31 +758,6 @@
     )(w_query, w_key, w_value, gains)
 
 
-def pack_pair_kernel(dp_ref, gate_ref, up_ref, out_ref):
-    count, _, both = out_ref.shape
-    cols = both // 2
-    for j in range(count):
-        out_ref[j, :, :cols] = gate_ref[:, j * cols : (j + 1) * cols]
-        out_ref[j, :, cols:] = up_ref[:, j * cols : (j + 1) * cols]
-
-
-def pack_pair(w_gate, w_up, n):
-    half, cols = w_gate.shape[0] // 2, w_gate.shape[1] // n
-    count = 4
-    part = pl.BlockSpec((half, count * cols), lambda j, dp: (dp[0], j))
-    return pl.pallas_call(
-        pack_pair_kernel,
-        grid_spec=pltpu.PrefetchScalarGridSpec(
-            num_scalar_prefetch=1,
-            grid=(n // count,),
-            in_specs=[part, part],
-            out_specs=pl.BlockSpec((count, half, 2 * cols), lambda j, dp: (j, 0, 0)),
-        ),
-        out_shape=jax.ShapeDtypeStruct((n, half, 2 * cols), BF16),
-        compiler_params=pltpu.CompilerParams(vmem_limit_bytes=ROOM),
-    )(lax.axis_index("dp").reshape(1), w_gate, w_up)
-
-
 def unpack_pair_kernel(own_ref, other_ref, gate_w, up_w, gate_ref, up_ref, sum_ref):
     count, half, both = own_ref.shape
     cols = both // 2
@@ -950,11 +919,192 @@
     return pl.multiple_of(((zc * n_wa + wac) * 2 + h) * half, half)
 
 
-def gather_kernel(n_ctx, n_wa, by_position, kinds, own_ref, *refs):
+def unit_rows(values):
+    return lax.rsqrt(jnp.mean(values * values, axis=1, keepdims=True) + EPS)
+
+
+def norm_back(grad, values, gain):
+    inverse = unit_rows(values)
+    d_unit = grad * gain
+    unit = values * inverse
+    return inverse * (d_unit - unit * jnp.mean(d_unit * unit, axis=1, keepdims=True))
+
+
+def after_attention(total, x, gain):
+    middle = x.astype(F32) + total
+    return middle, middle * unit_rows(middle) * gain
+
+
+def after_ffn_back(total, middle, gain, d_out):
+    d_middle = d_out.astype(F32) + norm_back(total, middle, gain)
+    return d_middle, d_middle
+
+
+def after_attention_back(total, x, gain, d_middle):
+    return (d_middle + norm_back(total, x.astype(F32), gain),)
+
+
+class PackColumns:
+    def __init__(self, w_gate, w_up, n):
+        self.operands = [w_gate, w_up]
+        half, cols = w_gate.shape[0] // 2, w_gate.shape[1] // n
+        self.outs = [jax.ShapeDtypeStruct((n, half, 2 * cols), BF16)]
+        self.scratch = [
+            pltpu.VMEM((half, w_gate.shape[1]), BF16),
+            pltpu.VMEM((half, w_gate.shape[1]), BF16),
+            pltpu.VMEM((n, half, 2 * cols), BF16),
+            pltpu.SemaphoreType.DMA((3,)),
+        ]
+
+    def bind(self, ins, outs, scratch):
+        self.rows_v, (self.packed, sem) = scratch[:2], scratch[2:]
+        half = self.packed.shape[1]
+        rows = pl.ds(pl.multiple_of(lax.axis_index("dp") * half, half), half)
+        self.loads = [
+            pltpu.make_async_copy(ins[at].at[rows], self.rows_v[at], sem.at[at]) for at in range(2)
+        ]
+        for load in self.loads:
+            load.start()
+        self.store = pltpu.make_async_copy(self.packed, outs[0], sem.at[2])
+        self.at = 0
+
+    def step(self):
+        self.at += 1
+        if self.at != 2:
+            return
+        for load in self.loads:
+            load.wait()
+        n, _, both = self.packed.shape
+        cols = both // 2
+        for j in range(n):
+            for at in range(2):
+                self.packed[j, :, at * cols : (at + 1) * cols] = self.rows_v[at][
+                    :, j * cols : (j + 1) * cols
+                ]
+        self.store.start()
+
+    def finish(self):
+        self.store.wait()
+
+
+class PairSum:
+    def __init__(self, halves, other):
+        self.operands = [halves, other]
+        self.outs = [jax.ShapeDtypeStruct(other.shape, BF16)]
+        self.scratch = [pltpu.VMEM(other.shape, BF16)] * 2 + [pltpu.SemaphoreType.DMA((3,))]
+
+    def bind(self, ins, outs, scratch):
+        self.mine_v, self.other_v, self.sem = scratch
+        mine = ins[0].at[:, lax.axis_index("dp")]
+        self.loads = [
+            pltpu.make_async_copy(mine, self.mine_v, self.sem.at[0]),
+            pltpu.make_async_copy(ins[1], self.other_v, self.sem.at[1]),
+        ]
+        for load in self.loads:
+            load.start()
+        self.store = pltpu.make_async_copy(self.mine_v, outs[0], self.sem.at[2])
+        self.at = 0
+
+    def step(self):
+        self.at += 1
+        if self.at != 2:
+            return
+        for load in self.loads:
+            load.wait()
+
+        def add(j, carry):
+            total = self.mine_v[j].astype(F32) + self.other_v[j].astype(F32)
+            self.mine_v[j] = total.astype(BF16)
+            return carry
+
+        lax.fori_loop(0, self.mine_v.shape[0], add, 0)
+        self.store.start()
+
+    def finish(self):
+        self.store.wait()
+
+
+class DownProducts:
+    def __init__(self, dy, w_down, hidden):
+        self.operands = [dy, w_down, hidden]
+        self.steps = dy.shape[0] // SIDE_ROWS
+        self.outs = [
+            jax.ShapeDtypeStruct(dy.shape, BF16),
+            jax.ShapeDtypeStruct(w_down.shape, BF16),
+        ]
+        self.scratch = [
+            pltpu.VMEM((2, SIDE_ROWS, dy.shape[1]), BF16),
+            pltpu.VMEM((2, SIDE_ROWS, dy.shape[1]), BF16),
+            pltpu.VMEM(w_down.shape, BF16),
+            pltpu.VMEM(hidden.shape, BF16),
+            pltpu.VMEM(w_down.shape, F32),
+            pltpu.VMEM(w_down.shape, BF16),
+            pltpu.SemaphoreType.DMA((7,)),
+        ]
+
+    def bind(self, ins, outs, scratch):
+        self.dy, (self.out, self.grad) = ins[0], outs
+        self.dy_v, self.stage, self.w_v, self.hidden_v, self.acc, self.grad_v, self.sem = scratch
+        self.loads = [
+            pltpu.make_async_copy(ins[1], self.w_v, self.sem.at[4]),
+            pltpu.make_async_copy(ins[2], self.hidden_v, self.sem.at[5]),
+        ]
+        for load in self.loads:
+            load.start()
+        self.load(0).start()
+        self.acc[...] = jnp.zeros_like(self.acc)
+        self.stored = []
+        self.at = 0
+
+    def load(self, g):
+        rows = pl.ds(g * SIDE_ROWS, SIDE_ROWS)
+        return pltpu.make_async_copy(self.dy.at[rows], self.dy_v.at[g % 2], self.sem.at[g % 2])
+
+    def step(self):
+        g = self.at
+        if g >= self.steps:
+            return
+        self.at += 1
+        if g == 0:
+            for load in self.loads:
+                load.wait()
+        self.load(g).wait()
+        if g + 1 < self.steps:
+            self.load(g + 1).start()
+        rows = pl.ds(g * SIDE_ROWS, SIDE_ROWS)
+        if g >= 2:
+            self.stored[g - 2].wait()
+        hidden = self.hidden_v[rows, :]
+        self.stage[g % 2] = dot(hidden, self.w_v[...]).astype(BF16)
+        self.acc[...] += t_dot(hidden, self.dy_v[g % 2])
+        store = pltpu.make_async_copy(self.stage.at[g % 2], self.out.at[rows], self.sem.at[2 + g % 2])
+        store.start()
+        self.stored.append(store)
+
+    def finish(self):
+        while self.at < self.steps:
+            self.step()
+        for store in self.stored[-2:]:
+            store.wait()
+        self.grad_v[...] = self.acc[...].astype(BF16)
+        made = pltpu.make_async_copy(self.grad_v, self.grad, self.sem.at[6])
+        made.start()
+        made.wait()
+
+
+def split_side(side, at, refs):
+    count = len(side.operands) if side else 0
+    return refs[at : at + count], refs[:at] + refs[at + count :]
+
+
+def gather_kernel(n_ctx, n_wa, by_position, kinds, side, own_ref, *refs):
     pairs = len(kinds)
     outs = sum(pair_outs(kind) for kind in kinds)
+    side_in, refs = split_side(side, pairs, refs)
     srcs, out_ref, dsts = refs[:pairs], refs[pairs], refs[pairs + 1 : pairs + outs + 1]
-    own_sem, send_sem, recv_sem, pair_sem, spread_sem = refs[pairs + outs + 1 :]
+    refs = refs[pairs + outs + 1 :]
+    side_out, refs = refs[: len(side.outs) if side else 0], refs[len(side.outs) if side else 0 :]
+    own_sem, send_sem, recv_sem, pair_sem, spread_sem = refs[:5]
     ctx = lax.axis_index("ctx")
     wa = lax.axis_index("wa")
     half = own_ref.shape[0] // 2
@@ -1010,6 +1160,9 @@
         made.start()
         own_copies.append(made)
     pair_waits = start_pairs(kinds, srcs, dsts, n_wa, pair_sem, spread_sem)
+    if side:
+        side.bind(side_in, side_out, refs[5:])
+        side.step()
 
     def across(k, h):
         for way in (-1, 1) if k else (1,):
@@ -1029,6 +1182,8 @@
                 send(cond, piece, zc, wa, h, {"wa": wa ^ 2})
                 send(cond, piece, zc, wa, h, {"wa": wa ^ 1})
             across(k - 1, h)
+            if side:
+                side.step()
         if k == 1:
             pair_waits = [wait() for wait in pair_waits]
     for h in range(2):
@@ -1044,11 +1199,14 @@
             pl.when(cond)(made.wait_send)
     for made in own_copies:
         made.wait()
+    if side:
+        side.finish()
     for wait in pair_waits:
         wait()
 
 
-def gather_tokens(own, pairs, n_ctx, n_wa, by_position, call_id):
+def gather_tokens(own, pairs, n_ctx, n_wa, by_position, call_id, side=None):
+    more = side.operands if side else []
     rows, width = own.shape
     n = n_ctx * n_wa
     kinds = tuple(kind for kind, _ in pairs)
@@ -1059,9 +1217,10 @@
         for pair in pairs
         for _ in range(pair_outs(pair[0]))
     ]
+    shapes += side.outs if side else []
     return pl.pallas_call(
-        partial(gather_kernel, n_ctx, n_wa, by_position, kinds),
-        in_specs=[anywhere] * (1 + len(pairs)),
+        partial(gather_kernel, n_ctx, n_wa, by_position, kinds, side),
+        in_specs=[anywhere] * (1 + len(pairs) + len(more)),
         out_specs=[anywhere] * len(shapes),
         out_shape=shapes,
         scratch_shapes=[
@@ -1070,21 +1229,28 @@
             pltpu.SemaphoreType.DMA((2 * n,)),
             pltpu.SemaphoreType.DMA((max(1, len(pairs)), 2)),
             pltpu.SemaphoreType.DMA((2, n)),
-        ],
-        compiler_params=pltpu.CompilerParams(collective_id=call_id, has_side_effects=True),
+        ]
+        + (side.scratch if side else []),
+        compiler_params=pltpu.CompilerParams(
+            collective_id=call_id, has_side_effects=True, vmem_limit_bytes=ROOM if side else None
+        ),
         cost_estimate=LINK_COST,
-    )(own, *[array for _, array in pairs])
-
-
-def scatter_kernel(n_ctx, n_wa, by_position, product, turned, kinds, *refs):
-    left_ref, right_ref = refs[0], refs[1]
-    refs = refs[2:] if product else refs[1:]
+    )(own, *[array for _, array in pairs], *more)
+
+
+def scatter_kernel(
+    n_ctx, n_wa, by_position, turned, kinds, side, finish, count, left_ref, right_ref, *refs
+):
+    row_ins, refs = refs[:count], refs[count:]
+    row_count = 1 if finish is after_attention_back else 2
     pairs = len(kinds)
     outs = sum(pair_outs(kind) for kind in kinds)
-    srcs, out_ref, dsts = refs[:pairs], refs[pairs], refs[pairs + 1 : pairs + outs + 1]
-    refs = refs[pairs + outs + 1 :]
-    part_ref = refs[0] if product else left_ref
-    s1, s2, s3, send_sem, recv1, recv2, recv3, pair_sem, spread_sem = refs[1 if product else 0 :]
+    side_in, refs = split_side(side, pairs, refs)
+    srcs, refs = refs[:pairs], refs[pairs:]
+    row_outs, refs = refs[:row_count], refs[row_count:]
+    dsts, refs = refs[:outs], refs[outs:]
+    side_out, refs = refs[: len(side.outs) if side else 0], refs[len(side.outs) if side else 0 :]
+    part_ref, s1, s2, s3, out_ref, send_sem, recv1, recv2, recv3, pair_sem, spread_sem = refs[:11]
     ctx = lax.axis_index("ctx")
     wa = lax.axis_index("wa")
     half = out_ref.shape[0] // 2
@@ -1093,6 +1259,8 @@
     sibling, across = {"wa": wa ^ 1}, {"wa": wa ^ 2}
     meet_neighbours(ctx, wa, n_ctx, n_wa, SPREAD in kinds)
     pair_waits = start_pairs(kinds, srcs, dsts, n_wa, pair_sem, spread_sem)
+    if side:
+        side.bind(side_in, side_out, refs[11:])
     sends = []
 
     def begin(cond, act):
@@ -1153,18 +1321,20 @@
         zc = jnp.where(later < 0, n_ctx - 1 - i, paired)
         return jnp.where(mirrored, n_ctx - 1 - zc, zc)
 
-    def multiply(zc):
-        count = n_wa * half
-
-        def step(h, carry):
-            if by_position:
-                begin_row = jnp.where(h == 0, zc, 2 * n_ctx - 1 - zc) * count
-            else:
-                begin_row = (zc * 2 + h) * count
+    def multiply(zc, yc):
+        def rows_of(begin_row, count):
             rows = pl.ds(pl.multiple_of(begin_row, count), count)
             left = left_ref[rows, :]
             product = dot_t(left, right_ref[...]) if turned else dot(left, right_ref[...])
             part_ref[rows, :] = product.astype(BF16)
+
+        if not by_position:
+            rows_of((zc * n_wa + yc * 2) * 2 * half, 4 * half)
+            return
+
+        def step(h, carry):
+            span = jnp.where(h == 0, zc, 2 * n_ctx - 1 - zc)
+            rows_of((span * n_wa + yc * 2) * half, 2 * half)
             return carry
 
         lax.fori_loop(0, 2, step, 0)
@@ -1178,17 +1348,18 @@
 
     targets = [target(i) for i in range(n_ctx)]
     for i, zc in enumerate(targets):
-        if product:
-            multiply(zc)
         for yc in (y ^ 1, y):
+            multiply(zc, yc)
             for h in range(2):
                 at = index1(zc, yc, h)
                 send(mine(zc, yc * 2 + ((wa & 1) ^ 1), h), s1.at[at], recv1.at[at], sibling)
-        if i:
-            cross(targets[i - 1])
-    cross(targets[-1])
+        cross(zc)
+        if side:
+            side.step()
     pair_waits = [wait() for wait in pair_waits]
     for i, zc in enumerate(targets):
+        if side and i:
+            side.step()
         for h in range(2):
             at = index1(zc, y, h)
             here = zc * 2 + h
@@ -1215,18 +1386,24 @@
                 ]
                 for take, extra in ways:
                     begin(take, lambda extra=extra: add_up(out_ref, h * half, base + extra))
+    for ref, values in zip(row_outs, finish(out_ref[...], *[ref[...] for ref in row_ins])):
+        ref[...] = values.astype(ref.dtype)
+    if side:
+        side.finish()
     for made in sends:
         made.wait_send()
     for wait in pair_waits:
         wait()
 
 
-def scatter_tokens(left, right, turned, pairs, n_ctx, n_wa, by_position, call_id):
+def scatter_tokens(
+    left, right, turned, finish, rows_in, pairs, n_ctx, n_wa, by_position, call_id, side=None
+):
     n = n_ctx * n_wa
     rows = left.shape[0] // n
-    product = right is not None
-    operands = [left, right] if product else [left]
-    width = (right.shape[0] if turned else right.shape[1]) if product else left.shape[1]
+    width = right.shape[0] if turned else right.shape[1]
+    more = side.operands if side else []
+    row_types = [BF16] if finish is after_attention_back else [F32, BF16]
     half = rows // 2
     kinds = tuple(kind for kind, _ in pairs)
     anywhere = pl.BlockSpec(memory_space=pl.ANY)
@@ -1236,28 +1413,33 @@
         for pair in pairs
         for _ in range(pair_outs(pair[0]))
     ]
+    shapes += side.outs if side else []
     return pl.pallas_call(
-        partial(scatter_kernel, n_ctx, n_wa, by_position, product, turned, kinds),
-        in_specs=[vmem] * len(operands) + [anywhere] * len(pairs),
-        out_specs=[vmem] + [anywhere] * len(shapes),
-        out_shape=[jax.ShapeDtypeStruct((rows, width), F32)] + shapes,
-        scratch_shapes=[pltpu.VMEM((rows * n, width), BF16)] * product
-        + [
+        partial(
+            scatter_kernel, n_ctx, n_wa, by_position, turned, kinds, side, finish, len(rows_in)
+        ),
+        in_specs=[vmem] * (2 + len(rows_in)) + [anywhere] * (len(pairs) + len(more)),
+        out_specs=[vmem] * len(row_types) + [anywhere] * len(shapes),
+        out_shape=[jax.ShapeDtypeStruct((rows, width), dtype) for dtype in row_types] + shapes,
+        scratch_shapes=[
+            pltpu.VMEM((rows * n, width), BF16),
             pltpu.VMEM((4 * n_ctx, half, width), BF16),
             pltpu.VMEM((2 * n_ctx, half, width), BF16),
             pltpu.VMEM((4 * n_ctx, half, width), BF16),
+            pltpu.VMEM((rows, width), F32),
             pltpu.SemaphoreType.DMA((8 * n_ctx,)),
             pltpu.SemaphoreType.DMA((4 * n_ctx,)),
             pltpu.SemaphoreType.DMA((2 * n_ctx,)),
             pltpu.SemaphoreType.DMA((4 * n_ctx,)),
             pltpu.SemaphoreType.DMA((max(1, len(pairs)), 2)),
             pltpu.SemaphoreType.DMA((2, n)),
-        ],
+        ]
+        + (side.scratch if side else []),
         compiler_params=pltpu.CompilerParams(
             collective_id=call_id, has_side_effects=True, vmem_limit_bytes=ROOM
         ),
         cost_estimate=LINK_COST,
-    )(*operands, *[array for _, array in pairs])
+    )(left, right, *rows_in, *[array for _, array in pairs], *more)
 
 
 def per_device_heads(
@@ -1298,8 +1480,8 @@
     gains_own = jnp.concatenate([attn_gain, ffn_gain, q_gain, k_gain])
     gains_row = jnp.pad(gains_own, (0, extra * 2 * LANES - gains_own.shape[0]))
     attn_cols = pack_attn(w_query, w_key, w_value, gains_row.reshape(extra, 2 * LANES), n)
-    x_all, attn_half, attn_other = gather_tokens(
-        tokens[0], [(SPREAD, attn_cols)], n_ctx, n_wa, True, 1
+    x_all, attn_half, attn_other, ff_blocks = gather_tokens(
+        tokens[0], [(SPREAD, attn_cols)], n_ctx, n_wa, True, 1, PackColumns(w_gate, w_up, n)
     )
     gains = attn_half[:, half:].reshape(n, -1).astype(F32)
     attn_gain32 = gains[:, :d_rows].reshape(-1)
@@ -1307,37 +1489,40 @@
     qgain32 = gains[:, 2 * d_rows : 2 * d_rows + per].reshape(-1)
     kgain32 = gains[:, 2 * d_rows + per : 2 * d_rows + 2 * per].reshape(-1)
 
-    w_gate_b, dy_b, x_all = lax.optimization_barrier((w_gate, out_grad[0], x_all))
-    ff_blocks = pack_pair(w_gate_b, w_up, n)
+    dy_b, x_all = lax.optimization_barrier((out_grad[0], x_all))
     ff_half = swap(ff_blocks)
     dy_all = lax.all_gather(dy_b, AXES, axis=0, tiled=True)
 
-    x_own = tokens[0].astype(F32)
+    attn_gain_row, ffn_gain_row = attn_gain32.reshape(1, width), ffn_gain32.reshape(1, width)
     cosine, sine = rope_tables(stream)
     head_gain = jnp.concatenate([qgain32, qgain32, kgain32, kgain32]).reshape(1, 2 * LANES)
     n1_all, raw, q_b, kv_b, att, inv, w_qkv = attend(
-        doc_starts, x_all, attn_gain32.reshape(1, width), attn_half, attn_other, head_gain, cosine, sine
-    )
-    (branch,) = scatter_tokens(att, w_out, False, [], n_ctx, n_wa, True, 3)
-    middle = x_own + branch
-    n2_own, n2_back = jax.vjp(rms_norm, middle, ffn_gain32)
-    n2_all, ff_other = gather_tokens(
-        n2_own.astype(BF16), [(WHOLE, ff_half)], n_ctx, n_wa, False, 2
-    )
-    down_part, d_n2_part, gu_grad, down_grad = ffn(n2_all, dy_all, ff_half, ff_other, w_down)
+        doc_starts, x_all, attn_gain_row, attn_half, attn_other, head_gain, cosine, sine
+    )
+    middle, n2_own = scatter_tokens(
+        att, w_out, False, after_attention, [tokens[0], ffn_gain_row], [], n_ctx, n_wa, True, 3
+    )
+    n2_all, ff_other = gather_tokens(n2_own, [(WHOLE, ff_half)], n_ctx, n_wa, False, 2)
+    hidden, d_gu, gu_grad, w_gu = ffn(n2_all, dy_all, ff_half, ff_other, w_down)
     gu_grad = gu_grad.reshape(n, 2, half, 2 * ff_cols)
-    d_n2, gu_other = scatter_tokens(d_n2_part, None, False, [(PICK, gu_grad)], n_ctx, n_wa, False, 4)
-    gu_mine = lax.dynamic_index_in_dim(gu_grad, dp, 1, keepdims=False)
-    gu_sum = (gu_mine.astype(F32) + gu_other.astype(F32)).astype(BF16)
-    down_part, d_n2 = lax.optimization_barrier((down_part, d_n2))
+    d_middle, d_branch, gu_other, down_part, down_grad = scatter_tokens(
+        d_gu,
+        w_gu,
+        True,
+        after_ffn_back,
+        [middle, ffn_gain_row, out_grad[0]],
+        [(PICK, gu_grad)],
+        n_ctx,
+        n_wa,
+        False,
+        4,
+        DownProducts(dy_all, w_down, hidden),
+    )
     down = lax.psum_scatter(down_part, AXES, scatter_dimension=0, tiled=True).astype(F32)
     layer_out = middle + down
-    d_mid_part, _ = n2_back(d_n2)
-    d_middle = out_grad[0].astype(F32) + d_mid_part
-    db_all, down_other = gather_tokens(
-        d_middle.astype(BF16), [(WHOLE, down_grad)], n_ctx, n_wa, True, 5
-    )
-    gu_sum, db_all = lax.optimization_barrier((gu_sum, db_all))
+    db_all, down_other, gu_sum = gather_tokens(
+        d_branch, [(WHOLE, down_grad)], n_ctx, n_wa, True, 5, PairSum(gu_grad, gu_other)
+    )
     gu_rows = swap(gu_sum)
     d_qkv, out_w_grad, head_grad = attend_back(
         doc_starts, db_all, w_out, q_b, kv_b, att, inv, raw, head_gain, cosine, sine
@@ -1356,14 +1541,19 @@
     qkv_out = jnp.concatenate(
         [qkv_sum, jnp.broadcast_to(head_row[None], (n,) + head_row.shape)], axis=1
     )
-    d_n1, qkv_rows, qkv_others = scatter_tokens(
-        d_qkv, w_qkv, True, [(SPREAD, qkv_out)], n_ctx, n_wa, True, 6
-    )
-    out_w_other, gu_others, d_n1 = lax.optimization_barrier((out_w_other, gu_others, d_n1))
-    _, n1_back = jax.vjp(rms_norm, x_own, attn_gain32)
-    d_x_part, _ = n1_back(d_n1)
-    input_grad = d_middle + d_x_part
-
+    input_grad, qkv_rows, qkv_others = scatter_tokens(
+        d_qkv,
+        w_qkv,
+        True,
+        after_attention_back,
+        [tokens[0], attn_gain_row, d_middle],
+        [(SPREAD, qkv_out)],
+        n_ctx,
+        n_wa,
+        True,
+        6,
+    )
+    out_w_other, gu_others, input_grad = lax.optimization_barrier((out_w_other, gu_others, input_grad))
     gate_grad, up_grad, gu_sums = unpack_pair(gu_rows, gu_others, w_gate, w_up)
     q_grad, k_grad, v_grad, attn_sums, head_sums = unpack_attn(
         qkv_rows, qkv_others, w_query, w_key, w_value
@@ -1375,7 +1565,7 @@
     ffn_gain_grad = jnp.sum(gu_sums, axis=1) / ffn_gain.astype(F32)
     return (
         layer_out.astype(BF16)[None],
-        input_grad.astype(BF16)[None],
+        input_grad[None],
         attn_gain_grad,
         q_grad,
         k_grad,

time: 597 us -> 581 us (0.973)
  other arithmetic: 23.8 us -> 12.3 us
  Pallas kernels: 521 us -> 510 us
    pallas_call x8 -> x7, Pallas kernels: 447 us -> 438 us  [the longest x3 225 us: scatter_tokens(): pl.pallas_call(partial(scatter_kernel, n_ctx, n_wa, by_position, turned,...]
    convert_element_type x3 -> x0, other arithmetic: 6.05 us -> none  [the longest x1 3.87 us: per_device_heads(): gu_sum = (gu_mine.astype(F32) + gu_other.astype(F32)).astype(BF16)]
  transfers between devices with their start and end apart: 8 -> 8, of which waited for: 1 -> 1; matrix products, arithmetic and copies ran while one was open for 4% -> 3% of each run, Pallas kernels for 59% -> 60%
where the time goes in v6:
time: 581 us; the launch traced here: 575 us
  Pallas kernels  510 us (88%)
  between operations  14.5 us (2%)
  other arithmetic  12.3 us (2%)
  starting transfers between devices  11.9 us (2%)
  waiting for transfers between devices  10.1 us (2%)
  local copies, waits for them, and re-layouts  9.81 us (2%)
  matrix products  6.6 us (1%)
    pallas_call x3, Pallas kernels, scatter_tokens(): pl.pallas_call(partial(scatter_kernel, n_ctx, n_wa, by_position, turned,...  225 us
    pallas_call x3, Pallas kernels, gather_tokens(): pl.pallas_call(partial(gather_kernel, n_ctx, n_wa, by_position, kinds, si...  180 us
    pallas_call x1, Pallas kernels, attend_back(): pl.pallas_call(attend_back_kernel, grid=(stream // bq,), in_specs=[pl.Blo...  34.9 us
    pallas_call x1, Pallas kernels, ffn(): pl.pallas_call(ffn_kernel, grid=(stream // bt,), in_specs=[rows(width), r...  33.7 us
    pallas_call x1, Pallas kernels, attend(): pl.pallas_call(attend_kernel, grid=(stream // bq,), in_specs=[pl.BlockSpe...  28.2 us
  transfers between devices with their start and end apart: 8, of which 1 were waited for; matrix products, arithmetic and copies ran while one was open for 3% of the time, Pallas kernels for 60%

profile of v6, /device:TPU:0, one launch (start us, length us, event | category | flops | bytes accessed | tf_op | source)
XLA Modules:
  0.0 575.5 jit_solution(4974752562018285265)
XLA Ops:
  7.2 0.0 all-gather.2.cloned.1.call-start
  7.2 0.8 fusion.8
  8.0 0.6 reshape.53.gains_ref
  8.6 2.1 shard_map.255.refs_0_
  10.7 62.5 %shard_map.256 = (bf16[2048,2048]{1,0:T(8,128)(2,1)}, bf16[16,80,256]{2,1,0:T(8,128)(2,1)}, bf16[16,80,256]{2,1,0:T(8,128)(2,1)}, bf16[16,64,1024]{2,1,0:T(8,128)(2,1)}) custom-call(bf16[128,2048]{1,0:T(8,128)(2,1)} %bitcast.39, bf16[16,80,256]{2,1,0:T(8,128)(2,1)} %shard_map.255.refs_0_, bf16[128,8192]{1,0:T(8,128)(2,1)} %gate_w.1, bf16[128,8192]{1,0:T(8,128)(2,1)} %up_w.1), custom_call_target="tpu_custom_call" | custom-call | flops 49999998976 | bytes 16777216 | tf_op jit(solution)/shard_map/pallas_call | solution.py:1221
  73.3 0.0 all-gather.2.cloned.1.call-update
  73.3 3.7 all-to-all-start
  77.0 0.0 reduce-scatter.2.cloned.1.call-start
  77.1 0.9 slice_convert_fusion
  78.0 0.2 copy.31
  78.2 0.1 fusion.12
  78.2 0.1 reshape.54
  78.3 0.1 reshape.55
  78.4 0.6 pad_maximum_fusion.1
  79.0 0.6 fusion.11
  79.6 28.2 %shard_map.257 = (bf16[2048,2048]{1,0:T(8,128)(2,1)}, f32[2048,256]{1,0:T(8,128)}, bf16[2048,128]{1,0:T(8,128)(2,1)}, bf16[2048,128]{1,0:T(8,128)(2,1)}, bf16[20...) custom-call(s32[1,8]{1,0:T(1,128)} %starts.3, bf16[2048,2048]{1,0:T(8,128)(2,1)} %get-tuple-element.63.x_ref, ...), custom_call_target="tpu_custom_call" | custom-call | flops 20000000000 | bytes 33554432 | tf_op jit(solution)/shard_map/pallas_call | solution.py:480
  107.8 83.8 %shard_map.258 = (f32[128,2048]{1,0:T(8,128)}, bf16[128,2048]{1,0:T(8,128)(2,1)}) custom-call(bf16[2048,128]{1,0:T(8,128)(2,1)} %get-tuple-element.66.left_ref.att_ref, bf16[128,2048]{1,0:T(8,128)(2,1)} %w_out_ref.1, bf16[128,2048]{1,0:T(8,128)(2,1)} %bitcast.40, f32[1,2048]{1,0:T(1,128)} %bitcast.35), custom_call_target="tpu_custom_call" | custom-call | flops 49999998976 | bytes 16777216 | tf_op jit(solution)/shard_map/pallas_call | solution.py:1417
  191.6 0.0 all-to-all-done.refs_0_.own_ref
  191.6 0.0 copy-start.7
  191.6 1.4 copy-done.7
  193.0 54.5 %shard_map.259 = (bf16[2048,2048]{1,0:T(8,128)(2,1)}, bf16[16,64,1024]{2,1,0:T(8,128)(2,1)}) custom-call(bf16[128,2048]{1,0:T(8,128)(2,1)} %get-tuple-element.68.own_ref, bf16[16,64,1024]{2,1,0:T(8,128)(2,1)} %copy-done.7), custom_call_target="tpu_custom_call" | custom-call | flops 49999998976 | bytes 16777216 | tf_op jit(solution)/shard_map/pallas_call | solution.py:1221
  247.5 0.0 all-gather.2.cloned.1.call-done.dy_ref.refs_4_
  247.5 33.7 %shard_map.260 = (bf16[2048,512]{1,0:T(8,128)(2,1)}, bf16[2048,1024]{1,0:T(8,128)(2,1)}, bf16[2048,1024]{1,0:T(8,128)(2,1)}, bf16[2048,1024]{1,0:T(8,128)(2,1)}) custom-call(bf16[2048,2048]{1,0:T(8,128)(2,1)} %get-tuple-element.70.n2_ref, bf16[2048,2048]{1,0:T(8,128)(2,1)} %all-gather.2.cloned.1.call-done.dy_ref.refs_4_, bf16[16,64,1024]{2,1,0:T(8,128)(2,1)} %copy-done.7, ...), custom_call_target="tpu_custom_call" | custom-call | flops 21474836480 | bytes 33554432 | tf_op jit(solution)/shard_map/pallas_call | solution.py:671
  281.2 67.9 %shard_map.261 = (f32[128,2048]{1,0:T(8,128)}, bf16[128,2048]{1,0:T(8,128)(2,1)}, bf16[16,64,1024]{2,1,0:T(8,128)(2,1)}, bf16[2048,2048]{1,0:T(8,128)(2,1)}, bf16[512,2048]{1,0:T(8,128)(2,1)}) custom-call(bf16[2048,1024]{1,0:T(8,128)(2,1)} %get-tuple-element.73.left_ref, bf16[2048,1024]{1,0:T(8,128)(2,1)} %get-tuple-element.74.right_ref, ...), custom_call_target="tpu_custom_call" | custom-call | flops 49999998976 | bytes 16777216 | tf_op jit(solution)/shard_map/pallas_call | solution.py:1417
  349.2 0.0 reduce-scatter.2.cloned.1.call-update
  349.2 62.5 %shard_map.262 = (bf16[2048,2048]{1,0:T(8,128)(2,1)}, bf16[512,2048]{1,0:T(8,128)(2,1)}, bf16[16,64,1024]{2,1,0:T(8,128)(2,1)}) custom-call(bf16[128,2048]{1,0:T(8,128)(2,1)} %get-tuple-element.78.own_ref, bf16[512,2048]{1,0:T(8,128)(2,1)} %get-tuple-element.79.refs_0_, bf16[16,2,64,1024]{3,2,1,0:T(8,128)(2,1)} %bitcast.43, ...), custom_call_target="tpu_custom_call" | custom-call | flops 49999998976 | bytes 16777216 | tf_op jit(solution)/shard_map/pallas_call | solution.py:1221
  411.7 3.8 all-to-all-start.1
  415.5 34.9 %shard_map.263 = (bf16[2048,256]{1,0:T(8,128)(2,1)}, bf16[128,2048]{1,0:T(8,128)(2,1)}, f32[8,128]{1,0:T(8,128)}) custom-call(s32[1,8]{1,0:T(1,128)} %starts.3, bf16[2048,2048]{1,0:T(8,128)(2,1)} %get-tuple-element.81.db_ref, bf16[128,2048]{1,0:T(8,128)(2,1)} %w_out_ref.1, bf16[2048,128]{1,0:T(8,128)(2,1)} %get-tuple-element.82.q_ref, ...), custom_call_target="tpu_custom_call" | custom-call | flops 30000001024 | bytes 33554432 | tf_op jit(solution)/shard_map/pallas_call | solution.py:599
  450.4 1.6 collective-permute-start.2
  452.0 6.6 %convolution_convert_fusion = bf16[2048,256]{1,0:T(8,128)(2,1)S(1)} fusion(bf16[2048,2048]{1,0:T(8,128)(2,1)} %get-tuple-element.87, bf16[2048,256]{1,0:T(8,128)(2,1)} %get-tuple-element.88.left_ref), kind=kOutput, calls=%fused_computation.1 | convolution fusion | flops 2148007936 | bytes 10485760 | tf_op jit(solution)/shard_map/dot_general | solution.py:1473
  458.6 0.7 collective-permute-start.1
  459.3 0.0 copy-done.8
  459.3 0.0 copy-done.9
  459.3 2.8 convert_add_fusion
  462.1 1.4 collective-permute-start
  463.6 0.0 collective-permute-done.2
  463.6 10.0 %collective-permute-done.1 = bf16[16,64,256]{2,1,0:T(8,128)(2,1)} collective-permute-done((bf16[16,64,256]{2,1,0:T(8,128)(2,1)S(1)}, bf16[16,64,256]{2,1,0:T(8,128)(2,1)}, u32[]{:S(2)}, u32[]{:S(2)}) %collective-permute-start.1) | collective-permute-done | bytes 524320 | tf_op jit(solution)/shard_map/ppermute | solution.py:1532
  473.6 0.0 all-to-all-done.1.own_ref
  473.6 0.6 collective-permute-start.3
  474.2 1.2 fusion
  475.4 0.9 pad_maximum_fusion.refs_3_
  476.3 73.0 %shard_map.264 = (bf16[128,2048]{1,0:T(8,128)(2,1)}, bf16[16,80,256]{2,1,0:T(8,128)(2,1)}, bf16[16,80,256]{2,1,0:T(8,128)(2,1)}) custom-call(bf16[2048,256]{1,0:T(8,128)(2,1)} %get-tuple-element.88.left_ref, bf16[2048,256]{1,0:T(8,128)(2,1)} %get-tuple-element.92.right_ref, bf16[128,2048]{1,0:T(8,128)(2,1)} %bitcast.41, f32[1,2048]{1,0:T(1,128)} %bitcast.34, ...), custom_call_target="tpu_custom_call" | custom-call | flops 49999998976 | bytes 16777216 | tf_op jit(solution)/shard_map/pallas_call | solution.py:1417
  549.3 0.0 copy-done.2
  549.3 0.0 copy-done.5
  549.3 0.0 copy-done.6
  549.3 0.0 copy-start.3
  549.4 1.1 copy-done.3
  550.4 1.1 copy-done.4
  551.5 1.4 shard_map.265
  552.9 0.1 reduce_sum.18
  553.0 0.1 fusion.13
  553.1 0.6 fusion.9
  553.7 0.0 collective-permute-done
  553.7 0.0 collective-permute-done.3.other_ref
  553.7 1.6 copy-done
  555.3 1.6 copy-done.1
  556.9 5.8 %shard_map.266 = (f32[128,8192]{1,0:T(8,128)}, f32[128,8192]{1,0:T(8,128)}, f32[128,128]{1,0:T(8,128)S(1)}) custom-call(bf16[16,64,1024]{2,1,0:T(8,128)(2,1)S(1)} %all-to-all-done.1.own_ref, bf16[16,64,1024]{2,1,0:T(8,128)(2,1)} %collective-permute-done.3.other_ref, bf16[128,8192]{1,0:T(8,128)(2,1)S(1)} %copy-done, bf16[128,8192]{1,0:T(8,128)(2,1)S(1)} %copy-done.1), custom_call_target="tpu_custom_call" | custom-call | tf_op jit(solution)/shard_map/pallas_call | solution.py:790
  562.7 0.1 reduce_sum.19
  562.8 0.5 convert_divide_fusion
  563.3 2.4 convert_add_fusion.2
  565.7 0.0 copy-done.10
  565.7 1.9 fusion.1
  567.7 0.0 copy-done.11
  567.7 0.8 copy.33
  (21 shorter events, 0.1 us)
Async XLA Ops:
  7.2 240.3 %all-gather.2.cloned.1.call-start = ((), (), s32[]{:S(2)}) async-start(), calls=%async_computation.3 | async-start | bytes 8912896 | tf_op jit(solution)/shard_map/all_gather | solution.py:1494
  73.3 118.3 %all-to-all-start = ((bf16[16,64,1024]{2,1,0:T(8,128)(2,1)}), bf16[16,64,1024]{2,1,0:T(8,128)(2,1)S(1)}, u32[]{:S(2)}, u32[]{:S(2)}) async-start(bf16[16,64,1024]{2,1,0:T(8,128)(2,1)} %get-tuple-element.69), calls=%async_computation | async-start | bytes 4194304 | tf_op jit(solution)/shard_map/all_to_all | solution.py:1476
  77.0 488.7 %reduce-scatter.2.cloned.1.call-start = ((), (), s32[]{:S(2)}) async-start(), calls=%async_computation.4 | async-start | bytes 8912896 | tf_op jit(solution)/shard_map/reduce_scatter | solution.py:1521
  191.6 1.4 copy-start.7
  411.7 61.9 %all-to-all-start.1 = ((bf16[16,64,1024]{2,1,0:T(8,128)(2,1)}), bf16[16,64,1024]{2,1,0:T(8,128)(2,1)S(1)}, u32[]{:S(2)}, u32[]{:S(2)}) async-start(bf16[16,64,1024]{2,1,0:T(8,128)(2,1)} %get-tuple-element.90), calls=%async_computation.2 | async-start | bytes 4194304 | tf_op jit(solution)/shard_map/all_to_all | solution.py:1476
  450.4 13.2 %collective-permute-start.2 = (f32[8,128]{1,0:T(8,128)}, f32[8,128]{1,0:T(8,128)S(1)}, u32[]{:S(2)}, u32[]{:S(2)}) collective-permute-start(f32[8,128]{1,0:T(8,128)} %get-tuple-element.89), channel_id=1, source_target_pairs={{0,16},{16,0},{1,17},{17,1},{2,18},{18,2},{3,19},{19,3},{4,20},{20... | collective-permute-start | bytes 12296 | tf_op jit(solution)/shard_map/ppermute | solution.py:1535
  452.0 7.3 %copy-start.8 = (bf16[512,2048]{1,0:T(8,128)(2,1)S(1)}, bf16[512,2048]{1,0:T(8,128)(2,1)}, u32[]{:S(2)}) copy-start(bf16[512,2048]{1,0:T(8,128)(2,1)} %get-tuple-element.79.refs_0_) | copy-start | bytes 6291460
  452.0 7.3 %copy-start.9 = (bf16[512,2048]{1,0:T(8,128)(2,1)S(1)}, bf16[512,2048]{1,0:T(8,128)(2,1)}, u32[]{:S(2)}) copy-start(bf16[512,2048]{1,0:T(8,128)(2,1)} %get-tuple-element.110) | copy-start | bytes 6291460
  458.6 14.9 %collective-permute-start.1 = (bf16[16,64,256]{2,1,0:T(8,128)(2,1)S(1)}, bf16[16,64,256]{2,1,0:T(8,128)(2,1)}, u32[]{:S(2)}, u32[]{:S(2)}) collective-permute-start(bf16[16,64,256]{2,1,0:T(8,128)(2,1)S(1)} %dynamic-slice_bitcast_fusion), channel_id=1, source_target_pairs={{0,16},{16,0},{1,17},{17,1},{2,18},{18,2},{3,19},{19,3},{4,20},{20... | collective-permute-start | bytes 1572872 | tf_op jit(solution)/shard_map/ppermute | solution.py:1532
  459.3 4.2 copy-start.12
  462.1 91.5 %collective-permute-start = (bf16[128,2048]{1,0:T(8,128)(2,1)}, bf16[128,2048]{1,0:T(8,128)(2,1)}, u32[]{:S(2)}, u32[]{:S(2)}) collective-permute-start(bf16[128,2048]{1,0:T(8,128)(2,1)} %get-tuple-element.86), channel_id=1, source_target_pairs={{0,16},{16,0},{1,17},{17,1},{2,18},{18,2},{3,19},{19,3},{4,20},{20... | collective-permute-start | bytes 1572872 | tf_op jit(solution)/shard_map/ppermute | solution.py:1530
  473.6 80.1 %collective-permute-start.3 = (bf16[16,64,1024]{2,1,0:T(8,128)(2,1)S(1)}, bf16[16,64,1024]{2,1,0:T(8,128)(2,1)}, u32[]{:S(2)}, u32[]{:S(2)}) collective-permute-start(bf16[16,64,1024]{2,1,0:T(8,128)(2,1)S(1)} %all-to-all-done.1.own_ref), channel_id=1, source_target_pairs={{0,16},{16,0},{1,17},{17,1},{2,18},{18,2},{3,19},{19,3},{4,20},{20... | collective-permute-start | bytes 6291464 | tf_op jit(solution)/shard_map/ppermute | solution.py:1537
  476.3 73.0 %copy-start.2 = (bf16[128,2048]{1,0:T(8,128)(2,1)S(1)}, bf16[128,2048]{1,0:T(8,128)(2,1)}, u32[]{:S(2)}) copy-start(bf16[128,2048]{1,0:T(8,128)(2,1)} %wq_ref.1) | copy-start | bytes 1572868
  476.3 73.0 %copy-start.5 = (bf16[128,512]{1,0:T(8,128)(2,1)S(1)}, bf16[128,512]{1,0:T(8,128)(2,1)}, u32[]{:S(2)}) copy-start(bf16[128,512]{1,0:T(8,128)(2,1)} %wk_ref.1) | copy-start | bytes 393220
  476.3 73.0 %copy-start.6 = (bf16[128,512]{1,0:T(8,128)(2,1)S(1)}, bf16[128,512]{1,0:T(8,128)(2,1)}, u32[]{:S(2)}) copy-start(bf16[128,512]{1,0:T(8,128)(2,1)} %wv_ref.1) | copy-start | bytes 393220
  549.3 1.1 copy-start.3
  550.4 1.1 copy-start.4
  553.7 1.6 copy-start
  555.3 1.6 copy-start.1
  556.9 5.9 %copy-start.13 = (bf16[128]{0:T(256)(128)(2,1)S(1)}, bf16[128]{0:T(256)(128)(2,1)}, u32[]{:S(2)}) copy-start(bf16[128]{0:T(256)(128)(2,1)} %param.26) | copy-start | bytes 772
  556.9 6.0 %copy-start.14 = (bf16[128]{0:T(256)(128)(2,1)S(1)}, bf16[128]{0:T(256)(128)(2,1)}, u32[]{:S(2)}) copy-start(bf16[128]{0:T(256)(128)(2,1)} %param.19) | copy-start | bytes 772
  562.7 3.0 copy-start.10
  563.3 4.3 copy-start.11
Sparse Core Ops, SparseCore 0:
  73.4 128.6 all-gather.1
  349.3 132.9 reduce-scatter.1

commit v7 on v6

--- a/solution.py
+++ b/solution.py
@@ -329,7 +329,7 @@
 AXES = ("ctx", "wa")
 LANES = 2 * HD
 ROWS_BLOCK = 256
-FFN_BLOCK = 256
+FFN_BLOCK = 512
 ROOM = 60 * 2**20
 SIDE_ROWS = 256
 LOG2E = 1.4426950408889634
@@ -695,7 +695,7 @@
     low = jnp.where(first, 0, half)
     high = half - low
     share = n // KV
-    gains_ref[...] = jnp.sum(own_ref[:, half : half + 8, :].astype(F32), axis=0)
+    gains_ref[...] = jnp.sum(own_ref[:, half:, :].astype(F32), axis=0)
     for begin, ref in ((low, own_ref), (high, other_ref)):
         rows = pl.ds(pl.multiple_of(begin, half), half)
         total = jnp.zeros((half, LANES), F32)
@@ -729,7 +729,7 @@
             jax.ShapeDtypeStruct(w_key.shape, F32),
             jax.ShapeDtypeStruct(w_value.shape, F32),
             jax.ShapeDtypeStruct((d_rows, LANES), F32),
-            jax.ShapeDtypeStruct((8, 2 * LANES), F32),
+            jax.ShapeDtypeStruct((own.shape[1] - d_rows // 2, 2 * LANES), F32),
         ],
         compiler_params=pltpu.CompilerParams(vmem_limit_bytes=32 * 2**20),
     )(own, other, w_query, w_key, w_value)

time: 581 us -> 580 us (level)
  no operation moved by 1% of the time
where the time goes in v7:
time: 580 us; the launch traced here: 574 us
  Pallas kernels  509 us (88%)
  between operations  14.5 us (2%)
  other arithmetic  12.3 us (2%)
  starting transfers between devices  11.9 us (2%)
  waiting for transfers between devices  10.1 us (2%)
  local copies, waits for them, and re-layouts  9.81 us (2%)
  matrix products  6.6 us (1%)
    pallas_call x3, Pallas kernels, scatter_tokens(): pl.pallas_call(partial(scatter_kernel, n_ctx, n_wa, by_position, turned,...  224 us
    pallas_call x3, Pallas kernels, gather_tokens(): pl.pallas_call(partial(gather_kernel, n_ctx, n_wa, by_position, kinds, si...  180 us
    pallas_call x1, Pallas kernels, attend_back(): pl.pallas_call(attend_back_kernel, grid=(stream // bq,), in_specs=[pl.Blo...  35.7 us
    pallas_call x1, Pallas kernels, ffn(): pl.pallas_call(ffn_kernel, grid=(stream // bt,), in_specs=[rows(width), r...  32.5 us
    pallas_call x1, Pallas kernels, attend(): pl.pallas_call(attend_kernel, grid=(stream // bq,), in_specs=[pl.BlockSpe...  28.6 us
  transfers between devices with their start and end apart: 8, of which 1 were waited for; matrix products, arithmetic and copies ran while one was open for 3% of the time, Pallas kernels for 60%

profile of v7, /device:TPU:0, one launch (start us, length us, event | category | flops | bytes accessed | tf_op | source)
XLA Modules:
  0.0 574.3 jit_solution(1897559898665780892)
XLA Ops:
  7.2 0.0 all-gather.2.cloned.1.call-start
  7.2 0.8 fusion.8
  8.0 0.6 reshape.53.gains_ref
  8.6 2.1 shard_map.255.refs_0_
  10.7 62.5 %shard_map.256 = (bf16[2048,2048]{1,0:T(8,128)(2,1)}, bf16[16,80,256]{2,1,0:T(8,128)(2,1)}, bf16[16,80,256]{2,1,0:T(8,128)(2,1)}, bf16[16,64,1024]{2,1,0:T(8,128)(2,1)}) custom-call(bf16[128,2048]{1,0:T(8,128)(2,1)} %bitcast.39, bf16[16,80,256]{2,1,0:T(8,128)(2,1)} %shard_map.255.refs_0_, bf16[128,8192]{1,0:T(8,128)(2,1)} %gate_w.1, bf16[128,8192]{1,0:T(8,128)(2,1)} %up_w.1), custom_call_target="tpu_custom_call" | custom-call | flops 49999998976 | bytes 16777216 | tf_op jit(solution)/shard_map/pallas_call | solution.py:1221
  73.3 0.0 all-gather.2.cloned.1.call-update
  73.3 3.7 all-to-all-start
  77.0 0.0 reduce-scatter.2.cloned.1.call-start
  77.1 0.9 slice_convert_fusion
  78.0 0.2 copy.31
  78.2 0.1 fusion.12
  78.2 0.1 reshape.54
  78.3 0.1 reshape.55
  78.4 0.6 pad_maximum_fusion.1
  79.0 0.6 fusion.11
  79.6 28.6 %shard_map.257 = (bf16[2048,2048]{1,0:T(8,128)(2,1)}, f32[2048,256]{1,0:T(8,128)}, bf16[2048,128]{1,0:T(8,128)(2,1)}, bf16[2048,128]{1,0:T(8,128)(2,1)}, bf16[20...) custom-call(s32[1,8]{1,0:T(1,128)} %starts.3, bf16[2048,2048]{1,0:T(8,128)(2,1)} %get-tuple-element.63.x_ref, ...), custom_call_target="tpu_custom_call" | custom-call | flops 20000000000 | bytes 33554432 | tf_op jit(solution)/shard_map/pallas_call | solution.py:480
  108.3 83.7 %shard_map.258 = (f32[128,2048]{1,0:T(8,128)}, bf16[128,2048]{1,0:T(8,128)(2,1)}) custom-call(bf16[2048,128]{1,0:T(8,128)(2,1)} %get-tuple-element.66.left_ref.att_ref, bf16[128,2048]{1,0:T(8,128)(2,1)} %w_out_ref.1, bf16[128,2048]{1,0:T(8,128)(2,1)} %bitcast.40, f32[1,2048]{1,0:T(1,128)} %bitcast.35), custom_call_target="tpu_custom_call" | custom-call | flops 49999998976 | bytes 16777216 | tf_op jit(solution)/shard_map/pallas_call | solution.py:1417
  192.0 0.0 all-to-all-done.refs_0_.own_ref
  192.0 0.0 copy-start.7
  192.0 1.4 copy-done.7
  193.4 54.3 %shard_map.259 = (bf16[2048,2048]{1,0:T(8,128)(2,1)}, bf16[16,64,1024]{2,1,0:T(8,128)(2,1)}) custom-call(bf16[128,2048]{1,0:T(8,128)(2,1)} %get-tuple-element.68.own_ref, bf16[16,64,1024]{2,1,0:T(8,128)(2,1)} %copy-done.7), custom_call_target="tpu_custom_call" | custom-call | flops 49999998976 | bytes 16777216 | tf_op jit(solution)/shard_map/pallas_call | solution.py:1221
  247.7 0.0 all-gather.2.cloned.1.call-done.dy_ref.refs_4_
  247.7 32.5 %shard_map.260 = (bf16[2048,512]{1,0:T(8,128)(2,1)}, bf16[2048,1024]{1,0:T(8,128)(2,1)}, bf16[2048,1024]{1,0:T(8,128)(2,1)}, bf16[2048,1024]{1,0:T(8,128)(2,1)}) custom-call(bf16[2048,2048]{1,0:T(8,128)(2,1)} %get-tuple-element.70.n2_ref, bf16[2048,2048]{1,0:T(8,128)(2,1)} %all-gather.2.cloned.1.call-done.dy_ref.refs_4_, bf16[16,64,1024]{2,1,0:T(8,128)(2,1)} %copy-done.7, ...), custom_call_target="tpu_custom_call" | custom-call | flops 21474836480 | bytes 33554432 | tf_op jit(solution)/shard_map/pallas_call | solution.py:671
  280.3 67.7 %shard_map.261 = (f32[128,2048]{1,0:T(8,128)}, bf16[128,2048]{1,0:T(8,128)(2,1)}, bf16[16,64,1024]{2,1,0:T(8,128)(2,1)}, bf16[2048,2048]{1,0:T(8,128)(2,1)}, bf16[512,2048]{1,0:T(8,128)(2,1)}) custom-call(bf16[2048,1024]{1,0:T(8,128)(2,1)} %get-tuple-element.73.left_ref, bf16[2048,1024]{1,0:T(8,128)(2,1)} %get-tuple-element.74.right_ref, ...), custom_call_target="tpu_custom_call" | custom-call | flops 49999998976 | bytes 16777216 | tf_op jit(solution)/shard_map/pallas_call | solution.py:1417
  348.0 0.0 reduce-scatter.2.cloned.1.call-update
  348.0 62.6 %shard_map.262 = (bf16[2048,2048]{1,0:T(8,128)(2,1)}, bf16[512,2048]{1,0:T(8,128)(2,1)}, bf16[16,64,1024]{2,1,0:T(8,128)(2,1)}) custom-call(bf16[128,2048]{1,0:T(8,128)(2,1)} %get-tuple-element.78.own_ref, bf16[512,2048]{1,0:T(8,128)(2,1)} %get-tuple-element.79.refs_0_, bf16[16,2,64,1024]{3,2,1,0:T(8,128)(2,1)} %bitcast.43, ...), custom_call_target="tpu_custom_call" | custom-call | flops 49999998976 | bytes 16777216 | tf_op jit(solution)/shard_map/pallas_call | solution.py:1221
  410.7 3.8 all-to-all-start.1
  414.5 35.7 %shard_map.263 = (bf16[2048,256]{1,0:T(8,128)(2,1)}, bf16[128,2048]{1,0:T(8,128)(2,1)}, f32[8,128]{1,0:T(8,128)}) custom-call(s32[1,8]{1,0:T(1,128)} %starts.3, bf16[2048,2048]{1,0:T(8,128)(2,1)} %get-tuple-element.81.db_ref, bf16[128,2048]{1,0:T(8,128)(2,1)} %w_out_ref.1, bf16[2048,128]{1,0:T(8,128)(2,1)} %get-tuple-element.82.q_ref, ...), custom_call_target="tpu_custom_call" | custom-call | flops 30000001024 | bytes 33554432 | tf_op jit(solution)/shard_map/pallas_call | solution.py:599
  450.2 0.6 collective-permute-start.2
  450.8 6.6 %convolution_convert_fusion = bf16[2048,256]{1,0:T(8,128)(2,1)S(1)} fusion(bf16[2048,2048]{1,0:T(8,128)(2,1)} %get-tuple-element.87, bf16[2048,256]{1,0:T(8,128)(2,1)} %get-tuple-element.88.left_ref), kind=kOutput, calls=%fused_computation.1 | convolution fusion | flops 2148007936 | bytes 10485760 | tf_op jit(solution)/shard_map/dot_general | solution.py:1473
  457.4 1.6 collective-permute-start.1
  459.1 0.0 copy-done.8
  459.1 0.0 copy-done.9
  459.1 2.8 convert_add_fusion
  461.9 0.5 collective-permute-start
  462.4 0.0 collective-permute-done.2
  462.4 0.0 copy-done.12
  462.4 10.0 %collective-permute-done.1 = bf16[16,64,256]{2,1,0:T(8,128)(2,1)} collective-permute-done((bf16[16,64,256]{2,1,0:T(8,128)(2,1)S(1)}, bf16[16,64,256]{2,1,0:T(8,128)(2,1)}, u32[]{:S(2)}, u32[]{:S(2)}) %collective-permute-start.1) | collective-permute-done | bytes 524320 | tf_op jit(solution)/shard_map/ppermute | solution.py:1532
  472.4 0.0 all-to-all-done.1.own_ref
  472.4 1.6 collective-permute-start.3
  474.0 1.2 fusion
  475.2 0.9 pad_maximum_fusion.refs_3_
  476.1 72.1 %shard_map.264 = (bf16[128,2048]{1,0:T(8,128)(2,1)}, bf16[16,80,256]{2,1,0:T(8,128)(2,1)}, bf16[16,80,256]{2,1,0:T(8,128)(2,1)}) custom-call(bf16[2048,256]{1,0:T(8,128)(2,1)} %get-tuple-element.88.left_ref, bf16[2048,256]{1,0:T(8,128)(2,1)} %get-tuple-element.92.right_ref, bf16[128,2048]{1,0:T(8,128)(2,1)} %bitcast.41, f32[1,2048]{1,0:T(1,128)} %bitcast.34, ...), custom_call_target="tpu_custom_call" | custom-call | flops 49999998976 | bytes 16777216 | tf_op jit(solution)/shard_map/pallas_call | solution.py:1417
  548.1 0.0 copy-done.2
  548.1 0.0 copy-done.5
  548.1 0.0 copy-done.6
  548.2 0.0 copy-start.3
  548.2 1.1 copy-done.3
  549.2 1.1 copy-done.4
  550.3 1.4 shard_map.265
  551.7 0.1 reduce_sum.18
  551.8 0.1 fusion.13
  551.9 0.6 fusion.9
  552.5 0.0 collective-permute-done
  552.5 0.0 collective-permute-done.3.other_ref
  552.5 1.6 copy-done
  554.1 1.6 copy-done.1
  555.7 5.8 %shard_map.266 = (f32[128,8192]{1,0:T(8,128)}, f32[128,8192]{1,0:T(8,128)}, f32[128,128]{1,0:T(8,128)S(1)}) custom-call(bf16[16,64,1024]{2,1,0:T(8,128)(2,1)S(1)} %all-to-all-done.1.own_ref, bf16[16,64,1024]{2,1,0:T(8,128)(2,1)} %collective-permute-done.3.other_ref, bf16[128,8192]{1,0:T(8,128)(2,1)S(1)} %copy-done, bf16[128,8192]{1,0:T(8,128)(2,1)S(1)} %copy-done.1), custom_call_target="tpu_custom_call" | custom-call | tf_op jit(solution)/shard_map/pallas_call | solution.py:790
  561.5 0.1 reduce_sum.19
  561.6 0.0 copy-done.13
  561.6 0.5 convert_divide_fusion
  562.2 2.4 convert_add_fusion.2
  564.5 1.9 fusion.1
  566.5 0.8 copy.33
  (21 shorter events, 0.1 us)
Async XLA Ops:
  7.2 240.6 %all-gather.2.cloned.1.call-start = ((), (), s32[]{:S(2)}) async-start(), calls=%async_computation.3 | async-start | bytes 8912896 | tf_op jit(solution)/shard_map/all_gather | solution.py:1494
  73.3 118.7 %all-to-all-start = ((bf16[16,64,1024]{2,1,0:T(8,128)(2,1)}), bf16[16,64,1024]{2,1,0:T(8,128)(2,1)S(1)}, u32[]{:S(2)}, u32[]{:S(2)}) async-start(bf16[16,64,1024]{2,1,0:T(8,128)(2,1)} %get-tuple-element.69), calls=%async_computation | async-start | bytes 4194304 | tf_op jit(solution)/shard_map/all_to_all | solution.py:1476
  77.0 487.5 %reduce-scatter.2.cloned.1.call-start = ((), (), s32[]{:S(2)}) async-start(), calls=%async_computation.4 | async-start | bytes 8912896 | tf_op jit(solution)/shard_map/reduce_scatter | solution.py:1521
  192.0 1.4 copy-start.7
  410.7 61.7 %all-to-all-start.1 = ((bf16[16,64,1024]{2,1,0:T(8,128)(2,1)}), bf16[16,64,1024]{2,1,0:T(8,128)(2,1)S(1)}, u32[]{:S(2)}, u32[]{:S(2)}) async-start(bf16[16,64,1024]{2,1,0:T(8,128)(2,1)} %get-tuple-element.90), calls=%async_computation.2 | async-start | bytes 4194304 | tf_op jit(solution)/shard_map/all_to_all | solution.py:1476
  450.2 12.2 %collective-permute-start.2 = (f32[8,128]{1,0:T(8,128)}, f32[8,128]{1,0:T(8,128)S(1)}, u32[]{:S(2)}, u32[]{:S(2)}) collective-permute-start(f32[8,128]{1,0:T(8,128)} %get-tuple-element.89), channel_id=1, source_target_pairs={{0,16},{16,0},{1,17},{17,1},{2,18},{18,2},{3,19},{19,3},{4,20},{20... | collective-permute-start | bytes 12296 | tf_op jit(solution)/shard_map/ppermute | solution.py:1535
  450.8 8.3 %copy-start.8 = (bf16[512,2048]{1,0:T(8,128)(2,1)S(1)}, bf16[512,2048]{1,0:T(8,128)(2,1)}, u32[]{:S(2)}) copy-start(bf16[512,2048]{1,0:T(8,128)(2,1)} %get-tuple-element.79.refs_0_) | copy-start | bytes 6291460
  450.8 8.3 %copy-start.9 = (bf16[512,2048]{1,0:T(8,128)(2,1)S(1)}, bf16[512,2048]{1,0:T(8,128)(2,1)}, u32[]{:S(2)}) copy-start(bf16[512,2048]{1,0:T(8,128)(2,1)} %get-tuple-element.110) | copy-start | bytes 6291460
  457.4 14.9 %collective-permute-start.1 = (bf16[16,64,256]{2,1,0:T(8,128)(2,1)S(1)}, bf16[16,64,256]{2,1,0:T(8,128)(2,1)}, u32[]{:S(2)}, u32[]{:S(2)}) collective-permute-start(bf16[16,64,256]{2,1,0:T(8,128)(2,1)S(1)} %dynamic-slice_bitcast_fusion), channel_id=1, source_target_pairs={{0,16},{16,0},{1,17},{17,1},{2,18},{18,2},{3,19},{19,3},{4,20},{20... | collective-permute-start | bytes 1572872 | tf_op jit(solution)/shard_map/ppermute | solution.py:1532
  459.1 3.3 copy-start.12
  461.9 90.6 %collective-permute-start = (bf16[128,2048]{1,0:T(8,128)(2,1)}, bf16[128,2048]{1,0:T(8,128)(2,1)}, u32[]{:S(2)}, u32[]{:S(2)}) collective-permute-start(bf16[128,2048]{1,0:T(8,128)(2,1)} %get-tuple-element.86), channel_id=1, source_target_pairs={{0,16},{16,0},{1,17},{17,1},{2,18},{18,2},{3,19},{19,3},{4,20},{20... | collective-permute-start | bytes 1572872 | tf_op jit(solution)/shard_map/ppermute | solution.py:1530
  472.4 80.1 %collective-permute-start.3 = (bf16[16,64,1024]{2,1,0:T(8,128)(2,1)S(1)}, bf16[16,64,1024]{2,1,0:T(8,128)(2,1)}, u32[]{:S(2)}, u32[]{:S(2)}) collective-permute-start(bf16[16,64,1024]{2,1,0:T(8,128)(2,1)S(1)} %all-to-all-done.1.own_ref), channel_id=1, source_target_pairs={{0,16},{16,0},{1,17},{17,1},{2,18},{18,2},{3,19},{19,3},{4,20},{20... | collective-permute-start | bytes 6291464 | tf_op jit(solution)/shard_map/ppermute | solution.py:1537
  476.1 72.1 %copy-start.2 = (bf16[128,2048]{1,0:T(8,128)(2,1)S(1)}, bf16[128,2048]{1,0:T(8,128)(2,1)}, u32[]{:S(2)}) copy-start(bf16[128,2048]{1,0:T(8,128)(2,1)} %wq_ref.1) | copy-start | bytes 1572868
  476.1 72.1 %copy-start.5 = (bf16[128,512]{1,0:T(8,128)(2,1)S(1)}, bf16[128,512]{1,0:T(8,128)(2,1)}, u32[]{:S(2)}) copy-start(bf16[128,512]{1,0:T(8,128)(2,1)} %wk_ref.1) | copy-start | bytes 393220
  476.1 72.1 %copy-start.6 = (bf16[128,512]{1,0:T(8,128)(2,1)S(1)}, bf16[128,512]{1,0:T(8,128)(2,1)}, u32[]{:S(2)}) copy-start(bf16[128,512]{1,0:T(8,128)(2,1)} %wv_ref.1) | copy-start | bytes 393220
  548.2 1.1 copy-start.3
  549.2 1.1 copy-start.4
  552.5 1.6 copy-start
  554.1 1.6 copy-start.1
  555.7 5.9 %copy-start.13 = (bf16[128]{0:T(256)(128)(2,1)S(1)}, bf16[128]{0:T(256)(128)(2,1)}, u32[]{:S(2)}) copy-start(bf16[128]{0:T(256)(128)(2,1)} %param.26) | copy-start | bytes 772
  555.7 6.0 %copy-start.14 = (bf16[128]{0:T(256)(128)(2,1)S(1)}, bf16[128]{0:T(256)(128)(2,1)}, u32[]{:S(2)}) copy-start(bf16[128]{0:T(256)(128)(2,1)} %param.19) | copy-start | bytes 772
  561.5 3.0 copy-start.10
  562.2 4.3 copy-start.11
Sparse Core Ops, SparseCore 0:
  73.4 128.6 all-gather.1
  348.1 132.9 reduce-scatter.1

commit v8 on v7

--- a/solution.py
+++ b/solution.py
@@ -516,7 +516,7 @@
 
 def attend_back_kernel(
     starts, db_ref, w_out_ref, q_ref, kv_ref, att_ref, inv_ref, raw_ref, head_gain_ref, cos_ref, sin_ref,
-    d_ref, w_grad_ref, gain_ref, dkv_ref, w_acc_ref,
+    d_ref, gain_ref, dkv_ref,
 ):
     block = pl.program_id(0)
     bq = db_ref.shape[0]
@@ -525,13 +525,11 @@
     @pl.when(block == 0)
     def _():
         dkv_ref[...] = jnp.zeros_like(dkv_ref)
-        w_acc_ref[...] = jnp.zeros_like(w_acc_ref)
         gain_ref[...] = jnp.zeros_like(gain_ref)
 
     db = db_ref[...]
     att = att_ref[...]
     da = dot_t(db, w_out_ref[...])
-    w_acc_ref[...] += t_dot(att, db)
     q2 = stack_heads(q_ref[...].astype(F32), True).astype(BF16)
     da2 = stack_heads(da, False).astype(BF16)
     prod = da.astype(BF16).astype(F32) * att.astype(F32)
@@ -580,7 +578,6 @@
             return carry
 
         lax.fori_loop(0, pl.num_programs(0), finish, 0)
-        w_grad_ref[...] = w_acc_ref[...].astype(BF16)
 
 
 def attend_back(starts, db_all, w_out, q, kv, att, inv, raw, head_gain, cosine, sine):
@@ -612,13 +609,12 @@
             whole((stream, LANES)),
             whole((stream, LANES)),
         ],
-        out_specs=[kept((stream, 2 * LANES)), kept(w_out.shape), kept((8, LANES))],
+        out_specs=[kept((stream, 2 * LANES)), kept((8, LANES))],
         out_shape=[
             jax.ShapeDtypeStruct((stream, 2 * LANES), BF16),
-            jax.ShapeDtypeStruct(w_out.shape, BF16),
             jax.ShapeDtypeStruct((8, LANES), F32),
         ],
-        scratch_shapes=[pltpu.VMEM((stream, LANES), F32), pltpu.VMEM(w_out.shape, F32)],
+        scratch_shapes=[pltpu.VMEM((stream, LANES), F32)],
         compiler_params=pltpu.CompilerParams(vmem_limit_bytes=ROOM),
         cost_estimate=pl.CostEstimate(flops=3 * 10**10, bytes_accessed=2**25, transcendentals=0),
     )(starts, db_all, w_out, q, kv, att, inv, raw, head_gain, cosine, sine)
@@ -1524,10 +1520,12 @@
         d_branch, [(WHOLE, down_grad)], n_ctx, n_wa, True, 5, PairSum(gu_grad, gu_other)
     )
     gu_rows = swap(gu_sum)
-    d_qkv, out_w_grad, head_grad = attend_back(
+    out_w_grad = t_mm(att, db_all).astype(BF16)
+    out_w_other = lax.ppermute(out_w_grad, "dp", swap_dp)
+    d_qkv, head_grad = attend_back(
         doc_starts, db_all, w_out, q_b, kv_b, att, inv, raw, head_gain, cosine, sine
     )
-    out_w_other = lax.ppermute(out_w_grad, "dp", swap_dp)
+    out_w_other, d_qkv = lax.optimization_barrier((out_w_other, d_qkv))
     qkv_grad = t_mm(n1_all, d_qkv).astype(BF16).reshape(n, 2, half, 2 * LANES)
     qkv_other = lax.ppermute(
         lax.dynamic_index_in_dim(qkv_grad, 1 - dp, 1, keepdims=False), "dp", swap_dp
@@ -1553,7 +1551,7 @@
         True,
         6,
     )
-    out_w_other, gu_others, input_grad = lax.optimization_barrier((out_w_other, gu_others, input_grad))
+    gu_others, input_grad = lax.optimization_barrier((gu_others, input_grad))
     gate_grad, up_grad, gu_sums = unpack_pair(gu_rows, gu_others, w_gate, w_up)
     q_grad, k_grad, v_grad, attn_sums, head_sums = unpack_attn(
         qkv_rows, qkv_others, w_query, w_key, w_value

time: 580 us -> 581 us (level)
  transfers between devices with their start and end apart: 8 -> 8, of which waited for: 1 -> 1; matrix products, arithmetic and copies ran while one was open for 3% -> 4% of each run, Pallas kernels for 60% -> 59%
where the time goes in v8:
time: 581 us; the launch traced here: 575 us
  Pallas kernels  505 us (87%)
  between operations  14.5 us (2%)
  starting transfers between devices  12.8 us (2%)
  local copies, waits for them, and re-layouts  11.9 us (2%)
  other arithmetic  11.1 us (2%)
  matrix products  11.1 us (2%)
  waiting for transfers between devices  8.7 us (1%)
    pallas_call x3, Pallas kernels, scatter_tokens(): pl.pallas_call(partial(scatter_kernel, n_ctx, n_wa, by_position, turned,...  221 us
    pallas_call x3, Pallas kernels, gather_tokens(): pl.pallas_call(partial(gather_kernel, n_ctx, n_wa, by_position, kinds, si...  179 us
    pallas_call x1, Pallas kernels, attend_back(): pl.pallas_call(attend_back_kernel, grid=(stream // bq,), in_specs=[pl.Blo...  34.4 us
    pallas_call x1, Pallas kernels, ffn(): pl.pallas_call(ffn_kernel, grid=(stream // bt,), in_specs=[rows(width), r...  32.5 us
    pallas_call x1, Pallas kernels, attend(): pl.pallas_call(attend_kernel, grid=(stream // bq,), in_specs=[pl.BlockSpe...  28.6 us
  transfers between devices with their start and end apart: 8, of which 1 were waited for; matrix products, arithmetic and copies ran while one was open for 4% of the time, Pallas kernels for 59%

profile of v8, /device:TPU:0, one launch (start us, length us, event | category | flops | bytes accessed | tf_op | source)
XLA Modules:
  0.0 575.1 jit_solution(2294674625126403133)
XLA Ops:
  7.2 0.0 all-gather.2.cloned.1.call-start
  7.2 0.8 fusion.8
  8.0 0.6 reshape.53.gains_ref
  8.6 2.1 shard_map.255.refs_0_
  10.7 62.5 %shard_map.256 = (bf16[2048,2048]{1,0:T(8,128)(2,1)}, bf16[16,80,256]{2,1,0:T(8,128)(2,1)}, bf16[16,80,256]{2,1,0:T(8,128)(2,1)}, bf16[16,64,1024]{2,1,0:T(8,128)(2,1)}) custom-call(bf16[128,2048]{1,0:T(8,128)(2,1)} %bitcast.41, bf16[16,80,256]{2,1,0:T(8,128)(2,1)} %shard_map.255.refs_0_, bf16[128,8192]{1,0:T(8,128)(2,1)} %gate_w.1, bf16[128,8192]{1,0:T(8,128)(2,1)} %up_w.1), custom_call_target="tpu_custom_call" | custom-call | flops 49999998976 | bytes 16777216 | tf_op jit(solution)/shard_map/pallas_call | solution.py:1217
  73.3 0.0 all-gather.2.cloned.1.call-update
  73.3 3.7 all-to-all-start
  77.0 0.0 reduce-scatter.2.cloned.1.call-start
  77.1 0.9 slice_convert_fusion
  78.0 0.2 copy.31
  78.2 0.1 fusion.12
  78.2 0.1 reshape.54
  78.3 0.1 reshape.55
  78.4 0.6 pad_maximum_fusion.1
  79.0 0.6 fusion.11
  79.6 28.6 %shard_map.257 = (bf16[2048,2048]{1,0:T(8,128)(2,1)}, f32[2048,256]{1,0:T(8,128)}, bf16[2048,128]{1,0:T(8,128)(2,1)}, bf16[2048,128]{1,0:T(8,128)(2,1)}, bf16[20...) custom-call(s32[1,8]{1,0:T(1,128)} %starts.3, bf16[2048,2048]{1,0:T(8,128)(2,1)} %get-tuple-element.63.x_ref, ...), custom_call_target="tpu_custom_call" | custom-call | flops 20000000000 | bytes 33554432 | tf_op jit(solution)/shard_map/pallas_call | solution.py:480
  108.3 83.7 %shard_map.258 = (f32[128,2048]{1,0:T(8,128)}, bf16[128,2048]{1,0:T(8,128)(2,1)}) custom-call(bf16[2048,128]{1,0:T(8,128)(2,1)} %get-tuple-element.66.left_ref.att_ref, bf16[128,2048]{1,0:T(8,128)(2,1)} %w_out_ref.1, bf16[128,2048]{1,0:T(8,128)(2,1)} %bitcast.42, f32[1,2048]{1,0:T(1,128)} %bitcast.37), custom_call_target="tpu_custom_call" | custom-call | flops 49999998976 | bytes 16777216 | tf_op jit(solution)/shard_map/pallas_call | solution.py:1413
  192.0 0.0 all-to-all-done.refs_0_.own_ref
  192.0 1.4 copy-done.7
  193.4 54.3 %shard_map.259 = (bf16[2048,2048]{1,0:T(8,128)(2,1)}, bf16[16,64,1024]{2,1,0:T(8,128)(2,1)}) custom-call(bf16[128,2048]{1,0:T(8,128)(2,1)} %get-tuple-element.68.own_ref, bf16[16,64,1024]{2,1,0:T(8,128)(2,1)} %copy-done.7), custom_call_target="tpu_custom_call" | custom-call | flops 49999998976 | bytes 16777216 | tf_op jit(solution)/shard_map/pallas_call | solution.py:1217
  247.7 0.0 all-gather.2.cloned.1.call-done.dy_ref.refs_4_
  247.8 32.5 %shard_map.260 = (bf16[2048,512]{1,0:T(8,128)(2,1)}, bf16[2048,1024]{1,0:T(8,128)(2,1)}, bf16[2048,1024]{1,0:T(8,128)(2,1)}, bf16[2048,1024]{1,0:T(8,128)(2,1)}) custom-call(bf16[2048,2048]{1,0:T(8,128)(2,1)} %get-tuple-element.70.n2_ref, bf16[2048,2048]{1,0:T(8,128)(2,1)} %all-gather.2.cloned.1.call-done.dy_ref.refs_4_, bf16[16,64,1024]{2,1,0:T(8,128)(2,1)} %copy-done.7, ...), custom_call_target="tpu_custom_call" | custom-call | flops 21474836480 | bytes 33554432 | tf_op jit(solution)/shard_map/pallas_call | solution.py:667
  280.3 67.9 %shard_map.261 = (f32[128,2048]{1,0:T(8,128)}, bf16[128,2048]{1,0:T(8,128)(2,1)}, bf16[16,64,1024]{2,1,0:T(8,128)(2,1)}, bf16[2048,2048]{1,0:T(8,128)(2,1)}, bf16[512,2048]{1,0:T(8,128)(2,1)}) custom-call(bf16[2048,1024]{1,0:T(8,128)(2,1)} %get-tuple-element.73.left_ref, bf16[2048,1024]{1,0:T(8,128)(2,1)} %get-tuple-element.74.right_ref, ...), custom_call_target="tpu_custom_call" | custom-call | flops 49999998976 | bytes 16777216 | tf_op jit(solution)/shard_map/pallas_call | solution.py:1413
  348.2 0.0 reduce-scatter.2.cloned.1.call-update
  348.2 0.0 copy-start.10
  348.3 62.4 %shard_map.262 = (bf16[2048,2048]{1,0:T(8,128)(2,1)}, bf16[512,2048]{1,0:T(8,128)(2,1)}, bf16[16,64,1024]{2,1,0:T(8,128)(2,1)}) custom-call(bf16[128,2048]{1,0:T(8,128)(2,1)} %get-tuple-element.79.own_ref, bf16[512,2048]{1,0:T(8,128)(2,1)} %get-tuple-element.80.refs_0_, bf16[16,2,64,1024]{3,2,1,0:T(8,128)(2,1)} %bitcast.45, ...), custom_call_target="tpu_custom_call" | custom-call | flops 49999998976 | bytes 16777216 | tf_op jit(solution)/shard_map/pallas_call | solution.py:1217
  410.7 0.0 copy-done.10
  410.7 4.7 convolution_convert_fusion.1
  415.4 1.5 collective-permute-start
  416.9 3.9 all-to-all-start.1
  420.9 34.4 %shard_map.263 = (bf16[2048,256]{1,0:T(8,128)(2,1)}, f32[8,128]{1,0:T(8,128)}) custom-call(s32[1,8]{1,0:T(1,128)} %starts.3, bf16[2048,2048]{1,0:T(8,128)(2,1)} %get-tuple-element.82.db_ref, bf16[128,2048]{1,0:T(8,128)(2,1)} %w_out_ref.1, bf16[2048,128]{1,0:T(8,128)(2,1)} %get-tuple-element.83.q_ref, bf16[2048,128]{1,0:T(8,128)(2,1)} %get-tuple-element.84.kv_ref, ...), custom_call_target="tpu_custom_call" | custom-call | flops 30000001024 | bytes 33554432 | tf_op jit(solution)/shard_map/pallas_call | solution.py:596
  455.3 0.6 collective-permute-start.2
  455.9 0.0 collective-permute-done
  455.9 6.4 %convolution_convert_fusion = bf16[2048,256]{1,0:T(8,128)(2,1)S(1)} fusion(bf16[2048,2048]{1,0:T(8,128)(2,1)} %get-tuple-element.78, bf16[2048,256]{1,0:T(8,128)(2,1)} %get-tuple-element.88.left_ref), kind=kOutput, calls=%fused_computation.1 | convolution fusion | flops 2148007936 | bytes 10485760 | tf_op jit(solution)/shard_map/dot_general | solution.py:1469
  462.3 0.0 copy-start.12
  462.3 1.0 copy-done.12
  463.3 1.5 collective-permute-start.1
  464.9 2.8 convert_add_fusion
  467.7 0.0 collective-permute-done.2
  467.7 0.0 copy-done.14
  467.7 1.1 convert_add_fusion.2
  468.8 8.6 %collective-permute-done.1 = bf16[16,64,256]{2,1,0:T(8,128)(2,1)S(1)} collective-permute-done((bf16[16,64,256]{2,1,0:T(8,128)(2,1)S(1)}, bf16[16,64,256]{2,1,0:T(8,128)(2,1)S(1)}, u32[]{:S(2)}, u32[]{:S(2)}) %collective-permute-start.1) | collective-permute-done | bytes 524320 | tf_op jit(solution)/shard_map/ppermute | solution.py:1530
  477.4 0.0 all-to-all-done.1.own_ref
  477.4 1.4 collective-permute-start.3
  478.9 1.2 fusion
  480.1 0.9 pad_maximum_fusion.refs_3_
  481.0 69.0 %shard_map.264 = (bf16[128,2048]{1,0:T(8,128)(2,1)}, bf16[16,80,256]{2,1,0:T(8,128)(2,1)}, bf16[16,80,256]{2,1,0:T(8,128)(2,1)}) custom-call(bf16[2048,256]{1,0:T(8,128)(2,1)} %get-tuple-element.88.left_ref, bf16[2048,256]{1,0:T(8,128)(2,1)} %get-tuple-element.92.right_ref, bf16[128,2048]{1,0:T(8,128)(2,1)} %bitcast.43, f32[1,2048]{1,0:T(1,128)} %bitcast.36, ...), custom_call_target="tpu_custom_call" | custom-call | flops 49999998976 | bytes 16777216 | tf_op jit(solution)/shard_map/pallas_call | solution.py:1413
  550.0 0.0 copy-done.2
  550.0 0.0 copy-done.5
  550.1 0.0 copy-done.6
  550.1 1.1 copy-done.3
  551.2 1.1 copy-done.4
  552.2 1.4 shard_map.265
  553.6 0.1 reduce_sum.18
  553.7 0.1 fusion.13
  553.8 0.6 fusion.9
  554.4 0.0 collective-permute-done.3.other_ref
  554.4 1.6 copy-done
  556.0 1.6 copy-done.1
  557.6 6.0 %shard_map.266 = (f32[128,8192]{1,0:T(8,128)}, f32[128,8192]{1,0:T(8,128)}, f32[128,128]{1,0:T(8,128)S(1)}) custom-call(bf16[16,64,1024]{2,1,0:T(8,128)(2,1)S(1)} %all-to-all-done.1.own_ref, bf16[16,64,1024]{2,1,0:T(8,128)(2,1)} %collective-permute-done.3.other_ref, bf16[128,8192]{1,0:T(8,128)(2,1)S(1)} %copy-done, bf16[128,8192]{1,0:T(8,128)(2,1)S(1)} %copy-done.1), custom_call_target="tpu_custom_call" | custom-call | tf_op jit(solution)/shard_map/pallas_call | solution.py:786
  563.6 0.1 reduce_sum.19
  563.7 0.5 convert_divide_fusion
  564.2 1.9 fusion.1
  566.2 1.9 copy.33
  (28 shorter events, 0.1 us)
Async XLA Ops:
  7.2 240.6 %all-gather.2.cloned.1.call-start = ((), (), s32[]{:S(2)}) async-start(), calls=%async_computation.3 | async-start | bytes 8912896 | tf_op jit(solution)/shard_map/all_gather | solution.py:1490
  73.3 118.7 %all-to-all-start = ((bf16[16,64,1024]{2,1,0:T(8,128)(2,1)}), bf16[16,64,1024]{2,1,0:T(8,128)(2,1)S(1)}, u32[]{:S(2)}, u32[]{:S(2)}) async-start(bf16[16,64,1024]{2,1,0:T(8,128)(2,1)} %get-tuple-element.69), calls=%async_computation | async-start | bytes 4194304 | tf_op jit(solution)/shard_map/all_to_all | solution.py:1472
  77.0 487.2 %reduce-scatter.2.cloned.1.call-start = ((), (), s32[]{:S(2)}) async-start(), calls=%async_computation.4 | async-start | bytes 8912896 | tf_op jit(solution)/shard_map/reduce_scatter | solution.py:1517
  192.0 1.4 copy-start.7
  348.2 62.4 %copy-start.10 = (bf16[2048,128]{1,0:T(8,128)(2,1)S(1)}, bf16[2048,128]{1,0:T(8,128)(2,1)}, u32[]{:S(2)}) copy-start(bf16[2048,128]{1,0:T(8,128)(2,1)} %get-tuple-element.66.left_ref.att_ref) | copy-start | bytes 1572868
  415.4 40.5 %collective-permute-start = (bf16[128,2048]{1,0:T(8,128)(2,1)S(1)}, bf16[128,2048]{1,0:T(8,128)(2,1)S(1)}, u32[]{:S(2)}, u32[]{:S(2)}) collective-permute-start(bf16[128,2048]{1,0:T(8,128)(2,1)S(1)} %convolution_convert_fusion.1), channel_id=1, source_target_pairs={{0,16},{16,0},{1,17},{17,1},{2,18},{18,2},{3,19},{19,3},{4,20},{20... | collective-permute-start | bytes 1572872 | tf_op jit(solution)/shard_map/ppermute | solution.py:1524
  416.9 60.5 %all-to-all-start.1 = ((bf16[16,64,1024]{2,1,0:T(8,128)(2,1)}), bf16[16,64,1024]{2,1,0:T(8,128)(2,1)S(1)}, u32[]{:S(2)}, u32[]{:S(2)}) async-start(bf16[16,64,1024]{2,1,0:T(8,128)(2,1)} %get-tuple-element.90), calls=%async_computation.2 | async-start | bytes 4194304 | tf_op jit(solution)/shard_map/all_to_all | solution.py:1472
  455.3 12.4 %collective-permute-start.2 = (f32[8,128]{1,0:T(8,128)}, f32[8,128]{1,0:T(8,128)S(1)}, u32[]{:S(2)}, u32[]{:S(2)}) collective-permute-start(f32[8,128]{1,0:T(8,128)} %get-tuple-element.89), channel_id=1, source_target_pairs={{0,16},{16,0},{1,17},{17,1},{2,18},{18,2},{3,19},{19,3},{4,20},{20... | collective-permute-start | bytes 12296 | tf_op jit(solution)/shard_map/ppermute | solution.py:1533
  455.9 6.4 %copy-start.13 = (bf16[128,2048]{1,0:T(8,128)(2,1)}, bf16[128,2048]{1,0:T(8,128)(2,1)S(1)}, u32[]{:S(2)}) copy-start(bf16[128,2048]{1,0:T(8,128)(2,1)S(1)} %collective-permute-done) | copy-start | bytes 1572868
  455.9 9.0 %copy-start.8 = (bf16[512,2048]{1,0:T(8,128)(2,1)S(1)}, bf16[512,2048]{1,0:T(8,128)(2,1)}, u32[]{:S(2)}) copy-start(bf16[512,2048]{1,0:T(8,128)(2,1)} %get-tuple-element.80.refs_0_) | copy-start | bytes 6291460
  455.9 9.0 %copy-start.9 = (bf16[512,2048]{1,0:T(8,128)(2,1)S(1)}, bf16[512,2048]{1,0:T(8,128)(2,1)}, u32[]{:S(2)}) copy-start(bf16[512,2048]{1,0:T(8,128)(2,1)} %get-tuple-element.110) | copy-start | bytes 6291460
  462.3 1.0 copy-start.12
  463.3 14.1 %collective-permute-start.1 = (bf16[16,64,256]{2,1,0:T(8,128)(2,1)S(1)}, bf16[16,64,256]{2,1,0:T(8,128)(2,1)S(1)}, u32[]{:S(2)}, u32[]{:S(2)}) collective-permute-start(bf16[16,64,256]{2,1,0:T(8,128)(2,1)S(1)} %dynamic-slice_bitcast_fusion), channel_id=1, source_target_pairs={{0,16},{16,0},{1,17},{17,1},{2,18},{18,2},{3,19},{19,3},{4,20},{20... | collective-permute-start | bytes 1572872 | tf_op jit(solution)/shard_map/ppermute | solution.py:1530
  464.8 2.8 copy-start.15
  464.8 2.8 copy-start.14
  477.4 77.0 %collective-permute-start.3 = (bf16[16,64,1024]{2,1,0:T(8,128)(2,1)S(1)}, bf16[16,64,1024]{2,1,0:T(8,128)(2,1)}, u32[]{:S(2)}, u32[]{:S(2)}) collective-permute-start(bf16[16,64,1024]{2,1,0:T(8,128)(2,1)S(1)} %all-to-all-done.1.own_ref), channel_id=1, source_target_pairs={{0,16},{16,0},{1,17},{17,1},{2,18},{18,2},{3,19},{19,3},{4,20},{20... | collective-permute-start | bytes 6291464 | tf_op jit(solution)/shard_map/ppermute | solution.py:1535
  481.0 69.1 %copy-start.2 = (bf16[128,2048]{1,0:T(8,128)(2,1)S(1)}, bf16[128,2048]{1,0:T(8,128)(2,1)}, u32[]{:S(2)}) copy-start(bf16[128,2048]{1,0:T(8,128)(2,1)} %wq_ref.1) | copy-start | bytes 1572868
  481.0 69.1 %copy-start.5 = (bf16[128,512]{1,0:T(8,128)(2,1)S(1)}, bf16[128,512]{1,0:T(8,128)(2,1)}, u32[]{:S(2)}) copy-start(bf16[128,512]{1,0:T(8,128)(2,1)} %wk_ref.1) | copy-start | bytes 393220
  481.0 69.1 %copy-start.6 = (bf16[128,512]{1,0:T(8,128)(2,1)S(1)}, bf16[128,512]{1,0:T(8,128)(2,1)}, u32[]{:S(2)}) copy-start(bf16[128,512]{1,0:T(8,128)(2,1)} %wv_ref.1) | copy-start | bytes 393220
  550.1 1.1 copy-start.3
  551.2 1.1 copy-start.4
  554.4 1.6 copy-start
  556.0 1.6 copy-start.1
  557.6 6.1 %copy-start.16 = (bf16[128]{0:T(256)(128)(2,1)S(1)}, bf16[128]{0:T(256)(128)(2,1)}, u32[]{:S(2)}) copy-start(bf16[128]{0:T(256)(128)(2,1)} %param.26) | copy-start | bytes 772
  557.6 6.1 %copy-start.17 = (bf16[128]{0:T(256)(128)(2,1)S(1)}, bf16[128]{0:T(256)(128)(2,1)}, u32[]{:S(2)}) copy-start(bf16[128]{0:T(256)(128)(2,1)} %param.19) | copy-start | bytes 772
  557.6 6.7 %copy-start.11 = (f32[128,2048]{1,0:T(8,128)S(1)}, f32[128,2048]{1,0:T(8,128)}, u32[]{:S(2)}) copy-start(f32[128,2048]{1,0:T(8,128)} %get-tuple-element.67.refs_0_) | copy-start | bytes 3145732
Sparse Core Ops, SparseCore 0:
  73.4 128.6 all-gather.1
  348.4 132.9 reduce-scatter.1
